TPU v7x, 512 devices: a whole 4x8x8 slice. The times are simulated.
512 devices in a mesh: rows: 64 (over x, z, core), cols: 8 (over y).
Axes of the slice: x: 4, y: 8, z: 8, core: 2. Of those that a mesh axis runs over, the one named last changes fastest.
Arguments:
- coeffs: bfloat16 [16384, 2048], P('rows'), may hold values from -0.5 to 0.5
- rotation: float32 [2048, 2048], P('rows', 'cols'), may hold values from -6 to 6
- phase_ops: bfloat16 [2, 128, 5, 128, 128], P(None, 'rows'), as said below
- block_links: int32 [128, 5], P('rows'), may hold values from 0 to 1, as said below
- atom_size: int32 [128], P('rows'), may hold values from 1 to 128, 12288 in all
Outputs:
- rotated: float32 [2048, 2048], P('rows', 'cols')
- phase_cos: float32 [2048, 2048], P('rows', 'cols')
- phase_sin: float32 [2048, 2048], P('rows', 'cols')
- orbitals: bfloat16 [16384, 2048], P('rows', 'cols')
Inputs may be any that keep to these rules, and one draw needn't show every extreme that they name: block_links[b, 2 + o] equals block_links[(b + o) mod 128, 2 - o], and block_links[b, 2] is 1. Each phase operator is symmetric as a 16384 x 16384 matrix: phase_ops[p, b, 2 + o] is the transpose of phase_ops[p, (b + o) mod 128, 2 - o].
All inputs are finite; a program needn't handle non-finite values. No bound on the sum of `atom_size` on one device may be relied on, other than what follows from the above.
Results may differ from a plain program's by a relative error of at most 0.0049.
Values may be sent and summed in bfloat16 or wider, within the bound.
No kernel may reach another device: no remote copies, remote signals or barrier semaphores. Data moves between devices by JAX's collectives and lax.ppermute only.
A program may use at most 64 MiB of HBM per device.

v0:
```python
import math

import jax
import jax.numpy as jnp
from jax import lax
from jax.sharding import PartitionSpec as P

highest = lax.Precision.HIGHEST


def padded_2(cells, sides, width):
    for axis, dim in sides:
        count = lax.axis_size(axis)
        head = lax.slice_in_dim(cells, 0, width, axis=dim)
        tail = lax.slice_in_dim(cells, cells.shape[dim] - width, cells.shape[dim], axis=dim)
        cells = jnp.concatenate(
            [
                lax.ppermute(tail, axis, [(i, (i + 1) % count) for i in range(count)]),
                cells,
                lax.ppermute(head, axis, [((i + 1) % count, i) for i in range(count)]),
            ],
            axis=dim,
        )
    return cells


def mat_product(left, right):
    return jnp.dot(left, right, precision=highest, preferred_element_type=jnp.float32)


def row_panel(block):
    return lax.all_gather(block, "cols", axis=1, tiled=True)


def column_panel(block):
    return lax.all_gather(block, "rows", axis=0, tiled=True)


def on_device(coeffs, rotation, phase_ops, block_links, atom_size):
    rows_dev, orbital_count = coeffs.shape
    blocks_dev = phase_ops.shape[1]
    span_blocks = phase_ops.shape[2]
    block_size = phase_ops.shape[3]
    reach_blocks = (span_blocks - 1) // 2
    row_count = orbital_count // lax.axis_size("rows")
    col_count = orbital_count // lax.axis_size("cols")
    row_start = lax.axis_index("rows") * row_count
    col_start = lax.axis_index("cols") * col_count
    within = lax.broadcasted_iota(jnp.int32, (blocks_dev, block_size), 1)
    live_rows = (within < atom_size[:, None]).reshape(rows_dev)
    masked = jnp.where(live_rows[:, None], coeffs, jnp.zeros_like(coeffs))
    own_cols = lax.dynamic_slice_in_dim(masked, col_start, col_count, 1)
    padded = padded_2(own_cols, (("rows", 0),), reach_blocks * block_size)
    stacked = jnp.stack(
        [
            padded[offset * block_size : (offset + blocks_dev) * block_size].reshape(
                blocks_dev, block_size, col_count
            )
            for offset in range(span_blocks)
        ],
        axis=1,
    )
    gated = phase_ops * block_links[None, :, :, None, None].astype(jnp.bfloat16)
    applied = jnp.einsum("pbtij,btjk->pbik", gated, stacked, preferred_element_type=jnp.float32)
    applied = applied.reshape(2, rows_dev, col_count).astype(jnp.bfloat16)
    scale_factor = 0.125 / math.sqrt(orbital_count)
    product = jnp.einsum("ni,pnj->ipj", masked, applied, preferred_element_type=jnp.float32)
    z_block = lax.psum_scatter(
        product.reshape(row_count * lax.axis_size("rows"), 2 * col_count),
        "rows",
        scatter_dimension=0,
        tiled=True,
    )
    partial_value = jnp.einsum("nj,pnj->pj", own_cols, applied, preferred_element_type=jnp.float32)
    spread = lax.dynamic_update_slice_in_dim(
        jnp.zeros((2, orbital_count), jnp.float32), partial_value, col_start, 1
    )
    diagonal = lax.psum(spread, ("rows", "cols"))
    diag_rows = lax.dynamic_slice_in_dim(diagonal, row_start, row_count, 1)
    diag_cols = lax.dynamic_slice_in_dim(diagonal, col_start, col_count, 1)
    cos_part = z_block[:, :col_count] * (diag_cols[0][None, :] - diag_rows[0][:, None])
    sin_part = z_block[:, col_count:] * (diag_cols[1][None, :] - diag_rows[1][:, None])
    gen_block = (cos_part + sin_part) * scale_factor
    panels = column_panel(jnp.concatenate([gen_block, z_block], axis=1))
    gen_cols = panels[:, :col_count]
    z_cols = panels[:, col_count:]
    row_stack = row_panel(jnp.concatenate([gen_block, rotation], axis=0))
    gen_rows = row_stack[:row_count]
    rot_rows = row_stack[row_count:]
    square_block = mat_product(gen_rows, gen_cols)
    square_cols = column_panel(square_block)
    square_rows = row_panel(square_block)
    index_down = lax.broadcasted_iota(jnp.int32, (orbital_count, col_count), 0)
    index_across = lax.broadcasted_iota(jnp.int32, (orbital_count, col_count), 1)
    ident_cols = (index_down == index_across + col_start).astype(jnp.float32)
    row_down = lax.broadcasted_iota(jnp.int32, (row_count, orbital_count), 0)
    row_across = lax.broadcasted_iota(jnp.int32, (row_count, orbital_count), 1)
    ident_rows = (row_down + row_start == row_across).astype(jnp.float32)
    forward_cols = ident_cols + gen_cols + 0.5 * square_cols
    backward_rows = ident_rows - gen_rows + 0.5 * square_rows
    half_cos = mat_product(backward_rows, z_cols[:, :col_count])
    half_sin = mat_product(backward_rows, z_cols[:, col_count:])
    half_rows = row_panel(jnp.concatenate([half_cos, half_sin], axis=0))
    phase_cos = mat_product(half_rows[:row_count], forward_cols)
    phase_sin = mat_product(half_rows[row_count:], forward_cols)
    rotated = mat_product(rot_rows, forward_cols)
    orbitals = jnp.dot(
        masked, forward_cols.astype(jnp.bfloat16), preferred_element_type=jnp.float32
    ).astype(jnp.bfloat16)
    return (rotated, phase_cos, phase_sin, orbitals)


def solution(mesh):
    placed = (
        P("rows", None),
        P("rows", "cols"),
        P(None, "rows", None, None, None),
        P("rows", None),
        P("rows"),
    )
    return jax.shard_map(
        on_device,
        mesh=mesh,
        in_specs=placed,
        out_specs=(P("rows", "cols"), P("rows", "cols"), P("rows", "cols"), P("rows", "cols")),
        check_vma=False,
    )
```

profile of v0, /device:TPU:1, one launch (start us, length us, event | category | flops | bytes accessed | tf_op | source)
XLA Modules:
  0.0 371.4 jit_solution(5924171254508570296)
XLA Ops:
  7.2 0.7 compare_bitcast_fusion
  8.0 1.4 broadcast_select_fusion
  9.4 5.4 %collective-permute-start = (bf16[256,256]{1,0:T(8,128)(2,1)S(1)}, bf16[256,256]{1,0:T(8,128)(2,1)S(1)}, u32[]{:S(2)}, u32[]{:S(2)}) collective-permute-start(bf16[256,256]{1,0:T(8,128)(2,1)S(1)} %get-tuple-element.5), channel_id=1, source_target_pairs={{0,8},{8,16},{16,24},{24,32},{32,40},{40,48},{48,56},{56,64},{64,7... | collective-permute-start | bytes 393224 | tf_op jit(solution)/shard_map/ppermute | solution.py:18
  14.8 5.3 %collective-permute-start.1 = (bf16[256,256]{1,0:T(8,128)(2,1)S(1)}, bf16[256,256]{1,0:T(8,128)(2,1)S(1)}, u32[]{:S(2)}, u32[]{:S(2)}) collective-permute-start(bf16[256,256]{1,0:T(8,128)(2,1)S(1)} %get-tuple-element.5), channel_id=1, source_target_pairs={{8,0},{16,8},{24,16},{32,24},{40,32},{48,40},{56,48},{64,56},{72,6... | collective-permute-start | bytes 393224 | tf_op jit(solution)/shard_map/ppermute | solution.py:20
  20.2 0.9 collective-permute-done.1
  21.2 0.4 fusion.7
  21.8 2.7 fusion.20
  24.7 107.1 %psum.7 = f32[2,2048]{1,0:T(2,128)S(1)} all-reduce(f32[2,2048]{1,0:T(2,128)S(1)} %bitcast_dynamic-update-slice_fusion), channel_id=1, replica_groups=mesh['rows'=64,'cols'=8] {'rows','cols'}, use_global_device_ids=true, to_apply=%region_1.2 | all-reduce | flops 4096 | bytes 32768 | tf_op jit(solution)/shard_map/psum | solution.py:78
  132.0 44.9 %reduce-scatter.2.cloned.1.call-done = f32[32,512]{1,0:T(8,128)} async-done(((f32[2048,512]{1,0:T(8,128)}), f32[32,512]{1,0:T(8,128)}) %reduce-scatter.2.cloned.1.call-update) | async-done | bytes 65552 | tf_op jit(solution)/shard_map/reduce_scatter | solution.py:68
  176.9 0.9 fusion.19
  177.7 1.5 pad_maximum_fusion.2
  179.3 20.4 %all_gather.15 = f32[64,2048]{1,0:T(8,128)S(1)} all-gather(f32[64,256]{1,0:T(8,128)S(1)} %pad_maximum_fusion.3), channel_id=1, replica_groups=mesh['rows'=64,'cols'=8] {'cols'}, dimensions={1}, use_global_device_ids=true | all-gather | bytes 589824 | tf_op jit(solution)/shard_map/all_gather | solution.py:32
  199.7 72.1 %all-gather.3.cloned.1.call-done = f32[2048,768]{1,0:T(8,128)} async-done(((f32[32,768]{1,0:T(8,128)}), f32[2048,768]{1,0:T(8,128)}) %all-gather.3.cloned.1.call-update) | async-done | bytes 6291472 | tf_op jit(solution)/shard_map/all_gather | solution.py:36
  271.8 3.3 fusion.4
  275.2 20.5 %all_gather.18 = f32[32,2048]{1,0:T(8,128)S(1)} all-gather(f32[32,256]{1,0:T(8,128)} %fusion.4), channel_id=1, replica_groups=mesh['rows'=64,'cols'=8] {'cols'}, dimensions={1}, use_global_device_ids=true | all-gather | bytes 294912 | tf_op jit(solution)/shard_map/all_gather | solution.py:32
  295.7 2.8 fusion
  298.5 2.8 fusion.2
  301.3 20.4 %all_gather.19 = f32[64,2048]{1,0:T(8,128)S(1)} all-gather(f32[64,256]{1,0:T(8,128)S(1)} %pad_maximum_fusion.4), channel_id=1, replica_groups=mesh['rows'=64,'cols'=8] {'cols'}, dimensions={1}, use_global_device_ids=true | all-gather | bytes 589824 | tf_op jit(solution)/shard_map/all_gather | solution.py:32
  321.7 34.3 %all-gather.5.cloned.1.call-done = f32[2048,256]{1,0:T(8,128)} async-done(((f32[32,256]{1,0:T(8,128)}), f32[2048,256]{1,0:T(8,128)}) %all-gather.5.cloned.1.call-update) | async-done | bytes 2097168 | tf_op jit(solution)/shard_map/all_gather | solution.py:36
  356.0 2.6 multiply_add_fusion
  358.6 1.1 convolution_convert_fusion
  359.7 1.7 fusion.15
  361.4 1.7 fusion.11
  363.2 1.7 fusion.13
  (33 shorter events, 0.7 us)
Async XLA Ops:
  7.2 13.0 %copy-start.2 = (s32[2,5]{1,0:T(2,128)S(1)}, s32[2,5]{1,0:T(2,128)}, u32[]{:S(2)}) copy-start(s32[2,5]{1,0:T(2,128)} %param.8) | copy-start | bytes 124
  7.2 169.7 %reduce-scatter.2.cloned.1.call-start = ((), (), s32[]{:S(2)}) async-start(), calls=%async_computation.1 | async-start | bytes 4259840 | tf_op jit(solution)/shard_map/reduce_scatter | solution.py:68
  8.0 13.3 %copy-start.1 = (bf16[2,2,5,128,128]{4,3,2,1,0:T(8,128)(2,1)S(1)}, bf16[2,2,5,128,128]{4,3,2,1,0:T(8,128)(2,1)}, u32[]{:S(2)}) copy-start(bf16[2,2,5,128,128]{4,3,2,1,0:T(8,128)(2,1)} %param.7) | copy-start | bytes 1966084
  9.4 10.7 %collective-permute-start = (bf16[256,256]{1,0:T(8,128)(2,1)S(1)}, bf16[256,256]{1,0:T(8,128)(2,1)S(1)}, u32[]{:S(2)}, u32[]{:S(2)}) collective-permute-start(bf16[256,256]{1,0:T(8,128)(2,1)S(1)} %get-tuple-element.5), channel_id=1, source_target_pairs={{0,8},{8,16},{16,24},{24,32},{32,40},{40,48},{48,56},{56,64},{64,7... | collective-permute-start | bytes 393224 | tf_op jit(solution)/shard_map/ppermute | solution.py:18
  14.8 6.3 %collective-permute-start.1 = (bf16[256,256]{1,0:T(8,128)(2,1)S(1)}, bf16[256,256]{1,0:T(8,128)(2,1)S(1)}, u32[]{:S(2)}, u32[]{:S(2)}) collective-permute-start(bf16[256,256]{1,0:T(8,128)(2,1)S(1)} %get-tuple-element.5), channel_id=1, source_target_pairs={{8,0},{16,8},{24,16},{32,24},{40,32},{48,40},{56,48},{64,56},{72,6... | collective-permute-start | bytes 393224 | tf_op jit(solution)/shard_map/ppermute | solution.py:20
  24.5 154.8 %copy-start = (f32[32,256]{1,0:T(8,128)S(1)}, f32[32,256]{1,0:T(8,128)}, u32[]{:S(2)}) copy-start(f32[32,256]{1,0:T(8,128)} %param.6) | copy-start | bytes 98308
  24.6 247.3 %all-gather.3.cloned.1.call-start = ((), (), s32[]{:S(2)}) async-start(), calls=%async_computation.2 | async-start | bytes 6389760 | tf_op jit(solution)/shard_map/all_gather | solution.py:36
  179.2 176.7 %all-gather.5.cloned.1.call-start = ((), (), s32[]{:S(2)}) async-start(), calls=%async_computation.3 | async-start | bytes 2129920 | tf_op jit(solution)/shard_map/all_gather | solution.py:36
Sparse Core Ops, SparseCore 0:
  24.7 152.1 reduce-scatter.1
  181.3 90.4 all-gather.2
  276.3 79.6 all-gather.4
where the time goes:
time: 372 us; the launch traced here: 371 us
  blocking collectives  168 us (45%)
  waiting for transfers between devices  152 us (41%)
  matrix products  18.2 us (5%)
  between operations  14 us (4%)
  starting transfers between devices  10.8 us (3%)
  other arithmetic  7.29 us (2%)
    psum x1, blocking collectives, on_device(): diagonal = lax.psum(spread, ('rows', 'cols'))  107 us
    all_gather x2, waiting for transfers between devices, column_panel(): return lax.all_gather(block, 'rows', axis=0, tiled=True)  106 us
    all_gather x3, blocking collectives, row_panel(): return lax.all_gather(block, 'cols', axis=1, tiled=True)  61.3 us
    reduce_scatter x1, waiting for transfers between devices, on_device(): lax.psum_scatter(product.reshape(row_count * lax.axis_size('rows'), 2 * c...  44.9 us
    dot_general x6, matrix products, mat_product(): jnp.dot(left, right, precision=highest, preferred_element_type=jnp.float32)  14 us
  transfers between devices with their start and end apart: 5, of which 4 were waited for; matrix products, arithmetic and copies ran while one was open for 2% of the time, Pallas kernels for 0%

commit v1 on v0

v1 whole, which is shorter than its diff:
```python
import math

import jax
import jax.numpy as jnp
from jax import lax
from jax.sharding import PartitionSpec as P

bf16 = jnp.bfloat16
f32 = jnp.float32

XS, ZS, CORES = 4, 8, 2


def row_index(x, z, core):
    return (x * ZS + z) * CORES + core


x_groups = [[row_index(x, z, k) for x in range(XS)] for z in range(ZS) for k in range(CORES)]
z_groups = [[row_index(x, z, k) for z in range(ZS)] for x in range(XS) for k in range(CORES)]
xz_groups = [
    [row_index(x, z, k) for x in range(XS) for z in range(ZS)] for k in range(CORES)
]


def swap(cells, axis, groups=None):
    return lax.all_to_all(cells, axis, 0, 0, tiled=True, axis_index_groups=groups)


def spread(cells, count, axis, groups=None):
    return swap(jnp.broadcast_to(cells[None], (count,) + cells.shape), axis, groups)


def other_core(cells):
    count = lax.axis_size("rows")
    return lax.ppermute(cells, "rows", [(i, i ^ 1) for i in range(count)])


def small_product(left, right):
    return jnp.dot(left, right, preferred_element_type=f32)


def three_parts(values):
    parts = []
    for _ in range(3):
        part = lax.reduce_precision(values, 8, 7)
        parts.append(part.astype(bf16))
        values = values - part
    return jnp.stack(parts)


def on_device(coeffs, rotation, phase_ops, block_links, atom_size):
    rows_dev, orbital_count = coeffs.shape
    blocks_dev = phase_ops.shape[1]
    span_blocks = phase_ops.shape[2]
    block_size = phase_ops.shape[3]
    reach_blocks = (span_blocks - 1) // 2
    rows_axis = lax.axis_size("rows")
    cols_axis = lax.axis_size("cols")
    row_count = orbital_count // rows_axis
    col_count = orbital_count // cols_axis
    both = 2 * col_count
    row_start = lax.axis_index("rows") * row_count
    col_start = lax.axis_index("cols") * col_count
    core = lax.axis_index("rows") % CORES
    scale_factor = 0.125 / math.sqrt(orbital_count)

    within = lax.broadcasted_iota(jnp.int32, (blocks_dev, block_size), 1)
    live_rows = (within < atom_size[:, None]).reshape(rows_dev)
    raw_cols = lax.dynamic_slice_in_dim(coeffs, col_start, col_count, 1)
    own_cols = jnp.where(live_rows[:, None], raw_cols, jnp.zeros_like(raw_cols))
    width = reach_blocks * block_size
    up = [(i, (i + 1) % rows_axis) for i in range(rows_axis)]
    down = [((i + 1) % rows_axis, i) for i in range(rows_axis)]
    padded = jnp.concatenate(
        [
            lax.ppermute(own_cols[rows_dev - width :], "rows", up),
            own_cols,
            lax.ppermute(own_cols[:width], "rows", down),
        ],
        axis=0,
    )
    masked = jnp.where(live_rows[:, None], coeffs, jnp.zeros_like(coeffs))
    stacked = jnp.stack(
        [
            padded[offset * block_size : (offset + blocks_dev) * block_size].reshape(
                blocks_dev, block_size, col_count
            )
            for offset in range(span_blocks)
        ],
        axis=1,
    )
    gated = phase_ops * block_links[None, :, :, None, None].astype(bf16)
    applied = jnp.einsum("pbtij,btjk->pbik", gated, stacked, preferred_element_type=f32)
    applied = applied.reshape(2, rows_dev, col_count).astype(bf16)

    product = jnp.einsum("ni,pnj->ipj", masked, applied, preferred_element_type=f32)
    product = product.reshape(XS, ZS, CORES, row_count, both)
    own_half = lax.dynamic_index_in_dim(product, core, 2, keepdims=False)
    far_half = lax.dynamic_index_in_dim(product, 1 - core, 2, keepdims=False)
    diag = jnp.einsum("nj,pnj->pj", own_cols, applied, preferred_element_type=f32)

    def diag_rows(values):
        return jnp.pad(three_parts(values.reshape(both)), ((0, 13), (0, 0)))

    def diag_sum(cells):
        return jnp.sum(cells[:, :3].astype(f32), axis=(0, 1))

    chip_rows = ZS * row_count
    sent = jnp.concatenate(
        [far_half.astype(bf16).reshape(XS * chip_rows, both), diag_rows(diag)], axis=0
    )
    got = other_core(sent)
    diag = diag.reshape(both) + diag_sum(got[None, XS * chip_rows :])
    half = own_half.reshape(XS, chip_rows, both) + got[: XS * chip_rows].reshape(
        XS, chip_rows, both
    ).astype(f32)

    def with_diag(cells, values):
        tail = jnp.broadcast_to(diag_rows(values)[None], (cells.shape[0], 16, both))
        return jnp.concatenate([cells.astype(bf16), tail], axis=1)

    got = swap(with_diag(half, diag), "rows", x_groups)
    diag = diag_sum(got[:, chip_rows:])
    chip = jnp.sum(got[:, :chip_rows].astype(f32), axis=0).reshape(ZS, row_count, both)
    got = swap(with_diag(chip, diag), "rows", z_groups)
    diag = diag_sum(got[:, row_count:])
    z_block = jnp.sum(got[:, :row_count].astype(f32), axis=0)
    z_half = z_block.astype(bf16)

    packed = jnp.concatenate(
        [
            jnp.concatenate([z_half, rotation.astype(bf16)], axis=1),
            jnp.pad(diag_rows(diag), ((0, 0), (0, col_count))),
        ],
        axis=0,
    )
    across = spread(packed, cols_axis, "cols")

    def rows_of(cells):
        return cells.transpose(1, 0, 2).reshape(cells.shape[1], -1)

    z_rows = [
        rows_of(across[:, :row_count, p * col_count : (p + 1) * col_count]) for p in range(2)
    ]
    rot_rows = rows_of(across[:, :row_count, both:])
    diag_all = jnp.sum(across[:, row_count : row_count + 3, :both].astype(f32), axis=1)
    diag_all = diag_all.reshape(cols_axis, 2, col_count).transpose(1, 0, 2).reshape(2, -1)

    def halves(cells):
        away = other_core(cells)
        pair = jnp.where(core == 0, jnp.stack([cells, away], 1), jnp.stack([away, cells], 1))
        return pair.reshape(orbital_count, -1)

    panel = spread(z_half, ZS, "rows", z_groups)
    panel = spread(panel, XS, "rows", x_groups)
    z_cols = halves(panel.reshape(XS * ZS, row_count, both))

    diag_cols = lax.dynamic_slice_in_dim(diag_all, col_start, col_count, 1)
    diag_down = lax.dynamic_slice_in_dim(diag_all, row_start, row_count, 1)

    def generator(cos_block, sin_block, across_diag, down_diag):
        cos_part = cos_block.astype(f32) * (across_diag[0][None, :] - down_diag[0][:, None])
        sin_part = sin_block.astype(f32) * (across_diag[1][None, :] - down_diag[1][:, None])
        return (cos_part + sin_part) * scale_factor

    gen_cols = generator(z_cols[:, :col_count], z_cols[:, col_count:], diag_cols, diag_all)
    gen_cols = gen_cols.astype(bf16)
    gen_rows = generator(z_rows[0], z_rows[1], diag_all, diag_down)
    gen_block = generator(z_block[:, :col_count], z_block[:, col_count:], diag_cols, diag_down)

    square = small_product(gen_rows.astype(bf16), gen_cols)
    step = (gen_block + 0.5 * square).astype(bf16)
    step_cols = spread(step, XS * ZS, "rows", xz_groups)
    square_rows = rows_of(spread(square.astype(bf16), cols_axis, "cols"))
    back_rows = (0.5 * square_rows.astype(f32) - gen_rows).astype(bf16)
    half_block = z_block + small_product(back_rows, z_cols)
    step_cols = halves(step_cols)
    half_across = spread(half_block.astype(bf16), cols_axis, "cols")
    half_rows = [
        rows_of(half_across[:, :, p * col_count : (p + 1) * col_count]) for p in range(2)
    ]
    rotated = rotation + small_product(rot_rows, step_cols)
    orbitals = (own_cols.astype(f32) + small_product(masked, step_cols)).astype(bf16)
    phase_cos = half_block[:, :col_count] + small_product(half_rows[0], step_cols)
    phase_sin = half_block[:, col_count:] + small_product(half_rows[1], step_cols)
    return (rotated, phase_cos, phase_sin, orbitals)


def solution(mesh):
    placed = (
        P("rows", None),
        P("rows", "cols"),
        P(None, "rows", None, None, None),
        P("rows", None),
        P("rows"),
    )
    return jax.shard_map(
        on_device,
        mesh=mesh,
        in_specs=placed,
        out_specs=(P("rows", "cols"), P("rows", "cols"), P("rows", "cols"), P("rows", "cols")),
        check_vma=False,
    )
```

time: 372 us -> 177 us (0.48)
  the two profiles are of different devices: /device:TPU:1 before, /device:TPU:64 now
where the time goes in v1:
time: 177 us; the launch traced here: 176 us
  blocking collectives  68.5 us (39%)
  waiting for transfers between devices  51.5 us (29%)
  starting transfers between devices  29.9 us (17%)
  local copies, waits for them, and re-layouts  10.1 us (6%)
  other arithmetic  8.68 us (5%)
  matrix products  6.3 us (4%)
    all_to_all x4, blocking collectives, swap(): lax.all_to_all(cells, axis, 0, 0, tiled=True, axis_index_groups=groups)  68.5 us
    all_to_all x4, waiting for transfers between devices, swap(): lax.all_to_all(cells, axis, 0, 0, tiled=True, axis_index_groups=groups)  45 us
    all_to_all x4, starting transfers between devices, swap(): lax.all_to_all(cells, axis, 0, 0, tiled=True, axis_index_groups=groups)  19.8 us
    ppermute x3, starting transfers between devices, other_core(): return lax.ppermute(cells, 'rows', [(i, i ^ 1) for i in range(count)])  5.74 us
    ppermute x1, waiting for transfers between devices, on_device(): lax.ppermute(own_cols[rows_dev - width:], 'rows', up)  5.64 us
    dot_general x6, matrix products, small_product(): return jnp.dot(left, right, preferred_element_type=f32)  5.15 us
    broadcast_in_dim x6, local copies, waits for them, and re-layouts, spread(): jnp.broadcast_to(cells[None], (count,) + cells.shape)  4.4 us
    select_n x2, other arithmetic, halves(): jnp.where(core == 0, jnp.stack([cells, away], 1), jnp.stack([away, cells]...  3.9 us
  transfers between devices with their start and end apart: 9, of which 6 were waited for; matrix products, arithmetic and copies ran while one was open for 4% of the time, Pallas kernels for 0%

profile of v1, /device:TPU:64, one launch (start us, length us, event | category | flops | bytes accessed | tf_op | source)
XLA Modules:
  0.0 176.2 jit_solution(10453075530399310073)
XLA Ops:
  2.4 1.9 %collective-permute-start.1 = (bf16[256,256]{1,0:T(8,128)(2,1)S(1)}, bf16[256,256]{1,0:T(8,128)(2,1)S(1)}, u32[]{:S(2)}, u32[]{:S(2)}) collective-permute-start(bf16[256,256]{1,0:T(8,128)(2,1)S(1)} %get-tuple-element.5), channel_id=1, source_target_pairs={{8,0},{16,8},{24,16},{32,24},{40,32},{48,40},{56,48},{64,56},{72,6... | collective-permute-start | bytes 393224 | tf_op jit(solution)/shard_map/ppermute | solution.py:78
  4.3 2.4 %collective-permute-start = (bf16[256,256]{1,0:T(8,128)(2,1)S(1)}, bf16[256,256]{1,0:T(8,128)(2,1)S(1)}, u32[]{:S(2)}, u32[]{:S(2)}) collective-permute-start(bf16[256,256]{1,0:T(8,128)(2,1)S(1)} %get-tuple-element.5), channel_id=1, source_target_pairs={{0,8},{8,16},{16,24},{24,32},{32,40},{40,48},{48,56},{56,64},{64,7... | collective-permute-start | bytes 393224 | tf_op jit(solution)/shard_map/ppermute | solution.py:76
  6.7 1.5 copy.62
  8.4 5.6 %collective-permute-done = bf16[256,256]{1,0:T(8,128)(2,1)S(1)} collective-permute-done((bf16[256,256]{1,0:T(8,128)(2,1)S(1)}, bf16[256,256]{1,0:T(8,128)(2,1)S(1)}, u32[]{:S(2)}, u32[]{:S(2)}) %collective-permute-start) | collective-permute-done | bytes 131104 | tf_op jit(solution)/shard_map/ppermute | solution.py:76
  15.9 1.7 copy-done
  17.5 1.9 %collective-permute-start.2 = (bf16[1040,512]{1,0:T(8,128)(2,1)S(1)}, bf16[1040,512]{1,0:T(8,128)(2,1)S(1)}, u32[]{:S(2)}, u32[]{:S(2)}) collective-permute-start(bf16[1040,512]{1,0:T(8,128)(2,1)S(1)} %pad_maximum_fusion.1), channel_id=1, source_target_pairs={{0,8},{8,0},{16,24},{24,16},{32,40},{40,32},{48,56},{56,48},{64,72... | collective-permute-start | bytes 3194888 | tf_op jit(solution)/shard_map/ppermute | solution.py:35
  19.5 1.8 %constant_dynamic-slice_fusion.2 = f32[4,8,1,32,512]{4,3,2,1,0:T(8,128)S(1)} fusion(f32[4,8,2,32,512]{4,3,2,1,0:T(8,128)} %copy-done, s32[]{:T(128)S(6)} %select_n.79), kind=kLoop, calls=%fused_computation.121 | loop fusion | bytes 4194308 | tf_op jit(solution)/shard_map/jit(dynamic_index_in_dim)/dynamic_slice | solution.py:98
  22.7 18.8 %all_to_all.40 = bf16[4,272,512]{2,1,0:T(8,128)(2,1)S(1)} all-to-all(bf16[4,272,512]{2,1,0:T(8,128)(2,1)S(1)} %pad_maximum_fusion), channel_id=1, replica_groups={{0,128,256,384},{8,136,264,392},{16,144,272,400},{24,152,280,408},{32,1..., dimensions={0} | all-to-all | bytes 2228224 | tf_op jit(solution)/shard_map/all_to_all | solution.py:26
  41.8 25.3 %all_to_all.41 = bf16[8,48,512]{2,1,0:T(8,128)(2,1)S(1)} all-to-all(bf16[8,48,512]{2,1,0:T(8,128)(2,1)S(1)} %pad_maximum_fusion.2), channel_id=1, replica_groups={{0,16,32,48,64,80,96,112},{8,24,40,56,72,88,104,120},{128,144,160,176,1..., dimensions={0} | all-to-all | bytes 786432 | tf_op jit(solution)/shard_map/all_to_all | solution.py:26
  67.2 12.9 %all_to_all.42 = bf16[8,32,512]{2,1,0:T(8,128)(2,1)S(1)} all-to-all(bf16[8,32,512]{2,1,0:T(8,128)(2,1)S(1)} %broadcast_in_dim.46), channel_id=1, replica_groups={{0,16,32,48,64,80,96,112},{8,24,40,56,72,88,104,120},{128,144,160,176,1..., dimensions={0} | all-to-all | bytes 524288 | tf_op jit(solution)/shard_map/all_to_all | solution.py:26
  81.2 3.5 %all-to-all-start.4 = ((bf16[4,8,32,512]{3,2,1,0:T(8,128)(2,1)}), bf16[4,8,32,512]{3,2,1,0:T(8,128)(2,1)S(1)}, u32[]{:S(2)}, u32[]{:S(2)}) async-start(bf16[4,8,32,512]{3,2,1,0:T(8,128)(2,1)} %broadcast_in_dim.47), calls=%async_computation.4 | async-start | bytes 2097152 | tf_op jit(solution)/shard_map/all_to_all | solution.py:26
  84.8 12.2 %all-to-all-done.4 = bf16[4,8,32,512]{3,2,1,0:T(8,128)(2,1)S(1)} async-done(((bf16[4,8,32,512]{3,2,1,0:T(8,128)(2,1)}), bf16[4,8,32,512]{3,2,1,0:T(8,128)(2,1)S(1)}, u32[]{:S(2)}, u32[]{:S(2)}) %all-to-all-start.4) | async-done | bytes 1048608 | tf_op jit(solution)/shard_map/all_to_all | solution.py:26
  98.0 7.1 %all-to-all-start.2 = ((bf16[8,48,768]{2,1,0:T(8,128)(2,1)}), bf16[8,48,768]{2,1,0:T(8,128)(2,1)S(1)}, u32[]{:S(2)}, u32[]{:S(2)}) async-start(bf16[8,48,768]{2,1,0:T(8,128)(2,1)} %broadcast_in_dim.45), calls=%async_computation.2 | async-start | bytes 1179648 | tf_op jit(solution)/shard_map/all_to_all | solution.py:26
  105.1 1.9 %collective-permute-start.3 = (bf16[32,32,512]{2,1,0:T(8,128)(2,1)S(1)}, bf16[32,32,512]{2,1,0:T(8,128)(2,1)}, u32[]{:S(2)}, u32[]{:S(2)}) collective-permute-start(bf16[32,32,512]{2,1,0:T(8,128)(2,1)S(1)} %bitcast.146), channel_id=1, source_target_pairs={{0,8},{8,0},{16,24},{24,16},{32,40},{40,32},{48,56},{56,48},{64,72... | collective-permute-start | bytes 3145736 | tf_op jit(solution)/shard_map/ppermute | solution.py:35
  107.0 12.9 %all-to-all-done.2 = bf16[8,48,768]{2,1,0:T(8,128)(2,1)S(1)} async-done(((bf16[8,48,768]{2,1,0:T(8,128)(2,1)}), bf16[8,48,768]{2,1,0:T(8,128)(2,1)S(1)}, u32[]{:S(2)}, u32[]{:S(2)}) %all-to-all-start.2) | async-done | bytes 589856 | tf_op jit(solution)/shard_map/all_to_all | solution.py:26
  120.9 2.6 %maximum_select_fusion = bf16[32,2,32,512]{3,2,1,0:T(8,128)(2,1)S(1)} fusion(bf16[32,1,32,512]{3,2,1,0:T(8,128)(2,1)} %bitcast.42, bf16[32,1,32,512]{3,2,1,0:T(8,128)(2,1)} %bitcast.147, pred[]{:T(512)S(6)} %eq.6), kind=kLoop, calls=%fused_computation | loop fusion | flops 3145728 | bytes 4194305 | tf_op jit(solution)/shard_map/jit(_where)/select_n | solution.py:151
  124.3 11.5 %all_to_all.43 = bf16[8,32,256]{2,1,0:T(8,128)(2,1)S(1)} all-to-all(bf16[8,32,256]{2,1,0:T(8,128)(2,1)S(1)} %broadcast_in_dim.86), channel_id=1, replica_groups=mesh['rows'=64,'cols'=8] {'cols'}, dimensions={0} | all-to-all | bytes 262144 | tf_op jit(solution)/shard_map/all_to_all | solution.py:26
  136.7 5.8 %all-to-all-start.5 = ((bf16[32,32,256]{2,1,0:T(8,128)(2,1)}), bf16[32,32,256]{2,1,0:T(8,128)(2,1)}, u32[]{:S(2)}, u32[]{:S(2)}) async-start(bf16[32,32,256]{2,1,0:T(8,128)(2,1)} %broadcast_in_dim.48), calls=%async_computation.5 | async-start | bytes 1048576 | tf_op jit(solution)/shard_map/all_to_all | solution.py:26
  144.7 11.5 %all-to-all-done.5 = bf16[32,32,256]{2,1,0:T(8,128)(2,1)} async-done(((bf16[32,32,256]{2,1,0:T(8,128)(2,1)}), bf16[32,32,256]{2,1,0:T(8,128)(2,1)}, u32[]{:S(2)}, u32[]{:S(2)}) %all-to-all-start.5) | async-done | bytes 524320 | tf_op jit(solution)/shard_map/all_to_all | solution.py:26
  156.2 1.5 broadcast_in_dim.87
  157.7 3.4 %all-to-all-start.7 = ((bf16[8,32,512]{2,1,0:T(8,128)(2,1)}), bf16[8,32,512]{2,1,0:T(8,128)(2,1)S(1)}, u32[]{:S(2)}, u32[]{:S(2)}) async-start(bf16[8,32,512]{2,1,0:T(8,128)(2,1)} %broadcast_in_dim.87), calls=%async_computation.7 | async-start | bytes 524288 | tf_op jit(solution)/shard_map/all_to_all | solution.py:26
  161.1 1.9 %collective-permute-start.4 = (bf16[32,32,256]{2,1,0:T(8,128)(2,1)}, bf16[32,32,256]{2,1,0:T(8,128)(2,1)S(1)}, u32[]{:S(2)}, u32[]{:S(2)}) collective-permute-start(bf16[32,32,256]{2,1,0:T(8,128)(2,1)} %all-to-all-done.5), channel_id=1, source_target_pairs={{0,8},{8,0},{16,24},{24,16},{32,40},{40,32},{48,56},{56,48},{64,72... | collective-permute-start | bytes 1572872 | tf_op jit(solution)/shard_map/ppermute | solution.py:35
  163.1 8.4 %all-to-all-done.7 = bf16[8,32,512]{2,1,0:T(8,128)(2,1)S(1)} async-done(((bf16[8,32,512]{2,1,0:T(8,128)(2,1)}), bf16[8,32,512]{2,1,0:T(8,128)(2,1)S(1)}, u32[]{:S(2)}, u32[]{:S(2)}) %all-to-all-start.7) | async-done | bytes 262176 | tf_op jit(solution)/shard_map/all_to_all | solution.py:26
  171.6 1.3 maximum_select_fusion.1
  (89 shorter events, 15.7 us)
Async XLA Ops:
  2.4 6.0 %copy-start.7 = (s32[2,5]{1,0:T(2,128)S(1)}, s32[2,5]{1,0:T(2,128)}, u32[]{:S(2)}) copy-start(s32[2,5]{1,0:T(2,128)} %param.8) | copy-start | bytes 124
  2.4 11.6 %collective-permute-start.1 = (bf16[256,256]{1,0:T(8,128)(2,1)S(1)}, bf16[256,256]{1,0:T(8,128)(2,1)S(1)}, u32[]{:S(2)}, u32[]{:S(2)}) collective-permute-start(bf16[256,256]{1,0:T(8,128)(2,1)S(1)} %get-tuple-element.5), channel_id=1, source_target_pairs={{8,0},{16,8},{24,16},{32,24},{40,32},{48,40},{56,48},{64,56},{72,6... | collective-permute-start | bytes 393224 | tf_op jit(solution)/shard_map/ppermute | solution.py:78
  4.3 9.7 %collective-permute-start = (bf16[256,256]{1,0:T(8,128)(2,1)S(1)}, bf16[256,256]{1,0:T(8,128)(2,1)S(1)}, u32[]{:S(2)}, u32[]{:S(2)}) collective-permute-start(bf16[256,256]{1,0:T(8,128)(2,1)S(1)} %get-tuple-element.5), channel_id=1, source_target_pairs={{0,8},{8,16},{16,24},{24,32},{32,40},{40,48},{48,56},{56,64},{64,7... | collective-permute-start | bytes 393224 | tf_op jit(solution)/shard_map/ppermute | solution.py:76
  8.2 5.9 %copy-start.6 = (bf16[2,2,5,128,128]{4,3,2,1,0:T(8,128)(2,1)S(1)}, bf16[2,2,5,128,128]{4,3,2,1,0:T(8,128)(2,1)}, u32[]{:S(2)}) copy-start(bf16[2,2,5,128,128]{4,3,2,1,0:T(8,128)(2,1)} %param.7) | copy-start | bytes 1966084
  15.6 1.9 %copy-start = (f32[4,8,2,32,512]{4,3,2,1,0:T(8,128)}, f32[4,8,2,32,512]{4,3,2,1,0:T(8,128)S(1)}, u32[]{:S(2)}) copy-start(f32[4,8,2,32,512]{4,3,2,1,0:T(8,128)S(1)} %fusion.56) | copy-start | bytes 12582916
  17.5 4.6 %collective-permute-start.2 = (bf16[1040,512]{1,0:T(8,128)(2,1)S(1)}, bf16[1040,512]{1,0:T(8,128)(2,1)S(1)}, u32[]{:S(2)}, u32[]{:S(2)}) collective-permute-start(bf16[1040,512]{1,0:T(8,128)(2,1)S(1)} %pad_maximum_fusion.1), channel_id=1, source_target_pairs={{0,8},{8,0},{16,24},{24,16},{32,40},{40,32},{48,56},{56,48},{64,72... | collective-permute-start | bytes 3194888 | tf_op jit(solution)/shard_map/ppermute | solution.py:35
  67.1 17.6 %copy-start.4 = (f32[32,256]{1,0:T(8,128)S(1)}, f32[32,256]{1,0:T(8,128)}, u32[]{:S(2)}) copy-start(f32[32,256]{1,0:T(8,128)} %param.6) | copy-start | bytes 98308
  81.2 15.9 %all-to-all-start.4 = ((bf16[4,8,32,512]{3,2,1,0:T(8,128)(2,1)}), bf16[4,8,32,512]{3,2,1,0:T(8,128)(2,1)S(1)}, u32[]{:S(2)}, u32[]{:S(2)}) async-start(bf16[4,8,32,512]{3,2,1,0:T(8,128)(2,1)} %broadcast_in_dim.47), calls=%async_computation.4 | async-start | bytes 2097152 | tf_op jit(solution)/shard_map/all_to_all | solution.py:26
  97.0 23.9 %copy-start.1 = (bf16[4,8,32,512]{3,2,1,0:T(8,128)(2,1)}, bf16[4,8,32,512]{3,2,1,0:T(8,128)(2,1)S(1)}, u32[]{:S(2)}) copy-start(bf16[4,8,32,512]{3,2,1,0:T(8,128)(2,1)S(1)} %all-to-all-done.4) | copy-start | bytes 3145732
  98.0 21.9 %all-to-all-start.2 = ((bf16[8,48,768]{2,1,0:T(8,128)(2,1)}), bf16[8,48,768]{2,1,0:T(8,128)(2,1)S(1)}, u32[]{:S(2)}, u32[]{:S(2)}) async-start(bf16[8,48,768]{2,1,0:T(8,128)(2,1)} %broadcast_in_dim.45), calls=%async_computation.2 | async-start | bytes 1179648 | tf_op jit(solution)/shard_map/all_to_all | solution.py:26
  105.1 15.8 %collective-permute-start.3 = (bf16[32,32,512]{2,1,0:T(8,128)(2,1)S(1)}, bf16[32,32,512]{2,1,0:T(8,128)(2,1)}, u32[]{:S(2)}, u32[]{:S(2)}) collective-permute-start(bf16[32,32,512]{2,1,0:T(8,128)(2,1)S(1)} %bitcast.146), channel_id=1, source_target_pairs={{0,8},{8,0},{16,24},{24,16},{32,40},{40,32},{48,56},{56,48},{64,72... | collective-permute-start | bytes 3145736 | tf_op jit(solution)/shard_map/ppermute | solution.py:35
  119.8 1.1 copy-start.2
  136.7 19.5 %all-to-all-start.5 = ((bf16[32,32,256]{2,1,0:T(8,128)(2,1)}), bf16[32,32,256]{2,1,0:T(8,128)(2,1)}, u32[]{:S(2)}, u32[]{:S(2)}) async-start(bf16[32,32,256]{2,1,0:T(8,128)(2,1)} %broadcast_in_dim.48), calls=%async_computation.5 | async-start | bytes 1048576 | tf_op jit(solution)/shard_map/all_to_all | solution.py:26
  143.6 19.4 %copy-start.3 = (bf16[8,4,8,256]{3,2,1,0:T(8,128)(2,1)S(1)}, bf16[8,4,8,256]{3,2,1,0:T(8,128)(2,1)}, u32[]{:S(2)}) copy-start(bf16[8,4,8,256]{3,2,1,0:T(8,128)(2,1)} %get-tuple-element.8) | copy-start | bytes 393220
  157.7 13.8 %all-to-all-start.7 = ((bf16[8,32,512]{2,1,0:T(8,128)(2,1)}), bf16[8,32,512]{2,1,0:T(8,128)(2,1)S(1)}, u32[]{:S(2)}, u32[]{:S(2)}) async-start(bf16[8,32,512]{2,1,0:T(8,128)(2,1)} %broadcast_in_dim.87), calls=%async_computation.7 | async-start | bytes 524288 | tf_op jit(solution)/shard_map/all_to_all | solution.py:26
  161.1 10.5 %collective-permute-start.4 = (bf16[32,32,256]{2,1,0:T(8,128)(2,1)}, bf16[32,32,256]{2,1,0:T(8,128)(2,1)S(1)}, u32[]{:S(2)}, u32[]{:S(2)}) collective-permute-start(bf16[32,32,256]{2,1,0:T(8,128)(2,1)} %all-to-all-done.5), channel_id=1, source_target_pairs={{0,8},{8,0},{16,24},{24,16},{32,40},{40,32},{48,56},{56,48},{64,72... | collective-permute-start | bytes 1572872 | tf_op jit(solution)/shard_map/ppermute | solution.py:35
  172.9 1.4 copy-start.5

commit v2 on v1

--- a/solution.py
+++ b/solution.py
@@ -15,8 +15,6 @@
     return (x * ZS + z) * CORES + core
 
 
-x_groups = [[row_index(x, z, k) for x in range(XS)] for z in range(ZS) for k in range(CORES)]
-z_groups = [[row_index(x, z, k) for z in range(ZS)] for x in range(XS) for k in range(CORES)]
 xz_groups = [
     [row_index(x, z, k) for x in range(XS) for z in range(ZS)] for k in range(CORES)
 ]
@@ -39,15 +37,6 @@
     return jnp.dot(left, right, preferred_element_type=f32)
 
 
-def three_parts(values):
-    parts = []
-    for _ in range(3):
-        part = lax.reduce_precision(values, 8, 7)
-        parts.append(part.astype(bf16))
-        values = values - part
-    return jnp.stack(parts)
-
-
 def on_device(coeffs, rotation, phase_ops, block_links, atom_size):
     rows_dev, orbital_count = coeffs.shape
     blocks_dev = phase_ops.shape[1]
@@ -63,6 +52,16 @@
     col_start = lax.axis_index("cols") * col_count
     core = lax.axis_index("rows") % CORES
     scale_factor = 0.125 / math.sqrt(orbital_count)
+
+    def lanes_out(cells):
+        lead, rows, wide = cells.shape[:-2], cells.shape[-2], cells.shape[-1]
+        cells = cells.reshape(lead + (rows, wide // 128, 128))
+        return jnp.swapaxes(cells, -3, -2).reshape(lead + (rows * wide // 128, 128))
+
+    def lanes_in(cells, rows):
+        lead = cells.shape[:-2]
+        cells = cells.reshape(lead + (-1, rows, 128))
+        return jnp.swapaxes(cells, -3, -2).reshape(lead + (rows, -1))
 
     within = lax.broadcasted_iota(jnp.int32, (blocks_dev, block_size), 1)
     live_rows = (within < atom_size[:, None]).reshape(rows_dev)
@@ -80,6 +79,9 @@
         axis=0,
     )
     masked = jnp.where(live_rows[:, None], coeffs, jnp.zeros_like(coeffs))
+    turned = masked.T.reshape(XS * ZS, CORES, row_count, rows_dev)
+    own_turned = lax.dynamic_index_in_dim(turned, core, 1, keepdims=False)
+    far_turned = other_core(lax.dynamic_index_in_dim(turned, 1 - core, 1, keepdims=False))
     stacked = jnp.stack(
         [
             padded[offset * block_size : (offset + blocks_dev) * block_size].reshape(
@@ -90,60 +92,49 @@
         axis=1,
     )
     gated = phase_ops * block_links[None, :, :, None, None].astype(bf16)
-    applied = jnp.einsum("pbtij,btjk->pbik", gated, stacked, preferred_element_type=f32)
-    applied = applied.reshape(2, rows_dev, col_count).astype(bf16)
+    applied = jnp.einsum("pbtij,btjk->bipk", gated, stacked, preferred_element_type=f32)
+    applied = applied.reshape(rows_dev, both).astype(bf16)
+    far_applied = other_core(applied)
 
-    product = jnp.einsum("ni,pnj->ipj", masked, applied, preferred_element_type=f32)
-    product = product.reshape(XS, ZS, CORES, row_count, both)
-    own_half = lax.dynamic_index_in_dim(product, core, 2, keepdims=False)
-    far_half = lax.dynamic_index_in_dim(product, 1 - core, 2, keepdims=False)
-    diag = jnp.einsum("nj,pnj->pj", own_cols, applied, preferred_element_type=f32)
+    product = small_product(own_turned.reshape(-1, rows_dev), applied)
+    product = product + small_product(far_turned.reshape(-1, rows_dev), far_applied)
 
-    def diag_rows(values):
-        return jnp.pad(three_parts(values.reshape(both)), ((0, 13), (0, 0)))
+    def diag_of(cols, values):
+        return jnp.sum(jnp.tile(cols, (1, 2)).astype(f32) * values.astype(f32), axis=0)
 
-    def diag_sum(cells):
-        return jnp.sum(cells[:, :3].astype(f32), axis=(0, 1))
+    far_cols = jnp.where(core == 0, padded[width + rows_dev :], padded[:width])
+    diag = diag_of(own_cols, applied) + diag_of(far_cols, far_applied)
 
-    chip_rows = ZS * row_count
-    sent = jnp.concatenate(
-        [far_half.astype(bf16).reshape(XS * chip_rows, both), diag_rows(diag)], axis=0
-    )
-    got = other_core(sent)
-    diag = diag.reshape(both) + diag_sum(got[None, XS * chip_rows :])
-    half = own_half.reshape(XS, chip_rows, both) + got[: XS * chip_rows].reshape(
-        XS, chip_rows, both
-    ).astype(f32)
+    def two_parts(values):
+        high = lax.reduce_precision(values, 8, 7)
+        return jnp.stack([high.astype(bf16), (values - high).astype(bf16)]).reshape(-1, 128)
 
-    def with_diag(cells, values):
-        tail = jnp.broadcast_to(diag_rows(values)[None], (cells.shape[0], 16, both))
-        return jnp.concatenate([cells.astype(bf16), tail], axis=1)
+    tail_rows = 2 * both // 128
 
-    got = swap(with_diag(half, diag), "rows", x_groups)
-    diag = diag_sum(got[:, chip_rows:])
-    chip = jnp.sum(got[:, :chip_rows].astype(f32), axis=0).reshape(ZS, row_count, both)
-    got = swap(with_diag(chip, diag), "rows", z_groups)
-    diag = diag_sum(got[:, row_count:])
-    z_block = jnp.sum(got[:, :row_count].astype(f32), axis=0)
+    def parts_sum(cells):
+        cells = cells.astype(f32).reshape(-1, 2, both)
+        return cells[:, 0] + cells[:, 1]
+
+    tail = jnp.broadcast_to(two_parts(diag)[None], (XS * ZS, tail_rows, 128))
+    pieces = lanes_out(product.astype(bf16).reshape(XS * ZS, row_count, both))
+    got = swap(jnp.concatenate([pieces, tail], axis=1), "rows", xz_groups)
+    body_rows = row_count * both // 128
+    diag = jnp.sum(parts_sum(got[:, body_rows:]), axis=0)
+    z_block = lanes_in(jnp.sum(got[:, :body_rows].astype(f32), axis=0), row_count)
     z_half = z_block.astype(bf16)
 
     packed = jnp.concatenate(
-        [
-            jnp.concatenate([z_half, rotation.astype(bf16)], axis=1),
-            jnp.pad(diag_rows(diag), ((0, 0), (0, col_count))),
-        ],
-        axis=0,
+        [lanes_out(z_half), lanes_out(rotation.astype(bf16)), two_parts(diag)], axis=0
     )
     across = spread(packed, cols_axis, "cols")
 
     def rows_of(cells):
         return cells.transpose(1, 0, 2).reshape(cells.shape[1], -1)
 
-    z_rows = [
-        rows_of(across[:, :row_count, p * col_count : (p + 1) * col_count]) for p in range(2)
-    ]
-    rot_rows = rows_of(across[:, :row_count, both:])
-    diag_all = jnp.sum(across[:, row_count : row_count + 3, :both].astype(f32), axis=1)
+    wide = lanes_in(across[:, :-tail_rows], row_count)
+    z_rows = [rows_of(wide[:, :, p * col_count : (p + 1) * col_count]) for p in range(2)]
+    rot_rows = rows_of(wide[:, :, both:])
+    diag_all = parts_sum(across[:, -tail_rows:])
     diag_all = diag_all.reshape(cols_axis, 2, col_count).transpose(1, 0, 2).reshape(2, -1)
 
     def halves(cells):
@@ -151,9 +142,8 @@
         pair = jnp.where(core == 0, jnp.stack([cells, away], 1), jnp.stack([away, cells], 1))
         return pair.reshape(orbital_count, -1)
 
-    panel = spread(z_half, ZS, "rows", z_groups)
-    panel = spread(panel, XS, "rows", x_groups)
-    z_cols = halves(panel.reshape(XS * ZS, row_count, both))
+    panel = spread(z_half, XS * ZS, "rows", xz_groups)
+    z_cols = halves(panel)
 
     diag_cols = lax.dynamic_slice_in_dim(diag_all, col_start, col_count, 1)
     diag_down = lax.dynamic_slice_in_dim(diag_all, row_start, row_count, 1)

time: 177 us -> 190 us (1.073)
  blocking collectives: 68.5 us -> 12.8 us
  waiting for transfers between devices: 51.5 us -> 95.1 us
  starting transfers between devices: 29.9 us -> 48.5 us
  matrix products: 6.3 us -> 9.34 us
    all_to_all x4 -> x1, blocking collectives: 68.5 us -> 12.8 us  [swap(): lax.all_to_all(cells, axis, 0, 0, tiled=True, axis_index_groups=groups)]
    all_to_all x4 -> x5, waiting for transfers between devices: 45 us -> 93.9 us  [swap(): lax.all_to_all(cells, axis, 0, 0, tiled=True, axis_index_groups=groups)]
    all_to_all x4 -> x5, starting transfers between devices: 19.8 us -> 34.5 us  [swap(): lax.all_to_all(cells, axis, 0, 0, tiled=True, axis_index_groups=groups)]
    ppermute x1, waiting for transfers between devices: 5.64 us -> 0.01 us  [on_device(): lax.ppermute(own_cols[rows_dev - width:], 'rows', up)]
    dot_general x6 -> x8, matrix products: 5.15 us -> 8.9 us  [small_product(): return jnp.dot(left, right, preferred_element_type=f32)]
    ppermute x3 -> x4, starting transfers between devices: 5.74 us -> 8.4 us  [other_core(): return lax.ppermute(cells, 'rows', [(i, i ^ 1) for i in range(count)])]
    broadcast_in_dim x6 -> x5, local copies, waits for them, and re-layouts: 4.4 us -> 3.54 us  [spread(): jnp.broadcast_to(cells[None], (count,) + cells.shape)]
  transfers between devices with their start and end apart: 9 -> 11, of which waited for: 6 -> 7; matrix products, arithmetic and copies ran while one was open for 4% -> 7% of each run, Pallas kernels for 0% -> 0%
where the time goes in v2:
time: 190 us; the launch traced here: 189 us
  waiting for transfers between devices  95.1 us (50%)
  starting transfers between devices  48.5 us (26%)
  blocking collectives  12.8 us (7%)
  local copies, waits for them, and re-layouts  11.8 us (6%)
  other arithmetic  10.2 us (5%)
  matrix products  9.34 us (5%)
    all_to_all x5, waiting for transfers between devices, swap(): lax.all_to_all(cells, axis, 0, 0, tiled=True, axis_index_groups=groups)  93.9 us
    all_to_all x5, starting transfers between devices, swap(): lax.all_to_all(cells, axis, 0, 0, tiled=True, axis_index_groups=groups)  34.5 us
    all_to_all x1, blocking collectives, swap(): lax.all_to_all(cells, axis, 0, 0, tiled=True, axis_index_groups=groups)  12.8 us
    dot_general x8, matrix products, small_product(): return jnp.dot(left, right, preferred_element_type=f32)  8.9 us
    ppermute x4, starting transfers between devices, other_core(): return lax.ppermute(cells, 'rows', [(i, i ^ 1) for i in range(count)])  8.4 us
    select_n x2, other arithmetic, halves(): jnp.where(core == 0, jnp.stack([cells, away], 1), jnp.stack([away, cells]...  3.94 us
  transfers between devices with their start and end apart: 11, of which 7 were waited for; matrix products, arithmetic and copies ran while one was open for 7% of the time, Pallas kernels for 0%

profile of v2, /device:TPU:64, one launch (start us, length us, event | category | flops | bytes accessed | tf_op | source)
XLA Modules:
  0.0 188.9 jit_solution(565014498794471743)
XLA Ops:
  2.4 1.9 %collective-permute-start = (bf16[256,256]{1,0:T(8,128)(2,1)S(1)}, bf16[256,256]{1,0:T(8,128)(2,1)S(1)}, u32[]{:S(2)}, u32[]{:S(2)}) collective-permute-start(bf16[256,256]{1,0:T(8,128)(2,1)S(1)} %dynamic-slice_select_fusion), channel_id=1, source_target_pairs={{0,8},{8,16},{16,24},{24,32},{32,40},{40,48},{48,56},{56,64},{64,7... | collective-permute-start | bytes 393224 | tf_op jit(solution)/shard_map/ppermute | solution.py:75
  4.3 3.6 %collective-permute-start.1 = (bf16[256,256]{1,0:T(8,128)(2,1)S(1)}, bf16[256,256]{1,0:T(8,128)(2,1)S(1)}, u32[]{:S(2)}, u32[]{:S(2)}) collective-permute-start(bf16[256,256]{1,0:T(8,128)(2,1)S(1)} %dynamic-slice_select_fusion), channel_id=1, source_target_pairs={{8,0},{16,8},{24,16},{32,24},{40,32},{48,40},{56,48},{64,56},{72,6... | collective-permute-start | bytes 393224 | tf_op jit(solution)/shard_map/ppermute | solution.py:77
  8.0 1.5 copy.30
  10.7 2.7 %collective-permute-start.2 = (bf16[32,32,256]{2,1,0:T(8,128)(2,1)}, bf16[32,32,256]{2,1,0:T(8,128)(2,1)}, u32[]{:S(2)}, u32[]{:S(2)}) collective-permute-start(bf16[32,32,256]{2,1,0:T(8,128)(2,1)} %get-tuple-element.4), channel_id=1, source_target_pairs={{0,8},{8,0},{16,24},{24,16},{32,40},{40,32},{48,56},{56,48},{64,72... | collective-permute-start | bytes 1572872 | tf_op jit(solution)/shard_map/ppermute | solution.py:33
  15.3 1.9 %collective-permute-start.3 = (bf16[256,512]{1,0:T(8,128)(2,1)S(1)}, bf16[256,512]{1,0:T(8,128)(2,1)S(1)}, u32[]{:S(2)}, u32[]{:S(2)}) collective-permute-start(bf16[256,512]{1,0:T(8,128)(2,1)S(1)} %bitcast.169), channel_id=1, source_target_pairs={{0,8},{8,0},{16,24},{24,16},{32,40},{40,32},{48,56},{56,48},{64,72... | collective-permute-start | bytes 786440 | tf_op jit(solution)/shard_map/ppermute | solution.py:33
  18.9 2.5 %add_convert_fusion = bf16[1024,512]{1,0:T(8,128)(2,1)} fusion(f32[1024,512]{1,0:T(8,128)S(1)} %fusion.31, bf16[1024,256]{1,0:T(8,128)(2,1)} %bitcast.16, bf16[256,512]{1,0:T(8,128)(2,1)S(1)} %collective-permute-done.3), kind=kOutput, calls=%fused_computation.3 | convolution fusion | flops 269484032 | bytes 3932160 | tf_op jit(solution)/shard_map/dot_general | solution.py:37
  21.4 1.3 reshape_reshape.3
  24.1 13.2 %all-to-all-start = ((bf16[32,136,128]{2,1,0:T(8,128)(2,1)}), bf16[32,136,128]{2,1,0:T(8,128)(2,1)S(1)}, u32[]{:S(2)}, u32[]{:S(2)}) async-start(bf16[32,136,128]{2,1,0:T(8,128)(2,1)} %pad_maximum_fusion), calls=%async_computation | async-start | bytes 2228224 | tf_op jit(solution)/shard_map/all_to_all | solution.py:24
  37.3 29.9 %all-to-all-done = bf16[32,136,128]{2,1,0:T(8,128)(2,1)S(1)} async-done(((bf16[32,136,128]{2,1,0:T(8,128)(2,1)}), bf16[32,136,128]{2,1,0:T(8,128)(2,1)S(1)}, u32[]{:S(2)}, u32[]{:S(2)}) %all-to-all-start) | async-done | bytes 1114144 | tf_op jit(solution)/shard_map/all_to_all | solution.py:24
  68.5 7.1 %all-to-all-start.1 = ((bf16[8,200,128]{2,1,0:T(8,128)(2,1)}), bf16[8,200,128]{2,1,0:T(8,128)(2,1)S(1)}, u32[]{:S(2)}, u32[]{:S(2)}) async-start(bf16[8,200,128]{2,1,0:T(8,128)(2,1)} %broadcast_in_dim.67), calls=%async_computation.1 | async-start | bytes 819200 | tf_op jit(solution)/shard_map/all_to_all | solution.py:24
  75.6 14.7 %all-to-all-done.1 = bf16[8,200,128]{2,1,0:T(8,128)(2,1)S(1)} async-done(((bf16[8,200,128]{2,1,0:T(8,128)(2,1)}), bf16[8,200,128]{2,1,0:T(8,128)(2,1)S(1)}, u32[]{:S(2)}, u32[]{:S(2)}) %all-to-all-start.1) | async-done | bytes 409632 | tf_op jit(solution)/shard_map/all_to_all | solution.py:24
  91.4 5.6 %all-to-all-start.2 = ((bf16[32,32,512]{2,1,0:T(8,128)(2,1)}), bf16[32,32,512]{2,1,0:T(8,128)(2,1)S(1)}, u32[]{:S(2)}, u32[]{:S(2)}) async-start(bf16[32,32,512]{2,1,0:T(8,128)(2,1)} %broadcast_in_dim.68), calls=%async_computation.2 | async-start | bytes 2097152 | tf_op jit(solution)/shard_map/all_to_all | solution.py:24
  97.7 27.9 %all-to-all-done.2 = bf16[32,32,512]{2,1,0:T(8,128)(2,1)S(1)} async-done(((bf16[32,32,512]{2,1,0:T(8,128)(2,1)}), bf16[32,32,512]{2,1,0:T(8,128)(2,1)S(1)}, u32[]{:S(2)}, u32[]{:S(2)}) %all-to-all-start.2) | async-done | bytes 1048608 | tf_op jit(solution)/shard_map/all_to_all | solution.py:24
  125.7 1.9 %collective-permute-start.4 = (bf16[32,32,512]{2,1,0:T(8,128)(2,1)S(1)}, bf16[32,32,512]{2,1,0:T(8,128)(2,1)}, u32[]{:S(2)}, u32[]{:S(2)}) collective-permute-start(bf16[32,32,512]{2,1,0:T(8,128)(2,1)S(1)} %all-to-all-done.2), channel_id=1, source_target_pairs={{0,8},{8,0},{16,24},{24,16},{32,40},{40,32},{48,56},{56,48},{64,72... | collective-permute-start | bytes 3145736 | tf_op jit(solution)/shard_map/ppermute | solution.py:33
  130.4 2.6 %maximum_select_fusion = bf16[32,2,32,512]{3,2,1,0:T(8,128)(2,1)S(1)} fusion(bf16[32,1,32,512]{3,2,1,0:T(8,128)(2,1)} %bitcast.41, bf16[32,1,32,512]{3,2,1,0:T(8,128)(2,1)} %bitcast.156, pred[]{:T(512)S(6)} %eq.4), kind=kLoop, calls=%fused_computation | loop fusion | flops 3145728 | bytes 4194305 | tf_op jit(solution)/shard_map/jit(_where)/select_n | solution.py:142
  133.9 12.8 %all_to_all.30 = bf16[8,32,256]{2,1,0:T(8,128)(2,1)} all-to-all(bf16[8,32,256]{2,1,0:T(8,128)(2,1)S(1)} %broadcast_in_dim.70), channel_id=1, replica_groups=mesh['rows'=64,'cols'=8] {'cols'}, dimensions={0} | all-to-all | bytes 262144 | tf_op jit(solution)/shard_map/all_to_all | solution.py:24
  147.6 5.2 %all-to-all-start.3 = ((bf16[32,32,256]{2,1,0:T(8,128)(2,1)}), bf16[32,32,256]{2,1,0:T(8,128)(2,1)}, u32[]{:S(2)}, u32[]{:S(2)}) async-start(bf16[32,32,256]{2,1,0:T(8,128)(2,1)} %broadcast_in_dim.69), calls=%async_computation.3 | async-start | bytes 1048576 | tf_op jit(solution)/shard_map/all_to_all | solution.py:24
  153.9 1.9 %fusion.30 = (bf16[32,512]{1,0:T(8,128)(2,1)S(1)}, f32[32,512]{1,0:T(8,128)}) fusion(bf16[32,2048]{1,0:T(8,128)(2,1)S(1)} %bitcast.179, bf16[2048,512]{1,0:T(8,128)(2,1)S(1)} %bitcast.155, f32[4,4,8,128]{3,2,1,0:T(8,128)} %bitcast.166), kind=kOutput, calls=%fused_computation.87 | convolution fusion | flops 67141632 | bytes 2392064 | tf_op jit(solution)/shard_map/dot_general | solution.py:37
  155.9 13.8 %all-to-all-done.3 = bf16[32,32,256]{2,1,0:T(8,128)(2,1)} async-done(((bf16[32,32,256]{2,1,0:T(8,128)(2,1)}), bf16[32,32,256]{2,1,0:T(8,128)(2,1)}, u32[]{:S(2)}, u32[]{:S(2)}) %all-to-all-start.3) | async-done | bytes 524320 | tf_op jit(solution)/shard_map/all_to_all | solution.py:24
  170.4 3.4 %all-to-all-start.5 = ((bf16[8,32,512]{2,1,0:T(8,128)(2,1)}), bf16[8,32,512]{2,1,0:T(8,128)(2,1)S(1)}, u32[]{:S(2)}, u32[]{:S(2)}) async-start(bf16[8,32,512]{2,1,0:T(8,128)(2,1)} %broadcast_in_dim.71), calls=%async_computation.5 | async-start | bytes 524288 | tf_op jit(solution)/shard_map/all_to_all | solution.py:24
  173.8 1.9 %collective-permute-start.5 = (bf16[32,32,256]{2,1,0:T(8,128)(2,1)}, bf16[32,32,256]{2,1,0:T(8,128)(2,1)S(1)}, u32[]{:S(2)}, u32[]{:S(2)}) collective-permute-start(bf16[32,32,256]{2,1,0:T(8,128)(2,1)} %all-to-all-done.3), channel_id=1, source_target_pairs={{0,8},{8,0},{16,24},{24,16},{32,40},{40,32},{48,56},{56,48},{64,72... | collective-permute-start | bytes 1572872 | tf_op jit(solution)/shard_map/ppermute | solution.py:33
  176.7 7.5 %all-to-all-done.5 = bf16[8,32,512]{2,1,0:T(8,128)(2,1)S(1)} async-done(((bf16[8,32,512]{2,1,0:T(8,128)(2,1)}), bf16[8,32,512]{2,1,0:T(8,128)(2,1)S(1)}, u32[]{:S(2)}, u32[]{:S(2)}) %all-to-all-start.5) | async-done | bytes 262176 | tf_op jit(solution)/shard_map/all_to_all | solution.py:24
  184.3 1.3 maximum_select_fusion.1
  185.7 1.1 fusion.2
  (105 shorter events, 20.1 us)
Async XLA Ops:
  2.4 12.1 %copy-start.1 = (bf16[256,256]{1,0:T(8,128)(2,1)}, bf16[256,256]{1,0:T(8,128)(2,1)S(1)}, u32[]{:S(2)}) copy-start(bf16[256,256]{1,0:T(8,128)(2,1)S(1)} %dynamic-slice_select_fusion) | copy-start | bytes 393220
  2.4 12.0 %collective-permute-start = (bf16[256,256]{1,0:T(8,128)(2,1)S(1)}, bf16[256,256]{1,0:T(8,128)(2,1)S(1)}, u32[]{:S(2)}, u32[]{:S(2)}) collective-permute-start(bf16[256,256]{1,0:T(8,128)(2,1)S(1)} %dynamic-slice_select_fusion), channel_id=1, source_target_pairs={{0,8},{8,16},{16,24},{24,32},{32,40},{40,48},{48,56},{56,64},{64,7... | collective-permute-start | bytes 393224 | tf_op jit(solution)/shard_map/ppermute | solution.py:75
  4.3 10.1 %collective-permute-start.1 = (bf16[256,256]{1,0:T(8,128)(2,1)S(1)}, bf16[256,256]{1,0:T(8,128)(2,1)S(1)}, u32[]{:S(2)}, u32[]{:S(2)}) collective-permute-start(bf16[256,256]{1,0:T(8,128)(2,1)S(1)} %dynamic-slice_select_fusion), channel_id=1, source_target_pairs={{8,0},{16,8},{24,16},{32,24},{40,32},{48,40},{56,48},{64,56},{72,6... | collective-permute-start | bytes 393224 | tf_op jit(solution)/shard_map/ppermute | solution.py:77
  9.4 4.9 %copy-start.14 = (s32[2,5]{1,0:T(2,128)S(1)}, s32[2,5]{1,0:T(2,128)}, u32[]{:S(2)}) copy-start(s32[2,5]{1,0:T(2,128)} %param.8) | copy-start | bytes 124
  9.6 5.0 %copy-start.13 = (bf16[2,2,5,128,128]{4,3,2,1,0:T(8,128)(2,1)S(1)}, bf16[2,2,5,128,128]{4,3,2,1,0:T(8,128)(2,1)}, u32[]{:S(2)}) copy-start(bf16[2,2,5,128,128]{4,3,2,1,0:T(8,128)(2,1)} %param.7) | copy-start | bytes 1966084
  10.7 8.2 %collective-permute-start.2 = (bf16[32,32,256]{2,1,0:T(8,128)(2,1)}, bf16[32,32,256]{2,1,0:T(8,128)(2,1)}, u32[]{:S(2)}, u32[]{:S(2)}) collective-permute-start(bf16[32,32,256]{2,1,0:T(8,128)(2,1)} %get-tuple-element.4), channel_id=1, source_target_pairs={{0,8},{8,0},{16,24},{24,16},{32,40},{40,32},{48,56},{56,48},{64,72... | collective-permute-start | bytes 1572872 | tf_op jit(solution)/shard_map/ppermute | solution.py:33
  14.5 2.8 %copy-start.3 = (bf16[32,1,32,256]{3,2,1,0:T(8,128)(2,1)S(1)}, bf16[32,1,32,256]{3,2,1,0:T(8,128)(2,1)}, u32[]{:S(2)}) copy-start(bf16[32,1,32,256]{3,2,1,0:T(8,128)(2,1)} %get-tuple-element.5) | copy-start | bytes 1572868
  15.3 3.4 %collective-permute-start.3 = (bf16[256,512]{1,0:T(8,128)(2,1)S(1)}, bf16[256,512]{1,0:T(8,128)(2,1)S(1)}, u32[]{:S(2)}, u32[]{:S(2)}) collective-permute-start(bf16[256,512]{1,0:T(8,128)(2,1)S(1)} %bitcast.169), channel_id=1, source_target_pairs={{0,8},{8,0},{16,24},{24,16},{32,40},{40,32},{48,56},{56,48},{64,72... | collective-permute-start | bytes 786440 | tf_op jit(solution)/shard_map/ppermute | solution.py:33
  23.0 14.3 %copy-start.8 = (f32[32,256]{1,0:T(8,128)S(1)}, f32[32,256]{1,0:T(8,128)}, u32[]{:S(2)}) copy-start(f32[32,256]{1,0:T(8,128)} %param.6) | copy-start | bytes 98308
  24.1 43.2 %all-to-all-start = ((bf16[32,136,128]{2,1,0:T(8,128)(2,1)}), bf16[32,136,128]{2,1,0:T(8,128)(2,1)S(1)}, u32[]{:S(2)}, u32[]{:S(2)}) async-start(bf16[32,136,128]{2,1,0:T(8,128)(2,1)} %pad_maximum_fusion), calls=%async_computation | async-start | bytes 2228224 | tf_op jit(solution)/shard_map/all_to_all | solution.py:24
  67.6 29.4 %copy-start.4 = (f32[128,128]{1,0:T(8,128)}, f32[128,128]{1,0:T(8,128)S(1)}, u32[]{:S(2)}) copy-start(f32[128,128]{1,0:T(8,128)S(1)} %convert_reduce_fusion) | copy-start | bytes 196612
  68.5 21.8 %all-to-all-start.1 = ((bf16[8,200,128]{2,1,0:T(8,128)(2,1)}), bf16[8,200,128]{2,1,0:T(8,128)(2,1)S(1)}, u32[]{:S(2)}, u32[]{:S(2)}) async-start(bf16[8,200,128]{2,1,0:T(8,128)(2,1)} %broadcast_in_dim.67), calls=%async_computation.1 | async-start | bytes 819200 | tf_op jit(solution)/shard_map/all_to_all | solution.py:24
  91.4 34.3 %all-to-all-start.2 = ((bf16[32,32,512]{2,1,0:T(8,128)(2,1)}), bf16[32,32,512]{2,1,0:T(8,128)(2,1)S(1)}, u32[]{:S(2)}, u32[]{:S(2)}) async-start(bf16[32,32,512]{2,1,0:T(8,128)(2,1)} %broadcast_in_dim.68), calls=%async_computation.2 | async-start | bytes 2097152 | tf_op jit(solution)/shard_map/all_to_all | solution.py:24
  125.7 4.7 %copy-start = (bf16[32,32,512]{2,1,0:T(8,128)(2,1)}, bf16[32,32,512]{2,1,0:T(8,128)(2,1)S(1)}, u32[]{:S(2)}) copy-start(bf16[32,32,512]{2,1,0:T(8,128)(2,1)S(1)} %all-to-all-done.2) | copy-start | bytes 3145732
  125.7 4.7 %collective-permute-start.4 = (bf16[32,32,512]{2,1,0:T(8,128)(2,1)S(1)}, bf16[32,32,512]{2,1,0:T(8,128)(2,1)}, u32[]{:S(2)}, u32[]{:S(2)}) collective-permute-start(bf16[32,32,512]{2,1,0:T(8,128)(2,1)S(1)} %all-to-all-done.2), channel_id=1, source_target_pairs={{0,8},{8,0},{16,24},{24,16},{32,40},{40,32},{48,56},{56,48},{64,72... | collective-permute-start | bytes 3145736 | tf_op jit(solution)/shard_map/ppermute | solution.py:33
  130.0 2.9 %copy-start.11 = (f32[32]{0:T(128)}, f32[32]{0:T(128)S(1)}, u32[]{:S(2)}) copy-start(f32[32]{0:T(128)S(1)} %get-tuple-element.26) | copy-start | bytes 388
  130.0 3.0 %copy-start.12 = (f32[32]{0:T(128)}, f32[32]{0:T(128)S(1)}, u32[]{:S(2)}) copy-start(f32[32]{0:T(128)S(1)} %get-tuple-element.27) | copy-start | bytes 388
  130.4 2.6 %copy-start.5 = (f32[8,4,8,256]{3,2,0,1:T(8,128)S(1)}, f32[8,4,8,256]{3,2,0,1:T(8,128)}, u32[]{:S(2)}) copy-start(f32[8,4,8,256]{3,2,0,1:T(8,128)} %copy.50) | copy-start | bytes 786436
  130.4 2.6 %copy-start.6 = (f32[8,4,8,256]{3,2,0,1:T(8,128)S(1)}, f32[8,4,8,256]{3,2,0,1:T(8,128)}, u32[]{:S(2)}) copy-start(f32[8,4,8,256]{3,2,0,1:T(8,128)} %copy.51) | copy-start | bytes 786436
  130.4 2.6 %copy-start.10 = (f32[4,4,8,128]{3,2,0,1:T(8,128)S(1)}, f32[4,4,8,128]{3,2,0,1:T(8,128)}, u32[]{:S(2)}) copy-start(f32[4,4,8,128]{3,2,0,1:T(8,128)} %copy.71) | copy-start | bytes 196612
  147.6 22.1 %all-to-all-start.3 = ((bf16[32,32,256]{2,1,0:T(8,128)(2,1)}), bf16[32,32,256]{2,1,0:T(8,128)(2,1)}, u32[]{:S(2)}, u32[]{:S(2)}) async-start(bf16[32,32,256]{2,1,0:T(8,128)(2,1)} %broadcast_in_dim.69), calls=%async_computation.3 | async-start | bytes 1048576 | tf_op jit(solution)/shard_map/all_to_all | solution.py:24
  169.7 16.0 %copy-start.2 = (bf16[256,256]{1,0:T(8,128)(2,1)S(1)}, bf16[256,256]{1,0:T(8,128)(2,1)}, u32[]{:S(2)}) copy-start(bf16[256,256]{1,0:T(8,128)(2,1)} %copy-done.1) | copy-start | bytes 393220
  170.4 13.8 %all-to-all-start.5 = ((bf16[8,32,512]{2,1,0:T(8,128)(2,1)}), bf16[8,32,512]{2,1,0:T(8,128)(2,1)S(1)}, u32[]{:S(2)}, u32[]{:S(2)}) async-start(bf16[8,32,512]{2,1,0:T(8,128)(2,1)} %broadcast_in_dim.71), calls=%async_computation.5 | async-start | bytes 524288 | tf_op jit(solution)/shard_map/all_to_all | solution.py:24
  173.8 10.5 %collective-permute-start.5 = (bf16[32,32,256]{2,1,0:T(8,128)(2,1)}, bf16[32,32,256]{2,1,0:T(8,128)(2,1)S(1)}, u32[]{:S(2)}, u32[]{:S(2)}) collective-permute-start(bf16[32,32,256]{2,1,0:T(8,128)(2,1)} %all-to-all-done.3), channel_id=1, source_target_pairs={{0,8},{8,0},{16,24},{24,16},{32,40},{40,32},{48,56},{56,48},{64,72... | collective-permute-start | bytes 1572872 | tf_op jit(solution)/shard_map/ppermute | solution.py:33
  (2 other events, 3.8 us)

commit v3 on v2

v3 whole, which is shorter than its diff:
```python
import math

import jax
import jax.numpy as jnp
from jax import lax
from jax.sharding import PartitionSpec as P

bf16 = jnp.bfloat16
f32 = jnp.float32

XS, ZS, CORES = 4, 8, 2


def row_index(x, z, core):
    return (x * ZS + z) * CORES + core


x_groups = [[row_index(x, z, k) for x in range(XS)] for z in range(ZS) for k in range(CORES)]
z_groups = [[row_index(x, z, k) for z in range(ZS)] for x in range(XS) for k in range(CORES)]


def swap(cells, axis, groups=None):
    return lax.all_to_all(cells, axis, 0, 0, tiled=True, axis_index_groups=groups)


def spread(cells, count, axis, groups=None):
    return swap(jnp.broadcast_to(cells[None], (count,) + cells.shape), axis, groups)


def other_core(cells):
    count = lax.axis_size("rows")
    return lax.ppermute(cells, "rows", [(i, i ^ 1) for i in range(count)])


def small_product(left, right):
    return jnp.dot(left, right, preferred_element_type=f32)


def on_device(coeffs, rotation, phase_ops, block_links, atom_size):
    rows_dev, orbital_count = coeffs.shape
    blocks_dev = phase_ops.shape[1]
    span_blocks = phase_ops.shape[2]
    block_size = phase_ops.shape[3]
    reach_blocks = (span_blocks - 1) // 2
    rows_axis = lax.axis_size("rows")
    cols_axis = lax.axis_size("cols")
    row_count = orbital_count // rows_axis
    col_count = orbital_count // cols_axis
    both = 2 * col_count
    row_start = lax.axis_index("rows") * row_count
    col_start = lax.axis_index("cols") * col_count
    core = lax.axis_index("rows") % CORES
    scale_factor = 0.125 / math.sqrt(orbital_count)

    within = lax.broadcasted_iota(jnp.int32, (blocks_dev, block_size), 1)
    live_rows = (within < atom_size[:, None]).reshape(rows_dev)
    raw_cols = lax.dynamic_slice_in_dim(coeffs, col_start, col_count, 1)
    own_cols = jnp.where(live_rows[:, None], raw_cols, jnp.zeros_like(raw_cols))
    width = reach_blocks * block_size
    up = [(i, (i + 1) % rows_axis) for i in range(rows_axis)]
    down = [((i + 1) % rows_axis, i) for i in range(rows_axis)]
    padded = jnp.concatenate(
        [
            lax.ppermute(own_cols[rows_dev - width :], "rows", up),
            own_cols,
            lax.ppermute(own_cols[:width], "rows", down),
        ],
        axis=0,
    )
    masked = jnp.where(live_rows[:, None], coeffs, jnp.zeros_like(coeffs))
    turned = masked.T.reshape(XS, ZS, CORES, row_count, rows_dev)

    def turned_half(which):
        half = lax.dynamic_index_in_dim(turned, which, 2, keepdims=False)
        return half.swapaxes(0, 1).reshape(-1, rows_dev)

    own_turned = turned_half(core)
    far_turned = other_core(turned_half(1 - core))
    stacked = jnp.stack(
        [
            padded[offset * block_size : (offset + blocks_dev) * block_size].reshape(
                blocks_dev, block_size, col_count
            )
            for offset in range(span_blocks)
        ],
        axis=1,
    )
    gated = phase_ops * block_links[None, :, :, None, None].astype(bf16)
    applied = jnp.einsum("pbtij,btjk->bipk", gated, stacked, preferred_element_type=f32)
    applied = applied.reshape(rows_dev, both).astype(bf16)
    far_applied = other_core(applied)

    product = small_product(own_turned, applied) + small_product(far_turned, far_applied)

    def diag_of(cols, values):
        return jnp.sum(jnp.tile(cols, (1, 2)).astype(f32) * values.astype(f32), axis=0)

    far_cols = jnp.where(core == 0, padded[width + rows_dev :], padded[:width])
    diag = diag_of(own_cols, applied) + diag_of(far_cols, far_applied)

    def with_diag(cells, values):
        high = lax.reduce_precision(values, 8, 7)
        tail = jnp.stack([high, values - high]).astype(bf16)
        tail = jnp.pad(tail, ((0, 6), (0, 0)))
        tail = jnp.broadcast_to(tail, cells.shape[:-2] + tail.shape)
        return jnp.concatenate([cells.astype(bf16), tail], axis=-2)

    def summed(cells):
        body, tail = cells[:, :-8].astype(f32), cells[:, -8:-6].astype(f32)
        return jnp.sum(body, axis=0), jnp.sum(tail, axis=(0, 1))

    group_rows = XS * row_count
    pieces = with_diag(product.reshape(ZS, group_rows, both), diag)
    chip, diag = summed(swap(pieces, "rows", z_groups))
    chip, diag = summed(spread(with_diag(chip, diag), XS, "rows", x_groups))
    own_x = lax.axis_index("rows") // (ZS * CORES)
    z_block = lax.dynamic_slice_in_dim(chip, own_x * row_count, row_count, 0)

    tail = jnp.pad(diag.reshape(2, col_count), ((0, row_count - 2), (0, 0)))
    packed = jnp.concatenate([z_block, rotation, tail], axis=1)
    across = lax.all_gather(packed, "cols", axis=0)

    def rows_of(cells):
        return cells.transpose(1, 0, 2).reshape(cells.shape[1], -1)

    z_rows = [rows_of(across[:, :, p * col_count : (p + 1) * col_count]) for p in range(2)]
    rot_rows = rows_of(across[:, :, both : both + col_count]).astype(bf16)
    diag_all = across[:, :2, both + col_count :].transpose(1, 0, 2).reshape(2, -1)

    panel = spread(chip.astype(bf16), ZS, "rows", z_groups)
    panel = panel.reshape(ZS, XS, row_count, both)
    away = other_core(panel)
    z_cols = jnp.where(core == 0, jnp.stack([panel, away], 2), jnp.stack([away, panel], 2))
    z_cols = z_cols.swapaxes(0, 1).reshape(orbital_count, both)

    diag_cols = lax.dynamic_slice_in_dim(diag_all, col_start, col_count, 1)
    diag_down = lax.dynamic_slice_in_dim(diag_all, row_start, row_count, 1)

    def generator(cos_block, sin_block, across_diag, down_diag):
        cos_part = cos_block.astype(f32) * (across_diag[0][None, :] - down_diag[0][:, None])
        sin_part = sin_block.astype(f32) * (across_diag[1][None, :] - down_diag[1][:, None])
        return (cos_part + sin_part) * scale_factor

    gen_cols = generator(z_cols[:, :col_count], z_cols[:, col_count:], diag_cols, diag_all)
    gen_cols = gen_cols.astype(bf16)
    gen_rows = generator(z_rows[0], z_rows[1], diag_all, diag_down)
    gen_block = generator(z_block[:, :col_count], z_block[:, col_count:], diag_cols, diag_down)

    def row_panels(block):
        cells = spread(block.astype(bf16), cols_axis, "cols")
        return [
            rows_of(cells[:, :, start : start + col_count])
            for start in range(0, block.shape[1], col_count)
        ]

    square = small_product(gen_rows.astype(bf16), gen_cols)
    first_rot = small_product(rot_rows, gen_cols)
    first_orb = small_product(masked, gen_cols)
    firsts = lax.all_gather(
        jnp.concatenate([first_orb, first_rot], axis=0).astype(bf16), "cols", axis=0
    )
    (square_rows,) = row_panels(square)
    back_rows = (0.5 * square_rows.astype(f32) - gen_rows).astype(bf16)
    half_block = z_block + small_product(back_rows, z_cols)
    half_rows = row_panels(half_block)
    first_cos = small_product(half_rows[0], gen_cols)
    first_sin = small_product(half_rows[1], gen_cols)
    first_rows = row_panels(jnp.concatenate([first_cos, first_sin], axis=1))
    first_rows = jnp.concatenate([rows_of(firsts), *first_rows], axis=0)
    second = 0.5 * small_product(first_rows, gen_cols)
    cuts = [rows_dev, rows_dev + row_count, rows_dev + 2 * row_count]
    second_orb, second_rot, second_cos, second_sin = jnp.split(second, cuts, axis=0)
    rotated = rotation + first_rot + second_rot
    orbitals = (own_cols.astype(f32) + first_orb + second_orb).astype(bf16)
    phase_cos = half_block[:, :col_count] + first_cos + second_cos
    phase_sin = half_block[:, col_count:] + first_sin + second_sin
    return (rotated, phase_cos, phase_sin, orbitals)


def solution(mesh):
    placed = (
        P("rows", None),
        P("rows", "cols"),
        P(None, "rows", None, None, None),
        P("rows", None),
        P("rows"),
    )
    return jax.shard_map(
        on_device,
        mesh=mesh,
        in_specs=placed,
        out_specs=(P("rows", "cols"), P("rows", "cols"), P("rows", "cols"), P("rows", "cols")),
        check_vma=False,
    )
```

time: 190 us -> 193 us (1.016)
  the two profiles are of different devices: /device:TPU:64 before, /device:TPU:1 now
where the time goes in v3:
time: 193 us; the launch traced here: 191 us
  blocking collectives  58 us (30%)
  waiting for transfers between devices  53.5 us (28%)
  starting transfers between devices  37.9 us (20%)
  between operations  14.7 us (8%)
  local copies, waits for them, and re-layouts  11.5 us (6%)
  other arithmetic  9.63 us (5%)
  matrix products  5.51 us (3%)
    all_to_all x3, blocking collectives, swap(): lax.all_to_all(cells, axis, 0, 0, tiled=True, axis_index_groups=groups)  58 us
    all_gather x1, waiting for transfers between devices, on_device(): across = lax.all_gather(packed, 'cols', axis=0)  28.2 us
    ppermute x3, starting transfers between devices, other_core(): return lax.ppermute(cells, 'rows', [(i, i ^ 1) for i in range(count)])  15.7 us
    all_to_all x3, waiting for transfers between devices, swap(): lax.all_to_all(cells, axis, 0, 0, tiled=True, axis_index_groups=groups)  14.5 us
    all_to_all x3, starting transfers between devices, swap(): lax.all_to_all(cells, axis, 0, 0, tiled=True, axis_index_groups=groups)  11.4 us
    all_gather x1, waiting for transfers between devices, on_device(): lax.all_gather(jnp.concatenate([first_orb, first_rot], axis=0).astype(bf1...  9.36 us
    ppermute x1, starting transfers between devices, on_device(): lax.ppermute(own_cols[rows_dev - width:], 'rows', up)  5.39 us
    ppermute x1, starting transfers between devices, on_device(): lax.ppermute(own_cols[:width], 'rows', down)  5.32 us
  transfers between devices with their start and end apart: 10, of which 6 were waited for; matrix products, arithmetic and copies ran while one was open for 7% of the time, Pallas kernels for 0%

profile of v3, /device:TPU:1, one launch (start us, length us, event | category | flops | bytes accessed | tf_op | source)
XLA Modules:
  0.0 190.7 jit_solution(3585829211677492713)
XLA Ops:
  8.9 5.4 %collective-permute-start = (bf16[256,256]{1,0:T(8,128)(2,1)S(1)}, bf16[256,256]{1,0:T(8,128)(2,1)S(1)}, u32[]{:S(2)}, u32[]{:S(2)}) collective-permute-start(bf16[256,256]{1,0:T(8,128)(2,1)S(1)} %dynamic-slice_select_fusion), channel_id=1, source_target_pairs={{0,8},{8,16},{16,24},{24,32},{32,40},{40,48},{48,56},{56,64},{64,7... | collective-permute-start | bytes 393224 | tf_op jit(solution)/shard_map/ppermute | solution.py:64
  14.3 5.3 %collective-permute-start.1 = (bf16[256,256]{1,0:T(8,128)(2,1)S(1)}, bf16[256,256]{1,0:T(8,128)(2,1)S(1)}, u32[]{:S(2)}, u32[]{:S(2)}) collective-permute-start(bf16[256,256]{1,0:T(8,128)(2,1)S(1)} %dynamic-slice_select_fusion), channel_id=1, source_target_pairs={{8,0},{16,8},{24,16},{32,24},{40,32},{48,40},{56,48},{64,56},{72,6... | collective-permute-start | bytes 393224 | tf_op jit(solution)/shard_map/ppermute | solution.py:66
  19.6 1.5 copy.76
  21.4 7.2 %collective-permute-start.2 = (bf16[1024,256]{1,0:T(8,128)(2,1)S(1)}, bf16[1024,256]{1,0:T(8,128)(2,1)S(1)}, u32[]{:S(2)}, u32[]{:S(2)}) collective-permute-start(bf16[1024,256]{1,0:T(8,128)(2,1)S(1)} %bitcast.177), channel_id=1, source_target_pairs={{0,8},{8,0},{16,24},{24,16},{32,40},{40,32},{48,56},{56,48},{64,72... | collective-permute-start | bytes 1572872 | tf_op jit(solution)/shard_map/ppermute | solution.py:32
  28.6 1.0 bitcast_convert_fusion
  31.5 1.9 %collective-permute-start.3 = (bf16[256,512]{1,0:T(8,128)(2,1)S(1)}, bf16[256,512]{1,0:T(8,128)(2,1)S(1)}, u32[]{:S(2)}, u32[]{:S(2)}) collective-permute-start(bf16[256,512]{1,0:T(8,128)(2,1)S(1)} %bitcast.167), channel_id=1, source_target_pairs={{0,8},{8,0},{16,24},{24,16},{32,40},{40,32},{48,56},{56,48},{64,72... | collective-permute-start | bytes 786440 | tf_op jit(solution)/shard_map/ppermute | solution.py:32
  35.6 33.0 %all_to_all.30 = bf16[8,136,512]{2,1,0:T(8,128)(2,1)S(1)} all-to-all(bf16[8,136,512]{2,1,0:T(8,128)(2,1)S(1)} %pad_maximum_fusion), channel_id=1, replica_groups={{0,16,32,48,64,80,96,112},{8,24,40,56,72,88,104,120},{128,144,160,176,1..., dimensions={0} | all-to-all | bytes 2228224 | tf_op jit(solution)/shard_map/all_to_all | solution.py:23
  69.8 3.5 %all-to-all-start.1 = ((bf16[4,136,512]{2,1,0:T(8,128)(2,1)}), bf16[4,136,512]{2,1,0:T(8,128)(2,1)S(1)}, u32[]{:S(2)}, u32[]{:S(2)}) async-start(bf16[4,136,512]{2,1,0:T(8,128)(2,1)} %broadcast_in_dim.62), calls=%async_computation.1 | async-start | bytes 1114112 | tf_op jit(solution)/shard_map/all_to_all | solution.py:23
  73.3 8.5 %all-to-all-done.1 = bf16[4,136,512]{2,1,0:T(8,128)(2,1)S(1)} async-done(((bf16[4,136,512]{2,1,0:T(8,128)(2,1)}), bf16[4,136,512]{2,1,0:T(8,128)(2,1)S(1)}, u32[]{:S(2)}, u32[]{:S(2)}) %all-to-all-start.1) | async-done | bytes 557088 | tf_op jit(solution)/shard_map/all_to_all | solution.py:23
  82.7 1.1 broadcast_in_dim.63
  83.7 3.6 %all-to-all-start.2 = ((bf16[8,128,512]{2,1,0:T(8,128)(2,1)}), bf16[8,128,512]{2,1,0:T(8,128)(2,1)S(1)}, u32[]{:S(2)}, u32[]{:S(2)}) async-start(bf16[8,128,512]{2,1,0:T(8,128)(2,1)} %broadcast_in_dim.63), calls=%async_computation.2 | async-start | bytes 2097152 | tf_op jit(solution)/shard_map/all_to_all | solution.py:23
  87.3 28.2 %all-gather.6.cloned.1.call-done = f32[256,1024]{1,0:T(8,128)} async-done(((f32[32,1024]{1,0:T(8,128)}), f32[256,1024]{1,0:T(8,128)}) %all-gather.6.cloned.1.call-update) | async-done | bytes 1048592 | tf_op jit(solution)/shard_map/all_gather | solution.py:121
  116.5 1.1 slice_bitcast_fusion.1
  117.6 6.6 %collective-permute-start.4 = (bf16[8,4,32,512]{3,2,1,0:T(8,128)(2,1)S(1)}, bf16[8,4,32,512]{3,2,1,0:T(8,128)(2,1)S(1)}, u32[]{:S(2)}, u32[]{:S(2)}) collective-permute-start(bf16[8,4,32,512]{3,2,1,0:T(8,128)(2,1)S(1)} %bitcast.150), channel_id=1, source_target_pairs={{0,8},{8,0},{16,24},{24,16},{32,40},{40,32},{48,56},{56,48},{64,72... | collective-permute-start | bytes 3145736 | tf_op jit(solution)/shard_map/ppermute | solution.py:32
  129.6 4.4 %all-to-all-start.3 = ((bf16[8,32,256]{2,1,0:T(8,128)(2,1)}), bf16[8,32,256]{2,1,0:T(8,128)(2,1)}, u32[]{:S(2)}, u32[]{:S(2)}) async-start(bf16[8,32,256]{2,1,0:T(8,128)(2,1)} %broadcast_in_dim.64), calls=%async_computation.3 | async-start | bytes 262144 | tf_op jit(solution)/shard_map/all_to_all | solution.py:23
  134.1 1.2 fusion.41
  136.0 6.0 %all-to-all-done.3 = bf16[8,32,256]{2,1,0:T(8,128)(2,1)} async-done(((bf16[8,32,256]{2,1,0:T(8,128)(2,1)}), bf16[8,32,256]{2,1,0:T(8,128)(2,1)}, u32[]{:S(2)}, u32[]{:S(2)}) %all-to-all-start.3) | async-done | bytes 131104 | tf_op jit(solution)/shard_map/all_to_all | solution.py:23
  142.0 1.2 fusion.24
  143.3 1.1 fusion.37
  144.4 11.7 %all_to_all.31 = bf16[8,32,512]{2,1,0:T(8,128)(2,1)S(1)} all-to-all(bf16[8,32,512]{2,1,0:T(8,128)(2,1)S(1)} %broadcast_in_dim.65), channel_id=1, replica_groups=mesh['rows'=64,'cols'=8] {'cols'}, dimensions={0} | all-to-all | bytes 524288 | tf_op jit(solution)/shard_map/all_to_all | solution.py:23
  156.8 13.2 %all_to_all.32 = bf16[8,32,512]{2,1,0:T(8,128)(2,1)S(1)} all-to-all(bf16[8,32,512]{2,1,0:T(8,128)(2,1)S(1)} %broadcast_in_dim.66), channel_id=1, replica_groups=mesh['rows'=64,'cols'=8] {'cols'}, dimensions={0} | all-to-all | bytes 524288 | tf_op jit(solution)/shard_map/all_to_all | solution.py:23
  170.1 9.4 %all-gather.4.cloned.1.call-done = bf16[8,288,256]{2,1,0:T(8,128)(2,1)} async-done(((bf16[1,288,256]{2,1,0:T(8,128)(2,1)}), bf16[8,288,256]{2,1,0:T(8,128)(2,1)}) %all-gather.4.cloned.1.call-update) | async-done | bytes 1179664 | tf_op jit(solution)/shard_map/all_gather | solution.py:159
  179.4 1.4 copy.98
  181.5 1.7 fusion.14
  (102 shorter events, 16.8 us)
Async XLA Ops:
  7.9 20.7 %copy-start.4 = (pred[256]{0:T(512)(128)(4,1)}, pred[256]{0:T(512)(128)(4,1)S(1)}, u32[]{:S(2)}) copy-start(pred[256]{0:T(512)(128)(4,1)S(1)} %compare_bitcast_fusion) | copy-start | bytes 772
  8.9 20.8 %collective-permute-start = (bf16[256,256]{1,0:T(8,128)(2,1)S(1)}, bf16[256,256]{1,0:T(8,128)(2,1)S(1)}, u32[]{:S(2)}, u32[]{:S(2)}) collective-permute-start(bf16[256,256]{1,0:T(8,128)(2,1)S(1)} %dynamic-slice_select_fusion), channel_id=1, source_target_pairs={{0,8},{8,16},{16,24},{24,32},{32,40},{40,48},{48,56},{56,64},{64,7... | collective-permute-start | bytes 393224 | tf_op jit(solution)/shard_map/ppermute | solution.py:64
  14.3 15.5 %collective-permute-start.1 = (bf16[256,256]{1,0:T(8,128)(2,1)S(1)}, bf16[256,256]{1,0:T(8,128)(2,1)S(1)}, u32[]{:S(2)}, u32[]{:S(2)}) collective-permute-start(bf16[256,256]{1,0:T(8,128)(2,1)S(1)} %dynamic-slice_select_fusion), channel_id=1, source_target_pairs={{8,0},{16,8},{24,16},{32,24},{40,32},{48,40},{56,48},{64,56},{72,6... | collective-permute-start | bytes 393224 | tf_op jit(solution)/shard_map/ppermute | solution.py:66
  21.2 8.5 %copy-start = (bf16[256,2048]{0,1:T(8,128)(2,1)}, bf16[256,2048]{0,1:T(8,128)(2,1)S(1)}, u32[]{:S(2)}) copy-start(bf16[256,2048]{0,1:T(8,128)(2,1)S(1)} %broadcast_select_fusion) | copy-start | bytes 3145732
  21.2 8.4 %copy-start.9 = (s32[2,5]{1,0:T(2,128)S(1)}, s32[2,5]{1,0:T(2,128)}, u32[]{:S(2)}) copy-start(s32[2,5]{1,0:T(2,128)} %param.8) | copy-start | bytes 124
  21.4 13.7 %collective-permute-start.2 = (bf16[1024,256]{1,0:T(8,128)(2,1)S(1)}, bf16[1024,256]{1,0:T(8,128)(2,1)S(1)}, u32[]{:S(2)}, u32[]{:S(2)}) collective-permute-start(bf16[1024,256]{1,0:T(8,128)(2,1)S(1)} %bitcast.177), channel_id=1, source_target_pairs={{0,8},{8,0},{16,24},{24,16},{32,40},{40,32},{48,56},{56,48},{64,72... | collective-permute-start | bytes 1572872 | tf_op jit(solution)/shard_map/ppermute | solution.py:32
  29.7 1.1 copy-start.8
  31.5 3.4 %collective-permute-start.3 = (bf16[256,512]{1,0:T(8,128)(2,1)S(1)}, bf16[256,512]{1,0:T(8,128)(2,1)S(1)}, u32[]{:S(2)}, u32[]{:S(2)}) collective-permute-start(bf16[256,512]{1,0:T(8,128)(2,1)S(1)} %bitcast.167), channel_id=1, source_target_pairs={{0,8},{8,0},{16,24},{24,16},{32,40},{40,32},{48,56},{56,48},{64,72... | collective-permute-start | bytes 786440 | tf_op jit(solution)/shard_map/ppermute | solution.py:32
  68.7 13.2 %copy-start.3 = (f32[32,256]{1,0:T(8,128)S(1)}, f32[32,256]{1,0:T(8,128)}, u32[]{:S(2)}) copy-start(f32[32,256]{1,0:T(8,128)} %param.6) | copy-start | bytes 98308
  69.8 12.0 %all-to-all-start.1 = ((bf16[4,136,512]{2,1,0:T(8,128)(2,1)}), bf16[4,136,512]{2,1,0:T(8,128)(2,1)S(1)}, u32[]{:S(2)}, u32[]{:S(2)}) async-start(bf16[4,136,512]{2,1,0:T(8,128)(2,1)} %broadcast_in_dim.62), calls=%async_computation.1 | async-start | bytes 1114112 | tf_op jit(solution)/shard_map/all_to_all | solution.py:23
  73.2 42.3 %all-gather.6.cloned.1.call-start = ((), (), s32[]{:S(2)}) async-start(), calls=%async_computation.7 | async-start | bytes 1179648 | tf_op jit(solution)/shard_map/all_gather | solution.py:121
  83.7 33.9 %all-to-all-start.2 = ((bf16[8,128,512]{2,1,0:T(8,128)(2,1)}), bf16[8,128,512]{2,1,0:T(8,128)(2,1)S(1)}, u32[]{:S(2)}, u32[]{:S(2)}) async-start(bf16[8,128,512]{2,1,0:T(8,128)(2,1)} %broadcast_in_dim.63), calls=%async_computation.2 | async-start | bytes 2097152 | tf_op jit(solution)/shard_map/all_to_all | solution.py:23
  117.6 8.8 %collective-permute-start.4 = (bf16[8,4,32,512]{3,2,1,0:T(8,128)(2,1)S(1)}, bf16[8,4,32,512]{3,2,1,0:T(8,128)(2,1)S(1)}, u32[]{:S(2)}, u32[]{:S(2)}) collective-permute-start(bf16[8,4,32,512]{3,2,1,0:T(8,128)(2,1)S(1)} %bitcast.150), channel_id=1, source_target_pairs={{0,8},{8,0},{16,24},{24,16},{32,40},{40,32},{48,56},{56,48},{64,72... | collective-permute-start | bytes 3145736 | tf_op jit(solution)/shard_map/ppermute | solution.py:32
  125.9 2.7 %copy-start.6 = (f32[32]{0:T(128)}, f32[32]{0:T(128)S(1)}, u32[]{:S(2)}) copy-start(f32[32]{0:T(128)S(1)} %get-tuple-element.28) | copy-start | bytes 388
  125.9 2.7 %copy-start.7 = (f32[32]{0:T(128)}, f32[32]{0:T(128)S(1)}, u32[]{:S(2)}) copy-start(f32[32]{0:T(128)S(1)} %get-tuple-element.29) | copy-start | bytes 388
  126.9 1.2 copy-start.1
  129.6 12.4 %all-to-all-start.3 = ((bf16[8,32,256]{2,1,0:T(8,128)(2,1)}), bf16[8,32,256]{2,1,0:T(8,128)(2,1)}, u32[]{:S(2)}, u32[]{:S(2)}) async-start(bf16[8,32,256]{2,1,0:T(8,128)(2,1)} %broadcast_in_dim.64), calls=%async_computation.3 | async-start | bytes 262144 | tf_op jit(solution)/shard_map/all_to_all | solution.py:23
  134.0 45.4 %all-gather.4.cloned.1.call-start = ((), (), s32[]{:S(2)}) async-start(), calls=%async_computation.6 | async-start | bytes 1327104 | tf_op jit(solution)/shard_map/all_gather | solution.py:159
  180.9 0.7 copy-start.5
  180.9 2.3 %copy-start.2 = (f32[32,512]{1,0:T(8,128)S(1)}, f32[32,512]{1,0:T(8,128)}, u32[]{:S(2)}) copy-start(f32[32,512]{1,0:T(8,128)} %get-tuple-element.33) | copy-start | bytes 196612
Sparse Core Ops, SparseCore 0:
  82.7 32.7 all-gather.5
  136.9 42.4 all-gather.3

commit v4 on v2

--- a/solution.py
+++ b/solution.py
@@ -15,6 +15,8 @@
     return (x * ZS + z) * CORES + core
 
 
+x_groups = [[row_index(x, z, k) for x in range(XS)] for z in range(ZS) for k in range(CORES)]
+z_groups = [[row_index(x, z, k) for z in range(ZS)] for x in range(XS) for k in range(CORES)]
 xz_groups = [
     [row_index(x, z, k) for x in range(XS) for z in range(ZS)] for k in range(CORES)
 ]
@@ -53,16 +55,6 @@
     core = lax.axis_index("rows") % CORES
     scale_factor = 0.125 / math.sqrt(orbital_count)
 
-    def lanes_out(cells):
-        lead, rows, wide = cells.shape[:-2], cells.shape[-2], cells.shape[-1]
-        cells = cells.reshape(lead + (rows, wide // 128, 128))
-        return jnp.swapaxes(cells, -3, -2).reshape(lead + (rows * wide // 128, 128))
-
-    def lanes_in(cells, rows):
-        lead = cells.shape[:-2]
-        cells = cells.reshape(lead + (-1, rows, 128))
-        return jnp.swapaxes(cells, -3, -2).reshape(lead + (rows, -1))
-
     within = lax.broadcasted_iota(jnp.int32, (blocks_dev, block_size), 1)
     live_rows = (within < atom_size[:, None]).reshape(rows_dev)
     raw_cols = lax.dynamic_slice_in_dim(coeffs, col_start, col_count, 1)
@@ -79,9 +71,13 @@
         axis=0,
     )
     masked = jnp.where(live_rows[:, None], coeffs, jnp.zeros_like(coeffs))
-    turned = masked.T.reshape(XS * ZS, CORES, row_count, rows_dev)
-    own_turned = lax.dynamic_index_in_dim(turned, core, 1, keepdims=False)
-    far_turned = other_core(lax.dynamic_index_in_dim(turned, 1 - core, 1, keepdims=False))
+    turned = masked.T.reshape(XS, ZS, CORES, row_count, rows_dev)
+
+    def turned_half(which):
+        return lax.dynamic_index_in_dim(turned, which, 2, keepdims=False).reshape(-1, rows_dev)
+
+    own_turned = turned_half(core)
+    far_turned = other_core(turned_half(1 - core))
     stacked = jnp.stack(
         [
             padded[offset * block_size : (offset + blocks_dev) * block_size].reshape(
@@ -96,8 +92,7 @@
     applied = applied.reshape(rows_dev, both).astype(bf16)
     far_applied = other_core(applied)
 
-    product = small_product(own_turned.reshape(-1, rows_dev), applied)
-    product = product + small_product(far_turned.reshape(-1, rows_dev), far_applied)
+    product = small_product(own_turned, applied) + small_product(far_turned, far_applied)
 
     def diag_of(cols, values):
         return jnp.sum(jnp.tile(cols, (1, 2)).astype(f32) * values.astype(f32), axis=0)
@@ -105,45 +100,47 @@
     far_cols = jnp.where(core == 0, padded[width + rows_dev :], padded[:width])
     diag = diag_of(own_cols, applied) + diag_of(far_cols, far_applied)
 
-    def two_parts(values):
+    def with_diag(cells, values):
         high = lax.reduce_precision(values, 8, 7)
-        return jnp.stack([high.astype(bf16), (values - high).astype(bf16)]).reshape(-1, 128)
+        tail = jnp.stack([high, values - high]).astype(bf16)
+        tail = jnp.pad(tail, ((0, 6), (0, 0)))
+        tail = jnp.broadcast_to(tail, cells.shape[:-2] + tail.shape)
+        return jnp.concatenate([cells.astype(bf16), tail], axis=-2)
 
-    tail_rows = 2 * both // 128
+    def summed(cells):
+        body, tail = cells[:, :-8].astype(f32), cells[:, -8:-6].astype(f32)
+        return jnp.sum(body, axis=0), jnp.sum(tail, axis=(0, 1))
 
-    def parts_sum(cells):
-        cells = cells.astype(f32).reshape(-1, 2, both)
-        return cells[:, 0] + cells[:, 1]
-
-    tail = jnp.broadcast_to(two_parts(diag)[None], (XS * ZS, tail_rows, 128))
-    pieces = lanes_out(product.astype(bf16).reshape(XS * ZS, row_count, both))
-    got = swap(jnp.concatenate([pieces, tail], axis=1), "rows", xz_groups)
-    body_rows = row_count * both // 128
-    diag = jnp.sum(parts_sum(got[:, body_rows:]), axis=0)
-    z_block = lanes_in(jnp.sum(got[:, :body_rows].astype(f32), axis=0), row_count)
+    pieces = with_diag(product.reshape(XS, ZS * row_count, both), diag)
+    chip, diag = summed(swap(pieces, "rows", x_groups))
+    pieces = with_diag(chip.reshape(ZS, row_count, both), diag)
+    z_block, diag = summed(swap(pieces, "rows", z_groups))
     z_half = z_block.astype(bf16)
 
-    packed = jnp.concatenate(
-        [lanes_out(z_half), lanes_out(rotation.astype(bf16)), two_parts(diag)], axis=0
-    )
+    high = lax.reduce_precision(diag, 8, 7)
+    terms = jnp.stack([high, diag - high]).astype(bf16).reshape(-1, 128)
+    terms = jnp.pad(terms, ((0, row_count - terms.shape[0]), (0, 0)))
+    packed = jnp.concatenate([z_half, rotation.astype(bf16), terms], axis=1)
     across = spread(packed, cols_axis, "cols")
 
     def rows_of(cells):
         return cells.transpose(1, 0, 2).reshape(cells.shape[1], -1)
 
-    wide = lanes_in(across[:, :-tail_rows], row_count)
-    z_rows = [rows_of(wide[:, :, p * col_count : (p + 1) * col_count]) for p in range(2)]
-    rot_rows = rows_of(wide[:, :, both:])
-    diag_all = parts_sum(across[:, -tail_rows:])
-    diag_all = diag_all.reshape(cols_axis, 2, col_count).transpose(1, 0, 2).reshape(2, -1)
+    z_rows = [rows_of(across[:, :, p * col_count : (p + 1) * col_count]) for p in range(2)]
+    rot_rows = rows_of(across[:, :, both : both + col_count])
+    terms = across[:, : 2 * both // 128, both + col_count :].astype(f32)
+    terms = terms.reshape(cols_axis, 2, 2, col_count)
+    diag_all = jnp.sum(terms, axis=1).transpose(1, 0, 2).reshape(2, -1)
 
     def halves(cells):
         away = other_core(cells)
         pair = jnp.where(core == 0, jnp.stack([cells, away], 1), jnp.stack([away, cells], 1))
         return pair.reshape(orbital_count, -1)
 
-    panel = spread(z_half, XS * ZS, "rows", xz_groups)
-    z_cols = halves(panel)
+    panel = spread(z_half, ZS, "rows", z_groups)
+    panel = spread(panel, XS, "rows", x_groups)
+    panel, diag_all = lax.optimization_barrier((panel, diag_all))
+    z_cols = halves(panel.reshape(XS * ZS, row_count, both))
 
     diag_cols = lax.dynamic_slice_in_dim(diag_all, col_start, col_count, 1)
     diag_down = lax.dynamic_slice_in_dim(diag_all, row_start, row_count, 1)

time: 190 us -> 176 us (0.926)
  blocking collectives: 12.8 us -> 51.4 us
  waiting for transfers between devices: 95.1 us -> 56.8 us
  starting transfers between devices: 48.5 us -> 42.2 us
  local copies, waits for them, and re-layouts: 11.8 us -> 6.8 us
  matrix products: 9.34 us -> 6.45 us
    all_to_all x5, waiting for transfers between devices: 93.9 us -> 54.2 us  [swap(): lax.all_to_all(cells, axis, 0, 0, tiled=True, axis_index_groups=groups)]
    all_to_all x1 -> x3, blocking collectives: 12.8 us -> 51.4 us  [swap(): lax.all_to_all(cells, axis, 0, 0, tiled=True, axis_index_groups=groups)]
    all_to_all x5, starting transfers between devices: 34.5 us -> 28.2 us  [swap(): lax.all_to_all(cells, axis, 0, 0, tiled=True, axis_index_groups=groups)]
    dot_general x8, matrix products: 8.9 us -> 6.01 us  [small_product(): return jnp.dot(left, right, preferred_element_type=f32)]
    broadcast_in_dim x5 -> x6, local copies, waits for them, and re-layouts: 3.54 us -> 4.24 us  [spread(): jnp.broadcast_to(cells[None], (count,) + cells.shape)]
  transfers between devices with their start and end apart: 11 -> 11, of which waited for: 7 -> 7; matrix products, arithmetic and copies ran while one was open for 7% -> 4% of each run, Pallas kernels for 0% -> 0%
where the time goes in v4:
time: 176 us; the launch traced here: 175 us
  waiting for transfers between devices  56.8 us (32%)
  blocking collectives  51.4 us (29%)
  starting transfers between devices  42.2 us (24%)
  other arithmetic  9.97 us (6%)
  local copies, waits for them, and re-layouts  6.8 us (4%)
  matrix products  6.45 us (4%)
    all_to_all x5, waiting for transfers between devices, swap(): lax.all_to_all(cells, axis, 0, 0, tiled=True, axis_index_groups=groups)  54.2 us
    all_to_all x3, blocking collectives, swap(): lax.all_to_all(cells, axis, 0, 0, tiled=True, axis_index_groups=groups)  51.4 us
    all_to_all x5, starting transfers between devices, swap(): lax.all_to_all(cells, axis, 0, 0, tiled=True, axis_index_groups=groups)  28.2 us
    ppermute x4, starting transfers between devices, other_core(): return lax.ppermute(cells, 'rows', [(i, i ^ 1) for i in range(count)])  8.41 us
    dot_general x8, matrix products, small_product(): return jnp.dot(left, right, preferred_element_type=f32)  6.01 us
    broadcast_in_dim x6, local copies, waits for them, and re-layouts, spread(): jnp.broadcast_to(cells[None], (count,) + cells.shape)  4.24 us
    select_n x2, other arithmetic, halves(): jnp.where(core == 0, jnp.stack([cells, away], 1), jnp.stack([away, cells]...  3.89 us
    ppermute x1, starting transfers between devices, on_device(): lax.ppermute(own_cols[:width], 'rows', down)  3.64 us
  transfers between devices with their start and end apart: 11, of which 7 were waited for; matrix products, arithmetic and copies ran while one was open for 4% of the time, Pallas kernels for 0%

profile of v4, /device:TPU:64, one launch (start us, length us, event | category | flops | bytes accessed | tf_op | source)
XLA Modules:
  0.0 174.8 jit_solution(15930790286027361482)
XLA Ops:
  2.4 1.9 %collective-permute-start = (bf16[256,256]{1,0:T(8,128)(2,1)S(1)}, bf16[256,256]{1,0:T(8,128)(2,1)S(1)}, u32[]{:S(2)}, u32[]{:S(2)}) collective-permute-start(bf16[256,256]{1,0:T(8,128)(2,1)S(1)} %dynamic-slice_select_fusion), channel_id=1, source_target_pairs={{0,8},{8,16},{16,24},{24,32},{32,40},{40,48},{48,56},{56,64},{64,7... | collective-permute-start | bytes 393224 | tf_op jit(solution)/shard_map/ppermute | solution.py:67
  4.3 3.6 %collective-permute-start.1 = (bf16[256,256]{1,0:T(8,128)(2,1)S(1)}, bf16[256,256]{1,0:T(8,128)(2,1)S(1)}, u32[]{:S(2)}, u32[]{:S(2)}) collective-permute-start(bf16[256,256]{1,0:T(8,128)(2,1)S(1)} %dynamic-slice_select_fusion), channel_id=1, source_target_pairs={{8,0},{16,8},{24,16},{32,24},{40,32},{48,40},{56,48},{64,56},{72,6... | collective-permute-start | bytes 393224 | tf_op jit(solution)/shard_map/ppermute | solution.py:69
  8.0 1.5 copy.57
  9.7 2.7 %collective-permute-start.2 = (bf16[1024,256]{1,0:T(8,128)(2,1)S(1)}, bf16[1024,256]{1,0:T(8,128)(2,1)S(1)}, u32[]{:S(2)}, u32[]{:S(2)}) collective-permute-start(bf16[1024,256]{1,0:T(8,128)(2,1)S(1)} %bitcast.150), channel_id=1, source_target_pairs={{0,8},{8,0},{16,24},{24,16},{32,40},{40,32},{48,56},{56,48},{64,72... | collective-permute-start | bytes 1572872 | tf_op jit(solution)/shard_map/ppermute | solution.py:35
  14.4 1.9 %collective-permute-start.3 = (bf16[256,512]{1,0:T(8,128)(2,1)S(1)}, bf16[256,512]{1,0:T(8,128)(2,1)S(1)}, u32[]{:S(2)}, u32[]{:S(2)}) collective-permute-start(bf16[256,512]{1,0:T(8,128)(2,1)S(1)} %bitcast.139), channel_id=1, source_target_pairs={{0,8},{8,0},{16,24},{24,16},{32,40},{40,32},{48,56},{56,48},{64,72... | collective-permute-start | bytes 786440 | tf_op jit(solution)/shard_map/ppermute | solution.py:35
  18.5 19.8 %all_to_all.40 = bf16[4,264,512]{2,1,0:T(8,128)(2,1)S(1)} all-to-all(bf16[4,264,512]{2,1,0:T(8,128)(2,1)S(1)} %pad_maximum_fusion), channel_id=1, replica_groups={{0,128,256,384},{8,136,264,392},{16,144,272,400},{24,152,280,408},{32,1..., dimensions={0} | all-to-all | bytes 2162688 | tf_op jit(solution)/shard_map/all_to_all | solution.py:26
  39.4 10.8 %all-to-all-start.1 = ((bf16[8,40,512]{2,1,0:T(8,128)(2,1)}), bf16[8,40,512]{2,1,0:T(8,128)(2,1)S(1)}, u32[]{:S(2)}, u32[]{:S(2)}) async-start(bf16[8,40,512]{2,1,0:T(8,128)(2,1)} %pad_maximum_fusion.1), calls=%async_computation.1 | async-start | bytes 655360 | tf_op jit(solution)/shard_map/all_to_all | solution.py:26
  50.1 11.2 %all-to-all-done.1 = bf16[8,40,512]{2,1,0:T(8,128)(2,1)S(1)} async-done(((bf16[8,40,512]{2,1,0:T(8,128)(2,1)}), bf16[8,40,512]{2,1,0:T(8,128)(2,1)S(1)}, u32[]{:S(2)}, u32[]{:S(2)}) %all-to-all-start.1) | async-done | bytes 327712 | tf_op jit(solution)/shard_map/all_to_all | solution.py:26
  62.1 4.8 %all-to-all-start.3 = ((bf16[8,32,512]{2,1,0:T(8,128)(2,1)}), bf16[8,32,512]{2,1,0:T(8,128)(2,1)S(1)}, u32[]{:S(2)}, u32[]{:S(2)}) async-start(bf16[8,32,512]{2,1,0:T(8,128)(2,1)} %broadcast_in_dim.73), calls=%async_computation.3 | async-start | bytes 524288 | tf_op jit(solution)/shard_map/all_to_all | solution.py:26
  67.0 9.0 %all-to-all-done.3 = bf16[8,32,512]{2,1,0:T(8,128)(2,1)S(1)} async-done(((bf16[8,32,512]{2,1,0:T(8,128)(2,1)}), bf16[8,32,512]{2,1,0:T(8,128)(2,1)S(1)}, u32[]{:S(2)}, u32[]{:S(2)}) %all-to-all-start.3) | async-done | bytes 262176 | tf_op jit(solution)/shard_map/all_to_all | solution.py:26
  76.0 19.5 %all_to_all.41 = bf16[8,32,896]{2,1,0:T(8,128)(2,1)S(1)} all-to-all(bf16[8,32,896]{2,1,0:T(8,128)(2,1)S(1)} %broadcast_in_dim.72), channel_id=1, replica_groups=mesh['rows'=64,'cols'=8] {'cols'}, dimensions={0} | all-to-all | bytes 917504 | tf_op jit(solution)/shard_map/all_to_all | solution.py:26
  96.6 3.5 %all-to-all-start.4 = ((bf16[4,8,32,512]{3,2,1,0:T(8,128)(2,1)}), bf16[4,8,32,512]{3,2,1,0:T(8,128)(2,1)S(1)}, u32[]{:S(2)}, u32[]{:S(2)}) async-start(bf16[4,8,32,512]{3,2,1,0:T(8,128)(2,1)} %broadcast_in_dim.74), calls=%async_computation.4 | async-start | bytes 2097152 | tf_op jit(solution)/shard_map/all_to_all | solution.py:26
  100.2 10.8 %all-to-all-done.4 = bf16[4,8,32,512]{3,2,1,0:T(8,128)(2,1)S(1)} async-done(((bf16[4,8,32,512]{3,2,1,0:T(8,128)(2,1)}), bf16[4,8,32,512]{3,2,1,0:T(8,128)(2,1)S(1)}, u32[]{:S(2)}, u32[]{:S(2)}) %all-to-all-start.4) | async-done | bytes 1048608 | tf_op jit(solution)/shard_map/all_to_all | solution.py:26
  111.0 1.9 %collective-permute-start.4 = (bf16[32,32,512]{2,1,0:T(8,128)(2,1)S(1)}, bf16[32,32,512]{2,1,0:T(8,128)(2,1)}, u32[]{:S(2)}, u32[]{:S(2)}) collective-permute-start(bf16[32,32,512]{2,1,0:T(8,128)(2,1)S(1)} %bitcast.130), channel_id=1, source_target_pairs={{0,8},{8,0},{16,24},{24,16},{32,40},{40,32},{48,56},{56,48},{64,72... | collective-permute-start | bytes 3145736 | tf_op jit(solution)/shard_map/ppermute | solution.py:35
  113.9 1.8 %collective-permute-done.4 = bf16[32,32,512]{2,1,0:T(8,128)(2,1)} collective-permute-done((bf16[32,32,512]{2,1,0:T(8,128)(2,1)S(1)}, bf16[32,32,512]{2,1,0:T(8,128)(2,1)}, u32[]{:S(2)}, u32[]{:S(2)}) %collective-permute-start.4) | collective-permute-done | bytes 1048608 | tf_op jit(solution)/shard_map/ppermute | solution.py:35
  115.7 2.6 %maximum_select_fusion = bf16[32,2,32,512]{3,2,1,0:T(8,128)(2,1)S(1)} fusion(bf16[32,1,32,512]{3,2,1,0:T(8,128)(2,1)} %bitcast.35, bf16[32,1,32,512]{3,2,1,0:T(8,128)(2,1)} %bitcast.131, pred[]{:T(512)S(6)} %eq.4), kind=kLoop, calls=%fused_computation | loop fusion | flops 3145728 | bytes 4194305 | tf_op jit(solution)/shard_map/jit(_where)/select_n | solution.py:137
  119.1 12.0 %all_to_all.42 = bf16[8,32,256]{2,1,0:T(8,128)(2,1)S(1)} all-to-all(bf16[8,32,256]{2,1,0:T(8,128)(2,1)S(1)} %broadcast_in_dim.76), channel_id=1, replica_groups=mesh['rows'=64,'cols'=8] {'cols'}, dimensions={0} | all-to-all | bytes 262144 | tf_op jit(solution)/shard_map/all_to_all | solution.py:26
  132.0 5.7 %all-to-all-start.5 = ((bf16[32,32,256]{2,1,0:T(8,128)(2,1)}), bf16[32,32,256]{2,1,0:T(8,128)(2,1)}, u32[]{:S(2)}, u32[]{:S(2)}) async-start(bf16[32,32,256]{2,1,0:T(8,128)(2,1)} %broadcast_in_dim.75), calls=%async_computation.5 | async-start | bytes 1048576 | tf_op jit(solution)/shard_map/all_to_all | solution.py:26
  140.0 14.8 %all-to-all-done.5 = bf16[32,32,256]{2,1,0:T(8,128)(2,1)} async-done(((bf16[32,32,256]{2,1,0:T(8,128)(2,1)}), bf16[32,32,256]{2,1,0:T(8,128)(2,1)}, u32[]{:S(2)}, u32[]{:S(2)}) %all-to-all-start.5) | async-done | bytes 524320 | tf_op jit(solution)/shard_map/all_to_all | solution.py:26
  154.8 1.5 broadcast_in_dim.77
  156.3 3.4 %all-to-all-start.7 = ((bf16[8,32,512]{2,1,0:T(8,128)(2,1)}), bf16[8,32,512]{2,1,0:T(8,128)(2,1)S(1)}, u32[]{:S(2)}, u32[]{:S(2)}) async-start(bf16[8,32,512]{2,1,0:T(8,128)(2,1)} %broadcast_in_dim.77), calls=%async_computation.7 | async-start | bytes 524288 | tf_op jit(solution)/shard_map/all_to_all | solution.py:26
  159.7 1.9 %collective-permute-start.5 = (bf16[32,32,256]{2,1,0:T(8,128)(2,1)}, bf16[32,32,256]{2,1,0:T(8,128)(2,1)S(1)}, u32[]{:S(2)}, u32[]{:S(2)}) collective-permute-start(bf16[32,32,256]{2,1,0:T(8,128)(2,1)} %all-to-all-done.5), channel_id=1, source_target_pairs={{0,8},{8,0},{16,24},{24,16},{32,40},{40,32},{48,56},{56,48},{64,72... | collective-permute-start | bytes 1572872 | tf_op jit(solution)/shard_map/ppermute | solution.py:35
  161.6 8.4 %all-to-all-done.7 = bf16[8,32,512]{2,1,0:T(8,128)(2,1)S(1)} async-done(((bf16[8,32,512]{2,1,0:T(8,128)(2,1)}), bf16[8,32,512]{2,1,0:T(8,128)(2,1)S(1)}, u32[]{:S(2)}, u32[]{:S(2)}) %all-to-all-start.7) | async-done | bytes 262176 | tf_op jit(solution)/shard_map/all_to_all | solution.py:26
  170.2 1.3 maximum_select_fusion.1
  (88 shorter events, 17.2 us)
Async XLA Ops:
  2.4 11.1 %collective-permute-start = (bf16[256,256]{1,0:T(8,128)(2,1)S(1)}, bf16[256,256]{1,0:T(8,128)(2,1)S(1)}, u32[]{:S(2)}, u32[]{:S(2)}) collective-permute-start(bf16[256,256]{1,0:T(8,128)(2,1)S(1)} %dynamic-slice_select_fusion), channel_id=1, source_target_pairs={{0,8},{8,16},{16,24},{24,32},{32,40},{40,48},{48,56},{56,64},{64,7... | collective-permute-start | bytes 393224 | tf_op jit(solution)/shard_map/ppermute | solution.py:67
  4.3 9.2 %collective-permute-start.1 = (bf16[256,256]{1,0:T(8,128)(2,1)S(1)}, bf16[256,256]{1,0:T(8,128)(2,1)S(1)}, u32[]{:S(2)}, u32[]{:S(2)}) collective-permute-start(bf16[256,256]{1,0:T(8,128)(2,1)S(1)} %dynamic-slice_select_fusion), channel_id=1, source_target_pairs={{8,0},{16,8},{24,16},{32,24},{40,32},{48,40},{56,48},{64,56},{72,6... | collective-permute-start | bytes 393224 | tf_op jit(solution)/shard_map/ppermute | solution.py:69
  9.5 4.0 %copy-start.6 = (s32[2,5]{1,0:T(2,128)S(1)}, s32[2,5]{1,0:T(2,128)}, u32[]{:S(2)}) copy-start(s32[2,5]{1,0:T(2,128)} %param.8) | copy-start | bytes 124
  9.7 8.3 %collective-permute-start.2 = (bf16[1024,256]{1,0:T(8,128)(2,1)S(1)}, bf16[1024,256]{1,0:T(8,128)(2,1)S(1)}, u32[]{:S(2)}, u32[]{:S(2)}) collective-permute-start(bf16[1024,256]{1,0:T(8,128)(2,1)S(1)} %bitcast.150), channel_id=1, source_target_pairs={{0,8},{8,0},{16,24},{24,16},{32,40},{40,32},{48,56},{56,48},{64,72... | collective-permute-start | bytes 1572872 | tf_op jit(solution)/shard_map/ppermute | solution.py:35
  12.3 1.3 copy-start.5
  14.4 3.4 %collective-permute-start.3 = (bf16[256,512]{1,0:T(8,128)(2,1)S(1)}, bf16[256,512]{1,0:T(8,128)(2,1)S(1)}, u32[]{:S(2)}, u32[]{:S(2)}) collective-permute-start(bf16[256,512]{1,0:T(8,128)(2,1)S(1)} %bitcast.139), channel_id=1, source_target_pairs={{0,8},{8,0},{16,24},{24,16},{32,40},{40,32},{48,56},{56,48},{64,72... | collective-permute-start | bytes 786440 | tf_op jit(solution)/shard_map/ppermute | solution.py:35
  18.5 31.6 %copy-start.3 = (f32[32,256]{1,0:T(8,128)S(1)}, f32[32,256]{1,0:T(8,128)}, u32[]{:S(2)}) copy-start(f32[32,256]{1,0:T(8,128)} %param.6) | copy-start | bytes 98308
  39.4 22.0 %all-to-all-start.1 = ((bf16[8,40,512]{2,1,0:T(8,128)(2,1)}), bf16[8,40,512]{2,1,0:T(8,128)(2,1)S(1)}, u32[]{:S(2)}, u32[]{:S(2)}) async-start(bf16[8,40,512]{2,1,0:T(8,128)(2,1)} %pad_maximum_fusion.1), calls=%async_computation.1 | async-start | bytes 655360 | tf_op jit(solution)/shard_map/all_to_all | solution.py:26
  62.1 13.8 %all-to-all-start.3 = ((bf16[8,32,512]{2,1,0:T(8,128)(2,1)}), bf16[8,32,512]{2,1,0:T(8,128)(2,1)S(1)}, u32[]{:S(2)}, u32[]{:S(2)}) async-start(bf16[8,32,512]{2,1,0:T(8,128)(2,1)} %broadcast_in_dim.73), calls=%async_computation.3 | async-start | bytes 524288 | tf_op jit(solution)/shard_map/all_to_all | solution.py:26
  95.5 18.2 %copy-start.1 = (bf16[8,32,896]{2,1,0:T(8,128)(2,1)}, bf16[8,32,896]{2,1,0:T(8,128)(2,1)S(1)}, u32[]{:S(2)}) copy-start(bf16[8,32,896]{2,1,0:T(8,128)(2,1)S(1)} %all_to_all.41) | copy-start | bytes 1376260
  96.6 14.4 %all-to-all-start.4 = ((bf16[4,8,32,512]{3,2,1,0:T(8,128)(2,1)}), bf16[4,8,32,512]{3,2,1,0:T(8,128)(2,1)S(1)}, u32[]{:S(2)}, u32[]{:S(2)}) async-start(bf16[4,8,32,512]{3,2,1,0:T(8,128)(2,1)} %broadcast_in_dim.74), calls=%async_computation.4 | async-start | bytes 2097152 | tf_op jit(solution)/shard_map/all_to_all | solution.py:26
  111.0 4.7 %copy-start = (bf16[4,8,32,512]{3,2,1,0:T(8,128)(2,1)}, bf16[4,8,32,512]{3,2,1,0:T(8,128)(2,1)S(1)}, u32[]{:S(2)}) copy-start(bf16[4,8,32,512]{3,2,1,0:T(8,128)(2,1)S(1)} %all-to-all-done.4) | copy-start | bytes 3145732
  111.0 4.7 %collective-permute-start.4 = (bf16[32,32,512]{2,1,0:T(8,128)(2,1)S(1)}, bf16[32,32,512]{2,1,0:T(8,128)(2,1)}, u32[]{:S(2)}, u32[]{:S(2)}) collective-permute-start(bf16[32,32,512]{2,1,0:T(8,128)(2,1)S(1)} %bitcast.130), channel_id=1, source_target_pairs={{0,8},{8,0},{16,24},{24,16},{32,40},{40,32},{48,56},{56,48},{64,72... | collective-permute-start | bytes 3145736 | tf_op jit(solution)/shard_map/ppermute | solution.py:35
  132.0 22.8 %all-to-all-start.5 = ((bf16[32,32,256]{2,1,0:T(8,128)(2,1)}), bf16[32,32,256]{2,1,0:T(8,128)(2,1)}, u32[]{:S(2)}, u32[]{:S(2)}) async-start(bf16[32,32,256]{2,1,0:T(8,128)(2,1)} %broadcast_in_dim.75), calls=%async_computation.5 | async-start | bytes 1048576 | tf_op jit(solution)/shard_map/all_to_all | solution.py:26
  138.9 22.8 %copy-start.2 = (bf16[8,4,8,256]{3,2,1,0:T(8,128)(2,1)S(1)}, bf16[8,4,8,256]{3,2,1,0:T(8,128)(2,1)}, u32[]{:S(2)}) copy-start(bf16[8,4,8,256]{3,2,1,0:T(8,128)(2,1)} %get-tuple-element.14) | copy-start | bytes 393220
  156.3 13.8 %all-to-all-start.7 = ((bf16[8,32,512]{2,1,0:T(8,128)(2,1)}), bf16[8,32,512]{2,1,0:T(8,128)(2,1)S(1)}, u32[]{:S(2)}, u32[]{:S(2)}) async-start(bf16[8,32,512]{2,1,0:T(8,128)(2,1)} %broadcast_in_dim.77), calls=%async_computation.7 | async-start | bytes 524288 | tf_op jit(solution)/shard_map/all_to_all | solution.py:26
  159.7 10.5 %collective-permute-start.5 = (bf16[32,32,256]{2,1,0:T(8,128)(2,1)}, bf16[32,32,256]{2,1,0:T(8,128)(2,1)S(1)}, u32[]{:S(2)}, u32[]{:S(2)}) collective-permute-start(bf16[32,32,256]{2,1,0:T(8,128)(2,1)} %all-to-all-done.5), channel_id=1, source_target_pairs={{0,8},{8,0},{16,24},{24,16},{32,40},{40,32},{48,56},{56,48},{64,72... | collective-permute-start | bytes 1572872 | tf_op jit(solution)/shard_map/ppermute | solution.py:35
  171.5 1.4 copy-start.4

commit v5 on v4

--- a/solution.py
+++ b/solution.py
@@ -3,6 +3,8 @@
 import jax
 import jax.numpy as jnp
 from jax import lax
+from jax.experimental import pallas as pl
+from jax.experimental.pallas import tpu as pltpu
 from jax.sharding import PartitionSpec as P
 
 bf16 = jnp.bfloat16
@@ -15,7 +17,6 @@
     return (x * ZS + z) * CORES + core
 
 
-x_groups = [[row_index(x, z, k) for x in range(XS)] for z in range(ZS) for k in range(CORES)]
 z_groups = [[row_index(x, z, k) for z in range(ZS)] for x in range(XS) for k in range(CORES)]
 xz_groups = [
     [row_index(x, z, k) for x in range(XS) for z in range(ZS)] for k in range(CORES)
@@ -33,6 +34,32 @@
 def other_core(cells):
     count = lax.axis_size("rows")
     return lax.ppermute(cells, "rows", [(i, i ^ 1) for i in range(count)])
+
+
+def along_x(cells, steps):
+    line, count = ZS * CORES, lax.axis_size("rows")
+    return lax.ppermute(cells, "rows", [(i, (i + steps * line) % count) for i in range(count)])
+
+
+def ordered_kernel(place_ref, *refs):
+    own_refs, away_ref, out_ref = refs[:XS], refs[XS], refs[XS + 1]
+    x, core = place_ref[0], place_ref[1]
+    for steps in range(XS):
+        source = lax.rem(x + XS - steps, XS)
+        out_ref[source, :, core] = own_refs[steps][...]
+        out_ref[source, :, 1 - core] = away_ref[steps]
+
+
+def ordered(place, own, away):
+    vmem = pl.BlockSpec(memory_space=pltpu.VMEM)
+    shape = (XS, ZS, CORES) + own[0].shape[1:]
+    return pl.pallas_call(
+        ordered_kernel,
+        out_shape=jax.ShapeDtypeStruct(shape, own[0].dtype),
+        in_specs=[pl.BlockSpec(memory_space=pltpu.SMEM)] + [vmem] * (XS + 1),
+        out_specs=vmem,
+        compiler_params=pltpu.CompilerParams(vmem_limit_bytes=24 * 2**20),
+    )(place, *own, away)
 
 
 def small_product(left, right):
@@ -53,6 +80,8 @@
     row_start = lax.axis_index("rows") * row_count
     col_start = lax.axis_index("cols") * col_count
     core = lax.axis_index("rows") % CORES
+    own_x = lax.axis_index("rows") // (ZS * CORES)
+    place = jnp.stack([own_x, core]).astype(jnp.int32)
     scale_factor = 0.125 / math.sqrt(orbital_count)
 
     within = lax.broadcasted_iota(jnp.int32, (blocks_dev, block_size), 1)
@@ -92,8 +121,6 @@
     applied = applied.reshape(rows_dev, both).astype(bf16)
     far_applied = other_core(applied)
 
-    product = small_product(own_turned, applied) + small_product(far_turned, far_applied)
-
     def diag_of(cols, values):
         return jnp.sum(jnp.tile(cols, (1, 2)).astype(f32) * values.astype(f32), axis=0)
 
@@ -111,16 +138,27 @@
         body, tail = cells[:, :-8].astype(f32), cells[:, -8:-6].astype(f32)
         return jnp.sum(body, axis=0), jnp.sum(tail, axis=(0, 1))
 
-    pieces = with_diag(product.reshape(XS, ZS * row_count, both), diag)
-    chip, diag = summed(swap(pieces, "rows", x_groups))
+    def product(steps):
+        start = ((own_x + steps) % XS) * (ZS * row_count)
+        own_part = lax.dynamic_slice_in_dim(own_turned, start, ZS * row_count, 0)
+        far_part = lax.dynamic_slice_in_dim(far_turned, start, ZS * row_count, 0)
+        return small_product(own_part, applied) + small_product(far_part, far_applied)
+
+    got = [along_x(with_diag(product(steps), diag), steps) for steps in (1, 3, 2)]
+    chip, diag_rest = summed(jnp.stack(got))
+    chip, diag = chip + product(0), diag + diag_rest
     pieces = with_diag(chip.reshape(ZS, row_count, both), diag)
     z_block, diag = summed(swap(pieces, "rows", z_groups))
     z_half = z_block.astype(bf16)
+
+    panel = spread(z_half, ZS, "rows", z_groups)
 
     high = lax.reduce_precision(diag, 8, 7)
     terms = jnp.stack([high, diag - high]).astype(bf16).reshape(-1, 128)
     terms = jnp.pad(terms, ((0, row_count - terms.shape[0]), (0, 0)))
     packed = jnp.concatenate([z_half, rotation.astype(bf16), terms], axis=1)
+    packed, panel = lax.optimization_barrier((packed, panel))
+    panels = [panel] + [along_x(panel, steps) for steps in (1, 2, 3)]
     across = spread(packed, cols_axis, "cols")
 
     def rows_of(cells):
@@ -132,15 +170,8 @@
     terms = terms.reshape(cols_axis, 2, 2, col_count)
     diag_all = jnp.sum(terms, axis=1).transpose(1, 0, 2).reshape(2, -1)
 
-    def halves(cells):
-        away = other_core(cells)
-        pair = jnp.where(core == 0, jnp.stack([cells, away], 1), jnp.stack([away, cells], 1))
-        return pair.reshape(orbital_count, -1)
-
-    panel = spread(z_half, ZS, "rows", z_groups)
-    panel = spread(panel, XS, "rows", x_groups)
-    panel, diag_all = lax.optimization_barrier((panel, diag_all))
-    z_cols = halves(panel.reshape(XS * ZS, row_count, both))
+    z_cols = ordered(place, panels, other_core(jnp.stack(panels)))
+    z_cols = z_cols.reshape(orbital_count, both)
 
     diag_cols = lax.dynamic_slice_in_dim(diag_all, col_start, col_count, 1)
     diag_down = lax.dynamic_slice_in_dim(diag_all, row_start, row_count, 1)
@@ -161,7 +192,10 @@
     square_rows = rows_of(spread(square.astype(bf16), cols_axis, "cols"))
     back_rows = (0.5 * square_rows.astype(f32) - gen_rows).astype(bf16)
     half_block = z_block + small_product(back_rows, z_cols)
-    step_cols = halves(step_cols)
+    step_away = other_core(step_cols)
+    step_cols = jnp.where(
+        core == 0, jnp.stack([step_cols, step_away], 1), jnp.stack([step_away, step_cols], 1)
+    ).reshape(orbital_count, col_count)
     half_across = spread(half_block.astype(bf16), cols_axis, "cols")
     half_rows = [
         rows_of(half_across[:, :, p * col_count : (p + 1) * col_count]) for p in range(2)

time: 176 us -> 173 us (0.983)
  blocking collectives: 51.4 us -> 16.4 us
  starting transfers between devices: 42.2 us -> 67.7 us
  local copies, waits for them, and re-layouts: 6.8 us -> 13.4 us
  other arithmetic: 9.97 us -> 8.05 us
    all_to_all x3 -> x1, blocking collectives: 51.4 us -> 16.4 us  [swap(): lax.all_to_all(cells, axis, 0, 0, tiled=True, axis_index_groups=groups)]
    ppermute x0 -> x6, starting transfers between devices: none -> 21.8 us  [along_x(): lax.ppermute(cells, 'rows', [(i, (i + steps * line) % count) for i in ran...]
    ppermute x0 -> x6, waiting for transfers between devices: none -> 14.2 us  [along_x(): lax.ppermute(cells, 'rows', [(i, (i + steps * line) % count) for i in ran...]
    all_to_all x5, waiting for transfers between devices: 54.2 us -> 42.1 us  [swap(): lax.all_to_all(cells, axis, 0, 0, tiled=True, axis_index_groups=groups)]
    unnamed x23 -> x52, local copies, waits for them, and re-layouts: 1.66 us -> 7.13 us
    select_n x2 -> x1, other arithmetic: 3.89 us -> 0.1 us  [on_device(): jnp.where(core == 0, jnp.stack([step_cols, step_away], 1), jnp.stack([ste...]
    all_to_all x5, starting transfers between devices: 28.2 us -> 32 us  [swap(): lax.all_to_all(cells, axis, 0, 0, tiled=True, axis_index_groups=groups)]
    broadcast_in_dim x6 -> x5, local copies, waits for them, and re-layouts: 4.24 us -> 3.11 us  [spread(): jnp.broadcast_to(cells[None], (count,) + cells.shape)]
  transfers between devices with their start and end apart: 11 -> 17, of which waited for: 7 -> 11; matrix products, arithmetic and copies ran while one was open for 4% -> 7% of each run, Pallas kernels for 0% -> 0%
where the time goes in v5:
time: 173 us; the launch traced here: 172 us
  starting transfers between devices  67.7 us (39%)
  waiting for transfers between devices  57.2 us (33%)
  blocking collectives  16.4 us (9%)
  local copies, waits for them, and re-layouts  13.4 us (8%)
  other arithmetic  8.05 us (5%)
  matrix products  6.73 us (4%)
    all_to_all x5, waiting for transfers between devices, swap(): lax.all_to_all(cells, axis, 0, 0, tiled=True, axis_index_groups=groups)  42.1 us
    all_to_all x5, starting transfers between devices, swap(): lax.all_to_all(cells, axis, 0, 0, tiled=True, axis_index_groups=groups)  32 us
    ppermute x6, starting transfers between devices, along_x(): lax.ppermute(cells, 'rows', [(i, (i + steps * line) % count) for i in ran...  21.8 us
    all_to_all x1, blocking collectives, swap(): lax.all_to_all(cells, axis, 0, 0, tiled=True, axis_index_groups=groups)  16.4 us
    ppermute x6, waiting for transfers between devices, along_x(): lax.ppermute(cells, 'rows', [(i, (i + steps * line) % count) for i in ran...  14.2 us
    ppermute x4, starting transfers between devices, other_core(): return lax.ppermute(cells, 'rows', [(i, i ^ 1) for i in range(count)])  8.41 us
    unnamed x52, local copies, waits for them, and re-layouts  7.13 us
    dot_general x14, matrix products, small_product(): return jnp.dot(left, right, preferred_element_type=f32)  6.28 us
  transfers between devices with their start and end apart: 17, of which 11 were waited for; matrix products, arithmetic and copies ran while one was open for 7% of the time, Pallas kernels for 0%

profile of v5, /device:TPU:64, one launch (start us, length us, event | category | flops | bytes accessed | tf_op | source)
XLA Modules:
  0.0 171.7 jit_solution(11027102882517599844)
XLA Ops:
  2.4 1.9 %collective-permute-start = (bf16[256,256]{1,0:T(8,128)(2,1)S(1)}, bf16[256,256]{1,0:T(8,128)(2,1)S(1)}, u32[]{:S(2)}, u32[]{:S(2)}) collective-permute-start(bf16[256,256]{1,0:T(8,128)(2,1)S(1)} %dynamic-slice_select_fusion), channel_id=1, source_target_pairs={{0,8},{8,16},{16,24},{24,32},{32,40},{40,48},{48,56},{56,64},{64,7... | collective-permute-start | bytes 393224 | tf_op jit(solution)/shard_map/ppermute | solution.py:96
  4.3 3.6 %collective-permute-start.1 = (bf16[256,256]{1,0:T(8,128)(2,1)S(1)}, bf16[256,256]{1,0:T(8,128)(2,1)S(1)}, u32[]{:S(2)}, u32[]{:S(2)}) collective-permute-start(bf16[256,256]{1,0:T(8,128)(2,1)S(1)} %dynamic-slice_select_fusion), channel_id=1, source_target_pairs={{8,0},{16,8},{24,16},{32,24},{40,32},{48,40},{56,48},{64,56},{72,6... | collective-permute-start | bytes 393224 | tf_op jit(solution)/shard_map/ppermute | solution.py:98
  9.7 2.7 %collective-permute-start.2 = (bf16[1024,256]{1,0:T(8,128)(2,1)S(1)}, bf16[1024,256]{1,0:T(8,128)(2,1)S(1)}, u32[]{:S(2)}, u32[]{:S(2)}) collective-permute-start(bf16[1024,256]{1,0:T(8,128)(2,1)S(1)} %bitcast.177), channel_id=1, source_target_pairs={{0,8},{8,0},{16,24},{24,16},{32,40},{40,32},{48,56},{56,48},{64,72... | collective-permute-start | bytes 1572872 | tf_op jit(solution)/shard_map/ppermute | solution.py:36
  15.4 1.9 %collective-permute-start.3 = (bf16[256,512]{1,0:T(8,128)(2,1)S(1)}, bf16[256,512]{1,0:T(8,128)(2,1)S(1)}, u32[]{:S(2)}, u32[]{:S(2)}) collective-permute-start(bf16[256,512]{1,0:T(8,128)(2,1)S(1)} %bitcast.147), channel_id=1, source_target_pairs={{0,8},{8,0},{16,24},{24,16},{32,40},{40,32},{48,56},{56,48},{64,72... | collective-permute-start | bytes 786440 | tf_op jit(solution)/shard_map/ppermute | solution.py:36
  20.4 3.4 %collective-permute-start.4 = (bf16[264,512]{1,0:T(8,128)(2,1)}, bf16[264,512]{1,0:T(8,128)(2,1)S(1)}, u32[]{:S(2)}, u32[]{:S(2)}) collective-permute-start(bf16[264,512]{1,0:T(8,128)(2,1)} %get-tuple-element.28), channel_id=1, source_target_pairs={{0,128},{8,136},{16,144},{24,152},{32,160},{40,168},{48,176},{56,1... | collective-permute-start | bytes 811016 | tf_op jit(solution)/shard_map/ppermute | solution.py:41
  23.8 3.6 %collective-permute-start.5 = (bf16[264,512]{1,0:T(8,128)(2,1)S(1)}, bf16[264,512]{1,0:T(8,128)(2,1)S(1)}, u32[]{:S(2)}, u32[]{:S(2)}) collective-permute-start(bf16[264,512]{1,0:T(8,128)(2,1)S(1)} %get-tuple-element.29), channel_id=1, source_target_pairs={{0,384},{8,392},{16,400},{24,408},{32,416},{40,424},{48,432},{56,4... | collective-permute-start | bytes 811016 | tf_op jit(solution)/shard_map/ppermute | solution.py:41
  27.4 3.7 %collective-permute-start.6 = (bf16[264,512]{1,0:T(8,128)(2,1)S(1)}, bf16[264,512]{1,0:T(8,128)(2,1)S(1)}, u32[]{:S(2)}, u32[]{:S(2)}) collective-permute-start(bf16[264,512]{1,0:T(8,128)(2,1)S(1)} %get-tuple-element.30), channel_id=1, source_target_pairs={{0,256},{8,264},{16,272},{24,280},{32,288},{40,296},{48,304},{56,3... | collective-permute-start | bytes 811016 | tf_op jit(solution)/shard_map/ppermute | solution.py:41
  32.2 6.8 %collective-permute-done.5 = bf16[264,512]{1,0:T(8,128)(2,1)S(1)} collective-permute-done((bf16[264,512]{1,0:T(8,128)(2,1)S(1)}, bf16[264,512]{1,0:T(8,128)(2,1)S(1)}, u32[]{:S(2)}, u32[]{:S(2)}) %collective-permute-start.5) | collective-permute-done | bytes 270368 | tf_op jit(solution)/shard_map/ppermute | solution.py:41
  40.3 11.6 %all-to-all-start = ((bf16[8,40,512]{2,1,0:T(8,128)(2,1)}), bf16[8,40,512]{2,1,0:T(8,128)(2,1)S(1)}, u32[]{:S(2)}, u32[]{:S(2)}) async-start(bf16[8,40,512]{2,1,0:T(8,128)(2,1)} %pad_maximum_fusion.5), calls=%async_computation | async-start | bytes 655360 | tf_op jit(solution)/shard_map/all_to_all | solution.py:27
  51.9 11.5 %all-to-all-done = bf16[8,40,512]{2,1,0:T(8,128)(2,1)S(1)} async-done(((bf16[8,40,512]{2,1,0:T(8,128)(2,1)}), bf16[8,40,512]{2,1,0:T(8,128)(2,1)S(1)}, u32[]{:S(2)}, u32[]{:S(2)}) %all-to-all-start) | async-done | bytes 327712 | tf_op jit(solution)/shard_map/all_to_all | solution.py:27
  64.7 4.8 %all-to-all-start.1 = ((bf16[8,32,512]{2,1,0:T(8,128)(2,1)}), bf16[8,32,512]{2,1,0:T(8,128)(2,1)S(1)}, u32[]{:S(2)}, u32[]{:S(2)}) async-start(bf16[8,32,512]{2,1,0:T(8,128)(2,1)} %broadcast_in_dim.62), calls=%async_computation.1 | async-start | bytes 524288 | tf_op jit(solution)/shard_map/all_to_all | solution.py:27
  69.6 9.0 %all-to-all-done.1.refs_0_ = bf16[8,32,512]{2,1,0:T(8,128)(2,1)S(1)} async-done(((bf16[8,32,512]{2,1,0:T(8,128)(2,1)}), bf16[8,32,512]{2,1,0:T(8,128)(2,1)S(1)}, u32[]{:S(2)}, u32[]{:S(2)}) %all-to-all-start.1) | async-done | bytes 262176 | tf_op jit(solution)/shard_map/all_to_all | solution.py:27
  79.4 7.0 %all-to-all-start.2 = ((bf16[8,32,896]{2,1,0:T(8,128)(2,1)}), bf16[8,32,896]{2,1,0:T(8,128)(2,1)S(1)}, u32[]{:S(2)}, u32[]{:S(2)}) async-start(bf16[8,32,896]{2,1,0:T(8,128)(2,1)} %broadcast_in_dim.63), calls=%async_computation.2 | async-start | bytes 917504 | tf_op jit(solution)/shard_map/all_to_all | solution.py:27
  86.3 4.0 %collective-permute-start.7 = (bf16[8,32,512]{2,1,0:T(8,128)(2,1)S(1)}, bf16[8,32,512]{2,1,0:T(8,128)(2,1)S(1)}, u32[]{:S(2)}, u32[]{:S(2)}) collective-permute-start(bf16[8,32,512]{2,1,0:T(8,128)(2,1)S(1)} %all-to-all-done.1.refs_0_), channel_id=1, source_target_pairs={{0,128},{8,136},{16,144},{24,152},{32,160},{40,168},{48,176},{56,1... | collective-permute-start | bytes 786440 | tf_op jit(solution)/shard_map/ppermute | solution.py:41
  90.3 5.1 %collective-permute-start.8 = (bf16[8,32,512]{2,1,0:T(8,128)(2,1)S(1)}, bf16[8,32,512]{2,1,0:T(8,128)(2,1)S(1)}, u32[]{:S(2)}, u32[]{:S(2)}) collective-permute-start(bf16[8,32,512]{2,1,0:T(8,128)(2,1)S(1)} %all-to-all-done.1.refs_0_), channel_id=1, source_target_pairs={{0,256},{8,264},{16,272},{24,280},{32,288},{40,296},{48,304},{56,3... | collective-permute-start | bytes 786440 | tf_op jit(solution)/shard_map/ppermute | solution.py:41
  95.4 1.9 %collective-permute-start.9 = (bf16[8,32,512]{2,1,0:T(8,128)(2,1)S(1)}, bf16[8,32,512]{2,1,0:T(8,128)(2,1)S(1)}, u32[]{:S(2)}, u32[]{:S(2)}) collective-permute-start(bf16[8,32,512]{2,1,0:T(8,128)(2,1)S(1)} %all-to-all-done.1.refs_0_), channel_id=1, source_target_pairs={{0,384},{8,392},{16,400},{24,408},{32,416},{40,424},{48,432},{56,4... | collective-permute-start | bytes 786440 | tf_op jit(solution)/shard_map/ppermute | solution.py:41
  98.8 2.8 %collective-permute-done.8.refs_2_ = bf16[8,32,512]{2,1,0:T(8,128)(2,1)S(1)} collective-permute-done((bf16[8,32,512]{2,1,0:T(8,128)(2,1)S(1)}, bf16[8,32,512]{2,1,0:T(8,128)(2,1)S(1)}, u32[]{:S(2)}, u32[]{:S(2)}) %collective-permute-start.8) | collective-permute-done | bytes 262176 | tf_op jit(solution)/shard_map/ppermute | solution.py:41
  101.6 2.5 %collective-permute-done.9.refs_3_ = bf16[8,32,512]{2,1,0:T(8,128)(2,1)S(1)} collective-permute-done((bf16[8,32,512]{2,1,0:T(8,128)(2,1)S(1)}, bf16[8,32,512]{2,1,0:T(8,128)(2,1)S(1)}, u32[]{:S(2)}, u32[]{:S(2)}) %collective-permute-start.9) | collective-permute-done | bytes 262176 | tf_op jit(solution)/shard_map/ppermute | solution.py:41
  114.7 16.4 %all_to_all.30 = bf16[8,32,256]{2,1,0:T(8,128)(2,1)} all-to-all(bf16[8,32,256]{2,1,0:T(8,128)(2,1)S(1)} %broadcast_in_dim.65), channel_id=1, replica_groups=mesh['rows'=64,'cols'=8] {'cols'}, dimensions={0} | all-to-all | bytes 262144 | tf_op jit(solution)/shard_map/all_to_all | solution.py:27
  132.0 5.3 %all-to-all-start.3 = ((bf16[32,32,256]{2,1,0:T(8,128)(2,1)}), bf16[32,32,256]{2,1,0:T(8,128)(2,1)S(1)}, u32[]{:S(2)}, u32[]{:S(2)}) async-start(bf16[32,32,256]{2,1,0:T(8,128)(2,1)} %broadcast_in_dim.64), calls=%async_computation.3 | async-start | bytes 1048576 | tf_op jit(solution)/shard_map/all_to_all | solution.py:27
  139.6 14.1 %all-to-all-done.3 = bf16[32,32,256]{2,1,0:T(8,128)(2,1)S(1)} async-done(((bf16[32,32,256]{2,1,0:T(8,128)(2,1)}), bf16[32,32,256]{2,1,0:T(8,128)(2,1)S(1)}, u32[]{:S(2)}, u32[]{:S(2)}) %all-to-all-start.3) | async-done | bytes 524320 | tf_op jit(solution)/shard_map/all_to_all | solution.py:27
  154.4 3.4 %all-to-all-start.5 = ((bf16[8,32,512]{2,1,0:T(8,128)(2,1)}), bf16[8,32,512]{2,1,0:T(8,128)(2,1)S(1)}, u32[]{:S(2)}, u32[]{:S(2)}) async-start(bf16[8,32,512]{2,1,0:T(8,128)(2,1)} %broadcast_in_dim.66), calls=%async_computation.5 | async-start | bytes 524288 | tf_op jit(solution)/shard_map/all_to_all | solution.py:27
  157.8 1.9 %collective-permute-start.11 = (bf16[32,32,256]{2,1,0:T(8,128)(2,1)S(1)}, bf16[32,32,256]{2,1,0:T(8,128)(2,1)S(1)}, u32[]{:S(2)}, u32[]{:S(2)}) collective-permute-start(bf16[32,32,256]{2,1,0:T(8,128)(2,1)S(1)} %all-to-all-done.3), channel_id=1, source_target_pairs={{0,8},{8,0},{16,24},{24,16},{32,40},{40,32},{48,56},{56,48},{64,72... | collective-permute-start | bytes 1572872 | tf_op jit(solution)/shard_map/ppermute | solution.py:36
  160.7 7.5 %all-to-all-done.5 = bf16[8,32,512]{2,1,0:T(8,128)(2,1)S(1)} async-done(((bf16[8,32,512]{2,1,0:T(8,128)(2,1)}), bf16[8,32,512]{2,1,0:T(8,128)(2,1)S(1)}, u32[]{:S(2)}, u32[]{:S(2)}) %all-to-all-start.5) | async-done | bytes 262176 | tf_op jit(solution)/shard_map/all_to_all | solution.py:27
  (132 shorter events, 33.8 us)
Async XLA Ops:
  2.4 11.1 %collective-permute-start = (bf16[256,256]{1,0:T(8,128)(2,1)S(1)}, bf16[256,256]{1,0:T(8,128)(2,1)S(1)}, u32[]{:S(2)}, u32[]{:S(2)}) collective-permute-start(bf16[256,256]{1,0:T(8,128)(2,1)S(1)} %dynamic-slice_select_fusion), channel_id=1, source_target_pairs={{0,8},{8,16},{16,24},{24,32},{32,40},{40,48},{48,56},{56,64},{64,7... | collective-permute-start | bytes 393224 | tf_op jit(solution)/shard_map/ppermute | solution.py:96
  4.3 9.2 %collective-permute-start.1 = (bf16[256,256]{1,0:T(8,128)(2,1)S(1)}, bf16[256,256]{1,0:T(8,128)(2,1)S(1)}, u32[]{:S(2)}, u32[]{:S(2)}) collective-permute-start(bf16[256,256]{1,0:T(8,128)(2,1)S(1)} %dynamic-slice_select_fusion), channel_id=1, source_target_pairs={{8,0},{16,8},{24,16},{32,24},{40,32},{48,40},{56,48},{64,56},{72,6... | collective-permute-start | bytes 393224 | tf_op jit(solution)/shard_map/ppermute | solution.py:98
  9.7 9.3 %collective-permute-start.2 = (bf16[1024,256]{1,0:T(8,128)(2,1)S(1)}, bf16[1024,256]{1,0:T(8,128)(2,1)S(1)}, u32[]{:S(2)}, u32[]{:S(2)}) collective-permute-start(bf16[1024,256]{1,0:T(8,128)(2,1)S(1)} %bitcast.177), channel_id=1, source_target_pairs={{0,8},{8,0},{16,24},{24,16},{32,40},{40,32},{48,56},{56,48},{64,72... | collective-permute-start | bytes 1572872 | tf_op jit(solution)/shard_map/ppermute | solution.py:36
  15.4 3.4 %collective-permute-start.3 = (bf16[256,512]{1,0:T(8,128)(2,1)S(1)}, bf16[256,512]{1,0:T(8,128)(2,1)S(1)}, u32[]{:S(2)}, u32[]{:S(2)}) collective-permute-start(bf16[256,512]{1,0:T(8,128)(2,1)S(1)} %bitcast.147), channel_id=1, source_target_pairs={{0,8},{8,0},{16,24},{24,16},{32,40},{40,32},{48,56},{56,48},{64,72... | collective-permute-start | bytes 786440 | tf_op jit(solution)/shard_map/ppermute | solution.py:36
  20.4 11.8 %collective-permute-start.4 = (bf16[264,512]{1,0:T(8,128)(2,1)}, bf16[264,512]{1,0:T(8,128)(2,1)S(1)}, u32[]{:S(2)}, u32[]{:S(2)}) collective-permute-start(bf16[264,512]{1,0:T(8,128)(2,1)} %get-tuple-element.28), channel_id=1, source_target_pairs={{0,128},{8,136},{16,144},{24,152},{32,160},{40,168},{48,176},{56,1... | collective-permute-start | bytes 811016 | tf_op jit(solution)/shard_map/ppermute | solution.py:41
  23.8 15.2 %collective-permute-start.5 = (bf16[264,512]{1,0:T(8,128)(2,1)S(1)}, bf16[264,512]{1,0:T(8,128)(2,1)S(1)}, u32[]{:S(2)}, u32[]{:S(2)}) collective-permute-start(bf16[264,512]{1,0:T(8,128)(2,1)S(1)} %get-tuple-element.29), channel_id=1, source_target_pairs={{0,384},{8,392},{16,400},{24,408},{32,416},{40,424},{48,432},{56,4... | collective-permute-start | bytes 811016 | tf_op jit(solution)/shard_map/ppermute | solution.py:41
  27.4 11.6 %collective-permute-start.6 = (bf16[264,512]{1,0:T(8,128)(2,1)S(1)}, bf16[264,512]{1,0:T(8,128)(2,1)S(1)}, u32[]{:S(2)}, u32[]{:S(2)}) collective-permute-start(bf16[264,512]{1,0:T(8,128)(2,1)S(1)} %get-tuple-element.30), channel_id=1, source_target_pairs={{0,256},{8,264},{16,272},{24,280},{32,288},{40,296},{48,304},{56,3... | collective-permute-start | bytes 811016 | tf_op jit(solution)/shard_map/ppermute | solution.py:41
  39.2 12.7 %copy-start.15 = (f32[32,256]{1,0:T(8,128)S(1)}, f32[32,256]{1,0:T(8,128)}, u32[]{:S(2)}) copy-start(f32[32,256]{1,0:T(8,128)} %param.6) | copy-start | bytes 98308
  40.3 23.0 %all-to-all-start = ((bf16[8,40,512]{2,1,0:T(8,128)(2,1)}), bf16[8,40,512]{2,1,0:T(8,128)(2,1)S(1)}, u32[]{:S(2)}, u32[]{:S(2)}) async-start(bf16[8,40,512]{2,1,0:T(8,128)(2,1)} %pad_maximum_fusion.5), calls=%async_computation | async-start | bytes 655360 | tf_op jit(solution)/shard_map/all_to_all | solution.py:27
  64.7 13.8 %all-to-all-start.1 = ((bf16[8,32,512]{2,1,0:T(8,128)(2,1)}), bf16[8,32,512]{2,1,0:T(8,128)(2,1)S(1)}, u32[]{:S(2)}, u32[]{:S(2)}) async-start(bf16[8,32,512]{2,1,0:T(8,128)(2,1)} %broadcast_in_dim.62), calls=%async_computation.1 | async-start | bytes 524288 | tf_op jit(solution)/shard_map/all_to_all | solution.py:27
  79.4 27.7 %all-to-all-start.2 = ((bf16[8,32,896]{2,1,0:T(8,128)(2,1)}), bf16[8,32,896]{2,1,0:T(8,128)(2,1)S(1)}, u32[]{:S(2)}, u32[]{:S(2)}) async-start(bf16[8,32,896]{2,1,0:T(8,128)(2,1)} %broadcast_in_dim.63), calls=%async_computation.2 | async-start | bytes 917504 | tf_op jit(solution)/shard_map/all_to_all | solution.py:27
  86.3 12.4 %collective-permute-start.7 = (bf16[8,32,512]{2,1,0:T(8,128)(2,1)S(1)}, bf16[8,32,512]{2,1,0:T(8,128)(2,1)S(1)}, u32[]{:S(2)}, u32[]{:S(2)}) collective-permute-start(bf16[8,32,512]{2,1,0:T(8,128)(2,1)S(1)} %all-to-all-done.1.refs_0_), channel_id=1, source_target_pairs={{0,128},{8,136},{16,144},{24,152},{32,160},{40,168},{48,176},{56,1... | collective-permute-start | bytes 786440 | tf_op jit(solution)/shard_map/ppermute | solution.py:41
  90.3 11.3 %collective-permute-start.8 = (bf16[8,32,512]{2,1,0:T(8,128)(2,1)S(1)}, bf16[8,32,512]{2,1,0:T(8,128)(2,1)S(1)}, u32[]{:S(2)}, u32[]{:S(2)}) collective-permute-start(bf16[8,32,512]{2,1,0:T(8,128)(2,1)S(1)} %all-to-all-done.1.refs_0_), channel_id=1, source_target_pairs={{0,256},{8,264},{16,272},{24,280},{32,288},{40,296},{48,304},{56,3... | collective-permute-start | bytes 786440 | tf_op jit(solution)/shard_map/ppermute | solution.py:41
  95.4 8.6 %collective-permute-start.9 = (bf16[8,32,512]{2,1,0:T(8,128)(2,1)S(1)}, bf16[8,32,512]{2,1,0:T(8,128)(2,1)S(1)}, u32[]{:S(2)}, u32[]{:S(2)}) collective-permute-start(bf16[8,32,512]{2,1,0:T(8,128)(2,1)S(1)} %all-to-all-done.1.refs_0_), channel_id=1, source_target_pairs={{0,384},{8,392},{16,400},{24,408},{32,416},{40,424},{48,432},{56,4... | collective-permute-start | bytes 786440 | tf_op jit(solution)/shard_map/ppermute | solution.py:41
  98.8 10.6 %copy-start = (bf16[8,32,512]{2,1,0:T(8,128)(2,1)}, bf16[8,32,512]{2,1,0:T(8,128)(2,1)S(1)}, u32[]{:S(2)}) copy-start(bf16[8,32,512]{2,1,0:T(8,128)(2,1)S(1)} %collective-permute-done.7.refs_1_) | copy-start | bytes 786436
  101.6 7.8 %copy-start.2 = (bf16[8,32,512]{2,1,0:T(8,128)(2,1)}, bf16[8,32,512]{2,1,0:T(8,128)(2,1)S(1)}, u32[]{:S(2)}) copy-start(bf16[8,32,512]{2,1,0:T(8,128)(2,1)S(1)} %collective-permute-done.8.refs_2_) | copy-start | bytes 786436
  105.2 4.8 %collective-permute-start.10 = (bf16[4,8,32,512]{3,2,1,0:T(8,128)(2,1)}, bf16[4,8,32,512]{3,2,1,0:T(8,128)(2,1)S(1)}, u32[]{:S(2)}, u32[]{:S(2)}) collective-permute-start(bf16[4,8,32,512]{3,2,1,0:T(8,128)(2,1)} %pad_maximum_fusion), channel_id=1, source_target_pairs={{0,8},{8,0},{16,24},{24,16},{32,40},{40,32},{48,56},{56,48},{64,72... | collective-permute-start | bytes 3145736 | tf_op jit(solution)/shard_map/ppermute | solution.py:36
  109.6 21.5 %copy-start.17 = (f32[1,8,256]{2,0,1:T(1,128)}, f32[1,8,256]{2,0,1:T(1,128)S(1)}, u32[]{:S(2)}) copy-start(f32[1,8,256]{2,0,1:T(1,128)S(1)} %get-tuple-element.27) | copy-start | bytes 24580
  114.7 23.3 %copy-start.9 = (bf16[8,32,896]{2,1,0:T(8,128)(2,1)S(1)}, bf16[8,32,896]{2,1,0:T(8,128)(2,1)}, u32[]{:S(2)}) copy-start(bf16[8,32,896]{2,1,0:T(8,128)(2,1)} %copy-done.8) | copy-start | bytes 1376260
  114.7 24.4 %copy-start.12 = (f32[32,512]{1,0:T(8,128)S(1)}, f32[32,512]{1,0:T(8,128)}, u32[]{:S(2)}) copy-start(f32[32,512]{1,0:T(8,128)} %copy-done.10) | copy-start | bytes 196612
  132.0 21.7 %all-to-all-start.3 = ((bf16[32,32,256]{2,1,0:T(8,128)(2,1)}), bf16[32,32,256]{2,1,0:T(8,128)(2,1)S(1)}, u32[]{:S(2)}, u32[]{:S(2)}) async-start(bf16[32,32,256]{2,1,0:T(8,128)(2,1)} %broadcast_in_dim.64), calls=%async_computation.3 | async-start | bytes 1048576 | tf_op jit(solution)/shard_map/all_to_all | solution.py:27
  153.7 14.7 %copy-start.7 = (bf16[256,2048]{0,1:T(8,128)(2,1)S(1)}, bf16[256,2048]{0,1:T(8,128)(2,1)}, u32[]{:S(2)}) copy-start(bf16[256,2048]{0,1:T(8,128)(2,1)} %copy-done.6) | copy-start | bytes 3145732
  154.4 13.8 %all-to-all-start.5 = ((bf16[8,32,512]{2,1,0:T(8,128)(2,1)}), bf16[8,32,512]{2,1,0:T(8,128)(2,1)S(1)}, u32[]{:S(2)}, u32[]{:S(2)}) async-start(bf16[8,32,512]{2,1,0:T(8,128)(2,1)} %broadcast_in_dim.66), calls=%async_computation.5 | async-start | bytes 524288 | tf_op jit(solution)/shard_map/all_to_all | solution.py:27
  157.8 10.5 %collective-permute-start.11 = (bf16[32,32,256]{2,1,0:T(8,128)(2,1)S(1)}, bf16[32,32,256]{2,1,0:T(8,128)(2,1)S(1)}, u32[]{:S(2)}, u32[]{:S(2)}) collective-permute-start(bf16[32,32,256]{2,1,0:T(8,128)(2,1)S(1)} %all-to-all-done.3), channel_id=1, source_target_pairs={{0,8},{8,0},{16,24},{24,16},{32,40},{40,32},{48,56},{56,48},{64,72... | collective-permute-start | bytes 1572872 | tf_op jit(solution)/shard_map/ppermute | solution.py:36
  (14 other events, 28.7 us)

commit v6 on v5

v6 whole, which is shorter than its diff:
```python
import functools
import math

import jax
import jax.numpy as jnp
from jax import lax
from jax.experimental import pallas as pl
from jax.experimental.pallas import tpu as pltpu
from jax.sharding import PartitionSpec as P

bf16 = jnp.bfloat16
f32 = jnp.float32

XS, ZS, CORES, COLS = 4, 8, 2, 8


def row_index(x, z, core):
    return (x * ZS + z) * CORES + core


z_groups = [[row_index(x, z, k) for z in range(ZS)] for x in range(XS) for k in range(CORES)]


def swap(cells, axis, groups=None):
    return lax.all_to_all(cells, axis, 0, 0, tiled=True, axis_index_groups=groups)


def other_core(cells):
    count = lax.axis_size("rows")
    return lax.ppermute(cells, "rows", [(i, i ^ 1) for i in range(count)])


def along_x(cells, steps):
    line, count = ZS * CORES, lax.axis_size("rows")
    return lax.ppermute(cells, "rows", [(i, (i + steps * line) % count) for i in range(count)])


def small_product(left, right):
    return jnp.dot(left, right, preferred_element_type=f32)


vmem = pl.BlockSpec(memory_space=pltpu.VMEM)
smem = pl.BlockSpec(memory_space=pltpu.SMEM)
anywhere = pl.BlockSpec(memory_space=pl.ANY)
params = pltpu.CompilerParams(vmem_limit_bytes=32 * 2**20)


def gathered(place_ref, own_refs, away_ref, out_ref, sems):
    x, core = place_ref[0], place_ref[1]
    copies = []
    for steps in range(XS):
        source = lax.rem(x + XS - steps, XS)
        copies.append((own_refs[steps], out_ref.at[source, :, core]))
        copies.append((away_ref.at[steps], out_ref.at[source, :, 1 - core]))
    copies = [pltpu.make_async_copy(*pair, sems.at[i]) for i, pair in enumerate(copies)]
    for copy in copies:
        copy.start()
    return copies


def chunk(panel_ref, k):
    per = ZS * XS // COLS
    cells = panel_ref[k * per // ZS, pl.ds(k * per % ZS, per)]
    return cells.reshape(-1, cells.shape[-1])


def sum_kernel(got_ref, rotation_ref, block_ref, z_ref, packed_ref):
    count, _, wide = z_ref.shape
    total = got_ref[0].astype(f32)
    for i in range(1, count):
        total = total + got_ref[i].astype(f32)
    block = total[:, :wide]
    block_ref[...] = block
    half = block.astype(bf16)
    diag = total[:4, wide:] + total[4:8, wide:]
    high = diag.astype(bf16).astype(f32)
    fill = jnp.zeros((block.shape[0] - 8, 128), f32)
    tail = jnp.concatenate([high, diag - high, fill], axis=0).astype(bf16)
    packed = jnp.concatenate([half, rotation_ref[...].astype(bf16), tail], axis=1)
    for i in range(count):
        z_ref[i] = half
        packed_ref[i] = packed


def square_kernel(
    scale, place_ref, across_ref, own0, own1, own2, own3, away_ref,
    z_ref, rows_ref, square_ref, step_ref, diag_ref, turned_ref, sems,
):
    copies = gathered(place_ref, (own0, own1, own2, own3), away_ref, z_ref, sems)
    mine, low, col = place_ref[2], place_ref[3], place_ref[4]
    rows, width = rows_ref.shape[1:]
    for p in range(2):
        parts = []
        for h in range(width // 128):
            terms = across_ref[:, :, -128:].astype(f32)
            k = p * (width // 128) + h
            parts.append(terms[:, k] + terms[:, 4 + k])
        diag_ref[p] = jnp.concatenate(parts, axis=1)
        turned_ref[p] = diag_ref[p].T
    lane = lax.broadcasted_iota(jnp.int32, (rows, COLS), 1)
    down = [
        jnp.sum(
            jnp.where(lane == mine, turned_ref[p, pl.ds(low, rows), :], 0.0),
            axis=1,
            keepdims=True,
        )
        for p in range(2)
    ]
    for k in range(COLS):
        cells = across_ref[k].astype(f32)
        cos_part = cells[:, :width] * (diag_ref[0, k : k + 1, :] - down[0])
        sin_part = cells[:, width : 2 * width] * (diag_ref[1, k : k + 1, :] - down[1])
        rows_ref[k] = (cos_part + sin_part) * scale
    across_diag = [diag_ref[p, pl.ds(col, 1), :] for p in range(2)]
    for copy in copies:
        copy.wait()
    square = jnp.zeros((rows, width), f32)
    for k in range(COLS):
        cells = chunk(z_ref, k).astype(f32)
        cos_part = cells[:, :width] * (across_diag[0] - turned_ref[0, :, k : k + 1])
        sin_part = cells[:, width:] * (across_diag[1] - turned_ref[1, :, k : k + 1])
        cells = ((cos_part + sin_part) * scale).astype(bf16)
        square = square + small_product(rows_ref[k].astype(bf16), cells)
    step = (rows_ref[col] + 0.5 * square).astype(bf16)
    square = square.astype(bf16)
    for k in range(COLS):
        square_ref[k] = square
        step_ref[k] = step


def half_kernel(square_ref, rows_ref, z_ref, block_ref, half_ref, sent_ref):
    total = block_ref[...]
    for k in range(COLS):
        back = (0.5 * square_ref[k].astype(f32) - rows_ref[k]).astype(bf16)
        total = total + small_product(back, chunk(z_ref, k))
    half_ref[...] = total
    sent = total.astype(bf16)
    for k in range(COLS):
        sent_ref[k] = sent


def final_kernel(
    place_ref, size_ref, half_ref, across_ref, coeffs_ref, rotation_ref, block_ref,
    own0, own1, own2, own3, away_ref,
    rotated_ref, cos_ref, sin_ref, orbitals_ref, step_ref, sems,
):
    copies = gathered(place_ref, (own0, own1, own2, own3), away_ref, step_ref, sems)
    col = place_ref[4]
    width = rotated_ref.shape[1]
    rotated = rotation_ref[...]
    cos_part, sin_part = block_ref[:, :width], block_ref[:, width:]
    start = pl.multiple_of(col * width, width)
    orbitals = coeffs_ref[:, pl.ds(start, width)].astype(f32)
    for copy in copies:
        copy.wait()
    for k in range(COLS):
        step = chunk(step_ref, k)
        cells = half_ref[k]
        cos_part = cos_part + small_product(cells[:, :width], step)
        sin_part = sin_part + small_product(cells[:, width:], step)
        rotated = rotated + small_product(across_ref[k, :, 2 * width : 3 * width], step)
        cells = coeffs_ref[:, k * width : (k + 1) * width]
        orbitals = orbitals + small_product(cells, step)
    rotated_ref[...] = rotated
    cos_ref[...] = cos_part
    sin_ref[...] = sin_part
    blocks = size_ref.shape[0]
    size = orbitals.shape[0] // blocks
    within = lax.broadcasted_iota(jnp.int32, (size, width), 0)
    for b in range(blocks):
        cells = orbitals[b * size : (b + 1) * size]
        cells = jnp.where(within < size_ref[b], cells, 0.0)
        orbitals_ref[b * size : (b + 1) * size, :] = cells.astype(bf16)


def call(kernel, shapes, in_specs, scratch, *operands):
    return pl.pallas_call(
        kernel,
        out_shape=[jax.ShapeDtypeStruct(*shape) for shape in shapes],
        in_specs=in_specs,
        out_specs=[vmem] * len(shapes),
        scratch_shapes=scratch,
        compiler_params=params,
    )(*operands)


def on_device(coeffs, rotation, phase_ops, block_links, atom_size):
    rows_dev, orbital_count = coeffs.shape
    blocks_dev = phase_ops.shape[1]
    span_blocks = phase_ops.shape[2]
    block_size = phase_ops.shape[3]
    reach_blocks = (span_blocks - 1) // 2
    rows_axis = lax.axis_size("rows")
    cols_axis = lax.axis_size("cols")
    row_count = orbital_count // rows_axis
    col_count = orbital_count // cols_axis
    both = 2 * col_count
    col_start = lax.axis_index("cols") * col_count
    core = lax.axis_index("rows") % CORES
    own_x = lax.axis_index("rows") // (ZS * CORES)
    per_col = rows_axis // cols_axis
    own_row = lax.axis_index("rows")
    place = [own_x, core, own_row // per_col, own_row % per_col * row_count]
    place = jnp.stack(place + [lax.axis_index("cols")]).astype(jnp.int32)
    scale_factor = 0.125 / math.sqrt(orbital_count)

    within = lax.broadcasted_iota(jnp.int32, (blocks_dev, block_size), 1)
    live_rows = (within < atom_size[:, None]).reshape(rows_dev)
    raw_cols = lax.dynamic_slice_in_dim(coeffs, col_start, col_count, 1)
    own_cols = jnp.where(live_rows[:, None], raw_cols, jnp.zeros_like(raw_cols))
    width = reach_blocks * block_size
    up = [(i, (i + 1) % rows_axis) for i in range(rows_axis)]
    down = [((i + 1) % rows_axis, i) for i in range(rows_axis)]
    padded = jnp.concatenate(
        [
            lax.ppermute(own_cols[rows_dev - width :], "rows", up),
            own_cols,
            lax.ppermute(own_cols[:width], "rows", down),
        ],
        axis=0,
    )
    turned = coeffs.T.reshape(XS, ZS, CORES, row_count, rows_dev)

    def turned_half(which):
        return lax.dynamic_index_in_dim(turned, which, 2, keepdims=False).reshape(-1, rows_dev)

    own_turned = turned_half(core)
    far_turned = other_core(turned_half(1 - core))
    stacked = jnp.stack(
        [
            padded[offset * block_size : (offset + blocks_dev) * block_size].reshape(
                blocks_dev, block_size, col_count
            )
            for offset in range(span_blocks)
        ],
        axis=1,
    )
    gated = phase_ops * block_links[None, :, :, None, None].astype(bf16)
    applied = jnp.einsum("pbtij,btjk->bipk", gated, stacked, preferred_element_type=f32)
    applied = jnp.where(live_rows[:, None], applied.reshape(rows_dev, both), 0.0).astype(bf16)
    far_applied = other_core(applied)

    def diag_of(cols, values):
        return jnp.sum(jnp.tile(cols, (1, 2)).astype(f32) * values.astype(f32), axis=0)

    far_cols = jnp.where(core == 0, padded[width + rows_dev :], padded[:width])
    diag = diag_of(own_cols, applied) + diag_of(far_cols, far_applied)

    def with_diag(cells, values):
        high = lax.reduce_precision(values, 8, 7)
        tail = jnp.stack([high, values - high]).astype(bf16)
        tail = jnp.pad(tail, ((0, 6), (0, 0)))
        tail = jnp.broadcast_to(tail, cells.shape[:-2] + tail.shape)
        return jnp.concatenate([cells.astype(bf16), tail], axis=-2)

    def summed(cells):
        body, tail = cells[:, :-8].astype(f32), cells[:, -8:-6].astype(f32)
        return jnp.sum(body, axis=0), jnp.sum(tail, axis=(0, 1))

    def product(steps):
        start = ((own_x + steps) % XS) * (ZS * row_count)
        own_part = lax.dynamic_slice_in_dim(own_turned, start, ZS * row_count, 0)
        far_part = lax.dynamic_slice_in_dim(far_turned, start, ZS * row_count, 0)
        return small_product(own_part, applied) + small_product(far_part, far_applied)

    got = [along_x(with_diag(product(steps), diag), steps) for steps in (1, 3, 2)]
    chip, diag_rest = summed(jnp.stack(got))
    chip, diag = chip + product(0), diag + diag_rest
    high = lax.reduce_precision(diag, 8, 7)
    terms = jnp.stack([high, diag - high]).astype(bf16).reshape(-1, 128)
    terms = jnp.pad(terms, ((0, row_count - terms.shape[0]), (0, 0)))
    terms = jnp.broadcast_to(terms[None], (ZS, row_count, 128))
    pieces = chip.astype(bf16).reshape(ZS, row_count, both)
    got = swap(jnp.concatenate([pieces, terms], axis=2), "rows", z_groups)
    z_block, z_sent, packed = call(
        sum_kernel,
        [
            ((row_count, both), f32),
            ((ZS, row_count, both), bf16),
            ((COLS, row_count, both + col_count + 128), bf16),
        ],
        [vmem] * 2,
        [],
        got,
        rotation,
    )

    panel = swap(z_sent, "rows", z_groups)
    packed, panel = lax.optimization_barrier((packed, panel))
    panels = [panel] + [along_x(panel, steps) for steps in (1, 2, 3)]
    across = swap(packed, "cols")
    away = other_core(jnp.stack(panels))
    block = (row_count, col_count)
    z_cols, gen_rows, square, step = call(
        functools.partial(square_kernel, scale_factor),
        [
            ((XS, ZS, CORES, row_count, both), bf16),
            ((COLS,) + block, f32),
            ((COLS,) + block, bf16),
            ((ZS,) + block, bf16),
        ],
        [smem, vmem] + [anywhere] * (XS + 1),
        [
            pltpu.VMEM((2, COLS, col_count), f32),
            pltpu.VMEM((2, col_count, COLS), f32),
            pltpu.SemaphoreType.DMA((2 * XS,)),
        ],
        place,
        across,
        *panels,
        away,
    )

    step = swap(step, "rows", z_groups)
    square, step = lax.optimization_barrier((square, step))
    steps_x = [step] + [along_x(step, steps) for steps in (1, 2, 3)]
    square = swap(square, "cols")
    half_block, half_sent = call(
        half_kernel,
        [((row_count, both), f32), ((COLS, row_count, both), bf16)],
        [vmem] * 4,
        [],
        square,
        gen_rows,
        z_cols,
        z_block,
    )
    step_away = other_core(jnp.stack(steps_x))
    half_rows = swap(half_sent, "cols")
    return tuple(
        call(
            final_kernel,
            [(block, f32)] * 3 + [((rows_dev, col_count), bf16)],
            [smem] * 2 + [vmem] * 5 + [anywhere] * (XS + 1),
            [
                pltpu.VMEM((XS, ZS, CORES, row_count, col_count), bf16),
                pltpu.SemaphoreType.DMA((2 * XS,)),
            ],
            place,
            atom_size,
            half_rows,
            across,
            coeffs,
            rotation,
            half_block,
            *steps_x,
            step_away,
        )
    )


def solution(mesh):
    placed = (
        P("rows", None),
        P("rows", "cols"),
        P(None, "rows", None, None, None),
        P("rows", None),
        P("rows"),
    )
    return jax.shard_map(
        on_device,
        mesh=mesh,
        in_specs=placed,
        out_specs=(P("rows", "cols"), P("rows", "cols"), P("rows", "cols"), P("rows", "cols")),
        check_vma=False,
    )
```

time: 173 us -> 184 us (1.064)
  the two profiles are of different devices: /device:TPU:64 before, /device:TPU:4 now
where the time goes in v6:
time: 184 us; the launch traced here: 183 us
  starting transfers between devices  70.7 us (38%)
  waiting for transfers between devices  50 us (27%)
  blocking collectives  39.9 us (22%)
  Pallas kernels  7.04 us (4%)
  other arithmetic  5.79 us (3%)
  local copies, waits for them, and re-layouts  5.19 us (3%)
  matrix products  3.31 us (2%)
    all_to_all x3, blocking collectives, swap(): lax.all_to_all(cells, axis, 0, 0, tiled=True, axis_index_groups=groups)  39.9 us
    ppermute x9, starting transfers between devices, along_x(): lax.ppermute(cells, 'rows', [(i, (i + steps * line) % count) for i in ran...  36.8 us
    all_to_all x3, waiting for transfers between devices, swap(): lax.all_to_all(cells, axis, 0, 0, tiled=True, axis_index_groups=groups)  33.3 us
    all_to_all x3, starting transfers between devices, swap(): lax.all_to_all(cells, axis, 0, 0, tiled=True, axis_index_groups=groups)  13.9 us
    ppermute x9, waiting for transfers between devices, along_x(): lax.ppermute(cells, 'rows', [(i, (i + steps * line) % count) for i in ran...  13.5 us
    ppermute x1, starting transfers between devices, on_device(): lax.ppermute(own_cols[:width], 'rows', down)  10.3 us
    ppermute x4, starting transfers between devices, other_core(): return lax.ppermute(cells, 'rows', [(i, i ^ 1) for i in range(count)])  7.79 us
    pallas_call x4, Pallas kernels, call(): pl.pallas_call(kernel, out_shape=[jax.ShapeDtypeStruct(*shape) for shape...  7.04 us
  transfers between devices with their start and end apart: 18, of which 10 were waited for; matrix products, arithmetic and copies ran while one was open for 3% of the time, Pallas kernels for 1%

profile of v6, /device:TPU:4, one launch (start us, length us, event | category | flops | bytes accessed | tf_op | source)
XLA Modules:
  0.0 183.3 jit_solution(1597088832746599271)
XLA Ops:
  3.1 10.3 %collective-permute-start.1 = (bf16[256,256]{1,0:T(8,128)(2,1)S(1)}, bf16[256,256]{1,0:T(8,128)(2,1)S(1)}, u32[]{:S(2)}, u32[]{:S(2)}) collective-permute-start(bf16[256,256]{1,0:T(8,128)(2,1)S(1)} %get-tuple-element.33), channel_id=1, source_target_pairs={{8,0},{16,8},{24,16},{32,24},{40,32},{48,40},{56,48},{64,56},{72,6... | collective-permute-start | bytes 393224 | tf_op jit(solution)/shard_map/ppermute | solution.py:218
  19.1 2.7 %collective-permute-done = bf16[256,256]{1,0:T(8,128)(2,1)S(1)} collective-permute-done((bf16[256,256]{1,0:T(8,128)(2,1)S(1)}, bf16[256,256]{1,0:T(8,128)(2,1)S(1)}, u32[]{:S(2)}, u32[]{:S(2)}) %collective-permute-start) | collective-permute-done | bytes 131104 | tf_op jit(solution)/shard_map/ppermute | solution.py:216
  29.0 3.4 %collective-permute-start.4 = (bf16[264,512]{1,0:T(8,128)(2,1)}, bf16[264,512]{1,0:T(8,128)(2,1)S(1)}, u32[]{:S(2)}, u32[]{:S(2)}) collective-permute-start(bf16[264,512]{1,0:T(8,128)(2,1)} %get-tuple-element.39), channel_id=1, source_target_pairs={{0,128},{8,136},{16,144},{24,152},{32,160},{40,168},{48,176},{56,1... | collective-permute-start | bytes 811016 | tf_op jit(solution)/shard_map/ppermute | solution.py:35
  32.4 2.4 %collective-permute-start.5 = (bf16[264,512]{1,0:T(8,128)(2,1)S(1)}, bf16[264,512]{1,0:T(8,128)(2,1)S(1)}, u32[]{:S(2)}, u32[]{:S(2)}) collective-permute-start(bf16[264,512]{1,0:T(8,128)(2,1)S(1)} %get-tuple-element.40), channel_id=1, source_target_pairs={{0,384},{8,392},{16,400},{24,408},{32,416},{40,424},{48,432},{56,4... | collective-permute-start | bytes 811016 | tf_op jit(solution)/shard_map/ppermute | solution.py:35
  34.9 7.1 %collective-permute-start.6 = (bf16[264,512]{1,0:T(8,128)(2,1)S(1)}, bf16[264,512]{1,0:T(8,128)(2,1)S(1)}, u32[]{:S(2)}, u32[]{:S(2)}) collective-permute-start(bf16[264,512]{1,0:T(8,128)(2,1)S(1)} %get-tuple-element.41), channel_id=1, source_target_pairs={{0,256},{8,264},{16,272},{24,280},{32,288},{40,296},{48,304},{56,3... | collective-permute-start | bytes 811016 | tf_op jit(solution)/shard_map/ppermute | solution.py:35
  42.2 3.1 %collective-permute-done.5 = bf16[264,512]{1,0:T(8,128)(2,1)S(1)} collective-permute-done((bf16[264,512]{1,0:T(8,128)(2,1)S(1)}, bf16[264,512]{1,0:T(8,128)(2,1)S(1)}, u32[]{:S(2)}, u32[]{:S(2)}) %collective-permute-start.5) | collective-permute-done | bytes 270368 | tf_op jit(solution)/shard_map/ppermute | solution.py:35
  45.3 2.9 %collective-permute-done.6 = bf16[264,512]{1,0:T(8,128)(2,1)S(1)} collective-permute-done((bf16[264,512]{1,0:T(8,128)(2,1)S(1)}, bf16[264,512]{1,0:T(8,128)(2,1)S(1)}, u32[]{:S(2)}, u32[]{:S(2)}) %collective-permute-start.6) | collective-permute-done | bytes 270368 | tf_op jit(solution)/shard_map/ppermute | solution.py:35
  48.7 15.1 %all_to_all.30.got_ref = bf16[8,32,640]{2,1,0:T(8,128)(2,1)S(1)} all-to-all(bf16[8,32,640]{2,1,0:T(8,128)(2,1)S(1)} %pad_maximum_fusion.6), channel_id=1, replica_groups={{0,16,32,48,64,80,96,112},{8,24,40,56,72,88,104,120},{128,144,160,176,1..., dimensions={0} | all-to-all | bytes 655360 | tf_op jit(solution)/shard_map/all_to_all | solution.py:25
  64.7 12.9 %all_to_all.31.own0 = bf16[8,32,512]{2,1,0:T(8,128)(2,1)S(1)} all-to-all(bf16[8,32,512]{2,1,0:T(8,128)(2,1)S(1)} %get-tuple-element.18), channel_id=1, replica_groups={{0,16,32,48,64,80,96,112},{8,24,40,56,72,88,104,120},{128,144,160,176,1..., dimensions={0} | all-to-all | bytes 524288 | tf_op jit(solution)/shard_map/all_to_all | solution.py:25
  77.6 5.9 %collective-permute-start.9 = (bf16[8,32,512]{2,1,0:T(8,128)(2,1)S(1)}, bf16[8,32,512]{2,1,0:T(8,128)(2,1)S(1)}, u32[]{:S(2)}, u32[]{:S(2)}) collective-permute-start(bf16[8,32,512]{2,1,0:T(8,128)(2,1)S(1)} %all_to_all.31.own0), channel_id=1, source_target_pairs={{0,384},{8,392},{16,400},{24,408},{32,416},{40,424},{48,432},{56,4... | collective-permute-start | bytes 786440 | tf_op jit(solution)/shard_map/ppermute | solution.py:35
  83.5 5.0 %collective-permute-start.8 = (bf16[8,32,512]{2,1,0:T(8,128)(2,1)S(1)}, bf16[8,32,512]{2,1,0:T(8,128)(2,1)S(1)}, u32[]{:S(2)}, u32[]{:S(2)}) collective-permute-start(bf16[8,32,512]{2,1,0:T(8,128)(2,1)S(1)} %all_to_all.31.own0), channel_id=1, source_target_pairs={{0,256},{8,264},{16,272},{24,280},{32,288},{40,296},{48,304},{56,3... | collective-permute-start | bytes 786440 | tf_op jit(solution)/shard_map/ppermute | solution.py:35
  90.9 4.0 %collective-permute-done.8.own2 = bf16[8,32,512]{2,1,0:T(8,128)(2,1)S(1)} collective-permute-done((bf16[8,32,512]{2,1,0:T(8,128)(2,1)S(1)}, bf16[8,32,512]{2,1,0:T(8,128)(2,1)S(1)}, u32[]{:S(2)}, u32[]{:S(2)}) %collective-permute-start.8) | collective-permute-done | bytes 262176 | tf_op jit(solution)/shard_map/ppermute | solution.py:35
  94.9 3.1 %collective-permute-done.7.own1 = bf16[8,32,512]{2,1,0:T(8,128)(2,1)S(1)} collective-permute-done((bf16[8,32,512]{2,1,0:T(8,128)(2,1)S(1)}, bf16[8,32,512]{2,1,0:T(8,128)(2,1)S(1)}, u32[]{:S(2)}, u32[]{:S(2)}) %collective-permute-start.7) | collective-permute-done | bytes 262176 | tf_op jit(solution)/shard_map/ppermute | solution.py:35
  101.0 7.1 %all-to-all-start.2 = ((bf16[8,32,896]{2,1,0:T(8,128)(2,1)}), bf16[8,32,896]{2,1,0:T(8,128)(2,1)S(1)}, u32[]{:S(2)}, u32[]{:S(2)}) async-start(bf16[8,32,896]{2,1,0:T(8,128)(2,1)} %get-tuple-element.19), calls=%async_computation.2 | async-start | bytes 917504 | tf_op jit(solution)/shard_map/all_to_all | solution.py:25
  108.2 16.7 %all-to-all-done.2.across_ref = bf16[8,32,896]{2,1,0:T(8,128)(2,1)S(1)} async-done(((bf16[8,32,896]{2,1,0:T(8,128)(2,1)}), bf16[8,32,896]{2,1,0:T(8,128)(2,1)S(1)}, u32[]{:S(2)}, u32[]{:S(2)}) %all-to-all-start.2) | async-done | bytes 458784 | tf_op jit(solution)/shard_map/all_to_all | solution.py:25
  124.9 2.6 %shard_map.85 = (bf16[4,8,2,32,512]{4,3,2,1,0:T(8,128)(2,1)S(1)}, f32[8,32,256]{2,1,0:T(8,128)S(1)}, bf16[8,32,256]{2,1,0:T(8,128)(2,1)}, bf16[8,32,256]{2,1,0:T(8,128)(2,1)S(1)}) custom-call(s32[5]{0:T(128)S(1)} %stack.86.place_ref, bf16[8,32,896]{2,1,0:T(8,128)(2,1)S(1)} %all-to-all-done.2.across_ref, bf16[8,32,512]{2,1,0:T(8,128)(2,1)S(1)} %all_to_all.31.own0, ...), custom_call_target="tpu_custom_call" | custom-call | tf_op jit(solution)/shard_map/pallas_call | solution.py:177
  128.9 11.9 %all_to_all.32.own0 = bf16[8,32,256]{2,1,0:T(8,128)(2,1)S(1)} all-to-all(bf16[8,32,256]{2,1,0:T(8,128)(2,1)S(1)} %get-tuple-element.22), channel_id=1, replica_groups={{0,16,32,48,64,80,96,112},{8,24,40,56,72,88,104,120},{128,144,160,176,1..., dimensions={0} | all-to-all | bytes 262144 | tf_op jit(solution)/shard_map/all_to_all | solution.py:25
  142.9 4.9 %collective-permute-start.12 = (bf16[8,32,256]{2,1,0:T(8,128)(2,1)S(1)}, bf16[8,32,256]{2,1,0:T(8,128)(2,1)S(1)}, u32[]{:S(2)}, u32[]{:S(2)}) collective-permute-start(bf16[8,32,256]{2,1,0:T(8,128)(2,1)S(1)} %all_to_all.32.own0), channel_id=1, source_target_pairs={{0,256},{8,264},{16,272},{24,280},{32,288},{40,296},{48,304},{56,3... | collective-permute-start | bytes 393224 | tf_op jit(solution)/shard_map/ppermute | solution.py:35
  147.9 3.9 %collective-permute-start.11 = (bf16[8,32,256]{2,1,0:T(8,128)(2,1)S(1)}, bf16[8,32,256]{2,1,0:T(8,128)(2,1)S(1)}, u32[]{:S(2)}, u32[]{:S(2)}) collective-permute-start(bf16[8,32,256]{2,1,0:T(8,128)(2,1)S(1)} %all_to_all.32.own0), channel_id=1, source_target_pairs={{0,128},{8,136},{16,144},{24,152},{32,160},{40,168},{48,176},{56,1... | collective-permute-start | bytes 393224 | tf_op jit(solution)/shard_map/ppermute | solution.py:35
  151.8 3.4 %all-to-all-start.4 = ((bf16[8,32,256]{2,1,0:T(8,128)(2,1)}), bf16[8,32,256]{2,1,0:T(8,128)(2,1)S(1)}, u32[]{:S(2)}, u32[]{:S(2)}) async-start(bf16[8,32,256]{2,1,0:T(8,128)(2,1)} %get-tuple-element.23), calls=%async_computation.4 | async-start | bytes 262144 | tf_op jit(solution)/shard_map/all_to_all | solution.py:25
  158.1 6.2 %all-to-all-done.4.square_ref = bf16[8,32,256]{2,1,0:T(8,128)(2,1)S(1)} async-done(((bf16[8,32,256]{2,1,0:T(8,128)(2,1)}), bf16[8,32,256]{2,1,0:T(8,128)(2,1)S(1)}, u32[]{:S(2)}, u32[]{:S(2)}) %all-to-all-start.4) | async-done | bytes 131104 | tf_op jit(solution)/shard_map/all_to_all | solution.py:25
  167.0 3.4 %all-to-all-start.5 = ((bf16[8,32,512]{2,1,0:T(8,128)(2,1)}), bf16[8,32,512]{2,1,0:T(8,128)(2,1)S(1)}, u32[]{:S(2)}, u32[]{:S(2)}) async-start(bf16[8,32,512]{2,1,0:T(8,128)(2,1)} %get-tuple-element.27), calls=%async_computation.5 | async-start | bytes 524288 | tf_op jit(solution)/shard_map/all_to_all | solution.py:25
  170.4 10.4 %all-to-all-done.5.half_ref = bf16[8,32,512]{2,1,0:T(8,128)(2,1)S(1)} async-done(((bf16[8,32,512]{2,1,0:T(8,128)(2,1)}), bf16[8,32,512]{2,1,0:T(8,128)(2,1)S(1)}, u32[]{:S(2)}, u32[]{:S(2)}) %all-to-all-start.5) | async-done | bytes 262176 | tf_op jit(solution)/shard_map/all_to_all | solution.py:25
  180.8 2.4 %shard_map.87 = (f32[32,256]{1,0:T(8,128)}, f32[32,256]{1,0:T(8,128)}, f32[32,256]{1,0:T(8,128)}, bf16[256,256]{1,0:T(8,128)(2,1)}) custom-call(s32[5]{0:T(128)S(1)} %stack.86.place_ref, s32[2]{0:T(128)S(1)} %copy-done.4, bf16[8,32,512]{2,1,0:T(8,128)(2,1)S(1)} %all-to-all-done.5.half_ref, bf16[8,32,896]{2,1,0:T(8,128)(2,1)S(1)} %all-to-all-done.2.across_ref, ...), custom_call_target="tpu_custom_call" | custom-call | tf_op jit(solution)/shard_map/pallas_call | solution.py:177
  (76 shorter events, 31.2 us)
Async XLA Ops:
  3.1 18.8 %collective-permute-start.1 = (bf16[256,256]{1,0:T(8,128)(2,1)S(1)}, bf16[256,256]{1,0:T(8,128)(2,1)S(1)}, u32[]{:S(2)}, u32[]{:S(2)}) collective-permute-start(bf16[256,256]{1,0:T(8,128)(2,1)S(1)} %get-tuple-element.33), channel_id=1, source_target_pairs={{8,0},{16,8},{24,16},{32,24},{40,32},{48,40},{56,48},{64,56},{72,6... | collective-permute-start | bytes 393224 | tf_op jit(solution)/shard_map/ppermute | solution.py:218
  13.4 8.4 %collective-permute-start = (bf16[256,256]{1,0:T(8,128)(2,1)S(1)}, bf16[256,256]{1,0:T(8,128)(2,1)S(1)}, u32[]{:S(2)}, u32[]{:S(2)}) collective-permute-start(bf16[256,256]{1,0:T(8,128)(2,1)S(1)} %get-tuple-element.33), channel_id=1, source_target_pairs={{0,8},{8,16},{16,24},{24,32},{32,40},{40,48},{48,56},{56,64},{64,7... | collective-permute-start | bytes 393224 | tf_op jit(solution)/shard_map/ppermute | solution.py:216
  15.4 3.7 %copy-start.6 = (s32[2,5]{1,0:T(2,128)S(1)}, s32[2,5]{1,0:T(2,128)}, u32[]{:S(2)}) copy-start(s32[2,5]{1,0:T(2,128)} %param.8) | copy-start | bytes 124
  17.0 5.0 %copy-start.5 = (f32[2,128,256]{2,1,0:T(8,128)S(1)}, f32[2,128,256]{2,1,0:T(8,128)}, u32[]{:S(2)}) copy-start(f32[2,128,256]{2,1,0:T(8,128)} %get-tuple-element.32) | copy-start | bytes 786436
  17.0 10.6 %collective-permute-start.2 = (bf16[1024,256]{1,0:T(8,128)(2,1)S(1)}, bf16[1024,256]{1,0:T(8,128)(2,1)S(1)}, u32[]{:S(2)}, u32[]{:S(2)}) collective-permute-start(bf16[1024,256]{1,0:T(8,128)(2,1)S(1)} %bitcast.91), channel_id=1, source_target_pairs={{0,8},{8,0},{16,24},{24,16},{32,40},{40,32},{48,56},{56,48},{64,72... | collective-permute-start | bytes 1572872 | tf_op jit(solution)/shard_map/ppermute | solution.py:30
  24.0 3.4 %collective-permute-start.3 = (bf16[256,512]{1,0:T(8,128)(2,1)S(1)}, bf16[256,512]{1,0:T(8,128)(2,1)S(1)}, u32[]{:S(2)}, u32[]{:S(2)}) collective-permute-start(bf16[256,512]{1,0:T(8,128)(2,1)S(1)} %select_convert_fusion.1), channel_id=1, source_target_pairs={{0,8},{8,0},{16,24},{24,16},{32,40},{40,32},{48,56},{56,48},{64,72... | collective-permute-start | bytes 786440 | tf_op jit(solution)/shard_map/ppermute | solution.py:30
  29.0 13.2 %collective-permute-start.4 = (bf16[264,512]{1,0:T(8,128)(2,1)}, bf16[264,512]{1,0:T(8,128)(2,1)S(1)}, u32[]{:S(2)}, u32[]{:S(2)}) collective-permute-start(bf16[264,512]{1,0:T(8,128)(2,1)} %get-tuple-element.39), channel_id=1, source_target_pairs={{0,128},{8,136},{16,144},{24,152},{32,160},{40,168},{48,176},{56,1... | collective-permute-start | bytes 811016 | tf_op jit(solution)/shard_map/ppermute | solution.py:35
  32.4 12.8 %collective-permute-start.5 = (bf16[264,512]{1,0:T(8,128)(2,1)S(1)}, bf16[264,512]{1,0:T(8,128)(2,1)S(1)}, u32[]{:S(2)}, u32[]{:S(2)}) collective-permute-start(bf16[264,512]{1,0:T(8,128)(2,1)S(1)} %get-tuple-element.40), channel_id=1, source_target_pairs={{0,384},{8,392},{16,400},{24,408},{32,416},{40,424},{48,432},{56,4... | collective-permute-start | bytes 811016 | tf_op jit(solution)/shard_map/ppermute | solution.py:35
  34.9 13.3 %collective-permute-start.6 = (bf16[264,512]{1,0:T(8,128)(2,1)S(1)}, bf16[264,512]{1,0:T(8,128)(2,1)S(1)}, u32[]{:S(2)}, u32[]{:S(2)}) collective-permute-start(bf16[264,512]{1,0:T(8,128)(2,1)S(1)} %get-tuple-element.41), channel_id=1, source_target_pairs={{0,256},{8,264},{16,272},{24,280},{32,288},{40,296},{48,304},{56,3... | collective-permute-start | bytes 811016 | tf_op jit(solution)/shard_map/ppermute | solution.py:35
  48.3 15.6 %copy-start.3 = (f32[32,256]{1,0:T(8,128)S(1)}, f32[32,256]{1,0:T(8,128)}, u32[]{:S(2)}) copy-start(f32[32,256]{1,0:T(8,128)} %rotation_ref.3) | copy-start | bytes 98308
  77.6 13.3 %collective-permute-start.9 = (bf16[8,32,512]{2,1,0:T(8,128)(2,1)S(1)}, bf16[8,32,512]{2,1,0:T(8,128)(2,1)S(1)}, u32[]{:S(2)}, u32[]{:S(2)}) collective-permute-start(bf16[8,32,512]{2,1,0:T(8,128)(2,1)S(1)} %all_to_all.31.own0), channel_id=1, source_target_pairs={{0,384},{8,392},{16,400},{24,408},{32,416},{40,424},{48,432},{56,4... | collective-permute-start | bytes 786440 | tf_op jit(solution)/shard_map/ppermute | solution.py:35
  83.5 11.5 %collective-permute-start.8 = (bf16[8,32,512]{2,1,0:T(8,128)(2,1)S(1)}, bf16[8,32,512]{2,1,0:T(8,128)(2,1)S(1)}, u32[]{:S(2)}, u32[]{:S(2)}) collective-permute-start(bf16[8,32,512]{2,1,0:T(8,128)(2,1)S(1)} %all_to_all.31.own0), channel_id=1, source_target_pairs={{0,256},{8,264},{16,272},{24,280},{32,288},{40,296},{48,304},{56,3... | collective-permute-start | bytes 786440 | tf_op jit(solution)/shard_map/ppermute | solution.py:35
  88.5 9.5 %collective-permute-start.7 = (bf16[8,32,512]{2,1,0:T(8,128)(2,1)S(1)}, bf16[8,32,512]{2,1,0:T(8,128)(2,1)S(1)}, u32[]{:S(2)}, u32[]{:S(2)}) collective-permute-start(bf16[8,32,512]{2,1,0:T(8,128)(2,1)S(1)} %all_to_all.31.own0), channel_id=1, source_target_pairs={{0,128},{8,136},{16,144},{24,152},{32,160},{40,168},{48,176},{56,1... | collective-permute-start | bytes 786440 | tf_op jit(solution)/shard_map/ppermute | solution.py:35
  99.1 25.8 %collective-permute-start.10 = (bf16[4,8,32,512]{3,2,1,0:T(8,128)(2,1)}, bf16[4,8,32,512]{3,2,1,0:T(8,128)(2,1)S(1)}, u32[]{:S(2)}, u32[]{:S(2)}) collective-permute-start(bf16[4,8,32,512]{3,2,1,0:T(8,128)(2,1)} %pad_maximum_fusion), channel_id=1, source_target_pairs={{0,8},{8,0},{16,24},{24,16},{32,40},{40,32},{48,56},{56,48},{64,72... | collective-permute-start | bytes 3145736 | tf_op jit(solution)/shard_map/ppermute | solution.py:30
  101.0 23.9 %all-to-all-start.2 = ((bf16[8,32,896]{2,1,0:T(8,128)(2,1)}), bf16[8,32,896]{2,1,0:T(8,128)(2,1)S(1)}, u32[]{:S(2)}, u32[]{:S(2)}) async-start(bf16[8,32,896]{2,1,0:T(8,128)(2,1)} %get-tuple-element.19), calls=%async_computation.2 | async-start | bytes 917504 | tf_op jit(solution)/shard_map/all_to_all | solution.py:25
  140.8 14.5 %collective-permute-start.13 = (bf16[8,32,256]{2,1,0:T(8,128)(2,1)S(1)}, bf16[8,32,256]{2,1,0:T(8,128)(2,1)S(1)}, u32[]{:S(2)}, u32[]{:S(2)}) collective-permute-start(bf16[8,32,256]{2,1,0:T(8,128)(2,1)S(1)} %all_to_all.32.own0), channel_id=1, source_target_pairs={{0,384},{8,392},{16,400},{24,408},{32,416},{40,424},{48,432},{56,4... | collective-permute-start | bytes 393224 | tf_op jit(solution)/shard_map/ppermute | solution.py:35
  142.9 12.3 %collective-permute-start.12 = (bf16[8,32,256]{2,1,0:T(8,128)(2,1)S(1)}, bf16[8,32,256]{2,1,0:T(8,128)(2,1)S(1)}, u32[]{:S(2)}, u32[]{:S(2)}) collective-permute-start(bf16[8,32,256]{2,1,0:T(8,128)(2,1)S(1)} %all_to_all.32.own0), channel_id=1, source_target_pairs={{0,256},{8,264},{16,272},{24,280},{32,288},{40,296},{48,304},{56,3... | collective-permute-start | bytes 393224 | tf_op jit(solution)/shard_map/ppermute | solution.py:35
  147.9 7.4 %collective-permute-start.11 = (bf16[8,32,256]{2,1,0:T(8,128)(2,1)S(1)}, bf16[8,32,256]{2,1,0:T(8,128)(2,1)S(1)}, u32[]{:S(2)}, u32[]{:S(2)}) collective-permute-start(bf16[8,32,256]{2,1,0:T(8,128)(2,1)S(1)} %all_to_all.32.own0), channel_id=1, source_target_pairs={{0,128},{8,136},{16,144},{24,152},{32,160},{40,168},{48,176},{56,1... | collective-permute-start | bytes 393224 | tf_op jit(solution)/shard_map/ppermute | solution.py:35
  151.8 12.4 %all-to-all-start.4 = ((bf16[8,32,256]{2,1,0:T(8,128)(2,1)}), bf16[8,32,256]{2,1,0:T(8,128)(2,1)S(1)}, u32[]{:S(2)}, u32[]{:S(2)}) async-start(bf16[8,32,256]{2,1,0:T(8,128)(2,1)} %get-tuple-element.23), calls=%async_computation.4 | async-start | bytes 262144 | tf_op jit(solution)/shard_map/all_to_all | solution.py:25
  155.2 25.6 %copy-start = (bf16[256,2048]{1,0:T(8,128)(2,1)S(1)}, bf16[256,2048]{1,0:T(8,128)(2,1)}, u32[]{:S(2)}) copy-start(bf16[256,2048]{1,0:T(8,128)(2,1)} %coeffs_ref.1) | copy-start | bytes 3145732
  155.2 25.6 %copy-start.4 = (s32[2]{0:T(128)S(1)}, s32[2]{0:T(128)}, u32[]{:S(2)}) copy-start(s32[2]{0:T(128)} %size_ref.1) | copy-start | bytes 28
  156.1 14.3 %collective-permute-start.14 = (bf16[4,8,32,256]{3,2,1,0:T(8,128)(2,1)}, bf16[4,8,32,256]{3,2,1,0:T(8,128)(2,1)S(1)}, u32[]{:S(2)}, u32[]{:S(2)}) collective-permute-start(bf16[4,8,32,256]{3,2,1,0:T(8,128)(2,1)} %pad_maximum_fusion.2), channel_id=1, source_target_pairs={{0,8},{8,0},{16,24},{24,16},{32,40},{40,32},{48,56},{56,48},{64,72... | collective-permute-start | bytes 1572872 | tf_op jit(solution)/shard_map/ppermute | solution.py:30
  164.2 1.6 copy-start.2
  167.0 13.8 %all-to-all-start.5 = ((bf16[8,32,512]{2,1,0:T(8,128)(2,1)}), bf16[8,32,512]{2,1,0:T(8,128)(2,1)S(1)}, u32[]{:S(2)}, u32[]{:S(2)}) async-start(bf16[8,32,512]{2,1,0:T(8,128)(2,1)} %get-tuple-element.27), calls=%async_computation.5 | async-start | bytes 524288 | tf_op jit(solution)/shard_map/all_to_all | solution.py:25
  (1 other events, 1.3 us)

commit v7 on v6

--- a/solution.py
+++ b/solution.py
@@ -42,26 +42,61 @@
 vmem = pl.BlockSpec(memory_space=pltpu.VMEM)
 smem = pl.BlockSpec(memory_space=pltpu.SMEM)
 anywhere = pl.BlockSpec(memory_space=pl.ANY)
-params = pltpu.CompilerParams(vmem_limit_bytes=32 * 2**20)
-
-
-def gathered(place_ref, own_refs, away_ref, out_ref, sems):
-    x, core = place_ref[0], place_ref[1]
-    copies = []
-    for steps in range(XS):
-        source = lax.rem(x + XS - steps, XS)
-        copies.append((own_refs[steps], out_ref.at[source, :, core]))
-        copies.append((away_ref.at[steps], out_ref.at[source, :, 1 - core]))
-    copies = [pltpu.make_async_copy(*pair, sems.at[i]) for i, pair in enumerate(copies)]
-    for copy in copies:
-        copy.start()
-    return copies
-
-
-def chunk(panel_ref, k):
-    per = ZS * XS // COLS
-    cells = panel_ref[k * per // ZS, pl.ds(k * per % ZS, per)]
-    return cells.reshape(-1, cells.shape[-1])
+
+
+def call(kernel, shapes, in_specs, scratch, *operands, bytes_accessed=2**20):
+    return pl.pallas_call(
+        kernel,
+        out_shape=[jax.ShapeDtypeStruct(*shape) for shape in shapes],
+        in_specs=in_specs,
+        out_specs=[vmem] * len(shapes),
+        scratch_shapes=scratch,
+        compiler_params=pltpu.CompilerParams(vmem_limit_bytes=12 * 2**20),
+        cost_estimate=pl.CostEstimate(
+            flops=0, bytes_accessed=bytes_accessed, transcendentals=0
+        ),
+    )(*operands)
+
+
+def within_rows(size_ref, cells):
+    blocks = size_ref.shape[0]
+    size = cells.shape[0] // blocks
+    within = lax.broadcasted_iota(jnp.int32, (size, cells.shape[1]), 0)
+    parts = [
+        jnp.where(within < size_ref[b], cells[b * size : (b + 1) * size], 0.0)
+        for b in range(blocks)
+    ]
+    return jnp.concatenate(parts, axis=0)
+
+
+def mask_kernel(place_ref, size_ref, coeffs_ref, cols_ref, slice_ref, sem):
+    width = cols_ref.shape[1]
+    start = pl.multiple_of(place_ref[4] * width, width)
+    copy = pltpu.make_async_copy(coeffs_ref.at[:, pl.ds(start, width)], slice_ref, sem)
+    copy.start()
+    copy.wait()
+    cols_ref[...] = within_rows(size_ref, slice_ref[...].astype(f32)).astype(bf16)
+
+
+def applied_kernel(size_ref, links_ref, up_ref, cols_ref, down_ref, ops_ref, out_ref, diag_ref):
+    phases, blocks, span, size, _ = ops_ref.shape
+    width = cols_ref.shape[1]
+    padded = jnp.concatenate([up_ref[...], cols_ref[...], down_ref[...]], axis=0)
+    first = up_ref.shape[0] - (span - 1) // 2 * size
+    own = cols_ref[...].astype(f32)
+    for p in range(phases):
+        parts = []
+        for b in range(blocks):
+            gated = [
+                ops_ref[p, b, t] * links_ref[b, t].astype(f32).astype(bf16) for t in range(span)
+            ]
+            start = first + b * size
+            near = padded[start : start + span * size]
+            parts.append(small_product(jnp.concatenate(gated, axis=1), near))
+        total = within_rows(size_ref, jnp.concatenate(parts, axis=0)).astype(bf16)
+        out_ref[:, p * width : (p + 1) * width] = total
+        sums = jnp.sum(total.astype(f32) * own, axis=0, keepdims=True)
+        diag_ref[:, p * width : (p + 1) * width] = sums
 
 
 def sum_kernel(got_ref, rotation_ref, block_ref, z_ref, packed_ref):
@@ -82,19 +117,32 @@
         packed_ref[i] = packed
 
 
-def square_kernel(
-    scale, place_ref, across_ref, own0, own1, own2, own3, away_ref,
-    z_ref, rows_ref, square_ref, step_ref, diag_ref, turned_ref, sems,
-):
-    copies = gathered(place_ref, (own0, own1, own2, own3), away_ref, z_ref, sems)
-    mine, low, col = place_ref[2], place_ref[3], place_ref[4]
+def gathered(place_ref, own_refs, away_ref, out_ref, sems):
+    x, core = place_ref[0], place_ref[1]
+    copies = []
+    for steps in range(XS):
+        source = lax.rem(x + XS - steps, XS)
+        copies.append((own_refs[steps], out_ref.at[source, :, core]))
+        copies.append((away_ref.at[steps], out_ref.at[source, :, 1 - core]))
+    copies = [pltpu.make_async_copy(*pair, sems.at[i]) for i, pair in enumerate(copies)]
+    for copy in copies:
+        copy.start()
+    return copies
+
+
+def chunk(panel_ref, k):
+    per = ZS * XS // COLS
+    cells = panel_ref[k * per // ZS, pl.ds(k * per % ZS, per)]
+    return cells.reshape(-1, cells.shape[-1])
+
+
+def rows_kernel(scale, place_ref, across_ref, rows_ref, diag_ref, turned_ref):
+    mine, low = place_ref[2], place_ref[3]
     rows, width = rows_ref.shape[1:]
+    terms = across_ref[:, :, -128:].astype(f32)
+    per = width // 128
     for p in range(2):
-        parts = []
-        for h in range(width // 128):
-            terms = across_ref[:, :, -128:].astype(f32)
-            k = p * (width // 128) + h
-            parts.append(terms[:, k] + terms[:, 4 + k])
+        parts = [terms[:, p * per + h] + terms[:, 2 * per + p * per + h] for h in range(per)]
         diag_ref[p] = jnp.concatenate(parts, axis=1)
         turned_ref[p] = diag_ref[p].T
     lane = lax.broadcasted_iota(jnp.int32, (rows, COLS), 1)
@@ -111,6 +159,15 @@
         cos_part = cells[:, :width] * (diag_ref[0, k : k + 1, :] - down[0])
         sin_part = cells[:, width : 2 * width] * (diag_ref[1, k : k + 1, :] - down[1])
         rows_ref[k] = (cos_part + sin_part) * scale
+
+
+def square_kernel(
+    scale, place_ref, rows_ref, diag_ref, turned_ref, own0, own1, own2, own3, away_ref,
+    z_ref, square_ref, step_ref, sems,
+):
+    copies = gathered(place_ref, (own0, own1, own2, own3), away_ref, z_ref, sems)
+    col = place_ref[4]
+    rows, width = rows_ref.shape[1:]
     across_diag = [diag_ref[p, pl.ds(col, 1), :] for p in range(2)]
     for copy in copies:
         copy.wait()
@@ -164,38 +221,18 @@
     rotated_ref[...] = rotated
     cos_ref[...] = cos_part
     sin_ref[...] = sin_part
-    blocks = size_ref.shape[0]
-    size = orbitals.shape[0] // blocks
-    within = lax.broadcasted_iota(jnp.int32, (size, width), 0)
-    for b in range(blocks):
-        cells = orbitals[b * size : (b + 1) * size]
-        cells = jnp.where(within < size_ref[b], cells, 0.0)
-        orbitals_ref[b * size : (b + 1) * size, :] = cells.astype(bf16)
-
-
-def call(kernel, shapes, in_specs, scratch, *operands):
-    return pl.pallas_call(
-        kernel,
-        out_shape=[jax.ShapeDtypeStruct(*shape) for shape in shapes],
-        in_specs=in_specs,
-        out_specs=[vmem] * len(shapes),
-        scratch_shapes=scratch,
-        compiler_params=params,
-    )(*operands)
+    orbitals_ref[...] = within_rows(size_ref, orbitals).astype(bf16)
 
 
 def on_device(coeffs, rotation, phase_ops, block_links, atom_size):
     rows_dev, orbital_count = coeffs.shape
-    blocks_dev = phase_ops.shape[1]
-    span_blocks = phase_ops.shape[2]
-    block_size = phase_ops.shape[3]
+    span_blocks, block_size = phase_ops.shape[2:4]
     reach_blocks = (span_blocks - 1) // 2
     rows_axis = lax.axis_size("rows")
     cols_axis = lax.axis_size("cols")
     row_count = orbital_count // rows_axis
     col_count = orbital_count // cols_axis
     both = 2 * col_count
-    col_start = lax.axis_index("cols") * col_count
     core = lax.axis_index("rows") % CORES
     own_x = lax.axis_index("rows") // (ZS * CORES)
     per_col = rows_axis // cols_axis
@@ -204,21 +241,20 @@
     place = jnp.stack(place + [lax.axis_index("cols")]).astype(jnp.int32)
     scale_factor = 0.125 / math.sqrt(orbital_count)
 
-    within = lax.broadcasted_iota(jnp.int32, (blocks_dev, block_size), 1)
-    live_rows = (within < atom_size[:, None]).reshape(rows_dev)
-    raw_cols = lax.dynamic_slice_in_dim(coeffs, col_start, col_count, 1)
-    own_cols = jnp.where(live_rows[:, None], raw_cols, jnp.zeros_like(raw_cols))
+    (own_cols,) = call(
+        mask_kernel,
+        [((rows_dev, col_count), bf16)],
+        [smem] * 2 + [anywhere],
+        [pltpu.VMEM((rows_dev, col_count), bf16), pltpu.SemaphoreType.DMA],
+        place,
+        atom_size,
+        coeffs,
+    )
     width = reach_blocks * block_size
     up = [(i, (i + 1) % rows_axis) for i in range(rows_axis)]
     down = [((i + 1) % rows_axis, i) for i in range(rows_axis)]
-    padded = jnp.concatenate(
-        [
-            lax.ppermute(own_cols[rows_dev - width :], "rows", up),
-            own_cols,
-            lax.ppermute(own_cols[:width], "rows", down),
-        ],
-        axis=0,
-    )
+    from_up = lax.ppermute(own_cols[rows_dev - width :], "rows", up)
+    from_down = lax.ppermute(own_cols[:width], "rows", down)
     turned = coeffs.T.reshape(XS, ZS, CORES, row_count, rows_dev)
 
     def turned_half(which):
@@ -226,25 +262,23 @@
 
     own_turned = turned_half(core)
     far_turned = other_core(turned_half(1 - core))
-    stacked = jnp.stack(
-        [
-            padded[offset * block_size : (offset + blocks_dev) * block_size].reshape(
-                blocks_dev, block_size, col_count
-            )
-            for offset in range(span_blocks)
-        ],
-        axis=1,
-    )
-    gated = phase_ops * block_links[None, :, :, None, None].astype(bf16)
-    applied = jnp.einsum("pbtij,btjk->bipk", gated, stacked, preferred_element_type=f32)
-    applied = jnp.where(live_rows[:, None], applied.reshape(rows_dev, both), 0.0).astype(bf16)
+    applied, own_diag = call(
+        applied_kernel,
+        [((rows_dev, both), bf16), ((1, both), f32)],
+        [smem] * 2 + [vmem] * 4,
+        [],
+        atom_size,
+        block_links,
+        from_up,
+        own_cols,
+        from_down,
+        phase_ops,
+    )
     far_applied = other_core(applied)
 
-    def diag_of(cols, values):
-        return jnp.sum(jnp.tile(cols, (1, 2)).astype(f32) * values.astype(f32), axis=0)
-
-    far_cols = jnp.where(core == 0, padded[width + rows_dev :], padded[:width])
-    diag = diag_of(own_cols, applied) + diag_of(far_cols, far_applied)
+    far_cols = jnp.where(core == 0, from_down[:rows_dev], from_up[-rows_dev:]).astype(f32)
+    far_diag = jnp.tile(far_cols, (1, 2)) * far_applied.astype(f32)
+    diag = own_diag[0] + jnp.sum(far_diag, axis=0)
 
     def with_diag(cells, values):
         high = lax.reduce_precision(values, 8, 7)
@@ -289,24 +323,35 @@
     packed, panel = lax.optimization_barrier((packed, panel))
     panels = [panel] + [along_x(panel, steps) for steps in (1, 2, 3)]
     across = swap(packed, "cols")
-    away = other_core(jnp.stack(panels))
+    stacked, across = lax.optimization_barrier((jnp.stack(panels), across))
+    away = other_core(stacked)
     block = (row_count, col_count)
-    z_cols, gen_rows, square, step = call(
+    gen_rows, diag_all, turned_diag = call(
+        functools.partial(rows_kernel, scale_factor),
+        [
+            ((COLS,) + block, f32),
+            ((2, COLS, col_count), f32),
+            ((2, col_count, COLS), f32),
+        ],
+        [smem, vmem],
+        [],
+        place,
+        across,
+        bytes_accessed=2**28,
+    )
+    z_cols, square, step = call(
         functools.partial(square_kernel, scale_factor),
         [
             ((XS, ZS, CORES, row_count, both), bf16),
-            ((COLS,) + block, f32),
             ((COLS,) + block, bf16),
             ((ZS,) + block, bf16),
         ],
-        [smem, vmem] + [anywhere] * (XS + 1),
-        [
-            pltpu.VMEM((2, COLS, col_count), f32),
-            pltpu.VMEM((2, col_count, COLS), f32),
-            pltpu.SemaphoreType.DMA((2 * XS,)),
-        ],
+        [smem] + [vmem] * 3 + [anywhere] * (XS + 1),
+        [pltpu.SemaphoreType.DMA((2 * XS,))],
         place,
-        across,
+        gen_rows,
+        diag_all,
+        turned_diag,
         *panels,
         away,
     )
@@ -324,7 +369,9 @@
         gen_rows,
         z_cols,
         z_block,
-    )
+        bytes_accessed=2**26,
+    )
+    *steps_x, half_sent = lax.optimization_barrier((*steps_x, half_sent))
     step_away = other_core(jnp.stack(steps_x))
     half_rows = swap(half_sent, "cols")
     return tuple(

time: 184 us -> 177 us (0.962)
  the two profiles are of different devices: /device:TPU:4 before, /device:TPU:1 now
where the time goes in v7:
time: 177 us; the launch traced here: 176 us
  starting transfers between devices  69 us (39%)
  blocking collectives  56 us (32%)
  waiting for transfers between devices  31 us (18%)
  Pallas kernels  8.52 us (5%)
  local copies, waits for them, and re-layouts  6.72 us (4%)
  matrix products  1.79 us (1%)
    all_to_all x4, blocking collectives, swap(): lax.all_to_all(cells, axis, 0, 0, tiled=True, axis_index_groups=groups)  56 us
    ppermute x9, starting transfers between devices, along_x(): lax.ppermute(cells, 'rows', [(i, (i + steps * line) % count) for i in ran...  25.6 us
    ppermute x9, waiting for transfers between devices, along_x(): lax.ppermute(cells, 'rows', [(i, (i + steps * line) % count) for i in ran...  23 us
    ppermute x4, starting transfers between devices, other_core(): return lax.ppermute(cells, 'rows', [(i, i ^ 1) for i in range(count)])  19.2 us
    all_to_all x2, starting transfers between devices, swap(): lax.all_to_all(cells, axis, 0, 0, tiled=True, axis_index_groups=groups)  13.5 us
    ppermute x1, starting transfers between devices, on_device(): from_down = lax.ppermute(own_cols[:width], 'rows', down)  8.79 us
    pallas_call x7, Pallas kernels, call(): pl.pallas_call(kernel, out_shape=[jax.ShapeDtypeStruct(*shape) for shape...  8.52 us
    unnamed x20, local copies, waits for them, and re-layouts  6.35 us
  transfers between devices with their start and end apart: 17, of which 9 were waited for; matrix products, arithmetic and copies ran while one was open for 1% of the time, Pallas kernels for 1%

profile of v7, /device:TPU:1, one launch (start us, length us, event | category | flops | bytes accessed | tf_op | source)
XLA Modules:
  0.0 175.7 jit_solution(8323218758231171410)
XLA Ops:
  3.3 8.8 %collective-permute-start.1 = (bf16[256,256]{1,0:T(8,128)(2,1)S(1)}, bf16[256,256]{1,0:T(8,128)(2,1)S(1)}, u32[]{:S(2)}, u32[]{:S(2)}) collective-permute-start(bf16[256,256]{1,0:T(8,128)(2,1)S(1)} %shard_map.84.cols_ref), channel_id=1, source_target_pairs={{8,0},{16,8},{24,16},{32,24},{40,32},{48,40},{56,48},{64,56},{72,6... | collective-permute-start | bytes 393224 | tf_op jit(solution)/shard_map/ppermute | solution.py:257
  15.5 4.6 %collective-permute-done.up_ref = bf16[256,256]{1,0:T(8,128)(2,1)S(1)} collective-permute-done((bf16[256,256]{1,0:T(8,128)(2,1)S(1)}, bf16[256,256]{1,0:T(8,128)(2,1)S(1)}, u32[]{:S(2)}, u32[]{:S(2)}) %collective-permute-start) | collective-permute-done | bytes 131104 | tf_op jit(solution)/shard_map/ppermute | solution.py:256
  21.1 8.8 %collective-permute-start.3 = (bf16[256,512]{1,0:T(8,128)(2,1)S(1)}, bf16[256,512]{1,0:T(8,128)(2,1)S(1)}, u32[]{:S(2)}, u32[]{:S(2)}) collective-permute-start(bf16[256,512]{1,0:T(8,128)(2,1)S(1)} %get-tuple-element.28), channel_id=1, source_target_pairs={{0,8},{8,0},{16,24},{24,16},{32,40},{40,32},{48,56},{56,48},{64,72... | collective-permute-start | bytes 786440 | tf_op jit(solution)/shard_map/ppermute | solution.py:30
  37.8 4.6 %collective-permute-start.5 = (bf16[264,512]{1,0:T(8,128)(2,1)S(1)}, bf16[264,512]{1,0:T(8,128)(2,1)S(1)}, u32[]{:S(2)}, u32[]{:S(2)}) collective-permute-start(bf16[264,512]{1,0:T(8,128)(2,1)S(1)} %get-tuple-element.57), channel_id=1, source_target_pairs={{0,384},{8,392},{16,400},{24,408},{32,416},{40,424},{48,432},{56,4... | collective-permute-start | bytes 811016 | tf_op jit(solution)/shard_map/ppermute | solution.py:35
  44.6 2.6 %collective-permute-done.4 = bf16[264,512]{1,0:T(8,128)(2,1)S(1)} collective-permute-done((bf16[264,512]{1,0:T(8,128)(2,1)}, bf16[264,512]{1,0:T(8,128)(2,1)S(1)}, u32[]{:S(2)}, u32[]{:S(2)}) %collective-permute-start.4) | collective-permute-done | bytes 270368 | tf_op jit(solution)/shard_map/ppermute | solution.py:35
  47.2 6.3 %collective-permute-done.5 = bf16[264,512]{1,0:T(8,128)(2,1)S(1)} collective-permute-done((bf16[264,512]{1,0:T(8,128)(2,1)S(1)}, bf16[264,512]{1,0:T(8,128)(2,1)S(1)}, u32[]{:S(2)}, u32[]{:S(2)}) %collective-permute-start.5) | collective-permute-done | bytes 270368 | tf_op jit(solution)/shard_map/ppermute | solution.py:35
  54.1 13.4 %all_to_all.30.got_ref = bf16[8,32,640]{2,1,0:T(8,128)(2,1)S(1)} all-to-all(bf16[8,32,640]{2,1,0:T(8,128)(2,1)S(1)} %pad_maximum_fusion.6), channel_id=1, replica_groups={{0,16,32,48,64,80,96,112},{8,24,40,56,72,88,104,120},{128,144,160,176,1..., dimensions={0} | all-to-all | bytes 655360 | tf_op jit(solution)/shard_map/all_to_all | solution.py:25
  68.4 12.9 %all_to_all.31.own0 = bf16[8,32,512]{2,1,0:T(8,128)(2,1)S(1)} all-to-all(bf16[8,32,512]{2,1,0:T(8,128)(2,1)S(1)} %get-tuple-element.31), channel_id=1, replica_groups={{0,16,32,48,64,80,96,112},{8,24,40,56,72,88,104,120},{128,144,160,176,1..., dimensions={0} | all-to-all | bytes 524288 | tf_op jit(solution)/shard_map/all_to_all | solution.py:25
  81.3 6.8 %all-to-all-start.2 = ((bf16[8,32,896]{2,1,0:T(8,128)(2,1)}), bf16[8,32,896]{2,1,0:T(8,128)(2,1)S(1)}, u32[]{:S(2)}, u32[]{:S(2)}) async-start(bf16[8,32,896]{2,1,0:T(8,128)(2,1)} %get-tuple-element.33), calls=%async_computation.2 | async-start | bytes 917504 | tf_op jit(solution)/shard_map/all_to_all | solution.py:25
  88.1 5.5 %collective-permute-start.9 = (bf16[8,32,512]{2,1,0:T(8,128)(2,1)S(1)}, bf16[8,32,512]{2,1,0:T(8,128)(2,1)S(1)}, u32[]{:S(2)}, u32[]{:S(2)}) collective-permute-start(bf16[8,32,512]{2,1,0:T(8,128)(2,1)S(1)} %all_to_all.31.own0), channel_id=1, source_target_pairs={{0,384},{8,392},{16,400},{24,408},{32,416},{40,424},{48,432},{56,4... | collective-permute-start | bytes 786440 | tf_op jit(solution)/shard_map/ppermute | solution.py:35
  95.5 2.5 %collective-permute-start.7 = (bf16[8,32,512]{2,1,0:T(8,128)(2,1)S(1)}, bf16[8,32,512]{2,1,0:T(8,128)(2,1)S(1)}, u32[]{:S(2)}, u32[]{:S(2)}) collective-permute-start(bf16[8,32,512]{2,1,0:T(8,128)(2,1)S(1)} %all_to_all.31.own0), channel_id=1, source_target_pairs={{0,128},{8,136},{16,144},{24,152},{32,160},{40,168},{48,176},{56,1... | collective-permute-start | bytes 786440 | tf_op jit(solution)/shard_map/ppermute | solution.py:35
  98.0 4.3 %collective-permute-done.8.own2 = bf16[8,32,512]{2,1,0:T(8,128)(2,1)S(1)} collective-permute-done((bf16[8,32,512]{2,1,0:T(8,128)(2,1)S(1)}, bf16[8,32,512]{2,1,0:T(8,128)(2,1)S(1)}, u32[]{:S(2)}, u32[]{:S(2)}) %collective-permute-start.8) | collective-permute-done | bytes 262176 | tf_op jit(solution)/shard_map/ppermute | solution.py:35
  102.3 6.0 %collective-permute-done.7.own1 = bf16[8,32,512]{2,1,0:T(8,128)(2,1)S(1)} collective-permute-done((bf16[8,32,512]{2,1,0:T(8,128)(2,1)S(1)}, bf16[8,32,512]{2,1,0:T(8,128)(2,1)S(1)}, u32[]{:S(2)}, u32[]{:S(2)}) %collective-permute-start.7) | collective-permute-done | bytes 262176 | tf_op jit(solution)/shard_map/ppermute | solution.py:35
  108.5 4.9 %collective-permute-start.10 = (bf16[4,8,32,512]{3,2,1,0:T(8,128)(2,1)S(1)}, bf16[4,8,32,512]{3,2,1,0:T(8,128)(2,1)S(1)}, u32[]{:S(2)}, u32[]{:S(2)}) collective-permute-start(bf16[4,8,32,512]{3,2,1,0:T(8,128)(2,1)S(1)} %pad_maximum_fusion), channel_id=1, source_target_pairs={{0,8},{8,0},{16,24},{24,16},{32,40},{40,32},{48,56},{56,48},{64,72... | collective-permute-start | bytes 3145736 | tf_op jit(solution)/shard_map/ppermute | solution.py:30
  115.7 2.3 %shard_map.88 = (bf16[4,8,2,32,512]{4,3,2,1,0:T(8,128)(2,1)S(1)}, bf16[8,32,256]{2,1,0:T(8,128)(2,1)}, bf16[8,32,256]{2,1,0:T(8,128)(2,1)S(1)}) custom-call(s32[5]{0:T(128)S(1)} %stack.83.place_ref, f32[8,32,256]{2,1,0:T(8,128)S(1)} %get-tuple-element.35.rows_ref, f32[2,8,256]{2,1,0:T(8,128)S(1)} %get-tuple-element.36.diag_ref, ...), custom_call_target="tpu_custom_call" | custom-call | bytes 1048576 | tf_op jit(solution)/shard_map/pallas_call | solution.py:48
  119.3 10.8 %all_to_all.32.own0 = bf16[8,32,256]{2,1,0:T(8,128)(2,1)S(1)} all-to-all(bf16[8,32,256]{2,1,0:T(8,128)(2,1)S(1)} %get-tuple-element.40), channel_id=1, replica_groups={{0,16,32,48,64,80,96,112},{8,24,40,56,72,88,104,120},{128,144,160,176,1..., dimensions={0} | all-to-all | bytes 262144 | tf_op jit(solution)/shard_map/all_to_all | solution.py:25
  130.1 6.6 %all-to-all-start.4 = ((bf16[8,32,256]{2,1,0:T(8,128)(2,1)}), bf16[8,32,256]{2,1,0:T(8,128)(2,1)S(1)}, u32[]{:S(2)}, u32[]{:S(2)}) async-start(bf16[8,32,256]{2,1,0:T(8,128)(2,1)} %get-tuple-element.42), calls=%async_computation.4 | async-start | bytes 262144 | tf_op jit(solution)/shard_map/all_to_all | solution.py:25
  136.8 2.4 %collective-permute-start.13 = (bf16[8,32,256]{2,1,0:T(8,128)(2,1)S(1)}, bf16[8,32,256]{2,1,0:T(8,128)(2,1)S(1)}, u32[]{:S(2)}, u32[]{:S(2)}) collective-permute-start(bf16[8,32,256]{2,1,0:T(8,128)(2,1)S(1)} %all_to_all.32.own0), channel_id=1, source_target_pairs={{0,384},{8,392},{16,400},{24,408},{32,416},{40,424},{48,432},{56,4... | collective-permute-start | bytes 393224 | tf_op jit(solution)/shard_map/ppermute | solution.py:35
  139.1 2.2 %collective-permute-start.12 = (bf16[8,32,256]{2,1,0:T(8,128)(2,1)S(1)}, bf16[8,32,256]{2,1,0:T(8,128)(2,1)S(1)}, u32[]{:S(2)}, u32[]{:S(2)}) collective-permute-start(bf16[8,32,256]{2,1,0:T(8,128)(2,1)S(1)} %all_to_all.32.own0), channel_id=1, source_target_pairs={{0,256},{8,264},{16,272},{24,280},{32,288},{40,296},{48,304},{56,3... | collective-permute-start | bytes 393224 | tf_op jit(solution)/shard_map/ppermute | solution.py:35
  141.3 2.8 %collective-permute-start.11 = (bf16[8,32,256]{2,1,0:T(8,128)(2,1)S(1)}, bf16[8,32,256]{2,1,0:T(8,128)(2,1)S(1)}, u32[]{:S(2)}, u32[]{:S(2)}) collective-permute-start(bf16[8,32,256]{2,1,0:T(8,128)(2,1)S(1)} %all_to_all.32.own0), channel_id=1, source_target_pairs={{0,128},{8,136},{16,144},{24,152},{32,160},{40,168},{48,176},{56,1... | collective-permute-start | bytes 393224 | tf_op jit(solution)/shard_map/ppermute | solution.py:35
  146.8 3.8 %collective-permute-done.11.own1 = bf16[8,32,256]{2,1,0:T(8,128)(2,1)S(1)} collective-permute-done((bf16[8,32,256]{2,1,0:T(8,128)(2,1)S(1)}, bf16[8,32,256]{2,1,0:T(8,128)(2,1)S(1)}, u32[]{:S(2)}, u32[]{:S(2)}) %collective-permute-start.11) | collective-permute-done | bytes 131104 | tf_op jit(solution)/shard_map/ppermute | solution.py:35
  150.7 3.6 %collective-permute-start.14 = (bf16[4,8,32,256]{3,2,1,0:T(8,128)(2,1)S(1)}, bf16[4,8,32,256]{3,2,1,0:T(8,128)(2,1)S(1)}, u32[]{:S(2)}, u32[]{:S(2)}) collective-permute-start(bf16[4,8,32,256]{3,2,1,0:T(8,128)(2,1)S(1)} %pad_maximum_fusion.2), channel_id=1, source_target_pairs={{0,8},{8,0},{16,24},{24,16},{32,40},{40,32},{48,56},{56,48},{64,72... | collective-permute-start | bytes 1572872 | tf_op jit(solution)/shard_map/ppermute | solution.py:30
  154.3 18.9 %all_to_all.33.half_ref = bf16[8,32,512]{2,1,0:T(8,128)(2,1)S(1)} all-to-all(bf16[8,32,512]{2,1,0:T(8,128)(2,1)S(1)} %get-tuple-element.46), channel_id=1, replica_groups=mesh['rows'=64,'cols'=8] {'cols'}, dimensions={0} | all-to-all | bytes 524288 | tf_op jit(solution)/shard_map/all_to_all | solution.py:25
  173.2 2.4 %shard_map.90 = (f32[32,256]{1,0:T(8,128)}, f32[32,256]{1,0:T(8,128)}, f32[32,256]{1,0:T(8,128)}, bf16[256,256]{1,0:T(8,128)(2,1)}) custom-call(s32[5]{0:T(128)S(1)} %stack.83.place_ref, s32[2]{0:T(128)S(1)} %copy-done.7, bf16[8,32,512]{2,1,0:T(8,128)(2,1)S(1)} %all_to_all.33.half_ref, bf16[8,32,896]{2,1,0:T(8,128)(2,1)S(1)} %all-to-all-done.2.across_ref, ...), custom_call_target="tpu_custom_call" | custom-call | bytes 1048576 | tf_op jit(solution)/shard_map/pallas_call | solution.py:48
  (69 shorter events, 26.7 us)
Async XLA Ops:
  0.6 19.5 %copy-start.7 = (s32[2]{0:T(128)S(1)}, s32[2]{0:T(128)}, u32[]{:S(2)}) copy-start(s32[2]{0:T(128)} %size_ref.5) | copy-start | bytes 28
  0.6 19.5 %copy-start.8 = (s32[2,5]{1,0:T(2,128)S(1)}, s32[2,5]{1,0:T(2,128)}, u32[]{:S(2)}) copy-start(s32[2,5]{1,0:T(2,128)} %links_ref.1) | copy-start | bytes 124
  2.7 17.5 %copy-start.4 = (bf16[2,2,5,128,128]{4,3,2,1,0:T(8,128)(2,1)S(1)}, bf16[2,2,5,128,128]{4,3,2,1,0:T(8,128)(2,1)}, u32[]{:S(2)}) copy-start(bf16[2,2,5,128,128]{4,3,2,1,0:T(8,128)(2,1)} %ops_ref.1) | copy-start | bytes 1966084
  3.3 12.2 %collective-permute-start.1 = (bf16[256,256]{1,0:T(8,128)(2,1)S(1)}, bf16[256,256]{1,0:T(8,128)(2,1)S(1)}, u32[]{:S(2)}, u32[]{:S(2)}) collective-permute-start(bf16[256,256]{1,0:T(8,128)(2,1)S(1)} %shard_map.84.cols_ref), channel_id=1, source_target_pairs={{8,0},{16,8},{24,16},{32,24},{40,32},{48,40},{56,48},{64,56},{72,6... | collective-permute-start | bytes 393224 | tf_op jit(solution)/shard_map/ppermute | solution.py:257
  12.1 8.0 %collective-permute-start = (bf16[256,256]{1,0:T(8,128)(2,1)S(1)}, bf16[256,256]{1,0:T(8,128)(2,1)S(1)}, u32[]{:S(2)}, u32[]{:S(2)}) collective-permute-start(bf16[256,256]{1,0:T(8,128)(2,1)S(1)} %shard_map.84.cols_ref), channel_id=1, source_target_pairs={{0,8},{8,16},{16,24},{24,32},{32,40},{40,48},{48,56},{56,64},{64,7... | collective-permute-start | bytes 393224 | tf_op jit(solution)/shard_map/ppermute | solution.py:256
  21.1 11.1 %collective-permute-start.3 = (bf16[256,512]{1,0:T(8,128)(2,1)S(1)}, bf16[256,512]{1,0:T(8,128)(2,1)S(1)}, u32[]{:S(2)}, u32[]{:S(2)}) collective-permute-start(bf16[256,512]{1,0:T(8,128)(2,1)S(1)} %get-tuple-element.28), channel_id=1, source_target_pairs={{0,8},{8,0},{16,24},{24,16},{32,40},{40,32},{48,56},{56,48},{64,72... | collective-permute-start | bytes 786440 | tf_op jit(solution)/shard_map/ppermute | solution.py:30
  30.0 3.8 %collective-permute-start.2 = (bf16[1024,256]{1,0:T(8,128)(2,1)S(1)}, bf16[1024,256]{1,0:T(8,128)(2,1)S(1)}, u32[]{:S(2)}, u32[]{:S(2)}) collective-permute-start(bf16[1024,256]{1,0:T(8,128)(2,1)S(1)} %bitcast.56), channel_id=1, source_target_pairs={{0,8},{8,0},{16,24},{24,16},{32,40},{40,32},{48,56},{56,48},{64,72... | collective-permute-start | bytes 1572872 | tf_op jit(solution)/shard_map/ppermute | solution.py:30
  35.9 11.2 %collective-permute-start.4 = (bf16[264,512]{1,0:T(8,128)(2,1)}, bf16[264,512]{1,0:T(8,128)(2,1)S(1)}, u32[]{:S(2)}, u32[]{:S(2)}) collective-permute-start(bf16[264,512]{1,0:T(8,128)(2,1)} %get-tuple-element.56), channel_id=1, source_target_pairs={{0,128},{8,136},{16,144},{24,152},{32,160},{40,168},{48,176},{56,1... | collective-permute-start | bytes 811016 | tf_op jit(solution)/shard_map/ppermute | solution.py:35
  37.8 15.6 %collective-permute-start.5 = (bf16[264,512]{1,0:T(8,128)(2,1)S(1)}, bf16[264,512]{1,0:T(8,128)(2,1)S(1)}, u32[]{:S(2)}, u32[]{:S(2)}) collective-permute-start(bf16[264,512]{1,0:T(8,128)(2,1)S(1)} %get-tuple-element.57), channel_id=1, source_target_pairs={{0,384},{8,392},{16,400},{24,408},{32,416},{40,424},{48,432},{56,4... | collective-permute-start | bytes 811016 | tf_op jit(solution)/shard_map/ppermute | solution.py:35
  42.4 11.1 %collective-permute-start.6 = (bf16[264,512]{1,0:T(8,128)(2,1)S(1)}, bf16[264,512]{1,0:T(8,128)(2,1)S(1)}, u32[]{:S(2)}, u32[]{:S(2)}) collective-permute-start(bf16[264,512]{1,0:T(8,128)(2,1)S(1)} %get-tuple-element.58), channel_id=1, source_target_pairs={{0,256},{8,264},{16,272},{24,280},{32,288},{40,296},{48,304},{56,3... | collective-permute-start | bytes 811016 | tf_op jit(solution)/shard_map/ppermute | solution.py:35
  53.6 13.9 %copy-start.5 = (f32[32,256]{1,0:T(8,128)S(1)}, f32[32,256]{1,0:T(8,128)}, u32[]{:S(2)}) copy-start(f32[32,256]{1,0:T(8,128)} %rotation_ref.3) | copy-start | bytes 98308
  81.3 27.1 %all-to-all-start.2 = ((bf16[8,32,896]{2,1,0:T(8,128)(2,1)}), bf16[8,32,896]{2,1,0:T(8,128)(2,1)S(1)}, u32[]{:S(2)}, u32[]{:S(2)}) async-start(bf16[8,32,896]{2,1,0:T(8,128)(2,1)} %get-tuple-element.33), calls=%async_computation.2 | async-start | bytes 917504 | tf_op jit(solution)/shard_map/all_to_all | solution.py:25
  88.1 9.9 %collective-permute-start.9 = (bf16[8,32,512]{2,1,0:T(8,128)(2,1)S(1)}, bf16[8,32,512]{2,1,0:T(8,128)(2,1)S(1)}, u32[]{:S(2)}, u32[]{:S(2)}) collective-permute-start(bf16[8,32,512]{2,1,0:T(8,128)(2,1)S(1)} %all_to_all.31.own0), channel_id=1, source_target_pairs={{0,384},{8,392},{16,400},{24,408},{32,416},{40,424},{48,432},{56,4... | collective-permute-start | bytes 786440 | tf_op jit(solution)/shard_map/ppermute | solution.py:35
  93.6 8.7 %collective-permute-start.8 = (bf16[8,32,512]{2,1,0:T(8,128)(2,1)S(1)}, bf16[8,32,512]{2,1,0:T(8,128)(2,1)S(1)}, u32[]{:S(2)}, u32[]{:S(2)}) collective-permute-start(bf16[8,32,512]{2,1,0:T(8,128)(2,1)S(1)} %all_to_all.31.own0), channel_id=1, source_target_pairs={{0,256},{8,264},{16,272},{24,280},{32,288},{40,296},{48,304},{56,3... | collective-permute-start | bytes 786440 | tf_op jit(solution)/shard_map/ppermute | solution.py:35
  95.5 12.8 %collective-permute-start.7 = (bf16[8,32,512]{2,1,0:T(8,128)(2,1)S(1)}, bf16[8,32,512]{2,1,0:T(8,128)(2,1)S(1)}, u32[]{:S(2)}, u32[]{:S(2)}) collective-permute-start(bf16[8,32,512]{2,1,0:T(8,128)(2,1)S(1)} %all_to_all.31.own0), channel_id=1, source_target_pairs={{0,128},{8,136},{16,144},{24,152},{32,160},{40,168},{48,176},{56,1... | collective-permute-start | bytes 786440 | tf_op jit(solution)/shard_map/ppermute | solution.py:35
  108.5 7.2 %collective-permute-start.10 = (bf16[4,8,32,512]{3,2,1,0:T(8,128)(2,1)S(1)}, bf16[4,8,32,512]{3,2,1,0:T(8,128)(2,1)S(1)}, u32[]{:S(2)}, u32[]{:S(2)}) collective-permute-start(bf16[4,8,32,512]{3,2,1,0:T(8,128)(2,1)S(1)} %pad_maximum_fusion), channel_id=1, source_target_pairs={{0,8},{8,0},{16,24},{24,16},{32,40},{40,32},{48,56},{56,48},{64,72... | collective-permute-start | bytes 3145736 | tf_op jit(solution)/shard_map/ppermute | solution.py:30
  118.0 1.3 copy-start.2
  130.1 14.6 %all-to-all-start.4 = ((bf16[8,32,256]{2,1,0:T(8,128)(2,1)}), bf16[8,32,256]{2,1,0:T(8,128)(2,1)S(1)}, u32[]{:S(2)}, u32[]{:S(2)}) async-start(bf16[8,32,256]{2,1,0:T(8,128)(2,1)} %get-tuple-element.42), calls=%async_computation.4 | async-start | bytes 262144 | tf_op jit(solution)/shard_map/all_to_all | solution.py:25
  136.8 36.5 %copy-start.1 = (bf16[256,2048]{1,0:T(8,128)(2,1)S(1)}, bf16[256,2048]{1,0:T(8,128)(2,1)}, u32[]{:S(2)}) copy-start(bf16[256,2048]{1,0:T(8,128)(2,1)} %coeffs_ref.3) | copy-start | bytes 3145732
  136.8 10.0 %collective-permute-start.13 = (bf16[8,32,256]{2,1,0:T(8,128)(2,1)S(1)}, bf16[8,32,256]{2,1,0:T(8,128)(2,1)S(1)}, u32[]{:S(2)}, u32[]{:S(2)}) collective-permute-start(bf16[8,32,256]{2,1,0:T(8,128)(2,1)S(1)} %all_to_all.32.own0), channel_id=1, source_target_pairs={{0,384},{8,392},{16,400},{24,408},{32,416},{40,424},{48,432},{56,4... | collective-permute-start | bytes 393224 | tf_op jit(solution)/shard_map/ppermute | solution.py:35
  139.1 7.7 %collective-permute-start.12 = (bf16[8,32,256]{2,1,0:T(8,128)(2,1)S(1)}, bf16[8,32,256]{2,1,0:T(8,128)(2,1)S(1)}, u32[]{:S(2)}, u32[]{:S(2)}) collective-permute-start(bf16[8,32,256]{2,1,0:T(8,128)(2,1)S(1)} %all_to_all.32.own0), channel_id=1, source_target_pairs={{0,256},{8,264},{16,272},{24,280},{32,288},{40,296},{48,304},{56,3... | collective-permute-start | bytes 393224 | tf_op jit(solution)/shard_map/ppermute | solution.py:35
  141.3 9.3 %collective-permute-start.11 = (bf16[8,32,256]{2,1,0:T(8,128)(2,1)S(1)}, bf16[8,32,256]{2,1,0:T(8,128)(2,1)S(1)}, u32[]{:S(2)}, u32[]{:S(2)}) collective-permute-start(bf16[8,32,256]{2,1,0:T(8,128)(2,1)S(1)} %all_to_all.32.own0), channel_id=1, source_target_pairs={{0,128},{8,136},{16,144},{24,152},{32,160},{40,168},{48,176},{56,1... | collective-permute-start | bytes 393224 | tf_op jit(solution)/shard_map/ppermute | solution.py:35
  144.7 1.6 copy-start.3
  150.7 22.5 %collective-permute-start.14 = (bf16[4,8,32,256]{3,2,1,0:T(8,128)(2,1)S(1)}, bf16[4,8,32,256]{3,2,1,0:T(8,128)(2,1)S(1)}, u32[]{:S(2)}, u32[]{:S(2)}) collective-permute-start(bf16[4,8,32,256]{3,2,1,0:T(8,128)(2,1)S(1)} %pad_maximum_fusion.2), channel_id=1, source_target_pairs={{0,8},{8,0},{16,24},{24,16},{32,40},{40,32},{48,56},{56,48},{64,72... | collective-permute-start | bytes 1572872 | tf_op jit(solution)/shard_map/ppermute | solution.py:30
  (2 other events, 1.9 us)

commit v8 on v7

--- a/solution.py
+++ b/solution.py
@@ -41,15 +41,15 @@
 
 vmem = pl.BlockSpec(memory_space=pltpu.VMEM)
 smem = pl.BlockSpec(memory_space=pltpu.SMEM)
-anywhere = pl.BlockSpec(memory_space=pl.ANY)
-
-
-def call(kernel, shapes, in_specs, scratch, *operands, bytes_accessed=2**20):
+hbm = pl.BlockSpec(memory_space=pltpu.HBM)
+
+
+def call(kernel, shapes, in_specs, scratch, *operands, out_specs=None, bytes_accessed=2**20):
     return pl.pallas_call(
         kernel,
         out_shape=[jax.ShapeDtypeStruct(*shape) for shape in shapes],
         in_specs=in_specs,
-        out_specs=[vmem] * len(shapes),
+        out_specs=out_specs or [vmem] * len(shapes),
         scratch_shapes=scratch,
         compiler_params=pltpu.CompilerParams(vmem_limit_bytes=12 * 2**20),
         cost_estimate=pl.CostEstimate(
@@ -69,13 +69,17 @@
     return jnp.concatenate(parts, axis=0)
 
 
-def mask_kernel(place_ref, size_ref, coeffs_ref, cols_ref, slice_ref, sem):
-    width = cols_ref.shape[1]
-    start = pl.multiple_of(place_ref[4] * width, width)
-    copy = pltpu.make_async_copy(coeffs_ref.at[:, pl.ds(start, width)], slice_ref, sem)
-    copy.start()
-    copy.wait()
-    cols_ref[...] = within_rows(size_ref, slice_ref[...].astype(f32)).astype(bf16)
+def turn_kernel(size, place_ref, coeffs_ref, own_ref, far_ref):
+    core = place_ref[1]
+    lanes = 128
+    for start in range(0, coeffs_ref.shape[1], lanes):
+        cells = coeffs_ref[:, start : start + lanes].astype(f32).T
+        for offset in range(0, lanes, CORES * size):
+            first = cells[offset : offset + size]
+            second = cells[offset + size : offset + 2 * size]
+            rows = pl.ds((start + offset) // CORES, size)
+            own_ref[rows, :] = jnp.where(core == 0, first, second).astype(bf16)
+            far_ref[rows, :] = jnp.where(core == 0, second, first).astype(bf16)
 
 
 def applied_kernel(size_ref, links_ref, up_ref, cols_ref, down_ref, ops_ref, out_ref, diag_ref):
@@ -99,6 +103,38 @@
         diag_ref[:, p * width : (p + 1) * width] = sums
 
 
+def product_kernel(
+    place_ref, own_ref, far_ref, applied_ref, far_applied_ref, up_ref, down_ref, own_diag_ref,
+    one_ref, three_ref, two_ref, none_ref, diag_ref,
+):
+    x, core = place_ref[0], place_ref[1]
+    rows, both = none_ref.shape
+    width = both // 2
+    near = up_ref.shape[0] - far_applied_ref.shape[0]
+    up = up_ref[near:, :].astype(f32)
+    cols = jnp.where(core == 0, down_ref[: far_applied_ref.shape[0], :].astype(f32), up)
+    sums = [
+        jnp.sum(
+            cols * far_applied_ref[:, p * width : (p + 1) * width].astype(f32),
+            axis=0,
+            keepdims=True,
+        )
+        for p in range(2)
+    ]
+    diag = own_diag_ref[...] + jnp.concatenate(sums, axis=1)
+    diag_ref[...] = diag
+    high = diag.astype(bf16).astype(f32)
+    fill = jnp.zeros((two_ref.shape[0] - rows - 2, both), f32)
+    tail = jnp.concatenate([high, diag - high, fill], axis=0).astype(bf16)
+    for steps, out_ref in ((2, two_ref), (1, one_ref), (3, three_ref), (0, none_ref)):
+        start = pl.multiple_of(lax.rem(x + steps, XS) * rows, rows)
+        total = small_product(own_ref[pl.ds(start, rows), :], applied_ref[...])
+        total = total + small_product(far_ref[pl.ds(start, rows), :], far_applied_ref[...])
+        out_ref[:rows, :] = total.astype(out_ref.dtype)
+        if steps:
+            out_ref[rows:, :] = tail
+
+
 def sum_kernel(got_ref, rotation_ref, block_ref, z_ref, packed_ref):
     count, _, wide = z_ref.shape
     total = got_ref[0].astype(f32)
@@ -117,17 +153,30 @@
         packed_ref[i] = packed
 
 
-def gathered(place_ref, own_refs, away_ref, out_ref, sems):
+def gathered(place_ref, own_ref, away_ref, out_ref, sems):
     x, core = place_ref[0], place_ref[1]
     copies = []
-    for steps in range(XS):
-        source = lax.rem(x + XS - steps, XS)
-        copies.append((own_refs[steps], out_ref.at[source, :, core]))
-        copies.append((away_ref.at[steps], out_ref.at[source, :, 1 - core]))
-    copies = [pltpu.make_async_copy(*pair, sems.at[i]) for i, pair in enumerate(copies)]
-    for copy in copies:
-        copy.start()
+    for source in range(XS):
+        steps = lax.rem(x + XS - source, XS)
+        pairs = ((own_ref, core), (away_ref, 1 - core))
+        copies.append(
+            [
+                pltpu.make_async_copy(
+                    ref.at[steps], out_ref.at[source, :, which], sems.at[source, i]
+                )
+                for i, (ref, which) in enumerate(pairs)
+            ]
+        )
+    for pair in copies:
+        for copy in pair:
+            copy.start()
     return copies
+
+
+def landed(copies, k):
+    if k * XS % COLS == 0:
+        for copy in copies[k * XS // COLS]:
+            copy.wait()
 
 
 def chunk(panel_ref, k):
@@ -162,17 +211,21 @@
 
 
 def square_kernel(
-    scale, place_ref, rows_ref, diag_ref, turned_ref, own0, own1, own2, own3, away_ref,
-    z_ref, square_ref, step_ref, sems,
+    scale, place_ref, rows_ref, diag_ref, turned_ref, own_ref, away_ref,
+    kept_ref, square_ref, step_ref, z_ref, sems, kept_sems,
 ):
-    copies = gathered(place_ref, (own0, own1, own2, own3), away_ref, z_ref, sems)
+    copies = gathered(place_ref, own_ref, away_ref, z_ref, sems)
+    kept = [
+        pltpu.make_async_copy(z_ref.at[x], kept_ref.at[x], kept_sems.at[x]) for x in range(XS)
+    ]
     col = place_ref[4]
     rows, width = rows_ref.shape[1:]
     across_diag = [diag_ref[p, pl.ds(col, 1), :] for p in range(2)]
-    for copy in copies:
-        copy.wait()
     square = jnp.zeros((rows, width), f32)
     for k in range(COLS):
+        landed(copies, k)
+        if k * XS % COLS == 0:
+            kept[k * XS // COLS].start()
         cells = chunk(z_ref, k).astype(f32)
         cos_part = cells[:, :width] * (across_diag[0] - turned_ref[0, :, k : k + 1])
         sin_part = cells[:, width:] * (across_diag[1] - turned_ref[1, :, k : k + 1])
@@ -183,11 +236,17 @@
     for k in range(COLS):
         square_ref[k] = square
         step_ref[k] = step
-
-
-def half_kernel(square_ref, rows_ref, z_ref, block_ref, half_ref, sent_ref):
+    for copy in kept:
+        copy.wait()
+
+
+def half_kernel(square_ref, rows_ref, kept_ref, block_ref, half_ref, sent_ref, z_ref, sems):
+    copies = [[pltpu.make_async_copy(kept_ref.at[x], z_ref.at[x], sems.at[x])] for x in range(XS)]
+    for copy, in copies:
+        copy.start()
     total = block_ref[...]
     for k in range(COLS):
+        landed(copies, k)
         back = (0.5 * square_ref[k].astype(f32) - rows_ref[k]).astype(bf16)
         total = total + small_product(back, chunk(z_ref, k))
     half_ref[...] = total
@@ -198,19 +257,18 @@
 
 def final_kernel(
     place_ref, size_ref, half_ref, across_ref, coeffs_ref, rotation_ref, block_ref,
-    own0, own1, own2, own3, away_ref,
+    own_ref, away_ref,
     rotated_ref, cos_ref, sin_ref, orbitals_ref, step_ref, sems,
 ):
-    copies = gathered(place_ref, (own0, own1, own2, own3), away_ref, step_ref, sems)
+    copies = gathered(place_ref, own_ref, away_ref, step_ref, sems)
     col = place_ref[4]
     width = rotated_ref.shape[1]
     rotated = rotation_ref[...]
     cos_part, sin_part = block_ref[:, :width], block_ref[:, width:]
     start = pl.multiple_of(col * width, width)
     orbitals = coeffs_ref[:, pl.ds(start, width)].astype(f32)
-    for copy in copies:
-        copy.wait()
-    for k in range(COLS):
+    for k in range(COLS):
+        landed(copies, k)
         step = chunk(step_ref, k)
         cells = half_ref[k]
         cos_part = cos_part + small_product(cells[:, :width], step)
@@ -241,27 +299,28 @@
     place = jnp.stack(place + [lax.axis_index("cols")]).astype(jnp.int32)
     scale_factor = 0.125 / math.sqrt(orbital_count)
 
-    (own_cols,) = call(
-        mask_kernel,
-        [((rows_dev, col_count), bf16)],
-        [smem] * 2 + [anywhere],
-        [pltpu.VMEM((rows_dev, col_count), bf16), pltpu.SemaphoreType.DMA],
-        place,
-        atom_size,
-        coeffs,
-    )
+    within = lax.broadcasted_iota(jnp.int32, (rows_dev // block_size, block_size), 1)
+    live_rows = (within < atom_size[:, None]).reshape(rows_dev)
+    own_cols = lax.dynamic_slice_in_dim(coeffs, lax.axis_index("cols") * col_count, col_count, 1)
+    own_cols = jnp.where(live_rows[:, None], own_cols, jnp.zeros_like(own_cols))
     width = reach_blocks * block_size
     up = [(i, (i + 1) % rows_axis) for i in range(rows_axis)]
     down = [((i + 1) % rows_axis, i) for i in range(rows_axis)]
     from_up = lax.ppermute(own_cols[rows_dev - width :], "rows", up)
     from_down = lax.ppermute(own_cols[:width], "rows", down)
-    turned = coeffs.T.reshape(XS, ZS, CORES, row_count, rows_dev)
-
-    def turned_half(which):
-        return lax.dynamic_index_in_dim(turned, which, 2, keepdims=False).reshape(-1, rows_dev)
-
-    own_turned = turned_half(core)
-    far_turned = other_core(turned_half(1 - core))
+    turn_coeffs, own_cols = lax.optimization_barrier((coeffs, own_cols))
+    half_shape = ((orbital_count // CORES, rows_dev), bf16)
+    own_turned, far_turned = call(
+        functools.partial(turn_kernel, row_count),
+        [half_shape] * 2,
+        [smem, vmem],
+        [],
+        place,
+        turn_coeffs,
+        bytes_accessed=2**26,
+    )
+    from_up, from_down, far_turned = lax.optimization_barrier((from_up, from_down, far_turned))
+    far_turned = other_core(far_turned)
     applied, own_diag = call(
         applied_kernel,
         [((rows_dev, both), bf16), ((1, both), f32)],
@@ -273,33 +332,30 @@
         own_cols,
         from_down,
         phase_ops,
+        bytes_accessed=2**22,
     )
     far_applied = other_core(applied)
 
-    far_cols = jnp.where(core == 0, from_down[:rows_dev], from_up[-rows_dev:]).astype(f32)
-    far_diag = jnp.tile(far_cols, (1, 2)) * far_applied.astype(f32)
-    diag = own_diag[0] + jnp.sum(far_diag, axis=0)
-
-    def with_diag(cells, values):
-        high = lax.reduce_precision(values, 8, 7)
-        tail = jnp.stack([high, values - high]).astype(bf16)
-        tail = jnp.pad(tail, ((0, 6), (0, 0)))
-        tail = jnp.broadcast_to(tail, cells.shape[:-2] + tail.shape)
-        return jnp.concatenate([cells.astype(bf16), tail], axis=-2)
-
-    def summed(cells):
-        body, tail = cells[:, :-8].astype(f32), cells[:, -8:-6].astype(f32)
-        return jnp.sum(body, axis=0), jnp.sum(tail, axis=(0, 1))
-
-    def product(steps):
-        start = ((own_x + steps) % XS) * (ZS * row_count)
-        own_part = lax.dynamic_slice_in_dim(own_turned, start, ZS * row_count, 0)
-        far_part = lax.dynamic_slice_in_dim(far_turned, start, ZS * row_count, 0)
-        return small_product(own_part, applied) + small_product(far_part, far_applied)
-
-    got = [along_x(with_diag(product(steps), diag), steps) for steps in (1, 3, 2)]
-    chip, diag_rest = summed(jnp.stack(got))
-    chip, diag = chip + product(0), diag + diag_rest
+    plane = ZS * row_count
+    sent = ((plane + 16, both), bf16)
+    one, three, two, chip, diag = call(
+        product_kernel,
+        [sent, sent, sent, ((plane, both), f32), ((1, both), f32)],
+        [smem] + [vmem] * 7,
+        [],
+        place,
+        own_turned,
+        far_turned,
+        applied,
+        far_applied,
+        from_up,
+        from_down,
+        own_diag,
+    )
+    got = [along_x(two, 2), along_x(one, 1), along_x(three, 3)]
+    got = [cells.astype(f32) for cells in got]
+    chip = chip + sum(cells[:plane] for cells in got)
+    diag = diag[0] + sum(cells[plane] + cells[plane + 1] for cells in got)
     high = lax.reduce_precision(diag, 8, 7)
     terms = jnp.stack([high, diag - high]).astype(bf16).reshape(-1, 128)
     terms = jnp.pad(terms, ((0, row_count - terms.shape[0]), (0, 0)))
@@ -346,14 +402,19 @@
             ((COLS,) + block, bf16),
             ((ZS,) + block, bf16),
         ],
-        [smem] + [vmem] * 3 + [anywhere] * (XS + 1),
-        [pltpu.SemaphoreType.DMA((2 * XS,))],
+        [smem] + [vmem] * 3 + [hbm] * 2,
+        [
+            pltpu.VMEM((XS, ZS, CORES, row_count, both), bf16),
+            pltpu.SemaphoreType.DMA((XS, 2)),
+            pltpu.SemaphoreType.DMA((XS,)),
+        ],
         place,
         gen_rows,
         diag_all,
         turned_diag,
-        *panels,
+        stacked,
         away,
+        out_specs=[hbm, vmem, vmem],
     )
 
     step = swap(step, "rows", z_groups)
@@ -363,8 +424,11 @@
     half_block, half_sent = call(
         half_kernel,
         [((row_count, both), f32), ((COLS, row_count, both), bf16)],
-        [vmem] * 4,
-        [],
+        [vmem] * 2 + [hbm, vmem],
+        [
+            pltpu.VMEM((XS, ZS, CORES, row_count, both), bf16),
+            pltpu.SemaphoreType.DMA((XS,)),
+        ],
         square,
         gen_rows,
         z_cols,
@@ -372,16 +436,17 @@
         bytes_accessed=2**26,
     )
     *steps_x, half_sent = lax.optimization_barrier((*steps_x, half_sent))
-    step_away = other_core(jnp.stack(steps_x))
+    step_stack = jnp.stack(steps_x)
+    step_away = other_core(step_stack)
     half_rows = swap(half_sent, "cols")
     return tuple(
         call(
             final_kernel,
             [(block, f32)] * 3 + [((rows_dev, col_count), bf16)],
-            [smem] * 2 + [vmem] * 5 + [anywhere] * (XS + 1),
+            [smem] * 2 + [vmem] * 5 + [hbm] * 2,
             [
                 pltpu.VMEM((XS, ZS, CORES, row_count, col_count), bf16),
-                pltpu.SemaphoreType.DMA((2 * XS,)),
+                pltpu.SemaphoreType.DMA((XS, 2)),
             ],
             place,
             atom_size,
@@ -390,7 +455,7 @@
             coeffs,
             rotation,
             half_block,
-            *steps_x,
+            step_stack,
             step_away,
         )
     )

time: 177 us -> 177 us (level)
  Pallas kernels: 8.52 us -> 11 us
  waiting for transfers between devices: 31 us -> 29.2 us
  matrix products: 1.79 us -> 0 us
    pallas_call x7 -> x8, Pallas kernels: 8.52 us -> 11 us  [call(): pl.pallas_call(kernel, out_shape=[jax.ShapeDtypeStruct(*shape) for shape...]
    ppermute x9, starting transfers between devices: 25.6 us -> 23.5 us  [along_x(): lax.ppermute(cells, 'rows', [(i, (i + steps * line) % count) for i in ran...]
    dot_general x8 -> x0, matrix products: 1.79 us -> none  [small_product(): return jnp.dot(left, right, preferred_element_type=f32)]
    unnamed x20 -> x18, local copies, waits for them, and re-layouts: 6.35 us -> 6.58 us
  transfers between devices with their start and end apart: 17 -> 17, of which waited for: 9 -> 10; matrix products, arithmetic and copies ran while one was open for 1% -> 0% of each run, Pallas kernels for 1% -> 2%
where the time goes in v8:
time: 177 us; the launch traced here: 176 us
  starting transfers between devices  67.9 us (38%)
  blocking collectives  57.6 us (33%)
  waiting for transfers between devices  29.2 us (16%)
  Pallas kernels  11 us (6%)
  local copies, waits for them, and re-layouts  6.7 us (4%)
  other arithmetic  2.39 us (1%)
    all_to_all x4, blocking collectives, swap(): lax.all_to_all(cells, axis, 0, 0, tiled=True, axis_index_groups=groups)  57.6 us
    ppermute x9, starting transfers between devices, along_x(): lax.ppermute(cells, 'rows', [(i, (i + steps * line) % count) for i in ran...  23.5 us
    ppermute x9, waiting for transfers between devices, along_x(): lax.ppermute(cells, 'rows', [(i, (i + steps * line) % count) for i in ran...  22.3 us
    ppermute x4, starting transfers between devices, other_core(): return lax.ppermute(cells, 'rows', [(i, i ^ 1) for i in range(count)])  20.1 us
    all_to_all x2, starting transfers between devices, swap(): lax.all_to_all(cells, axis, 0, 0, tiled=True, axis_index_groups=groups)  13.6 us
    pallas_call x8, Pallas kernels, call(): pl.pallas_call(kernel, out_shape=[jax.ShapeDtypeStruct(*shape) for shape...  11 us
    ppermute x1, starting transfers between devices, on_device(): from_down = lax.ppermute(own_cols[:width], 'rows', down)  8.79 us
    unnamed x18, local copies, waits for them, and re-layouts  6.58 us
  transfers between devices with their start and end apart: 17, of which 10 were waited for; matrix products, arithmetic and copies ran while one was open for 0% of the time, Pallas kernels for 2%

profile of v8, /device:TPU:1, one launch (start us, length us, event | category | flops | bytes accessed | tf_op | source)
XLA Modules:
  0.0 175.9 jit_solution(9423874783908111151)
XLA Ops:
  2.4 8.8 %collective-permute-start.1 = (bf16[256,256]{1,0:T(8,128)(2,1)S(1)}, bf16[256,256]{1,0:T(8,128)(2,1)S(1)}, u32[]{:S(2)}, u32[]{:S(2)}) collective-permute-start(bf16[256,256]{1,0:T(8,128)(2,1)S(1)} %dynamic-slice_select_fusion.cols_ref), channel_id=1, source_target_pairs={{8,0},{16,8},{24,16},{32,24},{40,32},{48,40},{56,48},{64,56},{72,6... | collective-permute-start | bytes 393224 | tf_op jit(solution)/shard_map/ppermute | solution.py:310
  15.4 3.9 %collective-permute-done.up_ref = bf16[256,256]{1,0:T(8,128)(2,1)S(1)} collective-permute-done((bf16[256,256]{1,0:T(8,128)(2,1)S(1)}, bf16[256,256]{1,0:T(8,128)(2,1)S(1)}, u32[]{:S(2)}, u32[]{:S(2)}) %collective-permute-start) | collective-permute-done | bytes 131104 | tf_op jit(solution)/shard_map/ppermute | solution.py:309
  19.2 8.8 %collective-permute-start.2 = (bf16[1024,256]{1,0:T(8,128)(2,1)S(1)}, bf16[1024,256]{1,0:T(8,128)(2,1)S(1)}, u32[]{:S(2)}, u32[]{:S(2)}) collective-permute-start(bf16[1024,256]{1,0:T(8,128)(2,1)S(1)} %get-tuple-element.43), channel_id=1, source_target_pairs={{0,8},{8,0},{16,24},{24,16},{32,40},{40,32},{48,56},{56,48},{64,72... | collective-permute-start | bytes 1572872 | tf_op jit(solution)/shard_map/ppermute | solution.py:30
  36.1 1.9 %collective-permute-start.4 = (bf16[272,512]{1,0:T(8,128)(2,1)S(1)}, bf16[272,512]{1,0:T(8,128)(2,1)S(1)}, u32[]{:S(2)}, u32[]{:S(2)}) collective-permute-start(bf16[272,512]{1,0:T(8,128)(2,1)S(1)} %get-tuple-element.50), channel_id=1, source_target_pairs={{0,256},{8,264},{16,272},{24,280},{32,288},{40,296},{48,304},{56,3... | collective-permute-start | bytes 835592 | tf_op jit(solution)/shard_map/ppermute | solution.py:35
  38.1 1.9 %collective-permute-start.5 = (bf16[272,512]{1,0:T(8,128)(2,1)S(1)}, bf16[272,512]{1,0:T(8,128)(2,1)S(1)}, u32[]{:S(2)}, u32[]{:S(2)}) collective-permute-start(bf16[272,512]{1,0:T(8,128)(2,1)S(1)} %get-tuple-element.51), channel_id=1, source_target_pairs={{0,128},{8,136},{16,144},{24,152},{32,160},{40,168},{48,176},{56,1... | collective-permute-start | bytes 835592 | tf_op jit(solution)/shard_map/ppermute | solution.py:35
  40.0 4.6 %collective-permute-start.6 = (bf16[272,512]{1,0:T(8,128)(2,1)S(1)}, bf16[272,512]{1,0:T(8,128)(2,1)S(1)}, u32[]{:S(2)}, u32[]{:S(2)}) collective-permute-start(bf16[272,512]{1,0:T(8,128)(2,1)S(1)} %get-tuple-element.52), channel_id=1, source_target_pairs={{0,384},{8,392},{16,400},{24,408},{32,416},{40,424},{48,432},{56,4... | collective-permute-start | bytes 835592 | tf_op jit(solution)/shard_map/ppermute | solution.py:35
  44.6 3.1 %collective-permute-done.4 = bf16[272,512]{1,0:T(8,128)(2,1)S(1)} collective-permute-done((bf16[272,512]{1,0:T(8,128)(2,1)S(1)}, bf16[272,512]{1,0:T(8,128)(2,1)S(1)}, u32[]{:S(2)}, u32[]{:S(2)}) %collective-permute-start.4) | collective-permute-done | bytes 278560 | tf_op jit(solution)/shard_map/ppermute | solution.py:35
  47.8 6.4 %collective-permute-done.5 = bf16[272,512]{1,0:T(8,128)(2,1)S(1)} collective-permute-done((bf16[272,512]{1,0:T(8,128)(2,1)S(1)}, bf16[272,512]{1,0:T(8,128)(2,1)S(1)}, u32[]{:S(2)}, u32[]{:S(2)}) %collective-permute-start.5) | collective-permute-done | bytes 278560 | tf_op jit(solution)/shard_map/ppermute | solution.py:35
  54.6 15.5 %all_to_all.30.got_ref = bf16[8,32,640]{2,1,0:T(8,128)(2,1)S(1)} all-to-all(bf16[8,32,640]{2,1,0:T(8,128)(2,1)S(1)} %pad_maximum_fusion.2), channel_id=1, replica_groups={{0,16,32,48,64,80,96,112},{8,24,40,56,72,88,104,120},{128,144,160,176,1..., dimensions={0} | all-to-all | bytes 655360 | tf_op jit(solution)/shard_map/all_to_all | solution.py:25
  71.0 12.6 %all_to_all.31 = bf16[8,32,512]{2,1,0:T(8,128)(2,1)S(1)} all-to-all(bf16[8,32,512]{2,1,0:T(8,128)(2,1)S(1)} %get-tuple-element.55), channel_id=1, replica_groups={{0,16,32,48,64,80,96,112},{8,24,40,56,72,88,104,120},{128,144,160,176,1..., dimensions={0} | all-to-all | bytes 524288 | tf_op jit(solution)/shard_map/all_to_all | solution.py:25
  83.6 6.8 %all-to-all-start.2 = ((bf16[8,32,896]{2,1,0:T(8,128)(2,1)}), bf16[8,32,896]{2,1,0:T(8,128)(2,1)S(1)}, u32[]{:S(2)}, u32[]{:S(2)}) async-start(bf16[8,32,896]{2,1,0:T(8,128)(2,1)} %get-tuple-element.57), calls=%async_computation.2 | async-start | bytes 917504 | tf_op jit(solution)/shard_map/all_to_all | solution.py:25
  94.2 3.4 %collective-permute-start.7 = (bf16[8,32,512]{2,1,0:T(8,128)(2,1)S(1)}, bf16[8,32,512]{2,1,0:T(8,128)(2,1)S(1)}, u32[]{:S(2)}, u32[]{:S(2)}) collective-permute-start(bf16[8,32,512]{2,1,0:T(8,128)(2,1)S(1)} %all_to_all.31), channel_id=1, source_target_pairs={{0,128},{8,136},{16,144},{24,152},{32,160},{40,168},{48,176},{56,1... | collective-permute-start | bytes 786440 | tf_op jit(solution)/shard_map/ppermute | solution.py:35
  97.6 3.3 %collective-permute-done.8 = bf16[8,32,512]{2,1,0:T(8,128)(2,1)S(1)} collective-permute-done((bf16[8,32,512]{2,1,0:T(8,128)(2,1)S(1)}, bf16[8,32,512]{2,1,0:T(8,128)(2,1)S(1)}, u32[]{:S(2)}, u32[]{:S(2)}) %collective-permute-start.8) | collective-permute-done | bytes 262176 | tf_op jit(solution)/shard_map/ppermute | solution.py:35
  100.9 6.8 %collective-permute-done.7 = bf16[8,32,512]{2,1,0:T(8,128)(2,1)S(1)} collective-permute-done((bf16[8,32,512]{2,1,0:T(8,128)(2,1)S(1)}, bf16[8,32,512]{2,1,0:T(8,128)(2,1)S(1)}, u32[]{:S(2)}, u32[]{:S(2)}) %collective-permute-start.7) | collective-permute-done | bytes 262176 | tf_op jit(solution)/shard_map/ppermute | solution.py:35
  107.9 4.2 %collective-permute-start.10 = (bf16[4,8,32,512]{3,2,1,0:T(8,128)(2,1)S(1)}, bf16[4,8,32,512]{3,2,1,0:T(8,128)(2,1)S(1)}, u32[]{:S(2)}, u32[]{:S(2)}) collective-permute-start(bf16[4,8,32,512]{3,2,1,0:T(8,128)(2,1)S(1)} %pad_maximum_fusion.own_ref), channel_id=1, source_target_pairs={{0,8},{8,0},{16,24},{24,16},{32,40},{40,32},{48,56},{56,48},{64,72... | collective-permute-start | bytes 3145736 | tf_op jit(solution)/shard_map/ppermute | solution.py:30
  114.4 2.8 %shard_map.89 = (bf16[4,8,2,32,512]{4,3,2,1,0:T(8,128)(2,1)S(1)}, bf16[8,32,256]{2,1,0:T(8,128)(2,1)}, bf16[8,32,256]{2,1,0:T(8,128)(2,1)S(1)}) custom-call(s32[5]{0:T(128)S(1)} %stack.59.place_ref, f32[8,32,256]{2,1,0:T(8,128)S(1)} %get-tuple-element.59.rows_ref, f32[2,8,256]{2,1,0:T(8,128)S(1)} %get-tuple-element.60.diag_ref, ...), custom_call_target="tpu_custom_call" | custom-call | bytes 1048576 | tf_op jit(solution)/shard_map/pallas_call | solution.py:48
  118.6 10.5 %all_to_all.32 = bf16[8,32,256]{2,1,0:T(8,128)(2,1)S(1)} all-to-all(bf16[8,32,256]{2,1,0:T(8,128)(2,1)S(1)} %get-tuple-element.64), channel_id=1, replica_groups={{0,16,32,48,64,80,96,112},{8,24,40,56,72,88,104,120},{128,144,160,176,1..., dimensions={0} | all-to-all | bytes 262144 | tf_op jit(solution)/shard_map/all_to_all | solution.py:25
  129.0 6.8 %all-to-all-start.4 = ((bf16[8,32,256]{2,1,0:T(8,128)(2,1)}), bf16[8,32,256]{2,1,0:T(8,128)(2,1)S(1)}, u32[]{:S(2)}, u32[]{:S(2)}) async-start(bf16[8,32,256]{2,1,0:T(8,128)(2,1)} %get-tuple-element.66), calls=%async_computation.4 | async-start | bytes 262144 | tf_op jit(solution)/shard_map/all_to_all | solution.py:25
  135.8 3.5 %collective-permute-start.13 = (bf16[8,32,256]{2,1,0:T(8,128)(2,1)S(1)}, bf16[8,32,256]{2,1,0:T(8,128)(2,1)S(1)}, u32[]{:S(2)}, u32[]{:S(2)}) collective-permute-start(bf16[8,32,256]{2,1,0:T(8,128)(2,1)S(1)} %all_to_all.32), channel_id=1, source_target_pairs={{0,384},{8,392},{16,400},{24,408},{32,416},{40,424},{48,432},{56,4... | collective-permute-start | bytes 393224 | tf_op jit(solution)/shard_map/ppermute | solution.py:35
  141.2 2.5 %collective-permute-start.11 = (bf16[8,32,256]{2,1,0:T(8,128)(2,1)S(1)}, bf16[8,32,256]{2,1,0:T(8,128)(2,1)S(1)}, u32[]{:S(2)}, u32[]{:S(2)}) collective-permute-start(bf16[8,32,256]{2,1,0:T(8,128)(2,1)S(1)} %all_to_all.32), channel_id=1, source_target_pairs={{0,128},{8,136},{16,144},{24,152},{32,160},{40,168},{48,176},{56,1... | collective-permute-start | bytes 393224 | tf_op jit(solution)/shard_map/ppermute | solution.py:35
  146.8 2.0 %collective-permute-done.11 = bf16[8,32,256]{2,1,0:T(8,128)(2,1)S(1)} collective-permute-done((bf16[8,32,256]{2,1,0:T(8,128)(2,1)S(1)}, bf16[8,32,256]{2,1,0:T(8,128)(2,1)S(1)}, u32[]{:S(2)}, u32[]{:S(2)}) %collective-permute-start.11) | collective-permute-done | bytes 131104 | tf_op jit(solution)/shard_map/ppermute | solution.py:35
  148.9 5.2 %collective-permute-start.14 = (bf16[4,8,32,256]{3,2,1,0:T(8,128)(2,1)S(1)}, bf16[4,8,32,256]{3,2,1,0:T(8,128)(2,1)S(1)}, u32[]{:S(2)}, u32[]{:S(2)}) collective-permute-start(bf16[4,8,32,256]{3,2,1,0:T(8,128)(2,1)S(1)} %pad_maximum_fusion.1.own_ref), channel_id=1, source_target_pairs={{0,8},{8,0},{16,24},{24,16},{32,40},{40,32},{48,56},{56,48},{64,72... | collective-permute-start | bytes 1572872 | tf_op jit(solution)/shard_map/ppermute | solution.py:30
  154.2 19.0 %all_to_all.33.half_ref = bf16[8,32,512]{2,1,0:T(8,128)(2,1)S(1)} all-to-all(bf16[8,32,512]{2,1,0:T(8,128)(2,1)S(1)} %get-tuple-element.70), channel_id=1, replica_groups=mesh['rows'=64,'cols'=8] {'cols'}, dimensions={0} | all-to-all | bytes 524288 | tf_op jit(solution)/shard_map/all_to_all | solution.py:25
  173.2 2.6 %shard_map.91 = (f32[32,256]{1,0:T(8,128)}, f32[32,256]{1,0:T(8,128)}, f32[32,256]{1,0:T(8,128)}, bf16[256,256]{1,0:T(8,128)(2,1)}) custom-call(s32[5]{0:T(128)S(1)} %stack.59.place_ref, s32[2]{0:T(128)S(1)} %copy-done.7, bf16[8,32,512]{2,1,0:T(8,128)(2,1)S(1)} %all_to_all.33.half_ref, bf16[8,32,896]{2,1,0:T(8,128)(2,1)S(1)} %all-to-all-done.2.across_ref, ...), custom_call_target="tpu_custom_call" | custom-call | bytes 1048576 | tf_op jit(solution)/shard_map/pallas_call | solution.py:48
  (56 shorter events, 28.0 us)
Async XLA Ops:
  2.4 13.0 %collective-permute-start.1 = (bf16[256,256]{1,0:T(8,128)(2,1)S(1)}, bf16[256,256]{1,0:T(8,128)(2,1)S(1)}, u32[]{:S(2)}, u32[]{:S(2)}) collective-permute-start(bf16[256,256]{1,0:T(8,128)(2,1)S(1)} %dynamic-slice_select_fusion.cols_ref), channel_id=1, source_target_pairs={{8,0},{16,8},{24,16},{32,24},{40,32},{48,40},{56,48},{64,56},{72,6... | collective-permute-start | bytes 393224 | tf_op jit(solution)/shard_map/ppermute | solution.py:310
  11.2 8.0 %collective-permute-start = (bf16[256,256]{1,0:T(8,128)(2,1)S(1)}, bf16[256,256]{1,0:T(8,128)(2,1)S(1)}, u32[]{:S(2)}, u32[]{:S(2)}) collective-permute-start(bf16[256,256]{1,0:T(8,128)(2,1)S(1)} %dynamic-slice_select_fusion.cols_ref), channel_id=1, source_target_pairs={{0,8},{8,16},{16,24},{24,32},{32,40},{40,48},{48,56},{56,64},{64,7... | collective-permute-start | bytes 393224 | tf_op jit(solution)/shard_map/ppermute | solution.py:309
  13.2 1.2 copy-start
  19.2 15.6 %collective-permute-start.2 = (bf16[1024,256]{1,0:T(8,128)(2,1)S(1)}, bf16[1024,256]{1,0:T(8,128)(2,1)S(1)}, u32[]{:S(2)}, u32[]{:S(2)}) collective-permute-start(bf16[1024,256]{1,0:T(8,128)(2,1)S(1)} %get-tuple-element.43), channel_id=1, source_target_pairs={{0,8},{8,0},{16,24},{24,16},{32,40},{40,32},{48,56},{56,48},{64,72... | collective-permute-start | bytes 1572872 | tf_op jit(solution)/shard_map/ppermute | solution.py:30
  28.0 1.1 copy-start.4
  31.4 3.4 %collective-permute-start.3 = (bf16[256,512]{1,0:T(8,128)(2,1)S(1)}, bf16[256,512]{1,0:T(8,128)(2,1)S(1)}, u32[]{:S(2)}, u32[]{:S(2)}) collective-permute-start(bf16[256,512]{1,0:T(8,128)(2,1)S(1)} %get-tuple-element.47.applied_ref), channel_id=1, source_target_pairs={{0,8},{8,0},{16,24},{24,16},{32,40},{40,32},{48,56},{56,48},{64,72... | collective-permute-start | bytes 786440 | tf_op jit(solution)/shard_map/ppermute | solution.py:30
  36.1 11.6 %collective-permute-start.4 = (bf16[272,512]{1,0:T(8,128)(2,1)S(1)}, bf16[272,512]{1,0:T(8,128)(2,1)S(1)}, u32[]{:S(2)}, u32[]{:S(2)}) collective-permute-start(bf16[272,512]{1,0:T(8,128)(2,1)S(1)} %get-tuple-element.50), channel_id=1, source_target_pairs={{0,256},{8,264},{16,272},{24,280},{32,288},{40,296},{48,304},{56,3... | collective-permute-start | bytes 835592 | tf_op jit(solution)/shard_map/ppermute | solution.py:35
  38.1 16.1 %collective-permute-start.5 = (bf16[272,512]{1,0:T(8,128)(2,1)S(1)}, bf16[272,512]{1,0:T(8,128)(2,1)S(1)}, u32[]{:S(2)}, u32[]{:S(2)}) collective-permute-start(bf16[272,512]{1,0:T(8,128)(2,1)S(1)} %get-tuple-element.51), channel_id=1, source_target_pairs={{0,128},{8,136},{16,144},{24,152},{32,160},{40,168},{48,176},{56,1... | collective-permute-start | bytes 835592 | tf_op jit(solution)/shard_map/ppermute | solution.py:35
  40.0 14.2 %collective-permute-start.6 = (bf16[272,512]{1,0:T(8,128)(2,1)S(1)}, bf16[272,512]{1,0:T(8,128)(2,1)S(1)}, u32[]{:S(2)}, u32[]{:S(2)}) collective-permute-start(bf16[272,512]{1,0:T(8,128)(2,1)S(1)} %get-tuple-element.52), channel_id=1, source_target_pairs={{0,384},{8,392},{16,400},{24,408},{32,416},{40,424},{48,432},{56,4... | collective-permute-start | bytes 835592 | tf_op jit(solution)/shard_map/ppermute | solution.py:35
  54.2 15.9 %copy-start.5 = (f32[32,256]{1,0:T(8,128)S(1)}, f32[32,256]{1,0:T(8,128)}, u32[]{:S(2)}) copy-start(f32[32,256]{1,0:T(8,128)} %rotation_ref.3) | copy-start | bytes 98308
  83.6 24.3 %all-to-all-start.2 = ((bf16[8,32,896]{2,1,0:T(8,128)(2,1)}), bf16[8,32,896]{2,1,0:T(8,128)(2,1)S(1)}, u32[]{:S(2)}, u32[]{:S(2)}) async-start(bf16[8,32,896]{2,1,0:T(8,128)(2,1)} %get-tuple-element.57), calls=%async_computation.2 | async-start | bytes 917504 | tf_op jit(solution)/shard_map/all_to_all | solution.py:25
  90.4 7.2 %collective-permute-start.9 = (bf16[8,32,512]{2,1,0:T(8,128)(2,1)S(1)}, bf16[8,32,512]{2,1,0:T(8,128)(2,1)S(1)}, u32[]{:S(2)}, u32[]{:S(2)}) collective-permute-start(bf16[8,32,512]{2,1,0:T(8,128)(2,1)S(1)} %all_to_all.31), channel_id=1, source_target_pairs={{0,384},{8,392},{16,400},{24,408},{32,416},{40,424},{48,432},{56,4... | collective-permute-start | bytes 786440 | tf_op jit(solution)/shard_map/ppermute | solution.py:35
  92.3 8.6 %collective-permute-start.8 = (bf16[8,32,512]{2,1,0:T(8,128)(2,1)S(1)}, bf16[8,32,512]{2,1,0:T(8,128)(2,1)S(1)}, u32[]{:S(2)}, u32[]{:S(2)}) collective-permute-start(bf16[8,32,512]{2,1,0:T(8,128)(2,1)S(1)} %all_to_all.31), channel_id=1, source_target_pairs={{0,256},{8,264},{16,272},{24,280},{32,288},{40,296},{48,304},{56,3... | collective-permute-start | bytes 786440 | tf_op jit(solution)/shard_map/ppermute | solution.py:35
  94.2 13.5 %collective-permute-start.7 = (bf16[8,32,512]{2,1,0:T(8,128)(2,1)S(1)}, bf16[8,32,512]{2,1,0:T(8,128)(2,1)S(1)}, u32[]{:S(2)}, u32[]{:S(2)}) collective-permute-start(bf16[8,32,512]{2,1,0:T(8,128)(2,1)S(1)} %all_to_all.31), channel_id=1, source_target_pairs={{0,128},{8,136},{16,144},{24,152},{32,160},{40,168},{48,176},{56,1... | collective-permute-start | bytes 786440 | tf_op jit(solution)/shard_map/ppermute | solution.py:35
  107.9 6.5 %collective-permute-start.10 = (bf16[4,8,32,512]{3,2,1,0:T(8,128)(2,1)S(1)}, bf16[4,8,32,512]{3,2,1,0:T(8,128)(2,1)S(1)}, u32[]{:S(2)}, u32[]{:S(2)}) collective-permute-start(bf16[4,8,32,512]{3,2,1,0:T(8,128)(2,1)S(1)} %pad_maximum_fusion.own_ref), channel_id=1, source_target_pairs={{0,8},{8,0},{16,24},{24,16},{32,40},{40,32},{48,56},{56,48},{64,72... | collective-permute-start | bytes 3145736 | tf_op jit(solution)/shard_map/ppermute | solution.py:30
  117.2 1.3 copy-start.2
  129.0 44.2 %copy-start.7 = (s32[2]{0:T(128)S(1)}, s32[2]{0:T(128)}, u32[]{:S(2)}) copy-start(s32[2]{0:T(128)} %size_ref.3) | copy-start | bytes 28
  129.0 14.8 %all-to-all-start.4 = ((bf16[8,32,256]{2,1,0:T(8,128)(2,1)}), bf16[8,32,256]{2,1,0:T(8,128)(2,1)S(1)}, u32[]{:S(2)}, u32[]{:S(2)}) async-start(bf16[8,32,256]{2,1,0:T(8,128)(2,1)} %get-tuple-element.66), calls=%async_computation.4 | async-start | bytes 262144 | tf_op jit(solution)/shard_map/all_to_all | solution.py:25
  135.8 37.4 %copy-start.1 = (bf16[256,2048]{1,0:T(8,128)(2,1)S(1)}, bf16[256,2048]{1,0:T(8,128)(2,1)}, u32[]{:S(2)}) copy-start(bf16[256,2048]{1,0:T(8,128)(2,1)} %coeffs_ref.2) | copy-start | bytes 3145732
  135.8 10.3 %collective-permute-start.13 = (bf16[8,32,256]{2,1,0:T(8,128)(2,1)S(1)}, bf16[8,32,256]{2,1,0:T(8,128)(2,1)S(1)}, u32[]{:S(2)}, u32[]{:S(2)}) collective-permute-start(bf16[8,32,256]{2,1,0:T(8,128)(2,1)S(1)} %all_to_all.32), channel_id=1, source_target_pairs={{0,384},{8,392},{16,400},{24,408},{32,416},{40,424},{48,432},{56,4... | collective-permute-start | bytes 393224 | tf_op jit(solution)/shard_map/ppermute | solution.py:35
  139.3 7.5 %collective-permute-start.12 = (bf16[8,32,256]{2,1,0:T(8,128)(2,1)S(1)}, bf16[8,32,256]{2,1,0:T(8,128)(2,1)S(1)}, u32[]{:S(2)}, u32[]{:S(2)}) collective-permute-start(bf16[8,32,256]{2,1,0:T(8,128)(2,1)S(1)} %all_to_all.32), channel_id=1, source_target_pairs={{0,256},{8,264},{16,272},{24,280},{32,288},{40,296},{48,304},{56,3... | collective-permute-start | bytes 393224 | tf_op jit(solution)/shard_map/ppermute | solution.py:35
  141.2 7.6 %collective-permute-start.11 = (bf16[8,32,256]{2,1,0:T(8,128)(2,1)S(1)}, bf16[8,32,256]{2,1,0:T(8,128)(2,1)S(1)}, u32[]{:S(2)}, u32[]{:S(2)}) collective-permute-start(bf16[8,32,256]{2,1,0:T(8,128)(2,1)S(1)} %all_to_all.32), channel_id=1, source_target_pairs={{0,128},{8,136},{16,144},{24,152},{32,160},{40,168},{48,176},{56,1... | collective-permute-start | bytes 393224 | tf_op jit(solution)/shard_map/ppermute | solution.py:35
  143.8 1.6 copy-start.3
  148.9 24.3 %collective-permute-start.14 = (bf16[4,8,32,256]{3,2,1,0:T(8,128)(2,1)S(1)}, bf16[4,8,32,256]{3,2,1,0:T(8,128)(2,1)S(1)}, u32[]{:S(2)}, u32[]{:S(2)}) collective-permute-start(bf16[4,8,32,256]{3,2,1,0:T(8,128)(2,1)S(1)} %pad_maximum_fusion.1.own_ref), channel_id=1, source_target_pairs={{0,8},{8,0},{16,24},{24,16},{32,40},{40,32},{48,56},{56,48},{64,72... | collective-permute-start | bytes 1572872 | tf_op jit(solution)/shard_map/ppermute | solution.py:30
  (2 other events, 1.3 us)

commit v9 on v8

--- a/solution.py
+++ b/solution.py
@@ -19,6 +19,7 @@
 
 
 z_groups = [[row_index(x, z, k) for z in range(ZS)] for x in range(XS) for k in range(CORES)]
+plane_groups = [[row_index(x, z, k) for z in range(ZS) for k in range(CORES)] for x in range(XS)]
 
 
 def swap(cells, axis, groups=None):
@@ -44,12 +45,12 @@
 hbm = pl.BlockSpec(memory_space=pltpu.HBM)
 
 
-def call(kernel, shapes, in_specs, scratch, *operands, out_specs=None, bytes_accessed=2**20):
+def call(kernel, shapes, in_specs, scratch, *operands, bytes_accessed=2**20):
     return pl.pallas_call(
         kernel,
         out_shape=[jax.ShapeDtypeStruct(*shape) for shape in shapes],
         in_specs=in_specs,
-        out_specs=out_specs or [vmem] * len(shapes),
+        out_specs=[vmem] * len(shapes),
         scratch_shapes=scratch,
         compiler_params=pltpu.CompilerParams(vmem_limit_bytes=12 * 2**20),
         cost_estimate=pl.CostEstimate(
@@ -69,35 +70,41 @@
     return jnp.concatenate(parts, axis=0)
 
 
-def turn_kernel(size, place_ref, coeffs_ref, own_ref, far_ref):
+def turn_kernel(
+    rows, place_ref, size_ref, links_ref, coeffs_ref, ops_ref, own_ref, far_ref, gated_ref
+):
     core = place_ref[1]
     lanes = 128
     for start in range(0, coeffs_ref.shape[1], lanes):
         cells = coeffs_ref[:, start : start + lanes].astype(f32).T
-        for offset in range(0, lanes, CORES * size):
-            first = cells[offset : offset + size]
-            second = cells[offset + size : offset + 2 * size]
-            rows = pl.ds((start + offset) // CORES, size)
-            own_ref[rows, :] = jnp.where(core == 0, first, second).astype(bf16)
-            far_ref[rows, :] = jnp.where(core == 0, second, first).astype(bf16)
-
-
-def applied_kernel(size_ref, links_ref, up_ref, cols_ref, down_ref, ops_ref, out_ref, diag_ref):
+        for offset in range(0, lanes, CORES * rows):
+            first = cells[offset : offset + rows]
+            second = cells[offset + rows : offset + 2 * rows]
+            where = pl.ds((start + offset) // CORES, rows)
+            own_ref[where, :] = jnp.where(core == 0, first, second).astype(bf16)
+            far_ref[where, :] = jnp.where(core == 0, second, first).astype(bf16)
     phases, blocks, span, size, _ = ops_ref.shape
+    within = lax.broadcasted_iota(jnp.int32, (size, size), 0)
+    for b in range(blocks):
+        for t in range(span):
+            kept = within < jnp.where(links_ref[b, t] != 0, size_ref[b], 0)
+            for p in range(phases):
+                cells = jnp.where(kept, ops_ref[p, b, t].astype(f32), 0.0)
+                gated_ref[p, b, :, t * size : (t + 1) * size] = cells.astype(bf16)
+
+
+def applied_kernel(up_ref, cols_ref, down_ref, gated_ref, out_ref, diag_ref):
+    phases, blocks, size, depth = gated_ref.shape
     width = cols_ref.shape[1]
     padded = jnp.concatenate([up_ref[...], cols_ref[...], down_ref[...]], axis=0)
-    first = up_ref.shape[0] - (span - 1) // 2 * size
+    first = up_ref.shape[0] - (depth // size - 1) // 2 * size
     own = cols_ref[...].astype(f32)
     for p in range(phases):
         parts = []
         for b in range(blocks):
-            gated = [
-                ops_ref[p, b, t] * links_ref[b, t].astype(f32).astype(bf16) for t in range(span)
-            ]
             start = first + b * size
-            near = padded[start : start + span * size]
-            parts.append(small_product(jnp.concatenate(gated, axis=1), near))
-        total = within_rows(size_ref, jnp.concatenate(parts, axis=0)).astype(bf16)
+            parts.append(small_product(gated_ref[p, b], padded[start : start + depth]))
+        total = jnp.concatenate(parts, axis=0).astype(bf16)
         out_ref[:, p * width : (p + 1) * width] = total
         sums = jnp.sum(total.astype(f32) * own, axis=0, keepdims=True)
         diag_ref[:, p * width : (p + 1) * width] = sums
@@ -185,8 +192,12 @@
     return cells.reshape(-1, cells.shape[-1])
 
 
-def rows_kernel(scale, place_ref, across_ref, rows_ref, diag_ref, turned_ref):
-    mine, low = place_ref[2], place_ref[3]
+def square_kernel(
+    scale, place_ref, across_ref, own_ref, away_ref,
+    z_ref, rows_ref, square_ref, step_ref, diag_ref, turned_ref, sems,
+):
+    copies = gathered(place_ref, own_ref, away_ref, z_ref, sems)
+    mine, low, col = place_ref[2], place_ref[3], place_ref[4]
     rows, width = rows_ref.shape[1:]
     terms = across_ref[:, :, -128:].astype(f32)
     per = width // 128
@@ -208,24 +219,10 @@
         cos_part = cells[:, :width] * (diag_ref[0, k : k + 1, :] - down[0])
         sin_part = cells[:, width : 2 * width] * (diag_ref[1, k : k + 1, :] - down[1])
         rows_ref[k] = (cos_part + sin_part) * scale
-
-
-def square_kernel(
-    scale, place_ref, rows_ref, diag_ref, turned_ref, own_ref, away_ref,
-    kept_ref, square_ref, step_ref, z_ref, sems, kept_sems,
-):
-    copies = gathered(place_ref, own_ref, away_ref, z_ref, sems)
-    kept = [
-        pltpu.make_async_copy(z_ref.at[x], kept_ref.at[x], kept_sems.at[x]) for x in range(XS)
-    ]
-    col = place_ref[4]
-    rows, width = rows_ref.shape[1:]
     across_diag = [diag_ref[p, pl.ds(col, 1), :] for p in range(2)]
     square = jnp.zeros((rows, width), f32)
     for k in range(COLS):
         landed(copies, k)
-        if k * XS % COLS == 0:
-            kept[k * XS // COLS].start()
         cells = chunk(z_ref, k).astype(f32)
         cos_part = cells[:, :width] * (across_diag[0] - turned_ref[0, :, k : k + 1])
         sin_part = cells[:, width:] * (across_diag[1] - turned_ref[1, :, k : k + 1])
@@ -233,20 +230,15 @@
         square = square + small_product(rows_ref[k].astype(bf16), cells)
     step = (rows_ref[col] + 0.5 * square).astype(bf16)
     square = square.astype(bf16)
-    for k in range(COLS):
+    for k in range(square_ref.shape[0]):
         square_ref[k] = square
+    for k in range(step_ref.shape[0]):
         step_ref[k] = step
-    for copy in kept:
-        copy.wait()
-
-
-def half_kernel(square_ref, rows_ref, kept_ref, block_ref, half_ref, sent_ref, z_ref, sems):
-    copies = [[pltpu.make_async_copy(kept_ref.at[x], z_ref.at[x], sems.at[x])] for x in range(XS)]
-    for copy, in copies:
-        copy.start()
+
+
+def half_kernel(square_ref, rows_ref, z_ref, block_ref, half_ref, sent_ref):
     total = block_ref[...]
     for k in range(COLS):
-        landed(copies, k)
         back = (0.5 * square_ref[k].astype(f32) - rows_ref[k]).astype(bf16)
         total = total + small_product(back, chunk(z_ref, k))
     half_ref[...] = total
@@ -257,25 +249,35 @@
 
 def final_kernel(
     place_ref, size_ref, half_ref, across_ref, coeffs_ref, rotation_ref, block_ref,
-    own_ref, away_ref,
+    own0, own1, own2, own3,
     rotated_ref, cos_ref, sin_ref, orbitals_ref, step_ref, sems,
 ):
-    copies = gathered(place_ref, own_ref, away_ref, step_ref, sems)
+    copies = [
+        pltpu.make_async_copy(ref, step_ref.at[steps], sems.at[steps])
+        for steps, ref in enumerate((own0, own1, own2, own3))
+    ]
+    for copy in copies:
+        copy.start()
     col = place_ref[4]
     width = rotated_ref.shape[1]
     rotated = rotation_ref[...]
     cos_part, sin_part = block_ref[:, :width], block_ref[:, width:]
     start = pl.multiple_of(col * width, width)
     orbitals = coeffs_ref[:, pl.ds(start, width)].astype(f32)
-    for k in range(COLS):
-        landed(copies, k)
-        step = chunk(step_ref, k)
-        cells = half_ref[k]
-        cos_part = cos_part + small_product(cells[:, :width], step)
-        sin_part = sin_part + small_product(cells[:, width:], step)
-        rotated = rotated + small_product(across_ref[k, :, 2 * width : 3 * width], step)
-        cells = coeffs_ref[:, k * width : (k + 1) * width]
-        orbitals = orbitals + small_product(cells, step)
+    per = COLS // XS
+    for steps in range(XS):
+        copies[steps].wait()
+        source = lax.rem(place_ref[0] + XS - steps, XS)
+        count = step_ref.shape[1] // per
+        for part in range(per):
+            k = source * per + part
+            step = step_ref[steps, part * count : (part + 1) * count].reshape(-1, width)
+            cells = half_ref[k]
+            cos_part = cos_part + small_product(cells[:, :width], step)
+            sin_part = sin_part + small_product(cells[:, width:], step)
+            rotated = rotated + small_product(across_ref[k, :, 2 * width : 3 * width], step)
+            cells = coeffs_ref[:, pl.ds(pl.multiple_of(k * width, width), width)]
+            orbitals = orbitals + small_product(cells, step)
     rotated_ref[...] = rotated
     cos_ref[...] = cos_part
     sin_ref[...] = sin_part
@@ -310,13 +312,17 @@
     from_down = lax.ppermute(own_cols[:width], "rows", down)
     turn_coeffs, own_cols = lax.optimization_barrier((coeffs, own_cols))
     half_shape = ((orbital_count // CORES, rows_dev), bf16)
-    own_turned, far_turned = call(
+    phases, blocks = phase_ops.shape[:2]
+    own_turned, far_turned, gated = call(
         functools.partial(turn_kernel, row_count),
-        [half_shape] * 2,
-        [smem, vmem],
+        [half_shape] * 2 + [((phases, blocks, block_size, span_blocks * block_size), bf16)],
+        [smem] * 3 + [vmem] * 2,
         [],
         place,
+        atom_size,
+        block_links,
         turn_coeffs,
+        phase_ops,
         bytes_accessed=2**26,
     )
     from_up, from_down, far_turned = lax.optimization_barrier((from_up, from_down, far_turned))
@@ -324,14 +330,12 @@
     applied, own_diag = call(
         applied_kernel,
         [((rows_dev, both), bf16), ((1, both), f32)],
-        [smem] * 2 + [vmem] * 4,
+        [vmem] * 4,
         [],
-        atom_size,
-        block_links,
         from_up,
         own_cols,
         from_down,
-        phase_ops,
+        gated,
         bytes_accessed=2**22,
     )
     far_applied = other_core(applied)
@@ -382,71 +386,50 @@
     stacked, across = lax.optimization_barrier((jnp.stack(panels), across))
     away = other_core(stacked)
     block = (row_count, col_count)
-    gen_rows, diag_all, turned_diag = call(
-        functools.partial(rows_kernel, scale_factor),
-        [
-            ((COLS,) + block, f32),
-            ((2, COLS, col_count), f32),
-            ((2, col_count, COLS), f32),
-        ],
-        [smem, vmem],
-        [],
-        place,
-        across,
-        bytes_accessed=2**28,
-    )
-    z_cols, square, step = call(
+    z_cols, gen_rows, square, step = call(
         functools.partial(square_kernel, scale_factor),
         [
             ((XS, ZS, CORES, row_count, both), bf16),
+            ((COLS,) + block, f32),
             ((COLS,) + block, bf16),
-            ((ZS,) + block, bf16),
+            ((ZS * CORES,) + block, bf16),
         ],
-        [smem] + [vmem] * 3 + [hbm] * 2,
+        [smem, vmem] + [hbm] * 2,
         [
-            pltpu.VMEM((XS, ZS, CORES, row_count, both), bf16),
+            pltpu.VMEM((2, COLS, col_count), f32),
+            pltpu.VMEM((2, col_count, COLS), f32),
             pltpu.SemaphoreType.DMA((XS, 2)),
-            pltpu.SemaphoreType.DMA((XS,)),
         ],
         place,
-        gen_rows,
-        diag_all,
-        turned_diag,
+        across,
         stacked,
         away,
-        out_specs=[hbm, vmem, vmem],
-    )
-
-    step = swap(step, "rows", z_groups)
+    )
+
+    step = swap(step, "rows", plane_groups)
     square, step = lax.optimization_barrier((square, step))
     steps_x = [step] + [along_x(step, steps) for steps in (1, 2, 3)]
     square = swap(square, "cols")
     half_block, half_sent = call(
         half_kernel,
         [((row_count, both), f32), ((COLS, row_count, both), bf16)],
-        [vmem] * 2 + [hbm, vmem],
-        [
-            pltpu.VMEM((XS, ZS, CORES, row_count, both), bf16),
-            pltpu.SemaphoreType.DMA((XS,)),
-        ],
+        [vmem] * 4,
+        [],
         square,
         gen_rows,
         z_cols,
         z_block,
         bytes_accessed=2**26,
     )
-    *steps_x, half_sent = lax.optimization_barrier((*steps_x, half_sent))
-    step_stack = jnp.stack(steps_x)
-    step_away = other_core(step_stack)
     half_rows = swap(half_sent, "cols")
     return tuple(
         call(
             final_kernel,
             [(block, f32)] * 3 + [((rows_dev, col_count), bf16)],
-            [smem] * 2 + [vmem] * 5 + [hbm] * 2,
+            [smem] * 2 + [vmem] * 5 + [hbm] * XS,
             [
-                pltpu.VMEM((XS, ZS, CORES, row_count, col_count), bf16),
-                pltpu.SemaphoreType.DMA((XS, 2)),
+                pltpu.VMEM((XS, ZS * CORES) + block, bf16),
+                pltpu.SemaphoreType.DMA((XS,)),
             ],
             place,
             atom_size,
@@ -455,8 +438,7 @@
             coeffs,
             rotation,
             half_block,
-            step_stack,
-            step_away,
+            *steps_x,
         )
     )
 

time: 177 us -> 173 us (0.977)
  starting transfers between devices: 67.9 us -> 58.7 us
  waiting for transfers between devices: 29.2 us -> 37.4 us
  local copies, waits for them, and re-layouts: 6.7 us -> 3.78 us
    ppermute x9, waiting for transfers between devices: 22.3 us -> 32.4 us  [along_x(): lax.ppermute(cells, 'rows', [(i, (i + steps * line) % count) for i in ran...]
    ppermute x4 -> x3, starting transfers between devices: 20.1 us -> 14.9 us  [other_core(): return lax.ppermute(cells, 'rows', [(i, i ^ 1) for i in range(count)])]
    all_to_all x2, starting transfers between devices: 13.6 us -> 10.2 us  [swap(): lax.all_to_all(cells, axis, 0, 0, tiled=True, axis_index_groups=groups)]
    unnamed x18 -> x14, local copies, waits for them, and re-layouts: 6.58 us -> 3.66 us
    ppermute x1, waiting for transfers between devices: 3.86 us -> 1.26 us  [on_device(): from_up = lax.ppermute(own_cols[rows_dev - width:], 'rows', up)]
    pallas_call x8 -> x7, Pallas kernels: 11 us -> 9.65 us  [call(): pl.pallas_call(kernel, out_shape=[jax.ShapeDtypeStruct(*shape) for shape...]
    ppermute x4 -> x3, waiting for transfers between devices: 2.94 us -> 3.77 us  [other_core(): return lax.ppermute(cells, 'rows', [(i, i ^ 1) for i in range(count)])]
  transfers between devices with their start and end apart: 17 -> 16, of which waited for: 10 -> 10; matrix products, arithmetic and copies ran while one was open for 0% -> 0% of each run, Pallas kernels for 2% -> 1%
where the time goes in v9:
time: 173 us; the launch traced here: 172 us
  blocking collectives  59.2 us (34%)
  starting transfers between devices  58.7 us (34%)
  waiting for transfers between devices  37.4 us (22%)
  Pallas kernels  9.65 us (6%)
  local copies, waits for them, and re-layouts  3.78 us (2%)
  other arithmetic  2.33 us (1%)
    all_to_all x4, blocking collectives, swap(): lax.all_to_all(cells, axis, 0, 0, tiled=True, axis_index_groups=groups)  59.2 us
    ppermute x9, waiting for transfers between devices, along_x(): lax.ppermute(cells, 'rows', [(i, (i + steps * line) % count) for i in ran...  32.4 us
    ppermute x9, starting transfers between devices, along_x(): lax.ppermute(cells, 'rows', [(i, (i + steps * line) % count) for i in ran...  22.8 us
    ppermute x3, starting transfers between devices, other_core(): return lax.ppermute(cells, 'rows', [(i, i ^ 1) for i in range(count)])  14.9 us
    all_to_all x2, starting transfers between devices, swap(): lax.all_to_all(cells, axis, 0, 0, tiled=True, axis_index_groups=groups)  10.2 us
    pallas_call x7, Pallas kernels, call(): pl.pallas_call(kernel, out_shape=[jax.ShapeDtypeStruct(*shape) for shape...  9.65 us
    ppermute x1, starting transfers between devices, on_device(): from_down = lax.ppermute(own_cols[:width], 'rows', down)  8.79 us
    ppermute x3, waiting for transfers between devices, other_core(): return lax.ppermute(cells, 'rows', [(i, i ^ 1) for i in range(count)])  3.77 us
  transfers between devices with their start and end apart: 16, of which 10 were waited for; matrix products, arithmetic and copies ran while one was open for 0% of the time, Pallas kernels for 1%

profile of v9, /device:TPU:1, one launch (start us, length us, event | category | flops | bytes accessed | tf_op | source)
XLA Modules:
  0.0 172.0 jit_solution(14641261948605107653)
XLA Ops:
  2.4 8.8 %collective-permute-start.1 = (bf16[256,256]{1,0:T(8,128)(2,1)S(1)}, bf16[256,256]{1,0:T(8,128)(2,1)S(1)}, u32[]{:S(2)}, u32[]{:S(2)}) collective-permute-start(bf16[256,256]{1,0:T(8,128)(2,1)S(1)} %dynamic-slice_select_fusion.cols_ref), channel_id=1, source_target_pairs={{8,0},{16,8},{24,16},{32,24},{40,32},{48,40},{56,48},{64,56},{72,6... | collective-permute-start | bytes 393224 | tf_op jit(solution)/shard_map/ppermute | solution.py:312
  19.2 8.8 %collective-permute-start.2 = (bf16[1024,256]{1,0:T(8,128)(2,1)S(1)}, bf16[1024,256]{1,0:T(8,128)(2,1)S(1)}, u32[]{:S(2)}, u32[]{:S(2)}) collective-permute-start(bf16[1024,256]{1,0:T(8,128)(2,1)S(1)} %get-tuple-element.37), channel_id=1, source_target_pairs={{0,8},{8,0},{16,24},{24,16},{32,40},{40,32},{48,56},{56,48},{64,72... | collective-permute-start | bytes 1572872 | tf_op jit(solution)/shard_map/ppermute | solution.py:31
  33.2 1.9 %collective-permute-start.4 = (bf16[272,512]{1,0:T(8,128)(2,1)S(1)}, bf16[272,512]{1,0:T(8,128)(2,1)S(1)}, u32[]{:S(2)}, u32[]{:S(2)}) collective-permute-start(bf16[272,512]{1,0:T(8,128)(2,1)S(1)} %get-tuple-element.45), channel_id=1, source_target_pairs={{0,256},{8,264},{16,272},{24,280},{32,288},{40,296},{48,304},{56,3... | collective-permute-start | bytes 835592 | tf_op jit(solution)/shard_map/ppermute | solution.py:36
  37.0 4.6 %collective-permute-start.6 = (bf16[272,512]{1,0:T(8,128)(2,1)S(1)}, bf16[272,512]{1,0:T(8,128)(2,1)S(1)}, u32[]{:S(2)}, u32[]{:S(2)}) collective-permute-start(bf16[272,512]{1,0:T(8,128)(2,1)S(1)} %get-tuple-element.47), channel_id=1, source_target_pairs={{0,384},{8,392},{16,400},{24,408},{32,416},{40,424},{48,432},{56,4... | collective-permute-start | bytes 835592 | tf_op jit(solution)/shard_map/ppermute | solution.py:36
  41.6 3.1 %collective-permute-done.4 = bf16[272,512]{1,0:T(8,128)(2,1)S(1)} collective-permute-done((bf16[272,512]{1,0:T(8,128)(2,1)S(1)}, bf16[272,512]{1,0:T(8,128)(2,1)S(1)}, u32[]{:S(2)}, u32[]{:S(2)}) %collective-permute-start.4) | collective-permute-done | bytes 278560 | tf_op jit(solution)/shard_map/ppermute | solution.py:36
  44.8 6.4 %collective-permute-done.5 = bf16[272,512]{1,0:T(8,128)(2,1)S(1)} collective-permute-done((bf16[272,512]{1,0:T(8,128)(2,1)S(1)}, bf16[272,512]{1,0:T(8,128)(2,1)S(1)}, u32[]{:S(2)}, u32[]{:S(2)}) %collective-permute-start.5) | collective-permute-done | bytes 278560 | tf_op jit(solution)/shard_map/ppermute | solution.py:36
  51.7 15.5 %all_to_all.30.got_ref = bf16[8,32,640]{2,1,0:T(8,128)(2,1)S(1)} all-to-all(bf16[8,32,640]{2,1,0:T(8,128)(2,1)S(1)} %pad_maximum_fusion.1), channel_id=1, replica_groups={{0,16,32,48,64,80,96,112},{8,24,40,56,72,88,104,120},{128,144,160,176,1..., dimensions={0} | all-to-all | bytes 655360 | tf_op jit(solution)/shard_map/all_to_all | solution.py:26
  68.0 12.6 %all_to_all.31 = bf16[8,32,512]{2,1,0:T(8,128)(2,1)S(1)} all-to-all(bf16[8,32,512]{2,1,0:T(8,128)(2,1)S(1)} %get-tuple-element.50), channel_id=1, replica_groups={{0,16,32,48,64,80,96,112},{8,24,40,56,72,88,104,120},{128,144,160,176,1..., dimensions={0} | all-to-all | bytes 524288 | tf_op jit(solution)/shard_map/all_to_all | solution.py:26
  80.6 6.8 %all-to-all-start.2 = ((bf16[8,32,896]{2,1,0:T(8,128)(2,1)}), bf16[8,32,896]{2,1,0:T(8,128)(2,1)S(1)}, u32[]{:S(2)}, u32[]{:S(2)}) async-start(bf16[8,32,896]{2,1,0:T(8,128)(2,1)} %get-tuple-element.52), calls=%async_computation.2 | async-start | bytes 917504 | tf_op jit(solution)/shard_map/all_to_all | solution.py:26
  91.3 3.4 %collective-permute-start.7 = (bf16[8,32,512]{2,1,0:T(8,128)(2,1)S(1)}, bf16[8,32,512]{2,1,0:T(8,128)(2,1)S(1)}, u32[]{:S(2)}, u32[]{:S(2)}) collective-permute-start(bf16[8,32,512]{2,1,0:T(8,128)(2,1)S(1)} %all_to_all.31), channel_id=1, source_target_pairs={{0,128},{8,136},{16,144},{24,152},{32,160},{40,168},{48,176},{56,1... | collective-permute-start | bytes 786440 | tf_op jit(solution)/shard_map/ppermute | solution.py:36
  94.6 3.3 %collective-permute-done.8 = bf16[8,32,512]{2,1,0:T(8,128)(2,1)S(1)} collective-permute-done((bf16[8,32,512]{2,1,0:T(8,128)(2,1)S(1)}, bf16[8,32,512]{2,1,0:T(8,128)(2,1)S(1)}, u32[]{:S(2)}, u32[]{:S(2)}) %collective-permute-start.8) | collective-permute-done | bytes 262176 | tf_op jit(solution)/shard_map/ppermute | solution.py:36
  97.9 6.8 %collective-permute-done.7 = bf16[8,32,512]{2,1,0:T(8,128)(2,1)S(1)} collective-permute-done((bf16[8,32,512]{2,1,0:T(8,128)(2,1)S(1)}, bf16[8,32,512]{2,1,0:T(8,128)(2,1)S(1)}, u32[]{:S(2)}, u32[]{:S(2)}) %collective-permute-start.7) | collective-permute-done | bytes 262176 | tf_op jit(solution)/shard_map/ppermute | solution.py:36
  104.9 4.2 %collective-permute-start.10 = (bf16[4,8,32,512]{3,2,1,0:T(8,128)(2,1)S(1)}, bf16[4,8,32,512]{3,2,1,0:T(8,128)(2,1)S(1)}, u32[]{:S(2)}, u32[]{:S(2)}) collective-permute-start(bf16[4,8,32,512]{3,2,1,0:T(8,128)(2,1)S(1)} %pad_maximum_fusion.own_ref), channel_id=1, source_target_pairs={{0,8},{8,0},{16,24},{24,16},{32,40},{40,32},{48,56},{56,48},{64,72... | collective-permute-start | bytes 3145736 | tf_op jit(solution)/shard_map/ppermute | solution.py:31
  109.1 2.3 %collective-permute-done.10.away_ref = bf16[4,8,32,512]{3,2,1,0:T(8,128)(2,1)S(1)} collective-permute-done((bf16[4,8,32,512]{3,2,1,0:T(8,128)(2,1)S(1)}, bf16[4,8,32,512]{3,2,1,0:T(8,128)(2,1)S(1)}, u32[]{:S(2)}, u32[]{:S(2)}) %collective-permute-start.10) | collective-permute-done | bytes 1048608 | tf_op jit(solution)/shard_map/ppermute | solution.py:31
  111.4 2.3 %shard_map.88 = (bf16[4,8,2,32,512]{4,3,2,1,0:T(8,128)(2,1)S(1)}, f32[8,32,256]{2,1,0:T(8,128)S(1)}, bf16[8,32,256]{2,1,0:T(8,128)(2,1)S(1)}, bf16[16,32,256]{2,1,0:T(8,128)(2,1)S(1)}) custom-call(s32[5]{0:T(128)S(1)} %stack.44.place_ref, bf16[8,32,896]{2,1,0:T(8,128)(2,1)S(1)} %all-to-all-done.2.across_ref, ...), custom_call_target="tpu_custom_call" | custom-call | bytes 1048576 | tf_op jit(solution)/shard_map/pallas_call | solution.py:49
  113.8 15.1 %all_to_all.32.own0 = bf16[16,32,256]{2,1,0:T(8,128)(2,1)S(1)} all-to-all(bf16[16,32,256]{2,1,0:T(8,128)(2,1)S(1)} %get-tuple-element.56), channel_id=1, replica_groups={{0,8,16,24,32,40,48,56,64,72,80,88,96,104,112,120},{128,136,144,152,160..., dimensions={0} | all-to-all | bytes 524288 | tf_op jit(solution)/shard_map/all_to_all | solution.py:26
  128.8 16.0 %all_to_all.33.square_ref = bf16[8,32,256]{2,1,0:T(8,128)(2,1)S(1)} all-to-all(bf16[8,32,256]{2,1,0:T(8,128)(2,1)S(1)} %get-tuple-element.57), channel_id=1, replica_groups=mesh['rows'=64,'cols'=8] {'cols'}, dimensions={0} | all-to-all | bytes 262144 | tf_op jit(solution)/shard_map/all_to_all | solution.py:26
  146.1 3.4 %all-to-all-start.5 = ((bf16[8,32,512]{2,1,0:T(8,128)(2,1)}), bf16[8,32,512]{2,1,0:T(8,128)(2,1)S(1)}, u32[]{:S(2)}, u32[]{:S(2)}) async-start(bf16[8,32,512]{2,1,0:T(8,128)(2,1)} %get-tuple-element.61), calls=%async_computation.5 | async-start | bytes 524288 | tf_op jit(solution)/shard_map/all_to_all | solution.py:26
  149.5 2.8 %collective-permute-start.13 = (bf16[16,32,256]{2,1,0:T(8,128)(2,1)S(1)}, bf16[16,32,256]{2,1,0:T(8,128)(2,1)S(1)}, u32[]{:S(2)}, u32[]{:S(2)}) collective-permute-start(bf16[16,32,256]{2,1,0:T(8,128)(2,1)S(1)} %all_to_all.32.own0), channel_id=1, source_target_pairs={{0,384},{8,392},{16,400},{24,408},{32,416},{40,424},{48,432},{56,4... | collective-permute-start | bytes 786440 | tf_op jit(solution)/shard_map/ppermute | solution.py:36
  154.2 2.5 %collective-permute-start.11 = (bf16[16,32,256]{2,1,0:T(8,128)(2,1)S(1)}, bf16[16,32,256]{2,1,0:T(8,128)(2,1)S(1)}, u32[]{:S(2)}, u32[]{:S(2)}) collective-permute-start(bf16[16,32,256]{2,1,0:T(8,128)(2,1)S(1)} %all_to_all.32.own0), channel_id=1, source_target_pairs={{0,128},{8,136},{16,144},{24,152},{32,160},{40,168},{48,176},{56,1... | collective-permute-start | bytes 786440 | tf_op jit(solution)/shard_map/ppermute | solution.py:36
  156.7 2.1 %collective-permute-done.13.own3 = bf16[16,32,256]{2,1,0:T(8,128)(2,1)S(1)} collective-permute-done((bf16[16,32,256]{2,1,0:T(8,128)(2,1)S(1)}, bf16[16,32,256]{2,1,0:T(8,128)(2,1)S(1)}, u32[]{:S(2)}, u32[]{:S(2)}) %collective-permute-start.13) | collective-permute-done | bytes 262176 | tf_op jit(solution)/shard_map/ppermute | solution.py:36
  158.8 4.0 %collective-permute-done.12.own2 = bf16[16,32,256]{2,1,0:T(8,128)(2,1)S(1)} collective-permute-done((bf16[16,32,256]{2,1,0:T(8,128)(2,1)S(1)}, bf16[16,32,256]{2,1,0:T(8,128)(2,1)S(1)}, u32[]{:S(2)}, u32[]{:S(2)}) %collective-permute-start.12) | collective-permute-done | bytes 262176 | tf_op jit(solution)/shard_map/ppermute | solution.py:36
  162.9 6.6 %collective-permute-done.11.own1 = bf16[16,32,256]{2,1,0:T(8,128)(2,1)S(1)} collective-permute-done((bf16[16,32,256]{2,1,0:T(8,128)(2,1)S(1)}, bf16[16,32,256]{2,1,0:T(8,128)(2,1)S(1)}, u32[]{:S(2)}, u32[]{:S(2)}) %collective-permute-start.11) | collective-permute-done | bytes 262176 | tf_op jit(solution)/shard_map/ppermute | solution.py:36
  169.5 2.5 %shard_map.90 = (f32[32,256]{1,0:T(8,128)}, f32[32,256]{1,0:T(8,128)}, f32[32,256]{1,0:T(8,128)}, bf16[256,256]{1,0:T(8,128)(2,1)}) custom-call(s32[5]{0:T(128)S(1)} %stack.44.place_ref, s32[2]{0:T(128)S(1)} %copy-done.5, bf16[8,32,512]{2,1,0:T(8,128)(2,1)S(1)} %all-to-all-done.5.half_ref, bf16[8,32,896]{2,1,0:T(8,128)(2,1)S(1)} %all-to-all-done.2.across_ref, ...), custom_call_target="tpu_custom_call" | custom-call | bytes 1048576 | tf_op jit(solution)/shard_map/pallas_call | solution.py:49
  (48 shorter events, 25.2 us)
Async XLA Ops:
  2.4 15.6 %collective-permute-start.1 = (bf16[256,256]{1,0:T(8,128)(2,1)S(1)}, bf16[256,256]{1,0:T(8,128)(2,1)S(1)}, u32[]{:S(2)}, u32[]{:S(2)}) collective-permute-start(bf16[256,256]{1,0:T(8,128)(2,1)S(1)} %dynamic-slice_select_fusion.cols_ref), channel_id=1, source_target_pairs={{8,0},{16,8},{24,16},{32,24},{40,32},{48,40},{56,48},{64,56},{72,6... | collective-permute-start | bytes 393224 | tf_op jit(solution)/shard_map/ppermute | solution.py:312
  11.2 8.0 %collective-permute-start = (bf16[256,256]{1,0:T(8,128)(2,1)S(1)}, bf16[256,256]{1,0:T(8,128)(2,1)S(1)}, u32[]{:S(2)}, u32[]{:S(2)}) collective-permute-start(bf16[256,256]{1,0:T(8,128)(2,1)S(1)} %dynamic-slice_select_fusion.cols_ref), channel_id=1, source_target_pairs={{0,8},{8,16},{16,24},{24,32},{32,40},{40,48},{48,56},{56,64},{64,7... | collective-permute-start | bytes 393224 | tf_op jit(solution)/shard_map/ppermute | solution.py:311
  13.2 1.2 copy-start
  14.4 1.1 copy-start.2
  15.5 0.7 copy-start.4
  16.2 0.7 copy-start.6
  19.2 12.6 %collective-permute-start.2 = (bf16[1024,256]{1,0:T(8,128)(2,1)S(1)}, bf16[1024,256]{1,0:T(8,128)(2,1)S(1)}, u32[]{:S(2)}, u32[]{:S(2)}) collective-permute-start(bf16[1024,256]{1,0:T(8,128)(2,1)S(1)} %get-tuple-element.37), channel_id=1, source_target_pairs={{0,8},{8,0},{16,24},{24,16},{32,40},{40,32},{48,56},{56,48},{64,72... | collective-permute-start | bytes 1572872 | tf_op jit(solution)/shard_map/ppermute | solution.py:31
  28.4 3.4 %collective-permute-start.3 = (bf16[256,512]{1,0:T(8,128)(2,1)S(1)}, bf16[256,512]{1,0:T(8,128)(2,1)S(1)}, u32[]{:S(2)}, u32[]{:S(2)}) collective-permute-start(bf16[256,512]{1,0:T(8,128)(2,1)S(1)} %get-tuple-element.42.applied_ref), channel_id=1, source_target_pairs={{0,8},{8,0},{16,24},{24,16},{32,40},{40,32},{48,56},{56,48},{64,72... | collective-permute-start | bytes 786440 | tf_op jit(solution)/shard_map/ppermute | solution.py:31
  33.2 11.6 %collective-permute-start.4 = (bf16[272,512]{1,0:T(8,128)(2,1)S(1)}, bf16[272,512]{1,0:T(8,128)(2,1)S(1)}, u32[]{:S(2)}, u32[]{:S(2)}) collective-permute-start(bf16[272,512]{1,0:T(8,128)(2,1)S(1)} %get-tuple-element.45), channel_id=1, source_target_pairs={{0,256},{8,264},{16,272},{24,280},{32,288},{40,296},{48,304},{56,3... | collective-permute-start | bytes 835592 | tf_op jit(solution)/shard_map/ppermute | solution.py:36
  35.1 16.1 %collective-permute-start.5 = (bf16[272,512]{1,0:T(8,128)(2,1)S(1)}, bf16[272,512]{1,0:T(8,128)(2,1)S(1)}, u32[]{:S(2)}, u32[]{:S(2)}) collective-permute-start(bf16[272,512]{1,0:T(8,128)(2,1)S(1)} %get-tuple-element.46), channel_id=1, source_target_pairs={{0,128},{8,136},{16,144},{24,152},{32,160},{40,168},{48,176},{56,1... | collective-permute-start | bytes 835592 | tf_op jit(solution)/shard_map/ppermute | solution.py:36
  37.0 14.2 %collective-permute-start.6 = (bf16[272,512]{1,0:T(8,128)(2,1)S(1)}, bf16[272,512]{1,0:T(8,128)(2,1)S(1)}, u32[]{:S(2)}, u32[]{:S(2)}) collective-permute-start(bf16[272,512]{1,0:T(8,128)(2,1)S(1)} %get-tuple-element.47), channel_id=1, source_target_pairs={{0,384},{8,392},{16,400},{24,408},{32,416},{40,424},{48,432},{56,4... | collective-permute-start | bytes 835592 | tf_op jit(solution)/shard_map/ppermute | solution.py:36
  51.3 15.9 %copy-start.3 = (f32[32,256]{1,0:T(8,128)S(1)}, f32[32,256]{1,0:T(8,128)}, u32[]{:S(2)}) copy-start(f32[32,256]{1,0:T(8,128)} %rotation_ref.3) | copy-start | bytes 98308
  80.6 24.3 %all-to-all-start.2 = ((bf16[8,32,896]{2,1,0:T(8,128)(2,1)}), bf16[8,32,896]{2,1,0:T(8,128)(2,1)S(1)}, u32[]{:S(2)}, u32[]{:S(2)}) async-start(bf16[8,32,896]{2,1,0:T(8,128)(2,1)} %get-tuple-element.52), calls=%async_computation.2 | async-start | bytes 917504 | tf_op jit(solution)/shard_map/all_to_all | solution.py:26
  87.4 7.2 %collective-permute-start.9 = (bf16[8,32,512]{2,1,0:T(8,128)(2,1)S(1)}, bf16[8,32,512]{2,1,0:T(8,128)(2,1)S(1)}, u32[]{:S(2)}, u32[]{:S(2)}) collective-permute-start(bf16[8,32,512]{2,1,0:T(8,128)(2,1)S(1)} %all_to_all.31), channel_id=1, source_target_pairs={{0,384},{8,392},{16,400},{24,408},{32,416},{40,424},{48,432},{56,4... | collective-permute-start | bytes 786440 | tf_op jit(solution)/shard_map/ppermute | solution.py:36
  89.3 8.6 %collective-permute-start.8 = (bf16[8,32,512]{2,1,0:T(8,128)(2,1)S(1)}, bf16[8,32,512]{2,1,0:T(8,128)(2,1)S(1)}, u32[]{:S(2)}, u32[]{:S(2)}) collective-permute-start(bf16[8,32,512]{2,1,0:T(8,128)(2,1)S(1)} %all_to_all.31), channel_id=1, source_target_pairs={{0,256},{8,264},{16,272},{24,280},{32,288},{40,296},{48,304},{56,3... | collective-permute-start | bytes 786440 | tf_op jit(solution)/shard_map/ppermute | solution.py:36
  91.3 13.5 %collective-permute-start.7 = (bf16[8,32,512]{2,1,0:T(8,128)(2,1)S(1)}, bf16[8,32,512]{2,1,0:T(8,128)(2,1)S(1)}, u32[]{:S(2)}, u32[]{:S(2)}) collective-permute-start(bf16[8,32,512]{2,1,0:T(8,128)(2,1)S(1)} %all_to_all.31), channel_id=1, source_target_pairs={{0,128},{8,136},{16,144},{24,152},{32,160},{40,168},{48,176},{56,1... | collective-permute-start | bytes 786440 | tf_op jit(solution)/shard_map/ppermute | solution.py:36
  104.9 6.5 %collective-permute-start.10 = (bf16[4,8,32,512]{3,2,1,0:T(8,128)(2,1)S(1)}, bf16[4,8,32,512]{3,2,1,0:T(8,128)(2,1)S(1)}, u32[]{:S(2)}, u32[]{:S(2)}) collective-permute-start(bf16[4,8,32,512]{3,2,1,0:T(8,128)(2,1)S(1)} %pad_maximum_fusion.own_ref), channel_id=1, source_target_pairs={{0,8},{8,0},{16,24},{24,16},{32,40},{40,32},{48,56},{56,48},{64,72... | collective-permute-start | bytes 3145736 | tf_op jit(solution)/shard_map/ppermute | solution.py:31
  113.7 55.8 %copy-start.1 = (bf16[256,2048]{1,0:T(8,128)(2,1)S(1)}, bf16[256,2048]{1,0:T(8,128)(2,1)}, u32[]{:S(2)}) copy-start(bf16[256,2048]{1,0:T(8,128)(2,1)} %coeffs_ref.2) | copy-start | bytes 3145732
  113.7 55.8 %copy-start.5 = (s32[2]{0:T(128)S(1)}, s32[2]{0:T(128)}, u32[]{:S(2)}) copy-start(s32[2]{0:T(128)} %size_ref.3) | copy-start | bytes 28
  146.1 23.4 %all-to-all-start.5 = ((bf16[8,32,512]{2,1,0:T(8,128)(2,1)}), bf16[8,32,512]{2,1,0:T(8,128)(2,1)S(1)}, u32[]{:S(2)}, u32[]{:S(2)}) async-start(bf16[8,32,512]{2,1,0:T(8,128)(2,1)} %get-tuple-element.61), calls=%async_computation.5 | async-start | bytes 524288 | tf_op jit(solution)/shard_map/all_to_all | solution.py:26
  149.5 9.4 %collective-permute-start.13 = (bf16[16,32,256]{2,1,0:T(8,128)(2,1)S(1)}, bf16[16,32,256]{2,1,0:T(8,128)(2,1)S(1)}, u32[]{:S(2)}, u32[]{:S(2)}) collective-permute-start(bf16[16,32,256]{2,1,0:T(8,128)(2,1)S(1)} %all_to_all.32.own0), channel_id=1, source_target_pairs={{0,384},{8,392},{16,400},{24,408},{32,416},{40,424},{48,432},{56,4... | collective-permute-start | bytes 786440 | tf_op jit(solution)/shard_map/ppermute | solution.py:36
  152.3 10.6 %collective-permute-start.12 = (bf16[16,32,256]{2,1,0:T(8,128)(2,1)S(1)}, bf16[16,32,256]{2,1,0:T(8,128)(2,1)S(1)}, u32[]{:S(2)}, u32[]{:S(2)}) collective-permute-start(bf16[16,32,256]{2,1,0:T(8,128)(2,1)S(1)} %all_to_all.32.own0), channel_id=1, source_target_pairs={{0,256},{8,264},{16,272},{24,280},{32,288},{40,296},{48,304},{56,3... | collective-permute-start | bytes 786440 | tf_op jit(solution)/shard_map/ppermute | solution.py:36
  154.2 15.3 %collective-permute-start.11 = (bf16[16,32,256]{2,1,0:T(8,128)(2,1)S(1)}, bf16[16,32,256]{2,1,0:T(8,128)(2,1)S(1)}, u32[]{:S(2)}, u32[]{:S(2)}) collective-permute-start(bf16[16,32,256]{2,1,0:T(8,128)(2,1)S(1)} %all_to_all.32.own0), channel_id=1, source_target_pairs={{0,128},{8,136},{16,144},{24,152},{32,160},{40,168},{48,176},{56,1... | collective-permute-start | bytes 786440 | tf_op jit(solution)/shard_map/ppermute | solution.py:36

commit v10 on v9

--- a/solution.py
+++ b/solution.py
@@ -45,7 +45,7 @@
 hbm = pl.BlockSpec(memory_space=pltpu.HBM)
 
 
-def call(kernel, shapes, in_specs, scratch, *operands, bytes_accessed=2**20):
+def call(kernel, shapes, in_specs, scratch, *operands, bytes_accessed=2**20, flops=0):
     return pl.pallas_call(
         kernel,
         out_shape=[jax.ShapeDtypeStruct(*shape) for shape in shapes],
@@ -54,7 +54,7 @@
         scratch_shapes=scratch,
         compiler_params=pltpu.CompilerParams(vmem_limit_bytes=12 * 2**20),
         cost_estimate=pl.CostEstimate(
-            flops=0, bytes_accessed=bytes_accessed, transcendentals=0
+            flops=flops, bytes_accessed=bytes_accessed, transcendentals=0
         ),
     )(*operands)
 
@@ -247,41 +247,51 @@
         sent_ref[k] = sent
 
 
-def final_kernel(
-    place_ref, size_ref, half_ref, across_ref, coeffs_ref, rotation_ref, block_ref,
-    own0, own1, own2, own3,
-    rotated_ref, cos_ref, sin_ref, orbitals_ref, step_ref, sems,
-):
+def pieces_of(place_ref, refs, step_ref, sems):
     copies = [
         pltpu.make_async_copy(ref, step_ref.at[steps], sems.at[steps])
-        for steps, ref in enumerate((own0, own1, own2, own3))
+        for steps, ref in enumerate(refs)
     ]
     for copy in copies:
         copy.start()
-    col = place_ref[4]
-    width = rotated_ref.shape[1]
-    rotated = rotation_ref[...]
-    cos_part, sin_part = block_ref[:, :width], block_ref[:, width:]
-    start = pl.multiple_of(col * width, width)
-    orbitals = coeffs_ref[:, pl.ds(start, width)].astype(f32)
+    width = step_ref.shape[-1]
     per = COLS // XS
+    count = step_ref.shape[1] // per
     for steps in range(XS):
         copies[steps].wait()
         source = lax.rem(place_ref[0] + XS - steps, XS)
-        count = step_ref.shape[1] // per
         for part in range(per):
-            k = source * per + part
-            step = step_ref[steps, part * count : (part + 1) * count].reshape(-1, width)
-            cells = half_ref[k]
-            cos_part = cos_part + small_product(cells[:, :width], step)
-            sin_part = sin_part + small_product(cells[:, width:], step)
-            rotated = rotated + small_product(across_ref[k, :, 2 * width : 3 * width], step)
-            cells = coeffs_ref[:, pl.ds(pl.multiple_of(k * width, width), width)]
-            orbitals = orbitals + small_product(cells, step)
+            cells = step_ref[steps, part * count : (part + 1) * count]
+            yield source * per + part, cells.reshape(-1, width)
+
+
+def orbitals_kernel(
+    place_ref, size_ref, across_ref, coeffs_ref, rotation_ref, own0, own1, own2, own3,
+    rotated_ref, orbitals_ref, step_ref, sems,
+):
+    width = rotated_ref.shape[1]
+    rotated = rotation_ref[...]
+    start = pl.multiple_of(place_ref[4] * width, width)
+    orbitals = coeffs_ref[:, pl.ds(start, width)].astype(f32)
+    for k, step in pieces_of(place_ref, (own0, own1, own2, own3), step_ref, sems):
+        rotated = rotated + small_product(across_ref[k, :, 2 * width : 3 * width], step)
+        cells = coeffs_ref[:, pl.ds(pl.multiple_of(k * width, width), width)]
+        orbitals = orbitals + small_product(cells, step)
     rotated_ref[...] = rotated
+    orbitals_ref[...] = within_rows(size_ref, orbitals).astype(bf16)
+
+
+def phases_kernel(
+    place_ref, half_ref, block_ref, own0, own1, own2, own3, cos_ref, sin_ref, step_ref, sems
+):
+    width = cos_ref.shape[1]
+    cos_part, sin_part = block_ref[:, :width], block_ref[:, width:]
+    for k, step in pieces_of(place_ref, (own0, own1, own2, own3), step_ref, sems):
+        cells = half_ref[k]
+        cos_part = cos_part + small_product(cells[:, :width], step)
+        sin_part = sin_part + small_product(cells[:, width:], step)
     cos_ref[...] = cos_part
     sin_ref[...] = sin_part
-    orbitals_ref[...] = within_rows(size_ref, orbitals).astype(bf16)
 
 
 def on_device(coeffs, rotation, phase_ops, block_links, atom_size):
@@ -419,28 +429,37 @@
         gen_rows,
         z_cols,
         z_block,
-        bytes_accessed=2**26,
+        flops=2**35,
     )
     half_rows = swap(half_sent, "cols")
-    return tuple(
-        call(
-            final_kernel,
-            [(block, f32)] * 3 + [((rows_dev, col_count), bf16)],
-            [smem] * 2 + [vmem] * 5 + [hbm] * XS,
-            [
-                pltpu.VMEM((XS, ZS * CORES) + block, bf16),
-                pltpu.SemaphoreType.DMA((XS,)),
-            ],
-            place,
-            atom_size,
-            half_rows,
-            across,
-            coeffs,
-            rotation,
-            half_block,
-            *steps_x,
-        )
-    )
+    panel_scratch = [
+        pltpu.VMEM((XS, ZS * CORES) + block, bf16),
+        pltpu.SemaphoreType.DMA((XS,)),
+    ]
+    rotated, orbitals = call(
+        orbitals_kernel,
+        [(block, f32), ((rows_dev, col_count), bf16)],
+        [smem] * 2 + [vmem] * 3 + [hbm] * XS,
+        panel_scratch,
+        place,
+        atom_size,
+        across,
+        coeffs,
+        rotation,
+        *steps_x,
+        flops=2**32,
+    )
+    phase_cos, phase_sin = call(
+        phases_kernel,
+        [(block, f32)] * 2,
+        [smem] + [vmem] * 2 + [hbm] * XS,
+        panel_scratch,
+        place,
+        half_rows,
+        half_block,
+        *steps_x,
+    )
+    return (rotated, phase_cos, phase_sin, orbitals)
 
 
 def solution(mesh):

time: 173 us -> 169 us (0.977); the launches traced: 172 us -> 166 us
  blocking collectives: 59.2 us -> 43 us
  starting transfers between devices: 58.7 us -> 66.2 us
  local copies, waits for them, and re-layouts: 3.78 us -> 6.71 us
  waiting for transfers between devices: 37.4 us -> 34.9 us
  Pallas kernels: 9.65 us -> 11.9 us
    all_to_all x4 -> x3, blocking collectives: 59.2 us -> 43 us  [swap(): lax.all_to_all(cells, axis, 0, 0, tiled=True, axis_index_groups=groups)]
    ppermute x9, waiting for transfers between devices: 32.4 us -> 23 us  [along_x(): lax.ppermute(cells, 'rows', [(i, (i + steps * line) % count) for i in ran...]
    all_to_all x2 -> x3, starting transfers between devices: 10.2 us -> 17.7 us  [swap(): lax.all_to_all(cells, axis, 0, 0, tiled=True, axis_index_groups=groups)]
    all_to_all x2 -> x3, waiting for transfers between devices: 0.01 us -> 6.9 us  [swap(): lax.all_to_all(cells, axis, 0, 0, tiled=True, axis_index_groups=groups)]
    unnamed x14 -> x18, local copies, waits for them, and re-layouts: 3.66 us -> 6.6 us
    pallas_call x7 -> x8, Pallas kernels: 9.65 us -> 11.9 us  [call(): pl.pallas_call(kernel, out_shape=[jax.ShapeDtypeStruct(*shape) for shape...]
  transfers between devices with their start and end apart: 16 -> 17, of which waited for: 10 -> 10; matrix products, arithmetic and copies ran while one was open for 0% -> 0% of each run, Pallas kernels for 1% -> 3%
where the time goes in v10:
time: 169 us; the launch traced here: 166 us
  starting transfers between devices  66.2 us (39%)
  blocking collectives  43 us (25%)
  waiting for transfers between devices  34.9 us (21%)
  Pallas kernels  11.9 us (7%)
  local copies, waits for them, and re-layouts  6.71 us (4%)
  other arithmetic  2.33 us (1%)
    all_to_all x3, blocking collectives, swap(): lax.all_to_all(cells, axis, 0, 0, tiled=True, axis_index_groups=groups)  43 us
    ppermute x9, waiting for transfers between devices, along_x(): lax.ppermute(cells, 'rows', [(i, (i + steps * line) % count) for i in ran...  23 us
    ppermute x9, starting transfers between devices, along_x(): lax.ppermute(cells, 'rows', [(i, (i + steps * line) % count) for i in ran...  22.8 us
    all_to_all x3, starting transfers between devices, swap(): lax.all_to_all(cells, axis, 0, 0, tiled=True, axis_index_groups=groups)  17.7 us
    ppermute x3, starting transfers between devices, other_core(): return lax.ppermute(cells, 'rows', [(i, i ^ 1) for i in range(count)])  14.9 us
    pallas_call x8, Pallas kernels, call(): pl.pallas_call(kernel, out_shape=[jax.ShapeDtypeStruct(*shape) for shape...  11.9 us
    ppermute x1, starting transfers between devices, on_device(): from_down = lax.ppermute(own_cols[:width], 'rows', down)  8.79 us
    all_to_all x3, waiting for transfers between devices, swap(): lax.all_to_all(cells, axis, 0, 0, tiled=True, axis_index_groups=groups)  6.9 us
  transfers between devices with their start and end apart: 17, of which 10 were waited for; matrix products, arithmetic and copies ran while one was open for 0% of the time, Pallas kernels for 3%

profile of v10, /device:TPU:1, one launch (start us, length us, event | category | flops | bytes accessed | tf_op | source)
XLA Modules:
  0.0 165.9 jit_solution(6104206495317874043)
XLA Ops:
  2.4 8.8 %collective-permute-start.1 = (bf16[256,256]{1,0:T(8,128)(2,1)S(1)}, bf16[256,256]{1,0:T(8,128)(2,1)S(1)}, u32[]{:S(2)}, u32[]{:S(2)}) collective-permute-start(bf16[256,256]{1,0:T(8,128)(2,1)S(1)} %dynamic-slice_select_fusion.cols_ref), channel_id=1, source_target_pairs={{8,0},{16,8},{24,16},{32,24},{40,32},{48,40},{56,48},{64,56},{72,6... | collective-permute-start | bytes 393224 | tf_op jit(solution)/shard_map/ppermute | solution.py:322
  19.2 8.8 %collective-permute-start.2 = (bf16[1024,256]{1,0:T(8,128)(2,1)S(1)}, bf16[1024,256]{1,0:T(8,128)(2,1)S(1)}, u32[]{:S(2)}, u32[]{:S(2)}) collective-permute-start(bf16[1024,256]{1,0:T(8,128)(2,1)S(1)} %get-tuple-element.41), channel_id=1, source_target_pairs={{0,8},{8,0},{16,24},{24,16},{32,40},{40,32},{48,56},{56,48},{64,72... | collective-permute-start | bytes 1572872 | tf_op jit(solution)/shard_map/ppermute | solution.py:31
  33.2 1.9 %collective-permute-start.4 = (bf16[272,512]{1,0:T(8,128)(2,1)S(1)}, bf16[272,512]{1,0:T(8,128)(2,1)S(1)}, u32[]{:S(2)}, u32[]{:S(2)}) collective-permute-start(bf16[272,512]{1,0:T(8,128)(2,1)S(1)} %get-tuple-element.49), channel_id=1, source_target_pairs={{0,256},{8,264},{16,272},{24,280},{32,288},{40,296},{48,304},{56,3... | collective-permute-start | bytes 835592 | tf_op jit(solution)/shard_map/ppermute | solution.py:36
  37.0 4.6 %collective-permute-start.6 = (bf16[272,512]{1,0:T(8,128)(2,1)S(1)}, bf16[272,512]{1,0:T(8,128)(2,1)S(1)}, u32[]{:S(2)}, u32[]{:S(2)}) collective-permute-start(bf16[272,512]{1,0:T(8,128)(2,1)S(1)} %get-tuple-element.51), channel_id=1, source_target_pairs={{0,384},{8,392},{16,400},{24,408},{32,416},{40,424},{48,432},{56,4... | collective-permute-start | bytes 835592 | tf_op jit(solution)/shard_map/ppermute | solution.py:36
  41.6 3.1 %collective-permute-done.4 = bf16[272,512]{1,0:T(8,128)(2,1)S(1)} collective-permute-done((bf16[272,512]{1,0:T(8,128)(2,1)S(1)}, bf16[272,512]{1,0:T(8,128)(2,1)S(1)}, u32[]{:S(2)}, u32[]{:S(2)}) %collective-permute-start.4) | collective-permute-done | bytes 278560 | tf_op jit(solution)/shard_map/ppermute | solution.py:36
  44.8 6.4 %collective-permute-done.5 = bf16[272,512]{1,0:T(8,128)(2,1)S(1)} collective-permute-done((bf16[272,512]{1,0:T(8,128)(2,1)S(1)}, bf16[272,512]{1,0:T(8,128)(2,1)S(1)}, u32[]{:S(2)}, u32[]{:S(2)}) %collective-permute-start.5) | collective-permute-done | bytes 278560 | tf_op jit(solution)/shard_map/ppermute | solution.py:36
  51.7 15.5 %all_to_all.30.got_ref = bf16[8,32,640]{2,1,0:T(8,128)(2,1)S(1)} all-to-all(bf16[8,32,640]{2,1,0:T(8,128)(2,1)S(1)} %pad_maximum_fusion.1), channel_id=1, replica_groups={{0,16,32,48,64,80,96,112},{8,24,40,56,72,88,104,120},{128,144,160,176,1..., dimensions={0} | all-to-all | bytes 655360 | tf_op jit(solution)/shard_map/all_to_all | solution.py:26
  68.0 12.6 %all_to_all.31 = bf16[8,32,512]{2,1,0:T(8,128)(2,1)S(1)} all-to-all(bf16[8,32,512]{2,1,0:T(8,128)(2,1)S(1)} %get-tuple-element.54), channel_id=1, replica_groups={{0,16,32,48,64,80,96,112},{8,24,40,56,72,88,104,120},{128,144,160,176,1..., dimensions={0} | all-to-all | bytes 524288 | tf_op jit(solution)/shard_map/all_to_all | solution.py:26
  80.6 6.8 %all-to-all-start.2 = ((bf16[8,32,896]{2,1,0:T(8,128)(2,1)}), bf16[8,32,896]{2,1,0:T(8,128)(2,1)S(1)}, u32[]{:S(2)}, u32[]{:S(2)}) async-start(bf16[8,32,896]{2,1,0:T(8,128)(2,1)} %get-tuple-element.56), calls=%async_computation.2 | async-start | bytes 917504 | tf_op jit(solution)/shard_map/all_to_all | solution.py:26
  91.2 3.4 %collective-permute-start.7 = (bf16[8,32,512]{2,1,0:T(8,128)(2,1)S(1)}, bf16[8,32,512]{2,1,0:T(8,128)(2,1)S(1)}, u32[]{:S(2)}, u32[]{:S(2)}) collective-permute-start(bf16[8,32,512]{2,1,0:T(8,128)(2,1)S(1)} %all_to_all.31), channel_id=1, source_target_pairs={{0,128},{8,136},{16,144},{24,152},{32,160},{40,168},{48,176},{56,1... | collective-permute-start | bytes 786440 | tf_op jit(solution)/shard_map/ppermute | solution.py:36
  94.6 3.3 %collective-permute-done.8 = bf16[8,32,512]{2,1,0:T(8,128)(2,1)S(1)} collective-permute-done((bf16[8,32,512]{2,1,0:T(8,128)(2,1)S(1)}, bf16[8,32,512]{2,1,0:T(8,128)(2,1)S(1)}, u32[]{:S(2)}, u32[]{:S(2)}) %collective-permute-start.8) | collective-permute-done | bytes 262176 | tf_op jit(solution)/shard_map/ppermute | solution.py:36
  97.9 6.8 %collective-permute-done.7 = bf16[8,32,512]{2,1,0:T(8,128)(2,1)S(1)} collective-permute-done((bf16[8,32,512]{2,1,0:T(8,128)(2,1)S(1)}, bf16[8,32,512]{2,1,0:T(8,128)(2,1)S(1)}, u32[]{:S(2)}, u32[]{:S(2)}) %collective-permute-start.7) | collective-permute-done | bytes 262176 | tf_op jit(solution)/shard_map/ppermute | solution.py:36
  104.9 4.2 %collective-permute-start.10 = (bf16[4,8,32,512]{3,2,1,0:T(8,128)(2,1)S(1)}, bf16[4,8,32,512]{3,2,1,0:T(8,128)(2,1)S(1)}, u32[]{:S(2)}, u32[]{:S(2)}) collective-permute-start(bf16[4,8,32,512]{3,2,1,0:T(8,128)(2,1)S(1)} %pad_maximum_fusion.own_ref), channel_id=1, source_target_pairs={{0,8},{8,0},{16,24},{24,16},{32,40},{40,32},{48,56},{56,48},{64,72... | collective-permute-start | bytes 3145736 | tf_op jit(solution)/shard_map/ppermute | solution.py:31
  109.1 2.3 %collective-permute-done.10.away_ref = bf16[4,8,32,512]{3,2,1,0:T(8,128)(2,1)S(1)} collective-permute-done((bf16[4,8,32,512]{3,2,1,0:T(8,128)(2,1)S(1)}, bf16[4,8,32,512]{3,2,1,0:T(8,128)(2,1)S(1)}, u32[]{:S(2)}, u32[]{:S(2)}) %collective-permute-start.10) | collective-permute-done | bytes 1048608 | tf_op jit(solution)/shard_map/ppermute | solution.py:31
  111.4 3.0 %shard_map.88 = (bf16[4,8,2,32,512]{4,3,2,1,0:T(8,128)(2,1)S(1)}, f32[8,32,256]{2,1,0:T(8,128)S(1)}, bf16[8,32,256]{2,1,0:T(8,128)(2,1)}, bf16[16,32,256]{2,1,0:T(8,128)(2,1)S(1)}) custom-call(s32[5]{0:T(128)S(1)} %stack.44.place_ref, bf16[8,32,896]{2,1,0:T(8,128)(2,1)S(1)} %all-to-all-done.2.across_ref, ...), custom_call_target="tpu_custom_call" | custom-call | bytes 1048576 | tf_op jit(solution)/shard_map/pallas_call | solution.py:49
  115.7 14.9 %all_to_all.32.own0 = bf16[16,32,256]{2,1,0:T(8,128)(2,1)S(1)} all-to-all(bf16[16,32,256]{2,1,0:T(8,128)(2,1)S(1)} %get-tuple-element.60), channel_id=1, replica_groups={{0,8,16,24,32,40,48,56,64,72,80,88,96,104,112,120},{128,136,144,152,160..., dimensions={0} | all-to-all | bytes 524288 | tf_op jit(solution)/shard_map/all_to_all | solution.py:26
  130.7 6.6 %all-to-all-start.4 = ((bf16[8,32,256]{2,1,0:T(8,128)(2,1)}), bf16[8,32,256]{2,1,0:T(8,128)(2,1)S(1)}, u32[]{:S(2)}, u32[]{:S(2)}) async-start(bf16[8,32,256]{2,1,0:T(8,128)(2,1)} %get-tuple-element.63), calls=%async_computation.4 | async-start | bytes 262144 | tf_op jit(solution)/shard_map/all_to_all | solution.py:26
  137.3 2.7 %collective-permute-start.13 = (bf16[16,32,256]{2,1,0:T(8,128)(2,1)S(1)}, bf16[16,32,256]{2,1,0:T(8,128)(2,1)S(1)}, u32[]{:S(2)}, u32[]{:S(2)}) collective-permute-start(bf16[16,32,256]{2,1,0:T(8,128)(2,1)S(1)} %all_to_all.32.own0), channel_id=1, source_target_pairs={{0,384},{8,392},{16,400},{24,408},{32,416},{40,424},{48,432},{56,4... | collective-permute-start | bytes 786440 | tf_op jit(solution)/shard_map/ppermute | solution.py:36
  142.0 2.5 %collective-permute-start.11 = (bf16[16,32,256]{2,1,0:T(8,128)(2,1)S(1)}, bf16[16,32,256]{2,1,0:T(8,128)(2,1)S(1)}, u32[]{:S(2)}, u32[]{:S(2)}) collective-permute-start(bf16[16,32,256]{2,1,0:T(8,128)(2,1)S(1)} %all_to_all.32.own0), channel_id=1, source_target_pairs={{0,128},{8,136},{16,144},{24,152},{32,160},{40,168},{48,176},{56,1... | collective-permute-start | bytes 786440 | tf_op jit(solution)/shard_map/ppermute | solution.py:36
  144.5 2.4 %all-to-all-done.4.square_ref = bf16[8,32,256]{2,1,0:T(8,128)(2,1)S(1)} async-done(((bf16[8,32,256]{2,1,0:T(8,128)(2,1)}), bf16[8,32,256]{2,1,0:T(8,128)(2,1)S(1)}, u32[]{:S(2)}, u32[]{:S(2)}) %all-to-all-start.4) | async-done | bytes 131104 | tf_op jit(solution)/shard_map/all_to_all | solution.py:26
  149.7 4.3 %all-to-all-start.5 = ((bf16[8,32,512]{2,1,0:T(8,128)(2,1)}), bf16[8,32,512]{2,1,0:T(8,128)(2,1)S(1)}, u32[]{:S(2)}, u32[]{:S(2)}) async-start(bf16[8,32,512]{2,1,0:T(8,128)(2,1)} %get-tuple-element.67), calls=%async_computation.5 | async-start | bytes 524288 | tf_op jit(solution)/shard_map/all_to_all | solution.py:26
  154.0 3.4 %collective-permute-done.11.own1 = bf16[16,32,256]{2,1,0:T(8,128)(2,1)S(1)} collective-permute-done((bf16[16,32,256]{2,1,0:T(8,128)(2,1)S(1)}, bf16[16,32,256]{2,1,0:T(8,128)(2,1)S(1)}, u32[]{:S(2)}, u32[]{:S(2)}) %collective-permute-start.11) | collective-permute-done | bytes 262176 | tf_op jit(solution)/shard_map/ppermute | solution.py:36
  157.3 2.3 %shard_map.89 = (f32[32,256]{1,0:T(8,128)}, bf16[256,256]{1,0:T(8,128)(2,1)}) custom-call(s32[5]{0:T(128)S(1)} %stack.44.place_ref, s32[2]{0:T(128)S(1)} %copy-done.6, bf16[8,32,896]{2,1,0:T(8,128)(2,1)S(1)} %all-to-all-done.2.across_ref, bf16[256,2048]{1,0:T(8,128)(2,1)S(1)} %copy-done.1, f32[32,256]{1,0:T(8,128)S(1)} %copy-done.3, ...), custom_call_target="tpu_custom_call" | custom-call | flops 4294967296 | bytes 1048576 | tf_op jit(solution)/shard_map/pallas_call | solution.py:49
  159.7 4.5 %all-to-all-done.5.half_ref = bf16[8,32,512]{2,1,0:T(8,128)(2,1)S(1)} async-done(((bf16[8,32,512]{2,1,0:T(8,128)(2,1)}), bf16[8,32,512]{2,1,0:T(8,128)(2,1)S(1)}, u32[]{:S(2)}, u32[]{:S(2)}) %all-to-all-start.5) | async-done | bytes 262176 | tf_op jit(solution)/shard_map/all_to_all | solution.py:26
  (54 shorter events, 29.9 us)
Async XLA Ops:
  2.4 15.6 %collective-permute-start.1 = (bf16[256,256]{1,0:T(8,128)(2,1)S(1)}, bf16[256,256]{1,0:T(8,128)(2,1)S(1)}, u32[]{:S(2)}, u32[]{:S(2)}) collective-permute-start(bf16[256,256]{1,0:T(8,128)(2,1)S(1)} %dynamic-slice_select_fusion.cols_ref), channel_id=1, source_target_pairs={{8,0},{16,8},{24,16},{32,24},{40,32},{48,40},{56,48},{64,56},{72,6... | collective-permute-start | bytes 393224 | tf_op jit(solution)/shard_map/ppermute | solution.py:322
  11.2 8.0 %collective-permute-start = (bf16[256,256]{1,0:T(8,128)(2,1)S(1)}, bf16[256,256]{1,0:T(8,128)(2,1)S(1)}, u32[]{:S(2)}, u32[]{:S(2)}) collective-permute-start(bf16[256,256]{1,0:T(8,128)(2,1)S(1)} %dynamic-slice_select_fusion.cols_ref), channel_id=1, source_target_pairs={{0,8},{8,16},{16,24},{24,32},{32,40},{40,48},{48,56},{56,64},{64,7... | collective-permute-start | bytes 393224 | tf_op jit(solution)/shard_map/ppermute | solution.py:321
  13.2 1.2 copy-start
  14.4 1.1 copy-start.2
  19.2 12.6 %collective-permute-start.2 = (bf16[1024,256]{1,0:T(8,128)(2,1)S(1)}, bf16[1024,256]{1,0:T(8,128)(2,1)S(1)}, u32[]{:S(2)}, u32[]{:S(2)}) collective-permute-start(bf16[1024,256]{1,0:T(8,128)(2,1)S(1)} %get-tuple-element.41), channel_id=1, source_target_pairs={{0,8},{8,0},{16,24},{24,16},{32,40},{40,32},{48,56},{56,48},{64,72... | collective-permute-start | bytes 1572872 | tf_op jit(solution)/shard_map/ppermute | solution.py:31
  28.4 3.4 %collective-permute-start.3 = (bf16[256,512]{1,0:T(8,128)(2,1)S(1)}, bf16[256,512]{1,0:T(8,128)(2,1)S(1)}, u32[]{:S(2)}, u32[]{:S(2)}) collective-permute-start(bf16[256,512]{1,0:T(8,128)(2,1)S(1)} %get-tuple-element.46.applied_ref), channel_id=1, source_target_pairs={{0,8},{8,0},{16,24},{24,16},{32,40},{40,32},{48,56},{56,48},{64,72... | collective-permute-start | bytes 786440 | tf_op jit(solution)/shard_map/ppermute | solution.py:31
  33.2 11.6 %collective-permute-start.4 = (bf16[272,512]{1,0:T(8,128)(2,1)S(1)}, bf16[272,512]{1,0:T(8,128)(2,1)S(1)}, u32[]{:S(2)}, u32[]{:S(2)}) collective-permute-start(bf16[272,512]{1,0:T(8,128)(2,1)S(1)} %get-tuple-element.49), channel_id=1, source_target_pairs={{0,256},{8,264},{16,272},{24,280},{32,288},{40,296},{48,304},{56,3... | collective-permute-start | bytes 835592 | tf_op jit(solution)/shard_map/ppermute | solution.py:36
  35.1 16.1 %collective-permute-start.5 = (bf16[272,512]{1,0:T(8,128)(2,1)S(1)}, bf16[272,512]{1,0:T(8,128)(2,1)S(1)}, u32[]{:S(2)}, u32[]{:S(2)}) collective-permute-start(bf16[272,512]{1,0:T(8,128)(2,1)S(1)} %get-tuple-element.50), channel_id=1, source_target_pairs={{0,128},{8,136},{16,144},{24,152},{32,160},{40,168},{48,176},{56,1... | collective-permute-start | bytes 835592 | tf_op jit(solution)/shard_map/ppermute | solution.py:36
  37.0 14.2 %collective-permute-start.6 = (bf16[272,512]{1,0:T(8,128)(2,1)S(1)}, bf16[272,512]{1,0:T(8,128)(2,1)S(1)}, u32[]{:S(2)}, u32[]{:S(2)}) collective-permute-start(bf16[272,512]{1,0:T(8,128)(2,1)S(1)} %get-tuple-element.51), channel_id=1, source_target_pairs={{0,384},{8,392},{16,400},{24,408},{32,416},{40,424},{48,432},{56,4... | collective-permute-start | bytes 835592 | tf_op jit(solution)/shard_map/ppermute | solution.py:36
  51.3 15.9 %copy-start.3 = (f32[32,256]{1,0:T(8,128)S(1)}, f32[32,256]{1,0:T(8,128)}, u32[]{:S(2)}) copy-start(f32[32,256]{1,0:T(8,128)} %rotation_ref.3) | copy-start | bytes 98308
  80.6 24.3 %all-to-all-start.2 = ((bf16[8,32,896]{2,1,0:T(8,128)(2,1)}), bf16[8,32,896]{2,1,0:T(8,128)(2,1)S(1)}, u32[]{:S(2)}, u32[]{:S(2)}) async-start(bf16[8,32,896]{2,1,0:T(8,128)(2,1)} %get-tuple-element.56), calls=%async_computation.2 | async-start | bytes 917504 | tf_op jit(solution)/shard_map/all_to_all | solution.py:26
  87.4 7.2 %collective-permute-start.9 = (bf16[8,32,512]{2,1,0:T(8,128)(2,1)S(1)}, bf16[8,32,512]{2,1,0:T(8,128)(2,1)S(1)}, u32[]{:S(2)}, u32[]{:S(2)}) collective-permute-start(bf16[8,32,512]{2,1,0:T(8,128)(2,1)S(1)} %all_to_all.31), channel_id=1, source_target_pairs={{0,384},{8,392},{16,400},{24,408},{32,416},{40,424},{48,432},{56,4... | collective-permute-start | bytes 786440 | tf_op jit(solution)/shard_map/ppermute | solution.py:36
  89.3 8.6 %collective-permute-start.8 = (bf16[8,32,512]{2,1,0:T(8,128)(2,1)S(1)}, bf16[8,32,512]{2,1,0:T(8,128)(2,1)S(1)}, u32[]{:S(2)}, u32[]{:S(2)}) collective-permute-start(bf16[8,32,512]{2,1,0:T(8,128)(2,1)S(1)} %all_to_all.31), channel_id=1, source_target_pairs={{0,256},{8,264},{16,272},{24,280},{32,288},{40,296},{48,304},{56,3... | collective-permute-start | bytes 786440 | tf_op jit(solution)/shard_map/ppermute | solution.py:36
  91.2 13.5 %collective-permute-start.7 = (bf16[8,32,512]{2,1,0:T(8,128)(2,1)S(1)}, bf16[8,32,512]{2,1,0:T(8,128)(2,1)S(1)}, u32[]{:S(2)}, u32[]{:S(2)}) collective-permute-start(bf16[8,32,512]{2,1,0:T(8,128)(2,1)S(1)} %all_to_all.31), channel_id=1, source_target_pairs={{0,128},{8,136},{16,144},{24,152},{32,160},{40,168},{48,176},{56,1... | collective-permute-start | bytes 786440 | tf_op jit(solution)/shard_map/ppermute | solution.py:36
  104.9 6.5 %collective-permute-start.10 = (bf16[4,8,32,512]{3,2,1,0:T(8,128)(2,1)S(1)}, bf16[4,8,32,512]{3,2,1,0:T(8,128)(2,1)S(1)}, u32[]{:S(2)}, u32[]{:S(2)}) collective-permute-start(bf16[4,8,32,512]{3,2,1,0:T(8,128)(2,1)S(1)} %pad_maximum_fusion.own_ref), channel_id=1, source_target_pairs={{0,8},{8,0},{16,24},{24,16},{32,40},{40,32},{48,56},{56,48},{64,72... | collective-permute-start | bytes 3145736 | tf_op jit(solution)/shard_map/ppermute | solution.py:31
  114.4 1.4 copy-start.7
  130.7 16.2 %all-to-all-start.4 = ((bf16[8,32,256]{2,1,0:T(8,128)(2,1)}), bf16[8,32,256]{2,1,0:T(8,128)(2,1)S(1)}, u32[]{:S(2)}, u32[]{:S(2)}) async-start(bf16[8,32,256]{2,1,0:T(8,128)(2,1)} %get-tuple-element.63), calls=%async_computation.4 | async-start | bytes 262144 | tf_op jit(solution)/shard_map/all_to_all | solution.py:26
  137.3 16.6 %collective-permute-start.13 = (bf16[16,32,256]{2,1,0:T(8,128)(2,1)S(1)}, bf16[16,32,256]{2,1,0:T(8,128)(2,1)S(1)}, u32[]{:S(2)}, u32[]{:S(2)}) collective-permute-start(bf16[16,32,256]{2,1,0:T(8,128)(2,1)S(1)} %all_to_all.32.own0), channel_id=1, source_target_pairs={{0,384},{8,392},{16,400},{24,408},{32,416},{40,424},{48,432},{56,4... | collective-permute-start | bytes 786440 | tf_op jit(solution)/shard_map/ppermute | solution.py:36
  140.0 13.9 %collective-permute-start.12 = (bf16[16,32,256]{2,1,0:T(8,128)(2,1)S(1)}, bf16[16,32,256]{2,1,0:T(8,128)(2,1)S(1)}, u32[]{:S(2)}, u32[]{:S(2)}) collective-permute-start(bf16[16,32,256]{2,1,0:T(8,128)(2,1)S(1)} %all_to_all.32.own0), channel_id=1, source_target_pairs={{0,256},{8,264},{16,272},{24,280},{32,288},{40,296},{48,304},{56,3... | collective-permute-start | bytes 786440 | tf_op jit(solution)/shard_map/ppermute | solution.py:36
  142.0 15.4 %collective-permute-start.11 = (bf16[16,32,256]{2,1,0:T(8,128)(2,1)S(1)}, bf16[16,32,256]{2,1,0:T(8,128)(2,1)S(1)}, u32[]{:S(2)}, u32[]{:S(2)}) collective-permute-start(bf16[16,32,256]{2,1,0:T(8,128)(2,1)S(1)} %all_to_all.32.own0), channel_id=1, source_target_pairs={{0,128},{8,136},{16,144},{24,152},{32,160},{40,168},{48,176},{56,1... | collective-permute-start | bytes 786440 | tf_op jit(solution)/shard_map/ppermute | solution.py:36
  146.9 1.6 copy-start.8
  148.5 8.8 %copy-start.1 = (bf16[256,2048]{1,0:T(8,128)(2,1)S(1)}, bf16[256,2048]{1,0:T(8,128)(2,1)}, u32[]{:S(2)}) copy-start(bf16[256,2048]{1,0:T(8,128)(2,1)} %coeffs_ref.2) | copy-start | bytes 3145732
  148.5 8.8 %copy-start.6 = (s32[2]{0:T(128)S(1)}, s32[2]{0:T(128)}, u32[]{:S(2)}) copy-start(s32[2]{0:T(128)} %size_ref.3) | copy-start | bytes 28
  149.7 14.5 %all-to-all-start.5 = ((bf16[8,32,512]{2,1,0:T(8,128)(2,1)}), bf16[8,32,512]{2,1,0:T(8,128)(2,1)S(1)}, u32[]{:S(2)}, u32[]{:S(2)}) async-start(bf16[8,32,512]{2,1,0:T(8,128)(2,1)} %get-tuple-element.67), calls=%async_computation.5 | async-start | bytes 524288 | tf_op jit(solution)/shard_map/all_to_all | solution.py:26
  (2 other events, 1.3 us)

commit v11 on v10

--- a/solution.py
+++ b/solution.py
@@ -19,7 +19,9 @@
 
 
 z_groups = [[row_index(x, z, k) for z in range(ZS)] for x in range(XS) for k in range(CORES)]
-plane_groups = [[row_index(x, z, k) for z in range(ZS) for k in range(CORES)] for x in range(XS)]
+z_order = [4, 5, 6, 7, 0, 1, 2, 3]
+col_order = [4, 5, 6, 7, 3, 2, 1, 0]
+plane_groups = [[row_index(x, z, k) for z in z_order for k in range(CORES)] for x in range(XS)]
 
 
 def swap(cells, axis, groups=None):
@@ -71,25 +73,27 @@
 
 
 def turn_kernel(
-    rows, place_ref, size_ref, links_ref, coeffs_ref, ops_ref, own_ref, far_ref, gated_ref
+    rows, place_ref, links_ref, live_ref, coeffs_ref, ops_ref, own_ref, far_ref, gated_ref
 ):
     core = place_ref[1]
     lanes = 128
+    live = live_ref[...] > 0
     for start in range(0, coeffs_ref.shape[1], lanes):
         cells = coeffs_ref[:, start : start + lanes].astype(f32).T
         for offset in range(0, lanes, CORES * rows):
             first = cells[offset : offset + rows]
             second = cells[offset + rows : offset + 2 * rows]
             where = pl.ds((start + offset) // CORES, rows)
-            own_ref[where, :] = jnp.where(core == 0, first, second).astype(bf16)
-            far_ref[where, :] = jnp.where(core == 0, second, first).astype(bf16)
+            own = jnp.where(core == 0, first, second)
+            far = jnp.where(core == 0, second, first)
+            own_ref[where, :] = jnp.where(live, own, 0.0).astype(bf16)
+            far_ref[where, :] = jnp.where(live, far, 0.0).astype(bf16)
     phases, blocks, span, size, _ = ops_ref.shape
-    within = lax.broadcasted_iota(jnp.int32, (size, size), 0)
     for b in range(blocks):
         for t in range(span):
-            kept = within < jnp.where(links_ref[b, t] != 0, size_ref[b], 0)
+            link = links_ref[b, t] != 0
             for p in range(phases):
-                cells = jnp.where(kept, ops_ref[p, b, t].astype(f32), 0.0)
+                cells = jnp.where(link, ops_ref[p, b, t].astype(f32), 0.0)
                 gated_ref[p, b, :, t * size : (t + 1) * size] = cells.astype(bf16)
 
 
@@ -193,8 +197,8 @@
 
 
 def square_kernel(
-    scale, place_ref, across_ref, own_ref, away_ref,
-    z_ref, rows_ref, square_ref, step_ref, diag_ref, turned_ref, sems,
+    scale, place_ref, across_ref, block_ref, own_ref, away_ref,
+    base_ref, sent_ref, step_ref, z_ref, rows_ref, diag_ref, turned_ref, sems,
 ):
     copies = gathered(place_ref, own_ref, away_ref, z_ref, sems)
     mine, low, col = place_ref[2], place_ref[3], place_ref[4]
@@ -221,26 +225,39 @@
         rows_ref[k] = (cos_part + sin_part) * scale
     across_diag = [diag_ref[p, pl.ds(col, 1), :] for p in range(2)]
     square = jnp.zeros((rows, width), f32)
+    base = block_ref[...]
     for k in range(COLS):
         landed(copies, k)
-        cells = chunk(z_ref, k).astype(f32)
+        near = rows_ref[k].astype(bf16)
+        panel = chunk(z_ref, k)
+        base = base - small_product(near, panel)
+        cells = panel.astype(f32)
         cos_part = cells[:, :width] * (across_diag[0] - turned_ref[0, :, k : k + 1])
         sin_part = cells[:, width:] * (across_diag[1] - turned_ref[1, :, k : k + 1])
         cells = ((cos_part + sin_part) * scale).astype(bf16)
-        square = square + small_product(rows_ref[k].astype(bf16), cells)
+        square = square + small_product(near, cells)
+    base_ref[...] = base
     step = (rows_ref[col] + 0.5 * square).astype(bf16)
-    square = square.astype(bf16)
-    for k in range(square_ref.shape[0]):
-        square_ref[k] = square
     for k in range(step_ref.shape[0]):
         step_ref[k] = step
-
-
-def half_kernel(square_ref, rows_ref, z_ref, block_ref, half_ref, sent_ref):
-    total = block_ref[...]
+    square = square.astype(bf16)
     for k in range(COLS):
-        back = (0.5 * square_ref[k].astype(f32) - rows_ref[k]).astype(bf16)
-        total = total + small_product(back, chunk(z_ref, k))
+        panel = chunk(z_ref, k)
+        for p in range(2):
+            cells = lax.dot_general(
+                square,
+                panel[:, p * width : (p + 1) * width],
+                (((1,), (1,)), ((), ())),
+                preferred_element_type=f32,
+            )
+            sent_ref[k, :, p * width : (p + 1) * width] = cells.astype(bf16)
+
+
+def half_kernel(got_ref, base_ref, half_ref, sent_ref):
+    total = got_ref[0].astype(f32)
+    for k in range(1, COLS):
+        total = total + got_ref[k].astype(f32)
+    total = base_ref[...] + 0.5 * total
     half_ref[...] = total
     sent = total.astype(bf16)
     for k in range(COLS):
@@ -261,7 +278,8 @@
         copies[steps].wait()
         source = lax.rem(place_ref[0] + XS - steps, XS)
         for part in range(per):
-            cells = step_ref[steps, part * count : (part + 1) * count]
+            first = z_order.index(part * ZS // per) * CORES
+            cells = step_ref[steps, first : first + count]
             yield source * per + part, cells.reshape(-1, width)
 
 
@@ -287,7 +305,8 @@
     width = cos_ref.shape[1]
     cos_part, sin_part = block_ref[:, :width], block_ref[:, width:]
     for k, step in pieces_of(place_ref, (own0, own1, own2, own3), step_ref, sems):
-        cells = half_ref[k]
+        where = sum(jnp.where(k == col, i, 0) for i, col in enumerate(col_order))
+        cells = half_ref[where]
         cos_part = cos_part + small_product(cells[:, :width], step)
         sin_part = sin_part + small_product(cells[:, width:], step)
     cos_ref[...] = cos_part
@@ -320,17 +339,17 @@
     down = [((i + 1) % rows_axis, i) for i in range(rows_axis)]
     from_up = lax.ppermute(own_cols[rows_dev - width :], "rows", up)
     from_down = lax.ppermute(own_cols[:width], "rows", down)
-    turn_coeffs, own_cols = lax.optimization_barrier((coeffs, own_cols))
+    turn_coeffs, own_cols, live_rows = lax.optimization_barrier((coeffs, own_cols, live_rows))
     half_shape = ((orbital_count // CORES, rows_dev), bf16)
     phases, blocks = phase_ops.shape[:2]
     own_turned, far_turned, gated = call(
         functools.partial(turn_kernel, row_count),
         [half_shape] * 2 + [((phases, blocks, block_size, span_blocks * block_size), bf16)],
-        [smem] * 3 + [vmem] * 2,
+        [smem] * 2 + [vmem] * 3,
         [],
         place,
-        atom_size,
         block_links,
+        live_rows.astype(f32)[None, :],
         turn_coeffs,
         phase_ops,
         bytes_accessed=2**26,
@@ -396,22 +415,24 @@
     stacked, across = lax.optimization_barrier((jnp.stack(panels), across))
     away = other_core(stacked)
     block = (row_count, col_count)
-    z_cols, gen_rows, square, step = call(
+    base, square, step = call(
         functools.partial(square_kernel, scale_factor),
         [
-            ((XS, ZS, CORES, row_count, both), bf16),
-            ((COLS,) + block, f32),
-            ((COLS,) + block, bf16),
+            ((row_count, both), f32),
+            ((COLS, row_count, both), bf16),
             ((ZS * CORES,) + block, bf16),
         ],
-        [smem, vmem] + [hbm] * 2,
+        [smem] + [vmem] * 2 + [hbm] * 2,
         [
+            pltpu.VMEM((XS, ZS, CORES, row_count, both), bf16),
+            pltpu.VMEM((COLS,) + block, f32),
             pltpu.VMEM((2, COLS, col_count), f32),
             pltpu.VMEM((2, col_count, COLS), f32),
             pltpu.SemaphoreType.DMA((XS, 2)),
         ],
         place,
         across,
+        z_block,
         stacked,
         away,
     )
@@ -423,15 +444,13 @@
     half_block, half_sent = call(
         half_kernel,
         [((row_count, both), f32), ((COLS, row_count, both), bf16)],
-        [vmem] * 4,
+        [vmem] * 2,
         [],
         square,
-        gen_rows,
-        z_cols,
-        z_block,
+        base,
         flops=2**35,
     )
-    half_rows = swap(half_sent, "cols")
+    half_rows = swap(half_sent, "cols", [col_order])
     panel_scratch = [
         pltpu.VMEM((XS, ZS * CORES) + block, bf16),
         pltpu.SemaphoreType.DMA((XS,)),

time: 169 us -> 163 us (0.964)
  waiting for transfers between devices: 34.9 us -> 30.7 us
  local copies, waits for them, and re-layouts: 6.71 us -> 3.76 us
  starting transfers between devices: 66.2 us -> 68.8 us
    all_to_all x3, waiting for transfers between devices: 6.9 us -> 3.52 us  [swap(): lax.all_to_all(cells, axis, 0, 0, tiled=True, axis_index_groups=groups)]
    unnamed x18 -> x12, local copies, waits for them, and re-layouts: 6.6 us -> 3.65 us
    all_to_all x3, starting transfers between devices: 17.7 us -> 20.1 us  [swap(): lax.all_to_all(cells, axis, 0, 0, tiled=True, axis_index_groups=groups)]
  transfers between devices with their start and end apart: 17 -> 17, of which waited for: 10 -> 9; matrix products, arithmetic and copies ran while one was open for 0% -> 0% of each run, Pallas kernels for 3% -> 3%
where the time goes in v11:
time: 163 us; the launch traced here: 161 us
  starting transfers between devices  68.8 us (42%)
  blocking collectives  42.4 us (26%)
  waiting for transfers between devices  30.7 us (19%)
  Pallas kernels  12.2 us (7%)
  local copies, waits for them, and re-layouts  3.76 us (2%)
  other arithmetic  1.68 us (1%)
    all_to_all x3, blocking collectives, swap(): lax.all_to_all(cells, axis, 0, 0, tiled=True, axis_index_groups=groups)  42.4 us
    ppermute x9, starting transfers between devices, along_x(): lax.ppermute(cells, 'rows', [(i, (i + steps * line) % count) for i in ran...  23 us
    ppermute x9, waiting for transfers between devices, along_x(): lax.ppermute(cells, 'rows', [(i, (i + steps * line) % count) for i in ran...  21.5 us
    all_to_all x3, starting transfers between devices, swap(): lax.all_to_all(cells, axis, 0, 0, tiled=True, axis_index_groups=groups)  20.1 us
    ppermute x3, starting transfers between devices, other_core(): return lax.ppermute(cells, 'rows', [(i, i ^ 1) for i in range(count)])  14.9 us
    pallas_call x8, Pallas kernels, call(): pl.pallas_call(kernel, out_shape=[jax.ShapeDtypeStruct(*shape) for shape...  12.2 us
    ppermute x1, starting transfers between devices, on_device(): from_down = lax.ppermute(own_cols[:width], 'rows', down)  8.79 us
    ppermute x3, waiting for transfers between devices, other_core(): return lax.ppermute(cells, 'rows', [(i, i ^ 1) for i in range(count)])  3.77 us
  transfers between devices with their start and end apart: 17, of which 9 were waited for; matrix products, arithmetic and copies ran while one was open for 0% of the time, Pallas kernels for 3%

profile of v11, /device:TPU:1, one launch (start us, length us, event | category | flops | bytes accessed | tf_op | source)
XLA Modules:
  0.0 160.5 jit_solution(1479290057844683468)
XLA Ops:
  2.4 8.8 %collective-permute-start.1 = (bf16[256,256]{1,0:T(8,128)(2,1)S(1)}, bf16[256,256]{1,0:T(8,128)(2,1)S(1)}, u32[]{:S(2)}, u32[]{:S(2)}) collective-permute-start(bf16[256,256]{1,0:T(8,128)(2,1)S(1)} %dynamic-slice_select_fusion.cols_ref), channel_id=1, source_target_pairs={{8,0},{16,8},{24,16},{32,24},{40,32},{48,40},{56,48},{64,56},{72,6... | collective-permute-start | bytes 393224 | tf_op jit(solution)/shard_map/ppermute | solution.py:341
  11.2 1.9 %collective-permute-start = (bf16[256,256]{1,0:T(8,128)(2,1)S(1)}, bf16[256,256]{1,0:T(8,128)(2,1)S(1)}, u32[]{:S(2)}, u32[]{:S(2)}) collective-permute-start(bf16[256,256]{1,0:T(8,128)(2,1)S(1)} %dynamic-slice_select_fusion.cols_ref), channel_id=1, source_target_pairs={{0,8},{8,16},{16,24},{24,32},{32,40},{40,48},{48,56},{56,64},{64,7... | collective-permute-start | bytes 393224 | tf_op jit(solution)/shard_map/ppermute | solution.py:340
  19.2 8.8 %collective-permute-start.2 = (bf16[1024,256]{1,0:T(8,128)(2,1)S(1)}, bf16[1024,256]{1,0:T(8,128)(2,1)S(1)}, u32[]{:S(2)}, u32[]{:S(2)}) collective-permute-start(bf16[1024,256]{1,0:T(8,128)(2,1)S(1)} %get-tuple-element.42), channel_id=1, source_target_pairs={{0,8},{8,0},{16,24},{24,16},{32,40},{40,32},{48,56},{56,48},{64,72... | collective-permute-start | bytes 1572872 | tf_op jit(solution)/shard_map/ppermute | solution.py:33
  28.4 1.9 %collective-permute-start.3 = (bf16[256,512]{1,0:T(8,128)(2,1)S(1)}, bf16[256,512]{1,0:T(8,128)(2,1)S(1)}, u32[]{:S(2)}, u32[]{:S(2)}) collective-permute-start(bf16[256,512]{1,0:T(8,128)(2,1)S(1)} %get-tuple-element.47.applied_ref), channel_id=1, source_target_pairs={{0,8},{8,0},{16,24},{24,16},{32,40},{40,32},{48,56},{56,48},{64,72... | collective-permute-start | bytes 786440 | tf_op jit(solution)/shard_map/ppermute | solution.py:33
  37.0 4.6 %collective-permute-start.6 = (bf16[272,512]{1,0:T(8,128)(2,1)S(1)}, bf16[272,512]{1,0:T(8,128)(2,1)S(1)}, u32[]{:S(2)}, u32[]{:S(2)}) collective-permute-start(bf16[272,512]{1,0:T(8,128)(2,1)S(1)} %get-tuple-element.52), channel_id=1, source_target_pairs={{0,384},{8,392},{16,400},{24,408},{32,416},{40,424},{48,432},{56,4... | collective-permute-start | bytes 835592 | tf_op jit(solution)/shard_map/ppermute | solution.py:38
  41.6 3.1 %collective-permute-done.4 = bf16[272,512]{1,0:T(8,128)(2,1)S(1)} collective-permute-done((bf16[272,512]{1,0:T(8,128)(2,1)S(1)}, bf16[272,512]{1,0:T(8,128)(2,1)S(1)}, u32[]{:S(2)}, u32[]{:S(2)}) %collective-permute-start.4) | collective-permute-done | bytes 278560 | tf_op jit(solution)/shard_map/ppermute | solution.py:38
  44.8 6.4 %collective-permute-done.5 = bf16[272,512]{1,0:T(8,128)(2,1)S(1)} collective-permute-done((bf16[272,512]{1,0:T(8,128)(2,1)S(1)}, bf16[272,512]{1,0:T(8,128)(2,1)S(1)}, u32[]{:S(2)}, u32[]{:S(2)}) %collective-permute-start.5) | collective-permute-done | bytes 278560 | tf_op jit(solution)/shard_map/ppermute | solution.py:38
  51.7 15.5 %all_to_all.30.got_ref = bf16[8,32,640]{2,1,0:T(8,128)(2,1)S(1)} all-to-all(bf16[8,32,640]{2,1,0:T(8,128)(2,1)S(1)} %pad_maximum_fusion.1), channel_id=1, replica_groups={{0,16,32,48,64,80,96,112},{8,24,40,56,72,88,104,120},{128,144,160,176,1..., dimensions={0} | all-to-all | bytes 655360 | tf_op jit(solution)/shard_map/all_to_all | solution.py:28
  68.0 12.6 %all_to_all.31 = bf16[8,32,512]{2,1,0:T(8,128)(2,1)S(1)} all-to-all(bf16[8,32,512]{2,1,0:T(8,128)(2,1)S(1)} %get-tuple-element.55), channel_id=1, replica_groups={{0,16,32,48,64,80,96,112},{8,24,40,56,72,88,104,120},{128,144,160,176,1..., dimensions={0} | all-to-all | bytes 524288 | tf_op jit(solution)/shard_map/all_to_all | solution.py:28
  80.6 6.8 %all-to-all-start.2 = ((bf16[8,32,896]{2,1,0:T(8,128)(2,1)}), bf16[8,32,896]{2,1,0:T(8,128)(2,1)S(1)}, u32[]{:S(2)}, u32[]{:S(2)}) async-start(bf16[8,32,896]{2,1,0:T(8,128)(2,1)} %get-tuple-element.57), calls=%async_computation.2 | async-start | bytes 917504 | tf_op jit(solution)/shard_map/all_to_all | solution.py:28
  91.3 3.4 %collective-permute-start.7 = (bf16[8,32,512]{2,1,0:T(8,128)(2,1)S(1)}, bf16[8,32,512]{2,1,0:T(8,128)(2,1)S(1)}, u32[]{:S(2)}, u32[]{:S(2)}) collective-permute-start(bf16[8,32,512]{2,1,0:T(8,128)(2,1)S(1)} %all_to_all.31), channel_id=1, source_target_pairs={{0,128},{8,136},{16,144},{24,152},{32,160},{40,168},{48,176},{56,1... | collective-permute-start | bytes 786440 | tf_op jit(solution)/shard_map/ppermute | solution.py:38
  94.6 3.3 %collective-permute-done.8 = bf16[8,32,512]{2,1,0:T(8,128)(2,1)S(1)} collective-permute-done((bf16[8,32,512]{2,1,0:T(8,128)(2,1)S(1)}, bf16[8,32,512]{2,1,0:T(8,128)(2,1)S(1)}, u32[]{:S(2)}, u32[]{:S(2)}) %collective-permute-start.8) | collective-permute-done | bytes 262176 | tf_op jit(solution)/shard_map/ppermute | solution.py:38
  98.0 6.8 %collective-permute-done.7 = bf16[8,32,512]{2,1,0:T(8,128)(2,1)S(1)} collective-permute-done((bf16[8,32,512]{2,1,0:T(8,128)(2,1)S(1)}, bf16[8,32,512]{2,1,0:T(8,128)(2,1)S(1)}, u32[]{:S(2)}, u32[]{:S(2)}) %collective-permute-start.7) | collective-permute-done | bytes 262176 | tf_op jit(solution)/shard_map/ppermute | solution.py:38
  104.9 4.2 %collective-permute-start.10 = (bf16[4,8,32,512]{3,2,1,0:T(8,128)(2,1)S(1)}, bf16[4,8,32,512]{3,2,1,0:T(8,128)(2,1)S(1)}, u32[]{:S(2)}, u32[]{:S(2)}) collective-permute-start(bf16[4,8,32,512]{3,2,1,0:T(8,128)(2,1)S(1)} %pad_maximum_fusion.own_ref), channel_id=1, source_target_pairs={{0,8},{8,0},{16,24},{24,16},{32,40},{40,32},{48,56},{56,48},{64,72... | collective-permute-start | bytes 3145736 | tf_op jit(solution)/shard_map/ppermute | solution.py:33
  109.1 2.3 %collective-permute-done.10.away_ref = bf16[4,8,32,512]{3,2,1,0:T(8,128)(2,1)S(1)} collective-permute-done((bf16[4,8,32,512]{3,2,1,0:T(8,128)(2,1)S(1)}, bf16[4,8,32,512]{3,2,1,0:T(8,128)(2,1)S(1)}, u32[]{:S(2)}, u32[]{:S(2)}) %collective-permute-start.10) | collective-permute-done | bytes 1048608 | tf_op jit(solution)/shard_map/ppermute | solution.py:33
  111.4 3.7 %shard_map.88 = (f32[32,512]{1,0:T(8,128)S(1)}, bf16[8,32,512]{2,1,0:T(8,128)(2,1)}, bf16[16,32,256]{2,1,0:T(8,128)(2,1)S(1)}) custom-call(s32[5]{0:T(128)S(1)} %stack.44.place_ref, bf16[8,32,896]{2,1,0:T(8,128)(2,1)S(1)} %all-to-all-done.2.across_ref, f32[32,512]{1,0:T(8,128)S(1)} %get-tuple-element.59.block_ref, ...), custom_call_target="tpu_custom_call" | custom-call | bytes 1048576 | tf_op jit(solution)/shard_map/pallas_call | solution.py:51
  115.1 14.4 %all_to_all.32.own0 = bf16[16,32,256]{2,1,0:T(8,128)(2,1)S(1)} all-to-all(bf16[16,32,256]{2,1,0:T(8,128)(2,1)S(1)} %get-tuple-element.62), channel_id=1, replica_groups={{64,72,80,88,96,104,112,120,0,8,16,24,32,40,48,56},{192,200,208,216,224..., dimensions={0} | all-to-all | bytes 524288 | tf_op jit(solution)/shard_map/all_to_all | solution.py:28
  129.5 6.7 %all-to-all-start.4 = ((bf16[8,32,512]{2,1,0:T(8,128)(2,1)}), bf16[8,32,512]{2,1,0:T(8,128)(2,1)S(1)}, u32[]{:S(2)}, u32[]{:S(2)}) async-start(bf16[8,32,512]{2,1,0:T(8,128)(2,1)} %get-tuple-element.65), calls=%async_computation.4 | async-start | bytes 524288 | tf_op jit(solution)/shard_map/all_to_all | solution.py:28
  136.1 3.0 %collective-permute-start.13 = (bf16[16,32,256]{2,1,0:T(8,128)(2,1)S(1)}, bf16[16,32,256]{2,1,0:T(8,128)(2,1)S(1)}, u32[]{:S(2)}, u32[]{:S(2)}) collective-permute-start(bf16[16,32,256]{2,1,0:T(8,128)(2,1)S(1)} %all_to_all.32.own0), channel_id=1, source_target_pairs={{0,384},{8,392},{16,400},{24,408},{32,416},{40,424},{48,432},{56,4... | collective-permute-start | bytes 786440 | tf_op jit(solution)/shard_map/ppermute | solution.py:38
  139.2 1.9 %collective-permute-start.12 = (bf16[16,32,256]{2,1,0:T(8,128)(2,1)S(1)}, bf16[16,32,256]{2,1,0:T(8,128)(2,1)S(1)}, u32[]{:S(2)}, u32[]{:S(2)}) collective-permute-start(bf16[16,32,256]{2,1,0:T(8,128)(2,1)S(1)} %all_to_all.32.own0), channel_id=1, source_target_pairs={{0,256},{8,264},{16,272},{24,280},{32,288},{40,296},{48,304},{56,3... | collective-permute-start | bytes 786440 | tf_op jit(solution)/shard_map/ppermute | solution.py:38
  141.1 2.5 %collective-permute-start.11 = (bf16[16,32,256]{2,1,0:T(8,128)(2,1)S(1)}, bf16[16,32,256]{2,1,0:T(8,128)(2,1)S(1)}, u32[]{:S(2)}, u32[]{:S(2)}) collective-permute-start(bf16[16,32,256]{2,1,0:T(8,128)(2,1)S(1)} %all_to_all.32.own0), channel_id=1, source_target_pairs={{0,128},{8,136},{16,144},{24,152},{32,160},{40,168},{48,176},{56,1... | collective-permute-start | bytes 786440 | tf_op jit(solution)/shard_map/ppermute | solution.py:38
  143.6 3.5 %all-to-all-done.4.got_ref = bf16[8,32,512]{2,1,0:T(8,128)(2,1)S(1)} async-done(((bf16[8,32,512]{2,1,0:T(8,128)(2,1)}), bf16[8,32,512]{2,1,0:T(8,128)(2,1)S(1)}, u32[]{:S(2)}, u32[]{:S(2)}) %all-to-all-start.4) | async-done | bytes 262176 | tf_op jit(solution)/shard_map/all_to_all | solution.py:28
  147.8 6.6 %all-to-all-start.5 = ((bf16[8,32,512]{2,1,0:T(8,128)(2,1)}), bf16[8,32,512]{2,1,0:T(8,128)(2,1)S(1)}, u32[]{:S(2)}, u32[]{:S(2)}) async-start(bf16[8,32,512]{2,1,0:T(8,128)(2,1)} %get-tuple-element.67), calls=%async_computation.5 | async-start | bytes 524288 | tf_op jit(solution)/shard_map/all_to_all | solution.py:28
  156.4 2.3 %shard_map.89 = (f32[32,256]{1,0:T(8,128)}, bf16[256,256]{1,0:T(8,128)(2,1)}) custom-call(s32[5]{0:T(128)S(1)} %stack.44.place_ref, s32[2]{0:T(128)S(1)} %copy-done.5, bf16[8,32,896]{2,1,0:T(8,128)(2,1)S(1)} %all-to-all-done.2.across_ref, bf16[256,2048]{1,0:T(8,128)(2,1)S(1)} %copy-done.1, f32[32,256]{1,0:T(8,128)S(1)} %copy-done.3, ...), custom_call_target="tpu_custom_call" | custom-call | flops 4294967296 | bytes 1048576 | tf_op jit(solution)/shard_map/pallas_call | solution.py:51
  (49 shorter events, 24.6 us)
Async XLA Ops:
  0.6 0.7 copy-start.5
  2.4 14.9 %collective-permute-start.1 = (bf16[256,256]{1,0:T(8,128)(2,1)S(1)}, bf16[256,256]{1,0:T(8,128)(2,1)S(1)}, u32[]{:S(2)}, u32[]{:S(2)}) collective-permute-start(bf16[256,256]{1,0:T(8,128)(2,1)S(1)} %dynamic-slice_select_fusion.cols_ref), channel_id=1, source_target_pairs={{8,0},{16,8},{24,16},{32,24},{40,32},{48,40},{56,48},{64,56},{72,6... | collective-permute-start | bytes 393224 | tf_op jit(solution)/shard_map/ppermute | solution.py:341
  11.2 8.0 %collective-permute-start = (bf16[256,256]{1,0:T(8,128)(2,1)S(1)}, bf16[256,256]{1,0:T(8,128)(2,1)S(1)}, u32[]{:S(2)}, u32[]{:S(2)}) collective-permute-start(bf16[256,256]{1,0:T(8,128)(2,1)S(1)} %dynamic-slice_select_fusion.cols_ref), channel_id=1, source_target_pairs={{0,8},{8,16},{16,24},{24,32},{32,40},{40,48},{48,56},{56,64},{64,7... | collective-permute-start | bytes 393224 | tf_op jit(solution)/shard_map/ppermute | solution.py:340
  13.3 0.7 copy-start.4
  13.9 1.2 copy-start
  15.2 1.1 copy-start.2
  19.2 12.6 %collective-permute-start.2 = (bf16[1024,256]{1,0:T(8,128)(2,1)S(1)}, bf16[1024,256]{1,0:T(8,128)(2,1)S(1)}, u32[]{:S(2)}, u32[]{:S(2)}) collective-permute-start(bf16[1024,256]{1,0:T(8,128)(2,1)S(1)} %get-tuple-element.42), channel_id=1, source_target_pairs={{0,8},{8,0},{16,24},{24,16},{32,40},{40,32},{48,56},{56,48},{64,72... | collective-permute-start | bytes 1572872 | tf_op jit(solution)/shard_map/ppermute | solution.py:33
  28.4 3.4 %collective-permute-start.3 = (bf16[256,512]{1,0:T(8,128)(2,1)S(1)}, bf16[256,512]{1,0:T(8,128)(2,1)S(1)}, u32[]{:S(2)}, u32[]{:S(2)}) collective-permute-start(bf16[256,512]{1,0:T(8,128)(2,1)S(1)} %get-tuple-element.47.applied_ref), channel_id=1, source_target_pairs={{0,8},{8,0},{16,24},{24,16},{32,40},{40,32},{48,56},{56,48},{64,72... | collective-permute-start | bytes 786440 | tf_op jit(solution)/shard_map/ppermute | solution.py:33
  33.2 11.6 %collective-permute-start.4 = (bf16[272,512]{1,0:T(8,128)(2,1)S(1)}, bf16[272,512]{1,0:T(8,128)(2,1)S(1)}, u32[]{:S(2)}, u32[]{:S(2)}) collective-permute-start(bf16[272,512]{1,0:T(8,128)(2,1)S(1)} %get-tuple-element.50), channel_id=1, source_target_pairs={{0,256},{8,264},{16,272},{24,280},{32,288},{40,296},{48,304},{56,3... | collective-permute-start | bytes 835592 | tf_op jit(solution)/shard_map/ppermute | solution.py:38
  35.1 16.1 %collective-permute-start.5 = (bf16[272,512]{1,0:T(8,128)(2,1)S(1)}, bf16[272,512]{1,0:T(8,128)(2,1)S(1)}, u32[]{:S(2)}, u32[]{:S(2)}) collective-permute-start(bf16[272,512]{1,0:T(8,128)(2,1)S(1)} %get-tuple-element.51), channel_id=1, source_target_pairs={{0,128},{8,136},{16,144},{24,152},{32,160},{40,168},{48,176},{56,1... | collective-permute-start | bytes 835592 | tf_op jit(solution)/shard_map/ppermute | solution.py:38
  37.0 14.2 %collective-permute-start.6 = (bf16[272,512]{1,0:T(8,128)(2,1)S(1)}, bf16[272,512]{1,0:T(8,128)(2,1)S(1)}, u32[]{:S(2)}, u32[]{:S(2)}) collective-permute-start(bf16[272,512]{1,0:T(8,128)(2,1)S(1)} %get-tuple-element.52), channel_id=1, source_target_pairs={{0,384},{8,392},{16,400},{24,408},{32,416},{40,424},{48,432},{56,4... | collective-permute-start | bytes 835592 | tf_op jit(solution)/shard_map/ppermute | solution.py:38
  51.7 15.5 %copy-start.3 = (f32[32,256]{1,0:T(8,128)S(1)}, f32[32,256]{1,0:T(8,128)}, u32[]{:S(2)}) copy-start(f32[32,256]{1,0:T(8,128)} %rotation_ref.3) | copy-start | bytes 98308
  80.6 24.3 %all-to-all-start.2 = ((bf16[8,32,896]{2,1,0:T(8,128)(2,1)}), bf16[8,32,896]{2,1,0:T(8,128)(2,1)S(1)}, u32[]{:S(2)}, u32[]{:S(2)}) async-start(bf16[8,32,896]{2,1,0:T(8,128)(2,1)} %get-tuple-element.57), calls=%async_computation.2 | async-start | bytes 917504 | tf_op jit(solution)/shard_map/all_to_all | solution.py:28
  87.4 7.2 %collective-permute-start.9 = (bf16[8,32,512]{2,1,0:T(8,128)(2,1)S(1)}, bf16[8,32,512]{2,1,0:T(8,128)(2,1)S(1)}, u32[]{:S(2)}, u32[]{:S(2)}) collective-permute-start(bf16[8,32,512]{2,1,0:T(8,128)(2,1)S(1)} %all_to_all.31), channel_id=1, source_target_pairs={{0,384},{8,392},{16,400},{24,408},{32,416},{40,424},{48,432},{56,4... | collective-permute-start | bytes 786440 | tf_op jit(solution)/shard_map/ppermute | solution.py:38
  89.3 8.6 %collective-permute-start.8 = (bf16[8,32,512]{2,1,0:T(8,128)(2,1)S(1)}, bf16[8,32,512]{2,1,0:T(8,128)(2,1)S(1)}, u32[]{:S(2)}, u32[]{:S(2)}) collective-permute-start(bf16[8,32,512]{2,1,0:T(8,128)(2,1)S(1)} %all_to_all.31), channel_id=1, source_target_pairs={{0,256},{8,264},{16,272},{24,280},{32,288},{40,296},{48,304},{56,3... | collective-permute-start | bytes 786440 | tf_op jit(solution)/shard_map/ppermute | solution.py:38
  91.3 13.5 %collective-permute-start.7 = (bf16[8,32,512]{2,1,0:T(8,128)(2,1)S(1)}, bf16[8,32,512]{2,1,0:T(8,128)(2,1)S(1)}, u32[]{:S(2)}, u32[]{:S(2)}) collective-permute-start(bf16[8,32,512]{2,1,0:T(8,128)(2,1)S(1)} %all_to_all.31), channel_id=1, source_target_pairs={{0,128},{8,136},{16,144},{24,152},{32,160},{40,168},{48,176},{56,1... | collective-permute-start | bytes 786440 | tf_op jit(solution)/shard_map/ppermute | solution.py:38
  104.9 6.5 %collective-permute-start.10 = (bf16[4,8,32,512]{3,2,1,0:T(8,128)(2,1)S(1)}, bf16[4,8,32,512]{3,2,1,0:T(8,128)(2,1)S(1)}, u32[]{:S(2)}, u32[]{:S(2)}) collective-permute-start(bf16[4,8,32,512]{3,2,1,0:T(8,128)(2,1)S(1)} %pad_maximum_fusion.own_ref), channel_id=1, source_target_pairs={{0,8},{8,0},{16,24},{24,16},{32,40},{40,32},{48,56},{56,48},{64,72... | collective-permute-start | bytes 3145736 | tf_op jit(solution)/shard_map/ppermute | solution.py:33
  129.5 17.6 %all-to-all-start.4 = ((bf16[8,32,512]{2,1,0:T(8,128)(2,1)}), bf16[8,32,512]{2,1,0:T(8,128)(2,1)S(1)}, u32[]{:S(2)}, u32[]{:S(2)}) async-start(bf16[8,32,512]{2,1,0:T(8,128)(2,1)} %get-tuple-element.65), calls=%async_computation.4 | async-start | bytes 524288 | tf_op jit(solution)/shard_map/all_to_all | solution.py:28
  136.1 18.4 %collective-permute-start.13 = (bf16[16,32,256]{2,1,0:T(8,128)(2,1)S(1)}, bf16[16,32,256]{2,1,0:T(8,128)(2,1)S(1)}, u32[]{:S(2)}, u32[]{:S(2)}) collective-permute-start(bf16[16,32,256]{2,1,0:T(8,128)(2,1)S(1)} %all_to_all.32.own0), channel_id=1, source_target_pairs={{0,384},{8,392},{16,400},{24,408},{32,416},{40,424},{48,432},{56,4... | collective-permute-start | bytes 786440 | tf_op jit(solution)/shard_map/ppermute | solution.py:38
  139.2 15.3 %collective-permute-start.12 = (bf16[16,32,256]{2,1,0:T(8,128)(2,1)S(1)}, bf16[16,32,256]{2,1,0:T(8,128)(2,1)S(1)}, u32[]{:S(2)}, u32[]{:S(2)}) collective-permute-start(bf16[16,32,256]{2,1,0:T(8,128)(2,1)S(1)} %all_to_all.32.own0), channel_id=1, source_target_pairs={{0,256},{8,264},{16,272},{24,280},{32,288},{40,296},{48,304},{56,3... | collective-permute-start | bytes 786440 | tf_op jit(solution)/shard_map/ppermute | solution.py:38
  141.1 15.3 %collective-permute-start.11 = (bf16[16,32,256]{2,1,0:T(8,128)(2,1)S(1)}, bf16[16,32,256]{2,1,0:T(8,128)(2,1)S(1)}, u32[]{:S(2)}, u32[]{:S(2)}) collective-permute-start(bf16[16,32,256]{2,1,0:T(8,128)(2,1)S(1)} %all_to_all.32.own0), channel_id=1, source_target_pairs={{0,128},{8,136},{16,144},{24,152},{32,160},{40,168},{48,176},{56,1... | collective-permute-start | bytes 786440 | tf_op jit(solution)/shard_map/ppermute | solution.py:38
  147.1 9.3 %copy-start.1 = (bf16[256,2048]{1,0:T(8,128)(2,1)S(1)}, bf16[256,2048]{1,0:T(8,128)(2,1)}, u32[]{:S(2)}) copy-start(bf16[256,2048]{1,0:T(8,128)(2,1)} %coeffs_ref.2) | copy-start | bytes 3145732
  147.8 10.9 %all-to-all-start.5 = ((bf16[8,32,512]{2,1,0:T(8,128)(2,1)}), bf16[8,32,512]{2,1,0:T(8,128)(2,1)S(1)}, u32[]{:S(2)}, u32[]{:S(2)}) async-start(bf16[8,32,512]{2,1,0:T(8,128)(2,1)} %get-tuple-element.67), calls=%async_computation.5 | async-start | bytes 524288 | tf_op jit(solution)/shard_map/all_to_all | solution.py:28

commit v12 on v11

--- a/solution.py
+++ b/solution.py
@@ -354,7 +354,7 @@
         phase_ops,
         bytes_accessed=2**26,
     )
-    from_up, from_down, far_turned = lax.optimization_barrier((from_up, from_down, far_turned))
+    from_down, from_up, far_turned = lax.optimization_barrier((from_down, from_up, far_turned))
     far_turned = other_core(far_turned)
     applied, own_diag = call(
         applied_kernel,

time: 163 us -> 160 us (0.982)
  waiting for transfers between devices: 30.7 us -> 26.4 us
    ppermute x1, starting transfers between devices: 1.92 us -> 5.39 us  [on_device(): from_up = lax.ppermute(own_cols[rows_dev - width:], 'rows', up)]
    ppermute x1, starting transfers between devices: 8.79 us -> 5.32 us  [on_device(): from_down = lax.ppermute(own_cols[:width], 'rows', down)]
    ppermute x9, waiting for transfers between devices: 21.5 us -> 19.3 us  [along_x(): lax.ppermute(cells, 'rows', [(i, (i + steps * line) % count) for i in ran...]
    ppermute x1, waiting for transfers between devices: 1.88 us -> 0.01 us  [on_device(): from_up = lax.ppermute(own_cols[rows_dev - width:], 'rows', up)]
    ppermute x9, starting transfers between devices: 23 us -> 24.9 us  [along_x(): lax.ppermute(cells, 'rows', [(i, (i + steps * line) % count) for i in ran...]
where the time goes in v12:
time: 160 us; the launch traced here: 157 us
  starting transfers between devices  70 us (44%)
  blocking collectives  42.4 us (26%)
  waiting for transfers between devices  26.4 us (16%)
  Pallas kernels  12.2 us (8%)
  local copies, waits for them, and re-layouts  3.76 us (2%)
  other arithmetic  1.68 us (1%)
    all_to_all x3, blocking collectives, swap(): lax.all_to_all(cells, axis, 0, 0, tiled=True, axis_index_groups=groups)  42.4 us
    ppermute x9, starting transfers between devices, along_x(): lax.ppermute(cells, 'rows', [(i, (i + steps * line) % count) for i in ran...  24.9 us
    all_to_all x3, starting transfers between devices, swap(): lax.all_to_all(cells, axis, 0, 0, tiled=True, axis_index_groups=groups)  20.1 us
    ppermute x9, waiting for transfers between devices, along_x(): lax.ppermute(cells, 'rows', [(i, (i + steps * line) % count) for i in ran...  19.3 us
    ppermute x3, starting transfers between devices, other_core(): return lax.ppermute(cells, 'rows', [(i, i ^ 1) for i in range(count)])  14.3 us
    pallas_call x8, Pallas kernels, call(): pl.pallas_call(kernel, out_shape=[jax.ShapeDtypeStruct(*shape) for shape...  12.2 us
    ppermute x1, starting transfers between devices, on_device(): from_up = lax.ppermute(own_cols[rows_dev - width:], 'rows', up)  5.39 us
    ppermute x1, starting transfers between devices, on_device(): from_down = lax.ppermute(own_cols[:width], 'rows', down)  5.32 us
  transfers between devices with their start and end apart: 17, of which 9 were waited for; matrix products, arithmetic and copies ran while one was open for 0% of the time, Pallas kernels for 3%

profile of v12, /device:TPU:1, one launch (start us, length us, event | category | flops | bytes accessed | tf_op | source)
XLA Modules:
  0.0 157.4 jit_solution(7692081077706026146)
XLA Ops:
  2.4 5.4 %collective-permute-start.1 = (bf16[256,256]{1,0:T(8,128)(2,1)S(1)}, bf16[256,256]{1,0:T(8,128)(2,1)S(1)}, u32[]{:S(2)}, u32[]{:S(2)}) collective-permute-start(bf16[256,256]{1,0:T(8,128)(2,1)S(1)} %dynamic-slice_select_fusion.cols_ref), channel_id=1, source_target_pairs={{0,8},{8,16},{16,24},{24,32},{32,40},{40,48},{48,56},{56,64},{64,7... | collective-permute-start | bytes 393224 | tf_op jit(solution)/shard_map/ppermute | solution.py:340
  7.8 5.3 %collective-permute-start = (bf16[256,256]{1,0:T(8,128)(2,1)S(1)}, bf16[256,256]{1,0:T(8,128)(2,1)S(1)}, u32[]{:S(2)}, u32[]{:S(2)}) collective-permute-start(bf16[256,256]{1,0:T(8,128)(2,1)S(1)} %dynamic-slice_select_fusion.cols_ref), channel_id=1, source_target_pairs={{8,0},{16,8},{24,16},{32,24},{40,32},{48,40},{56,48},{64,56},{72,6... | collective-permute-start | bytes 393224 | tf_op jit(solution)/shard_map/ppermute | solution.py:341
  17.3 7.2 %collective-permute-start.2 = (bf16[1024,256]{1,0:T(8,128)(2,1)S(1)}, bf16[1024,256]{1,0:T(8,128)(2,1)S(1)}, u32[]{:S(2)}, u32[]{:S(2)}) collective-permute-start(bf16[1024,256]{1,0:T(8,128)(2,1)S(1)} %get-tuple-element.42), channel_id=1, source_target_pairs={{0,8},{8,0},{16,24},{24,16},{32,40},{40,32},{48,56},{56,48},{64,72... | collective-permute-start | bytes 1572872 | tf_op jit(solution)/shard_map/ppermute | solution.py:33
  29.7 2.4 %collective-permute-start.4 = (bf16[272,512]{1,0:T(8,128)(2,1)S(1)}, bf16[272,512]{1,0:T(8,128)(2,1)S(1)}, u32[]{:S(2)}, u32[]{:S(2)}) collective-permute-start(bf16[272,512]{1,0:T(8,128)(2,1)S(1)} %get-tuple-element.50), channel_id=1, source_target_pairs={{0,256},{8,264},{16,272},{24,280},{32,288},{40,296},{48,304},{56,3... | collective-permute-start | bytes 835592 | tf_op jit(solution)/shard_map/ppermute | solution.py:38
  32.2 2.5 %collective-permute-start.5 = (bf16[272,512]{1,0:T(8,128)(2,1)S(1)}, bf16[272,512]{1,0:T(8,128)(2,1)S(1)}, u32[]{:S(2)}, u32[]{:S(2)}) collective-permute-start(bf16[272,512]{1,0:T(8,128)(2,1)S(1)} %get-tuple-element.51), channel_id=1, source_target_pairs={{0,128},{8,136},{16,144},{24,152},{32,160},{40,168},{48,176},{56,1... | collective-permute-start | bytes 835592 | tf_op jit(solution)/shard_map/ppermute | solution.py:38
  34.7 4.0 %collective-permute-start.6 = (bf16[272,512]{1,0:T(8,128)(2,1)S(1)}, bf16[272,512]{1,0:T(8,128)(2,1)S(1)}, u32[]{:S(2)}, u32[]{:S(2)}) collective-permute-start(bf16[272,512]{1,0:T(8,128)(2,1)S(1)} %get-tuple-element.52), channel_id=1, source_target_pairs={{0,384},{8,392},{16,400},{24,408},{32,416},{40,424},{48,432},{56,4... | collective-permute-start | bytes 835592 | tf_op jit(solution)/shard_map/ppermute | solution.py:38
  38.7 2.6 %collective-permute-done.4 = bf16[272,512]{1,0:T(8,128)(2,1)S(1)} collective-permute-done((bf16[272,512]{1,0:T(8,128)(2,1)S(1)}, bf16[272,512]{1,0:T(8,128)(2,1)S(1)}, u32[]{:S(2)}, u32[]{:S(2)}) %collective-permute-start.4) | collective-permute-done | bytes 278560 | tf_op jit(solution)/shard_map/ppermute | solution.py:38
  41.4 6.3 %collective-permute-done.5 = bf16[272,512]{1,0:T(8,128)(2,1)S(1)} collective-permute-done((bf16[272,512]{1,0:T(8,128)(2,1)S(1)}, bf16[272,512]{1,0:T(8,128)(2,1)S(1)}, u32[]{:S(2)}, u32[]{:S(2)}) %collective-permute-start.5) | collective-permute-done | bytes 278560 | tf_op jit(solution)/shard_map/ppermute | solution.py:38
  48.2 15.5 %all_to_all.30.got_ref = bf16[8,32,640]{2,1,0:T(8,128)(2,1)S(1)} all-to-all(bf16[8,32,640]{2,1,0:T(8,128)(2,1)S(1)} %pad_maximum_fusion.1), channel_id=1, replica_groups={{0,16,32,48,64,80,96,112},{8,24,40,56,72,88,104,120},{128,144,160,176,1..., dimensions={0} | all-to-all | bytes 655360 | tf_op jit(solution)/shard_map/all_to_all | solution.py:28
  64.5 12.6 %all_to_all.31 = bf16[8,32,512]{2,1,0:T(8,128)(2,1)S(1)} all-to-all(bf16[8,32,512]{2,1,0:T(8,128)(2,1)S(1)} %get-tuple-element.55), channel_id=1, replica_groups={{0,16,32,48,64,80,96,112},{8,24,40,56,72,88,104,120},{128,144,160,176,1..., dimensions={0} | all-to-all | bytes 524288 | tf_op jit(solution)/shard_map/all_to_all | solution.py:28
  77.1 6.8 %all-to-all-start.2 = ((bf16[8,32,896]{2,1,0:T(8,128)(2,1)}), bf16[8,32,896]{2,1,0:T(8,128)(2,1)S(1)}, u32[]{:S(2)}, u32[]{:S(2)}) async-start(bf16[8,32,896]{2,1,0:T(8,128)(2,1)} %get-tuple-element.57), calls=%async_computation.2 | async-start | bytes 917504 | tf_op jit(solution)/shard_map/all_to_all | solution.py:28
  85.9 3.5 %collective-permute-start.8 = (bf16[8,32,512]{2,1,0:T(8,128)(2,1)S(1)}, bf16[8,32,512]{2,1,0:T(8,128)(2,1)S(1)}, u32[]{:S(2)}, u32[]{:S(2)}) collective-permute-start(bf16[8,32,512]{2,1,0:T(8,128)(2,1)S(1)} %all_to_all.31), channel_id=1, source_target_pairs={{0,256},{8,264},{16,272},{24,280},{32,288},{40,296},{48,304},{56,3... | collective-permute-start | bytes 786440 | tf_op jit(solution)/shard_map/ppermute | solution.py:38
  89.4 2.8 %collective-permute-start.7 = (bf16[8,32,512]{2,1,0:T(8,128)(2,1)S(1)}, bf16[8,32,512]{2,1,0:T(8,128)(2,1)S(1)}, u32[]{:S(2)}, u32[]{:S(2)}) collective-permute-start(bf16[8,32,512]{2,1,0:T(8,128)(2,1)S(1)} %all_to_all.31), channel_id=1, source_target_pairs={{0,128},{8,136},{16,144},{24,152},{32,160},{40,168},{48,176},{56,1... | collective-permute-start | bytes 786440 | tf_op jit(solution)/shard_map/ppermute | solution.py:38
  94.5 6.3 %collective-permute-done.7 = bf16[8,32,512]{2,1,0:T(8,128)(2,1)S(1)} collective-permute-done((bf16[8,32,512]{2,1,0:T(8,128)(2,1)S(1)}, bf16[8,32,512]{2,1,0:T(8,128)(2,1)S(1)}, u32[]{:S(2)}, u32[]{:S(2)}) %collective-permute-start.7) | collective-permute-done | bytes 262176 | tf_op jit(solution)/shard_map/ppermute | solution.py:38
  100.9 5.2 %collective-permute-start.10 = (bf16[4,8,32,512]{3,2,1,0:T(8,128)(2,1)S(1)}, bf16[4,8,32,512]{3,2,1,0:T(8,128)(2,1)S(1)}, u32[]{:S(2)}, u32[]{:S(2)}) collective-permute-start(bf16[4,8,32,512]{3,2,1,0:T(8,128)(2,1)S(1)} %pad_maximum_fusion.own_ref), channel_id=1, source_target_pairs={{0,8},{8,0},{16,24},{24,16},{32,40},{40,32},{48,56},{56,48},{64,72... | collective-permute-start | bytes 3145736 | tf_op jit(solution)/shard_map/ppermute | solution.py:33
  108.4 3.7 %shard_map.88 = (f32[32,512]{1,0:T(8,128)S(1)}, bf16[8,32,512]{2,1,0:T(8,128)(2,1)}, bf16[16,32,256]{2,1,0:T(8,128)(2,1)S(1)}) custom-call(s32[5]{0:T(128)S(1)} %stack.44.place_ref, bf16[8,32,896]{2,1,0:T(8,128)(2,1)S(1)} %all-to-all-done.2.across_ref, f32[32,512]{1,0:T(8,128)S(1)} %get-tuple-element.59.block_ref, ...), custom_call_target="tpu_custom_call" | custom-call | bytes 1048576 | tf_op jit(solution)/shard_map/pallas_call | solution.py:51
  112.1 14.4 %all_to_all.32.own0 = bf16[16,32,256]{2,1,0:T(8,128)(2,1)S(1)} all-to-all(bf16[16,32,256]{2,1,0:T(8,128)(2,1)S(1)} %get-tuple-element.62), channel_id=1, replica_groups={{64,72,80,88,96,104,112,120,0,8,16,24,32,40,48,56},{192,200,208,216,224..., dimensions={0} | all-to-all | bytes 524288 | tf_op jit(solution)/shard_map/all_to_all | solution.py:28
  126.4 6.7 %all-to-all-start.4 = ((bf16[8,32,512]{2,1,0:T(8,128)(2,1)}), bf16[8,32,512]{2,1,0:T(8,128)(2,1)S(1)}, u32[]{:S(2)}, u32[]{:S(2)}) async-start(bf16[8,32,512]{2,1,0:T(8,128)(2,1)} %get-tuple-element.65), calls=%async_computation.4 | async-start | bytes 524288 | tf_op jit(solution)/shard_map/all_to_all | solution.py:28
  133.1 2.9 %collective-permute-start.13 = (bf16[16,32,256]{2,1,0:T(8,128)(2,1)S(1)}, bf16[16,32,256]{2,1,0:T(8,128)(2,1)S(1)}, u32[]{:S(2)}, u32[]{:S(2)}) collective-permute-start(bf16[16,32,256]{2,1,0:T(8,128)(2,1)S(1)} %all_to_all.32.own0), channel_id=1, source_target_pairs={{0,384},{8,392},{16,400},{24,408},{32,416},{40,424},{48,432},{56,4... | collective-permute-start | bytes 786440 | tf_op jit(solution)/shard_map/ppermute | solution.py:38
  136.0 2.4 %collective-permute-start.12 = (bf16[16,32,256]{2,1,0:T(8,128)(2,1)S(1)}, bf16[16,32,256]{2,1,0:T(8,128)(2,1)S(1)}, u32[]{:S(2)}, u32[]{:S(2)}) collective-permute-start(bf16[16,32,256]{2,1,0:T(8,128)(2,1)S(1)} %all_to_all.32.own0), channel_id=1, source_target_pairs={{0,256},{8,264},{16,272},{24,280},{32,288},{40,296},{48,304},{56,3... | collective-permute-start | bytes 786440 | tf_op jit(solution)/shard_map/ppermute | solution.py:38
  138.4 2.4 %collective-permute-start.11 = (bf16[16,32,256]{2,1,0:T(8,128)(2,1)S(1)}, bf16[16,32,256]{2,1,0:T(8,128)(2,1)S(1)}, u32[]{:S(2)}, u32[]{:S(2)}) collective-permute-start(bf16[16,32,256]{2,1,0:T(8,128)(2,1)S(1)} %all_to_all.32.own0), channel_id=1, source_target_pairs={{0,128},{8,136},{16,144},{24,152},{32,160},{40,168},{48,176},{56,1... | collective-permute-start | bytes 786440 | tf_op jit(solution)/shard_map/ppermute | solution.py:38
  140.9 3.2 %all-to-all-done.4.got_ref = bf16[8,32,512]{2,1,0:T(8,128)(2,1)S(1)} async-done(((bf16[8,32,512]{2,1,0:T(8,128)(2,1)}), bf16[8,32,512]{2,1,0:T(8,128)(2,1)S(1)}, u32[]{:S(2)}, u32[]{:S(2)}) %all-to-all-start.4) | async-done | bytes 262176 | tf_op jit(solution)/shard_map/all_to_all | solution.py:28
  144.8 6.6 %all-to-all-start.5 = ((bf16[8,32,512]{2,1,0:T(8,128)(2,1)}), bf16[8,32,512]{2,1,0:T(8,128)(2,1)S(1)}, u32[]{:S(2)}, u32[]{:S(2)}) async-start(bf16[8,32,512]{2,1,0:T(8,128)(2,1)} %get-tuple-element.67), calls=%async_computation.5 | async-start | bytes 524288 | tf_op jit(solution)/shard_map/all_to_all | solution.py:28
  153.2 2.3 %shard_map.89 = (f32[32,256]{1,0:T(8,128)}, bf16[256,256]{1,0:T(8,128)(2,1)}) custom-call(s32[5]{0:T(128)S(1)} %stack.44.place_ref, s32[2]{0:T(128)S(1)} %copy-done.5, bf16[8,32,896]{2,1,0:T(8,128)(2,1)S(1)} %all-to-all-done.2.across_ref, bf16[256,2048]{1,0:T(8,128)(2,1)S(1)} %copy-done.1, f32[32,256]{1,0:T(8,128)S(1)} %copy-done.3, ...), custom_call_target="tpu_custom_call" | custom-call | flops 4294967296 | bytes 1048576 | tf_op jit(solution)/shard_map/pallas_call | solution.py:51
  (49 shorter events, 23.4 us)
Async XLA Ops:
  0.6 0.7 copy-start.5
  2.4 14.9 %collective-permute-start.1 = (bf16[256,256]{1,0:T(8,128)(2,1)S(1)}, bf16[256,256]{1,0:T(8,128)(2,1)S(1)}, u32[]{:S(2)}, u32[]{:S(2)}) collective-permute-start(bf16[256,256]{1,0:T(8,128)(2,1)S(1)} %dynamic-slice_select_fusion.cols_ref), channel_id=1, source_target_pairs={{0,8},{8,16},{16,24},{24,32},{32,40},{40,48},{48,56},{56,64},{64,7... | collective-permute-start | bytes 393224 | tf_op jit(solution)/shard_map/ppermute | solution.py:340
  7.8 9.6 %collective-permute-start = (bf16[256,256]{1,0:T(8,128)(2,1)S(1)}, bf16[256,256]{1,0:T(8,128)(2,1)S(1)}, u32[]{:S(2)}, u32[]{:S(2)}) collective-permute-start(bf16[256,256]{1,0:T(8,128)(2,1)S(1)} %dynamic-slice_select_fusion.cols_ref), channel_id=1, source_target_pairs={{8,0},{16,8},{24,16},{32,24},{40,32},{48,40},{56,48},{64,56},{72,6... | collective-permute-start | bytes 393224 | tf_op jit(solution)/shard_map/ppermute | solution.py:341
  13.3 0.7 copy-start.4
  13.9 1.2 copy-start
  15.2 1.1 copy-start.2
  17.3 11.1 %collective-permute-start.2 = (bf16[1024,256]{1,0:T(8,128)(2,1)S(1)}, bf16[1024,256]{1,0:T(8,128)(2,1)S(1)}, u32[]{:S(2)}, u32[]{:S(2)}) collective-permute-start(bf16[1024,256]{1,0:T(8,128)(2,1)S(1)} %get-tuple-element.42), channel_id=1, source_target_pairs={{0,8},{8,0},{16,24},{24,16},{32,40},{40,32},{48,56},{56,48},{64,72... | collective-permute-start | bytes 1572872 | tf_op jit(solution)/shard_map/ppermute | solution.py:33
  25.0 3.4 %collective-permute-start.3 = (bf16[256,512]{1,0:T(8,128)(2,1)S(1)}, bf16[256,512]{1,0:T(8,128)(2,1)S(1)}, u32[]{:S(2)}, u32[]{:S(2)}) collective-permute-start(bf16[256,512]{1,0:T(8,128)(2,1)S(1)} %get-tuple-element.47.applied_ref), channel_id=1, source_target_pairs={{0,8},{8,0},{16,24},{24,16},{32,40},{40,32},{48,56},{56,48},{64,72... | collective-permute-start | bytes 786440 | tf_op jit(solution)/shard_map/ppermute | solution.py:33
  29.7 11.6 %collective-permute-start.4 = (bf16[272,512]{1,0:T(8,128)(2,1)S(1)}, bf16[272,512]{1,0:T(8,128)(2,1)S(1)}, u32[]{:S(2)}, u32[]{:S(2)}) collective-permute-start(bf16[272,512]{1,0:T(8,128)(2,1)S(1)} %get-tuple-element.50), channel_id=1, source_target_pairs={{0,256},{8,264},{16,272},{24,280},{32,288},{40,296},{48,304},{56,3... | collective-permute-start | bytes 835592 | tf_op jit(solution)/shard_map/ppermute | solution.py:38
  32.2 15.5 %collective-permute-start.5 = (bf16[272,512]{1,0:T(8,128)(2,1)S(1)}, bf16[272,512]{1,0:T(8,128)(2,1)S(1)}, u32[]{:S(2)}, u32[]{:S(2)}) collective-permute-start(bf16[272,512]{1,0:T(8,128)(2,1)S(1)} %get-tuple-element.51), channel_id=1, source_target_pairs={{0,128},{8,136},{16,144},{24,152},{32,160},{40,168},{48,176},{56,1... | collective-permute-start | bytes 835592 | tf_op jit(solution)/shard_map/ppermute | solution.py:38
  34.7 13.1 %collective-permute-start.6 = (bf16[272,512]{1,0:T(8,128)(2,1)S(1)}, bf16[272,512]{1,0:T(8,128)(2,1)S(1)}, u32[]{:S(2)}, u32[]{:S(2)}) collective-permute-start(bf16[272,512]{1,0:T(8,128)(2,1)S(1)} %get-tuple-element.52), channel_id=1, source_target_pairs={{0,384},{8,392},{16,400},{24,408},{32,416},{40,424},{48,432},{56,4... | collective-permute-start | bytes 835592 | tf_op jit(solution)/shard_map/ppermute | solution.py:38
  48.2 15.5 %copy-start.3 = (f32[32,256]{1,0:T(8,128)S(1)}, f32[32,256]{1,0:T(8,128)}, u32[]{:S(2)}) copy-start(f32[32,256]{1,0:T(8,128)} %rotation_ref.3) | copy-start | bytes 98308
  77.1 23.8 %all-to-all-start.2 = ((bf16[8,32,896]{2,1,0:T(8,128)(2,1)}), bf16[8,32,896]{2,1,0:T(8,128)(2,1)S(1)}, u32[]{:S(2)}, u32[]{:S(2)}) async-start(bf16[8,32,896]{2,1,0:T(8,128)(2,1)} %get-tuple-element.57), calls=%async_computation.2 | async-start | bytes 917504 | tf_op jit(solution)/shard_map/all_to_all | solution.py:28
  83.9 8.2 %collective-permute-start.9 = (bf16[8,32,512]{2,1,0:T(8,128)(2,1)S(1)}, bf16[8,32,512]{2,1,0:T(8,128)(2,1)S(1)}, u32[]{:S(2)}, u32[]{:S(2)}) collective-permute-start(bf16[8,32,512]{2,1,0:T(8,128)(2,1)S(1)} %all_to_all.31), channel_id=1, source_target_pairs={{0,384},{8,392},{16,400},{24,408},{32,416},{40,424},{48,432},{56,4... | collective-permute-start | bytes 786440 | tf_op jit(solution)/shard_map/ppermute | solution.py:38
  85.9 8.6 %collective-permute-start.8 = (bf16[8,32,512]{2,1,0:T(8,128)(2,1)S(1)}, bf16[8,32,512]{2,1,0:T(8,128)(2,1)S(1)}, u32[]{:S(2)}, u32[]{:S(2)}) collective-permute-start(bf16[8,32,512]{2,1,0:T(8,128)(2,1)S(1)} %all_to_all.31), channel_id=1, source_target_pairs={{0,256},{8,264},{16,272},{24,280},{32,288},{40,296},{48,304},{56,3... | collective-permute-start | bytes 786440 | tf_op jit(solution)/shard_map/ppermute | solution.py:38
  89.4 11.4 %collective-permute-start.7 = (bf16[8,32,512]{2,1,0:T(8,128)(2,1)S(1)}, bf16[8,32,512]{2,1,0:T(8,128)(2,1)S(1)}, u32[]{:S(2)}, u32[]{:S(2)}) collective-permute-start(bf16[8,32,512]{2,1,0:T(8,128)(2,1)S(1)} %all_to_all.31), channel_id=1, source_target_pairs={{0,128},{8,136},{16,144},{24,152},{32,160},{40,168},{48,176},{56,1... | collective-permute-start | bytes 786440 | tf_op jit(solution)/shard_map/ppermute | solution.py:38
  100.9 7.4 %collective-permute-start.10 = (bf16[4,8,32,512]{3,2,1,0:T(8,128)(2,1)S(1)}, bf16[4,8,32,512]{3,2,1,0:T(8,128)(2,1)S(1)}, u32[]{:S(2)}, u32[]{:S(2)}) collective-permute-start(bf16[4,8,32,512]{3,2,1,0:T(8,128)(2,1)S(1)} %pad_maximum_fusion.own_ref), channel_id=1, source_target_pairs={{0,8},{8,0},{16,24},{24,16},{32,40},{40,32},{48,56},{56,48},{64,72... | collective-permute-start | bytes 3145736 | tf_op jit(solution)/shard_map/ppermute | solution.py:33
  126.4 17.6 %all-to-all-start.4 = ((bf16[8,32,512]{2,1,0:T(8,128)(2,1)}), bf16[8,32,512]{2,1,0:T(8,128)(2,1)S(1)}, u32[]{:S(2)}, u32[]{:S(2)}) async-start(bf16[8,32,512]{2,1,0:T(8,128)(2,1)} %get-tuple-element.65), calls=%async_computation.4 | async-start | bytes 524288 | tf_op jit(solution)/shard_map/all_to_all | solution.py:28
  133.1 18.4 %collective-permute-start.13 = (bf16[16,32,256]{2,1,0:T(8,128)(2,1)S(1)}, bf16[16,32,256]{2,1,0:T(8,128)(2,1)S(1)}, u32[]{:S(2)}, u32[]{:S(2)}) collective-permute-start(bf16[16,32,256]{2,1,0:T(8,128)(2,1)S(1)} %all_to_all.32.own0), channel_id=1, source_target_pairs={{0,384},{8,392},{16,400},{24,408},{32,416},{40,424},{48,432},{56,4... | collective-permute-start | bytes 786440 | tf_op jit(solution)/shard_map/ppermute | solution.py:38
  136.0 15.5 %collective-permute-start.12 = (bf16[16,32,256]{2,1,0:T(8,128)(2,1)S(1)}, bf16[16,32,256]{2,1,0:T(8,128)(2,1)S(1)}, u32[]{:S(2)}, u32[]{:S(2)}) collective-permute-start(bf16[16,32,256]{2,1,0:T(8,128)(2,1)S(1)} %all_to_all.32.own0), channel_id=1, source_target_pairs={{0,256},{8,264},{16,272},{24,280},{32,288},{40,296},{48,304},{56,3... | collective-permute-start | bytes 786440 | tf_op jit(solution)/shard_map/ppermute | solution.py:38
  138.4 14.8 %collective-permute-start.11 = (bf16[16,32,256]{2,1,0:T(8,128)(2,1)S(1)}, bf16[16,32,256]{2,1,0:T(8,128)(2,1)S(1)}, u32[]{:S(2)}, u32[]{:S(2)}) collective-permute-start(bf16[16,32,256]{2,1,0:T(8,128)(2,1)S(1)} %all_to_all.32.own0), channel_id=1, source_target_pairs={{0,128},{8,136},{16,144},{24,152},{32,160},{40,168},{48,176},{56,1... | collective-permute-start | bytes 786440 | tf_op jit(solution)/shard_map/ppermute | solution.py:38
  144.1 9.2 %copy-start.1 = (bf16[256,2048]{1,0:T(8,128)(2,1)S(1)}, bf16[256,2048]{1,0:T(8,128)(2,1)}, u32[]{:S(2)}) copy-start(bf16[256,2048]{1,0:T(8,128)(2,1)} %coeffs_ref.2) | copy-start | bytes 3145732
  144.8 10.8 %all-to-all-start.5 = ((bf16[8,32,512]{2,1,0:T(8,128)(2,1)}), bf16[8,32,512]{2,1,0:T(8,128)(2,1)S(1)}, u32[]{:S(2)}, u32[]{:S(2)}) async-start(bf16[8,32,512]{2,1,0:T(8,128)(2,1)} %get-tuple-element.67), calls=%async_computation.5 | async-start | bytes 524288 | tf_op jit(solution)/shard_map/all_to_all | solution.py:28

commit v13 on v12

--- a/solution.py
+++ b/solution.py
@@ -44,7 +44,6 @@
 
 vmem = pl.BlockSpec(memory_space=pltpu.VMEM)
 smem = pl.BlockSpec(memory_space=pltpu.SMEM)
-hbm = pl.BlockSpec(memory_space=pltpu.HBM)
 
 
 def call(kernel, shapes, in_specs, scratch, *operands, bytes_accessed=2**20, flops=0):
@@ -164,43 +163,21 @@
         packed_ref[i] = packed
 
 
-def gathered(place_ref, own_ref, away_ref, out_ref, sems):
-    x, core = place_ref[0], place_ref[1]
-    copies = []
-    for source in range(XS):
-        steps = lax.rem(x + XS - source, XS)
-        pairs = ((own_ref, core), (away_ref, 1 - core))
-        copies.append(
-            [
-                pltpu.make_async_copy(
-                    ref.at[steps], out_ref.at[source, :, which], sems.at[source, i]
-                )
-                for i, (ref, which) in enumerate(pairs)
-            ]
-        )
-    for pair in copies:
-        for copy in pair:
-            copy.start()
-    return copies
-
-
-def landed(copies, k):
-    if k * XS % COLS == 0:
-        for copy in copies[k * XS // COLS]:
-            copy.wait()
-
-
-def chunk(panel_ref, k):
+def chunk(place_ref, own_ref, away_ref, k):
+    core = place_ref[1]
     per = ZS * XS // COLS
-    cells = panel_ref[k * per // ZS, pl.ds(k * per % ZS, per)]
-    return cells.reshape(-1, cells.shape[-1])
+    steps = lax.rem(place_ref[0] + XS - k * per // ZS, XS)
+    parts = []
+    for z in range(k * per % ZS, k * per % ZS + per):
+        own, away = own_ref[steps, z], away_ref[steps, z]
+        parts += [jnp.where(core == 0, own, away), jnp.where(core == 0, away, own)]
+    return jnp.concatenate(parts, axis=0)
 
 
 def square_kernel(
     scale, place_ref, across_ref, block_ref, own_ref, away_ref,
-    base_ref, sent_ref, step_ref, z_ref, rows_ref, diag_ref, turned_ref, sems,
+    base_ref, sent_ref, step_ref, rows_ref, diag_ref, turned_ref,
 ):
-    copies = gathered(place_ref, own_ref, away_ref, z_ref, sems)
     mine, low, col = place_ref[2], place_ref[3], place_ref[4]
     rows, width = rows_ref.shape[1:]
     terms = across_ref[:, :, -128:].astype(f32)
@@ -227,9 +204,8 @@
     square = jnp.zeros((rows, width), f32)
     base = block_ref[...]
     for k in range(COLS):
-        landed(copies, k)
         near = rows_ref[k].astype(bf16)
-        panel = chunk(z_ref, k)
+        panel = chunk(place_ref, own_ref, away_ref, k)
         base = base - small_product(near, panel)
         cells = panel.astype(f32)
         cos_part = cells[:, :width] * (across_diag[0] - turned_ref[0, :, k : k + 1])
@@ -242,7 +218,7 @@
         step_ref[k] = step
     square = square.astype(bf16)
     for k in range(COLS):
-        panel = chunk(z_ref, k)
+        panel = chunk(place_ref, own_ref, away_ref, k)
         for p in range(2):
             cells = lax.dot_general(
                 square,
@@ -264,34 +240,26 @@
         sent_ref[k] = sent
 
 
-def pieces_of(place_ref, refs, step_ref, sems):
-    copies = [
-        pltpu.make_async_copy(ref, step_ref.at[steps], sems.at[steps])
-        for steps, ref in enumerate(refs)
-    ]
-    for copy in copies:
-        copy.start()
-    width = step_ref.shape[-1]
+def pieces_of(place_ref, refs):
+    width = refs[0].shape[-1]
     per = COLS // XS
-    count = step_ref.shape[1] // per
-    for steps in range(XS):
-        copies[steps].wait()
+    count = refs[0].shape[0] // per
+    for steps, ref in enumerate(refs):
         source = lax.rem(place_ref[0] + XS - steps, XS)
         for part in range(per):
             first = z_order.index(part * ZS // per) * CORES
-            cells = step_ref[steps, first : first + count]
-            yield source * per + part, cells.reshape(-1, width)
+            yield source * per + part, ref[first : first + count].reshape(-1, width)
 
 
 def orbitals_kernel(
     place_ref, size_ref, across_ref, coeffs_ref, rotation_ref, own0, own1, own2, own3,
-    rotated_ref, orbitals_ref, step_ref, sems,
+    rotated_ref, orbitals_ref,
 ):
     width = rotated_ref.shape[1]
     rotated = rotation_ref[...]
     start = pl.multiple_of(place_ref[4] * width, width)
     orbitals = coeffs_ref[:, pl.ds(start, width)].astype(f32)
-    for k, step in pieces_of(place_ref, (own0, own1, own2, own3), step_ref, sems):
+    for k, step in pieces_of(place_ref, (own0, own1, own2, own3)):
         rotated = rotated + small_product(across_ref[k, :, 2 * width : 3 * width], step)
         cells = coeffs_ref[:, pl.ds(pl.multiple_of(k * width, width), width)]
         orbitals = orbitals + small_product(cells, step)
@@ -300,17 +268,18 @@
 
 
 def phases_kernel(
-    place_ref, half_ref, block_ref, own0, own1, own2, own3, cos_ref, sin_ref, step_ref, sems
+    place_ref, half_ref, block_ref, own0, own1, own2, own3, cos_ref, sin_ref
 ):
     width = cos_ref.shape[1]
-    cos_part, sin_part = block_ref[:, :width], block_ref[:, width:]
-    for k, step in pieces_of(place_ref, (own0, own1, own2, own3), step_ref, sems):
+    total = jnp.concatenate([block_ref[:, :width], block_ref[:, width:]], axis=0)
+    for k, step in pieces_of(place_ref, (own0, own1, own2, own3)):
         where = sum(jnp.where(k == col, i, 0) for i, col in enumerate(col_order))
         cells = half_ref[where]
-        cos_part = cos_part + small_product(cells[:, :width], step)
-        sin_part = sin_part + small_product(cells[:, width:], step)
-    cos_ref[...] = cos_part
-    sin_ref[...] = sin_part
+        cells = jnp.concatenate([cells[:, :width], cells[:, width:]], axis=0)
+        total = total + small_product(cells, step)
+    rows = cos_ref.shape[0]
+    cos_ref[...] = total[:rows]
+    sin_ref[...] = total[rows:]
 
 
 def on_device(coeffs, rotation, phase_ops, block_links, atom_size):
@@ -422,13 +391,11 @@
             ((COLS, row_count, both), bf16),
             ((ZS * CORES,) + block, bf16),
         ],
-        [smem] + [vmem] * 2 + [hbm] * 2,
+        [smem] + [vmem] * 4,
         [
-            pltpu.VMEM((XS, ZS, CORES, row_count, both), bf16),
             pltpu.VMEM((COLS,) + block, f32),
             pltpu.VMEM((2, COLS, col_count), f32),
             pltpu.VMEM((2, col_count, COLS), f32),
-            pltpu.SemaphoreType.DMA((XS, 2)),
         ],
         place,
         across,
@@ -451,15 +418,11 @@
         flops=2**35,
     )
     half_rows = swap(half_sent, "cols", [col_order])
-    panel_scratch = [
-        pltpu.VMEM((XS, ZS * CORES) + block, bf16),
-        pltpu.SemaphoreType.DMA((XS,)),
-    ]
     rotated, orbitals = call(
         orbitals_kernel,
         [(block, f32), ((rows_dev, col_count), bf16)],
-        [smem] * 2 + [vmem] * 3 + [hbm] * XS,
-        panel_scratch,
+        [smem] * 2 + [vmem] * (3 + XS),
+        [],
         place,
         atom_size,
         across,
@@ -471,8 +434,8 @@
     phase_cos, phase_sin = call(
         phases_kernel,
         [(block, f32)] * 2,
-        [smem] + [vmem] * 2 + [hbm] * XS,
-        panel_scratch,
+        [smem] + [vmem] * (2 + XS),
+        [],
         place,
         half_rows,
         half_block,

time: 160 us -> 159 us (level)
  no operation moved by 1% of the time
where the time goes in v13:
time: 159 us; the launch traced here: 157 us
  starting transfers between devices  70 us (44%)
  blocking collectives  42.4 us (27%)
  waiting for transfers between devices  26.9 us (17%)
  Pallas kernels  10.8 us (7%)
  local copies, waits for them, and re-layouts  3.76 us (2%)
  other arithmetic  1.68 us (1%)
    all_to_all x3, blocking collectives, swap(): lax.all_to_all(cells, axis, 0, 0, tiled=True, axis_index_groups=groups)  42.4 us
    ppermute x9, starting transfers between devices, along_x(): lax.ppermute(cells, 'rows', [(i, (i + steps * line) % count) for i in ran...  24.9 us
    all_to_all x3, starting transfers between devices, swap(): lax.all_to_all(cells, axis, 0, 0, tiled=True, axis_index_groups=groups)  20.1 us
    ppermute x9, waiting for transfers between devices, along_x(): lax.ppermute(cells, 'rows', [(i, (i + steps * line) % count) for i in ran...  19.3 us
    ppermute x3, starting transfers between devices, other_core(): return lax.ppermute(cells, 'rows', [(i, i ^ 1) for i in range(count)])  14.3 us
    pallas_call x8, Pallas kernels, call(): pl.pallas_call(kernel, out_shape=[jax.ShapeDtypeStruct(*shape) for shape...  10.8 us
    ppermute x1, starting transfers between devices, on_device(): from_up = lax.ppermute(own_cols[rows_dev - width:], 'rows', up)  5.39 us
    ppermute x1, starting transfers between devices, on_device(): from_down = lax.ppermute(own_cols[:width], 'rows', down)  5.32 us
  transfers between devices with their start and end apart: 17, of which 9 were waited for; matrix products, arithmetic and copies ran while one was open for 0% of the time, Pallas kernels for 3%

profile of v13, /device:TPU:1, one launch (start us, length us, event | category | flops | bytes accessed | tf_op | source)
XLA Modules:
  0.0 156.5 jit_solution(3853850055823159582)
XLA Ops:
  2.4 5.4 %collective-permute-start.1 = (bf16[256,256]{1,0:T(8,128)(2,1)S(1)}, bf16[256,256]{1,0:T(8,128)(2,1)S(1)}, u32[]{:S(2)}, u32[]{:S(2)}) collective-permute-start(bf16[256,256]{1,0:T(8,128)(2,1)S(1)} %dynamic-slice_select_fusion.cols_ref), channel_id=1, source_target_pairs={{0,8},{8,16},{16,24},{24,32},{32,40},{40,48},{48,56},{56,64},{64,7... | collective-permute-start | bytes 393224 | tf_op jit(solution)/shard_map/ppermute | solution.py:309
  7.8 5.3 %collective-permute-start = (bf16[256,256]{1,0:T(8,128)(2,1)S(1)}, bf16[256,256]{1,0:T(8,128)(2,1)S(1)}, u32[]{:S(2)}, u32[]{:S(2)}) collective-permute-start(bf16[256,256]{1,0:T(8,128)(2,1)S(1)} %dynamic-slice_select_fusion.cols_ref), channel_id=1, source_target_pairs={{8,0},{16,8},{24,16},{32,24},{40,32},{48,40},{56,48},{64,56},{72,6... | collective-permute-start | bytes 393224 | tf_op jit(solution)/shard_map/ppermute | solution.py:310
  17.3 7.2 %collective-permute-start.2 = (bf16[1024,256]{1,0:T(8,128)(2,1)S(1)}, bf16[1024,256]{1,0:T(8,128)(2,1)S(1)}, u32[]{:S(2)}, u32[]{:S(2)}) collective-permute-start(bf16[1024,256]{1,0:T(8,128)(2,1)S(1)} %get-tuple-element.42), channel_id=1, source_target_pairs={{0,8},{8,0},{16,24},{24,16},{32,40},{40,32},{48,56},{56,48},{64,72... | collective-permute-start | bytes 1572872 | tf_op jit(solution)/shard_map/ppermute | solution.py:33
  29.7 2.4 %collective-permute-start.4 = (bf16[272,512]{1,0:T(8,128)(2,1)S(1)}, bf16[272,512]{1,0:T(8,128)(2,1)S(1)}, u32[]{:S(2)}, u32[]{:S(2)}) collective-permute-start(bf16[272,512]{1,0:T(8,128)(2,1)S(1)} %get-tuple-element.50), channel_id=1, source_target_pairs={{0,256},{8,264},{16,272},{24,280},{32,288},{40,296},{48,304},{56,3... | collective-permute-start | bytes 835592 | tf_op jit(solution)/shard_map/ppermute | solution.py:38
  32.2 2.5 %collective-permute-start.5 = (bf16[272,512]{1,0:T(8,128)(2,1)S(1)}, bf16[272,512]{1,0:T(8,128)(2,1)S(1)}, u32[]{:S(2)}, u32[]{:S(2)}) collective-permute-start(bf16[272,512]{1,0:T(8,128)(2,1)S(1)} %get-tuple-element.51), channel_id=1, source_target_pairs={{0,128},{8,136},{16,144},{24,152},{32,160},{40,168},{48,176},{56,1... | collective-permute-start | bytes 835592 | tf_op jit(solution)/shard_map/ppermute | solution.py:38
  34.7 4.0 %collective-permute-start.6 = (bf16[272,512]{1,0:T(8,128)(2,1)S(1)}, bf16[272,512]{1,0:T(8,128)(2,1)S(1)}, u32[]{:S(2)}, u32[]{:S(2)}) collective-permute-start(bf16[272,512]{1,0:T(8,128)(2,1)S(1)} %get-tuple-element.52), channel_id=1, source_target_pairs={{0,384},{8,392},{16,400},{24,408},{32,416},{40,424},{48,432},{56,4... | collective-permute-start | bytes 835592 | tf_op jit(solution)/shard_map/ppermute | solution.py:38
  38.7 2.6 %collective-permute-done.4 = bf16[272,512]{1,0:T(8,128)(2,1)S(1)} collective-permute-done((bf16[272,512]{1,0:T(8,128)(2,1)S(1)}, bf16[272,512]{1,0:T(8,128)(2,1)S(1)}, u32[]{:S(2)}, u32[]{:S(2)}) %collective-permute-start.4) | collective-permute-done | bytes 278560 | tf_op jit(solution)/shard_map/ppermute | solution.py:38
  41.4 6.3 %collective-permute-done.5 = bf16[272,512]{1,0:T(8,128)(2,1)S(1)} collective-permute-done((bf16[272,512]{1,0:T(8,128)(2,1)S(1)}, bf16[272,512]{1,0:T(8,128)(2,1)S(1)}, u32[]{:S(2)}, u32[]{:S(2)}) %collective-permute-start.5) | collective-permute-done | bytes 278560 | tf_op jit(solution)/shard_map/ppermute | solution.py:38
  48.2 15.5 %all_to_all.30.got_ref = bf16[8,32,640]{2,1,0:T(8,128)(2,1)S(1)} all-to-all(bf16[8,32,640]{2,1,0:T(8,128)(2,1)S(1)} %pad_maximum_fusion.1), channel_id=1, replica_groups={{0,16,32,48,64,80,96,112},{8,24,40,56,72,88,104,120},{128,144,160,176,1..., dimensions={0} | all-to-all | bytes 655360 | tf_op jit(solution)/shard_map/all_to_all | solution.py:28
  64.5 12.6 %all_to_all.31 = bf16[8,32,512]{2,1,0:T(8,128)(2,1)S(1)} all-to-all(bf16[8,32,512]{2,1,0:T(8,128)(2,1)S(1)} %get-tuple-element.55), channel_id=1, replica_groups={{0,16,32,48,64,80,96,112},{8,24,40,56,72,88,104,120},{128,144,160,176,1..., dimensions={0} | all-to-all | bytes 524288 | tf_op jit(solution)/shard_map/all_to_all | solution.py:28
  77.1 6.8 %all-to-all-start.2 = ((bf16[8,32,896]{2,1,0:T(8,128)(2,1)}), bf16[8,32,896]{2,1,0:T(8,128)(2,1)S(1)}, u32[]{:S(2)}, u32[]{:S(2)}) async-start(bf16[8,32,896]{2,1,0:T(8,128)(2,1)} %get-tuple-element.57), calls=%async_computation.2 | async-start | bytes 917504 | tf_op jit(solution)/shard_map/all_to_all | solution.py:28
  85.9 3.5 %collective-permute-start.8 = (bf16[8,32,512]{2,1,0:T(8,128)(2,1)S(1)}, bf16[8,32,512]{2,1,0:T(8,128)(2,1)S(1)}, u32[]{:S(2)}, u32[]{:S(2)}) collective-permute-start(bf16[8,32,512]{2,1,0:T(8,128)(2,1)S(1)} %all_to_all.31), channel_id=1, source_target_pairs={{0,256},{8,264},{16,272},{24,280},{32,288},{40,296},{48,304},{56,3... | collective-permute-start | bytes 786440 | tf_op jit(solution)/shard_map/ppermute | solution.py:38
  89.4 2.8 %collective-permute-start.7 = (bf16[8,32,512]{2,1,0:T(8,128)(2,1)S(1)}, bf16[8,32,512]{2,1,0:T(8,128)(2,1)S(1)}, u32[]{:S(2)}, u32[]{:S(2)}) collective-permute-start(bf16[8,32,512]{2,1,0:T(8,128)(2,1)S(1)} %all_to_all.31), channel_id=1, source_target_pairs={{0,128},{8,136},{16,144},{24,152},{32,160},{40,168},{48,176},{56,1... | collective-permute-start | bytes 786440 | tf_op jit(solution)/shard_map/ppermute | solution.py:38
  92.2 2.3 %collective-permute-done.8 = bf16[8,32,512]{2,1,0:T(8,128)(2,1)S(1)} collective-permute-done((bf16[8,32,512]{2,1,0:T(8,128)(2,1)S(1)}, bf16[8,32,512]{2,1,0:T(8,128)(2,1)S(1)}, u32[]{:S(2)}, u32[]{:S(2)}) %collective-permute-start.8) | collective-permute-done | bytes 262176 | tf_op jit(solution)/shard_map/ppermute | solution.py:38
  94.5 6.3 %collective-permute-done.7 = bf16[8,32,512]{2,1,0:T(8,128)(2,1)S(1)} collective-permute-done((bf16[8,32,512]{2,1,0:T(8,128)(2,1)S(1)}, bf16[8,32,512]{2,1,0:T(8,128)(2,1)S(1)}, u32[]{:S(2)}, u32[]{:S(2)}) %collective-permute-start.7) | collective-permute-done | bytes 262176 | tf_op jit(solution)/shard_map/ppermute | solution.py:38
  100.9 5.2 %collective-permute-start.10 = (bf16[4,8,32,512]{3,2,1,0:T(8,128)(2,1)S(1)}, bf16[4,8,32,512]{3,2,1,0:T(8,128)(2,1)S(1)}, u32[]{:S(2)}, u32[]{:S(2)}) collective-permute-start(bf16[4,8,32,512]{3,2,1,0:T(8,128)(2,1)S(1)} %pad_maximum_fusion.own_ref), channel_id=1, source_target_pairs={{0,8},{8,0},{16,24},{24,16},{32,40},{40,32},{48,56},{56,48},{64,72... | collective-permute-start | bytes 3145736 | tf_op jit(solution)/shard_map/ppermute | solution.py:33
  108.4 3.1 %shard_map.88 = (f32[32,512]{1,0:T(8,128)S(1)}, bf16[8,32,512]{2,1,0:T(8,128)(2,1)}, bf16[16,32,256]{2,1,0:T(8,128)(2,1)S(1)}) custom-call(s32[5]{0:T(128)S(1)} %stack.44.place_ref, bf16[8,32,896]{2,1,0:T(8,128)(2,1)S(1)} %all-to-all-done.2.across_ref, f32[32,512]{1,0:T(8,128)S(1)} %get-tuple-element.59.block_ref, ...), custom_call_target="tpu_custom_call" | custom-call | bytes 1048576 | tf_op jit(solution)/shard_map/pallas_call | solution.py:50
  111.5 14.4 %all_to_all.32.own0 = bf16[16,32,256]{2,1,0:T(8,128)(2,1)S(1)} all-to-all(bf16[16,32,256]{2,1,0:T(8,128)(2,1)S(1)} %get-tuple-element.62), channel_id=1, replica_groups={{64,72,80,88,96,104,112,120,0,8,16,24,32,40,48,56},{192,200,208,216,224..., dimensions={0} | all-to-all | bytes 524288 | tf_op jit(solution)/shard_map/all_to_all | solution.py:28
  125.9 6.7 %all-to-all-start.4 = ((bf16[8,32,512]{2,1,0:T(8,128)(2,1)}), bf16[8,32,512]{2,1,0:T(8,128)(2,1)S(1)}, u32[]{:S(2)}, u32[]{:S(2)}) async-start(bf16[8,32,512]{2,1,0:T(8,128)(2,1)} %get-tuple-element.65), calls=%async_computation.4 | async-start | bytes 524288 | tf_op jit(solution)/shard_map/all_to_all | solution.py:28
  132.5 2.9 %collective-permute-start.13 = (bf16[16,32,256]{2,1,0:T(8,128)(2,1)S(1)}, bf16[16,32,256]{2,1,0:T(8,128)(2,1)S(1)}, u32[]{:S(2)}, u32[]{:S(2)}) collective-permute-start(bf16[16,32,256]{2,1,0:T(8,128)(2,1)S(1)} %all_to_all.32.own0), channel_id=1, source_target_pairs={{0,384},{8,392},{16,400},{24,408},{32,416},{40,424},{48,432},{56,4... | collective-permute-start | bytes 786440 | tf_op jit(solution)/shard_map/ppermute | solution.py:38
  135.4 2.4 %collective-permute-start.12 = (bf16[16,32,256]{2,1,0:T(8,128)(2,1)S(1)}, bf16[16,32,256]{2,1,0:T(8,128)(2,1)S(1)}, u32[]{:S(2)}, u32[]{:S(2)}) collective-permute-start(bf16[16,32,256]{2,1,0:T(8,128)(2,1)S(1)} %all_to_all.32.own0), channel_id=1, source_target_pairs={{0,256},{8,264},{16,272},{24,280},{32,288},{40,296},{48,304},{56,3... | collective-permute-start | bytes 786440 | tf_op jit(solution)/shard_map/ppermute | solution.py:38
  137.8 2.4 %collective-permute-start.11 = (bf16[16,32,256]{2,1,0:T(8,128)(2,1)S(1)}, bf16[16,32,256]{2,1,0:T(8,128)(2,1)S(1)}, u32[]{:S(2)}, u32[]{:S(2)}) collective-permute-start(bf16[16,32,256]{2,1,0:T(8,128)(2,1)S(1)} %all_to_all.32.own0), channel_id=1, source_target_pairs={{0,128},{8,136},{16,144},{24,152},{32,160},{40,168},{48,176},{56,1... | collective-permute-start | bytes 786440 | tf_op jit(solution)/shard_map/ppermute | solution.py:38
  140.3 3.2 %all-to-all-done.4.got_ref = bf16[8,32,512]{2,1,0:T(8,128)(2,1)S(1)} async-done(((bf16[8,32,512]{2,1,0:T(8,128)(2,1)}), bf16[8,32,512]{2,1,0:T(8,128)(2,1)S(1)}, u32[]{:S(2)}, u32[]{:S(2)}) %all-to-all-start.4) | async-done | bytes 262176 | tf_op jit(solution)/shard_map/all_to_all | solution.py:28
  144.2 6.6 %all-to-all-start.5 = ((bf16[8,32,512]{2,1,0:T(8,128)(2,1)}), bf16[8,32,512]{2,1,0:T(8,128)(2,1)S(1)}, u32[]{:S(2)}, u32[]{:S(2)}) async-start(bf16[8,32,512]{2,1,0:T(8,128)(2,1)} %get-tuple-element.67), calls=%async_computation.5 | async-start | bytes 524288 | tf_op jit(solution)/shard_map/all_to_all | solution.py:28
  (49 shorter events, 23.1 us)
Async XLA Ops:
  0.6 0.7 copy-start.5
  2.4 14.9 %collective-permute-start.1 = (bf16[256,256]{1,0:T(8,128)(2,1)S(1)}, bf16[256,256]{1,0:T(8,128)(2,1)S(1)}, u32[]{:S(2)}, u32[]{:S(2)}) collective-permute-start(bf16[256,256]{1,0:T(8,128)(2,1)S(1)} %dynamic-slice_select_fusion.cols_ref), channel_id=1, source_target_pairs={{0,8},{8,16},{16,24},{24,32},{32,40},{40,48},{48,56},{56,64},{64,7... | collective-permute-start | bytes 393224 | tf_op jit(solution)/shard_map/ppermute | solution.py:309
  7.8 9.6 %collective-permute-start = (bf16[256,256]{1,0:T(8,128)(2,1)S(1)}, bf16[256,256]{1,0:T(8,128)(2,1)S(1)}, u32[]{:S(2)}, u32[]{:S(2)}) collective-permute-start(bf16[256,256]{1,0:T(8,128)(2,1)S(1)} %dynamic-slice_select_fusion.cols_ref), channel_id=1, source_target_pairs={{8,0},{16,8},{24,16},{32,24},{40,32},{48,40},{56,48},{64,56},{72,6... | collective-permute-start | bytes 393224 | tf_op jit(solution)/shard_map/ppermute | solution.py:310
  13.3 0.7 copy-start.4
  13.9 1.2 copy-start
  15.2 1.1 copy-start.2
  17.3 11.1 %collective-permute-start.2 = (bf16[1024,256]{1,0:T(8,128)(2,1)S(1)}, bf16[1024,256]{1,0:T(8,128)(2,1)S(1)}, u32[]{:S(2)}, u32[]{:S(2)}) collective-permute-start(bf16[1024,256]{1,0:T(8,128)(2,1)S(1)} %get-tuple-element.42), channel_id=1, source_target_pairs={{0,8},{8,0},{16,24},{24,16},{32,40},{40,32},{48,56},{56,48},{64,72... | collective-permute-start | bytes 1572872 | tf_op jit(solution)/shard_map/ppermute | solution.py:33
  25.0 3.4 %collective-permute-start.3 = (bf16[256,512]{1,0:T(8,128)(2,1)S(1)}, bf16[256,512]{1,0:T(8,128)(2,1)S(1)}, u32[]{:S(2)}, u32[]{:S(2)}) collective-permute-start(bf16[256,512]{1,0:T(8,128)(2,1)S(1)} %get-tuple-element.47.applied_ref), channel_id=1, source_target_pairs={{0,8},{8,0},{16,24},{24,16},{32,40},{40,32},{48,56},{56,48},{64,72... | collective-permute-start | bytes 786440 | tf_op jit(solution)/shard_map/ppermute | solution.py:33
  29.7 11.6 %collective-permute-start.4 = (bf16[272,512]{1,0:T(8,128)(2,1)S(1)}, bf16[272,512]{1,0:T(8,128)(2,1)S(1)}, u32[]{:S(2)}, u32[]{:S(2)}) collective-permute-start(bf16[272,512]{1,0:T(8,128)(2,1)S(1)} %get-tuple-element.50), channel_id=1, source_target_pairs={{0,256},{8,264},{16,272},{24,280},{32,288},{40,296},{48,304},{56,3... | collective-permute-start | bytes 835592 | tf_op jit(solution)/shard_map/ppermute | solution.py:38
  32.2 15.5 %collective-permute-start.5 = (bf16[272,512]{1,0:T(8,128)(2,1)S(1)}, bf16[272,512]{1,0:T(8,128)(2,1)S(1)}, u32[]{:S(2)}, u32[]{:S(2)}) collective-permute-start(bf16[272,512]{1,0:T(8,128)(2,1)S(1)} %get-tuple-element.51), channel_id=1, source_target_pairs={{0,128},{8,136},{16,144},{24,152},{32,160},{40,168},{48,176},{56,1... | collective-permute-start | bytes 835592 | tf_op jit(solution)/shard_map/ppermute | solution.py:38
  34.7 13.1 %collective-permute-start.6 = (bf16[272,512]{1,0:T(8,128)(2,1)S(1)}, bf16[272,512]{1,0:T(8,128)(2,1)S(1)}, u32[]{:S(2)}, u32[]{:S(2)}) collective-permute-start(bf16[272,512]{1,0:T(8,128)(2,1)S(1)} %get-tuple-element.52), channel_id=1, source_target_pairs={{0,384},{8,392},{16,400},{24,408},{32,416},{40,424},{48,432},{56,4... | collective-permute-start | bytes 835592 | tf_op jit(solution)/shard_map/ppermute | solution.py:38
  48.2 15.5 %copy-start.3 = (f32[32,256]{1,0:T(8,128)S(1)}, f32[32,256]{1,0:T(8,128)}, u32[]{:S(2)}) copy-start(f32[32,256]{1,0:T(8,128)} %rotation_ref.3) | copy-start | bytes 98308
  77.1 23.8 %all-to-all-start.2 = ((bf16[8,32,896]{2,1,0:T(8,128)(2,1)}), bf16[8,32,896]{2,1,0:T(8,128)(2,1)S(1)}, u32[]{:S(2)}, u32[]{:S(2)}) async-start(bf16[8,32,896]{2,1,0:T(8,128)(2,1)} %get-tuple-element.57), calls=%async_computation.2 | async-start | bytes 917504 | tf_op jit(solution)/shard_map/all_to_all | solution.py:28
  83.9 8.2 %collective-permute-start.9 = (bf16[8,32,512]{2,1,0:T(8,128)(2,1)S(1)}, bf16[8,32,512]{2,1,0:T(8,128)(2,1)S(1)}, u32[]{:S(2)}, u32[]{:S(2)}) collective-permute-start(bf16[8,32,512]{2,1,0:T(8,128)(2,1)S(1)} %all_to_all.31), channel_id=1, source_target_pairs={{0,384},{8,392},{16,400},{24,408},{32,416},{40,424},{48,432},{56,4... | collective-permute-start | bytes 786440 | tf_op jit(solution)/shard_map/ppermute | solution.py:38
  85.9 8.6 %collective-permute-start.8 = (bf16[8,32,512]{2,1,0:T(8,128)(2,1)S(1)}, bf16[8,32,512]{2,1,0:T(8,128)(2,1)S(1)}, u32[]{:S(2)}, u32[]{:S(2)}) collective-permute-start(bf16[8,32,512]{2,1,0:T(8,128)(2,1)S(1)} %all_to_all.31), channel_id=1, source_target_pairs={{0,256},{8,264},{16,272},{24,280},{32,288},{40,296},{48,304},{56,3... | collective-permute-start | bytes 786440 | tf_op jit(solution)/shard_map/ppermute | solution.py:38
  89.4 11.4 %collective-permute-start.7 = (bf16[8,32,512]{2,1,0:T(8,128)(2,1)S(1)}, bf16[8,32,512]{2,1,0:T(8,128)(2,1)S(1)}, u32[]{:S(2)}, u32[]{:S(2)}) collective-permute-start(bf16[8,32,512]{2,1,0:T(8,128)(2,1)S(1)} %all_to_all.31), channel_id=1, source_target_pairs={{0,128},{8,136},{16,144},{24,152},{32,160},{40,168},{48,176},{56,1... | collective-permute-start | bytes 786440 | tf_op jit(solution)/shard_map/ppermute | solution.py:38
  100.9 7.4 %collective-permute-start.10 = (bf16[4,8,32,512]{3,2,1,0:T(8,128)(2,1)S(1)}, bf16[4,8,32,512]{3,2,1,0:T(8,128)(2,1)S(1)}, u32[]{:S(2)}, u32[]{:S(2)}) collective-permute-start(bf16[4,8,32,512]{3,2,1,0:T(8,128)(2,1)S(1)} %pad_maximum_fusion.own_ref), channel_id=1, source_target_pairs={{0,8},{8,0},{16,24},{24,16},{32,40},{40,32},{48,56},{56,48},{64,72... | collective-permute-start | bytes 3145736 | tf_op jit(solution)/shard_map/ppermute | solution.py:33
  125.9 17.6 %all-to-all-start.4 = ((bf16[8,32,512]{2,1,0:T(8,128)(2,1)}), bf16[8,32,512]{2,1,0:T(8,128)(2,1)S(1)}, u32[]{:S(2)}, u32[]{:S(2)}) async-start(bf16[8,32,512]{2,1,0:T(8,128)(2,1)} %get-tuple-element.65), calls=%async_computation.4 | async-start | bytes 524288 | tf_op jit(solution)/shard_map/all_to_all | solution.py:28
  132.5 18.4 %collective-permute-start.13 = (bf16[16,32,256]{2,1,0:T(8,128)(2,1)S(1)}, bf16[16,32,256]{2,1,0:T(8,128)(2,1)S(1)}, u32[]{:S(2)}, u32[]{:S(2)}) collective-permute-start(bf16[16,32,256]{2,1,0:T(8,128)(2,1)S(1)} %all_to_all.32.own0), channel_id=1, source_target_pairs={{0,384},{8,392},{16,400},{24,408},{32,416},{40,424},{48,432},{56,4... | collective-permute-start | bytes 786440 | tf_op jit(solution)/shard_map/ppermute | solution.py:38
  135.4 15.5 %collective-permute-start.12 = (bf16[16,32,256]{2,1,0:T(8,128)(2,1)S(1)}, bf16[16,32,256]{2,1,0:T(8,128)(2,1)S(1)}, u32[]{:S(2)}, u32[]{:S(2)}) collective-permute-start(bf16[16,32,256]{2,1,0:T(8,128)(2,1)S(1)} %all_to_all.32.own0), channel_id=1, source_target_pairs={{0,256},{8,264},{16,272},{24,280},{32,288},{40,296},{48,304},{56,3... | collective-permute-start | bytes 786440 | tf_op jit(solution)/shard_map/ppermute | solution.py:38
  137.8 14.8 %collective-permute-start.11 = (bf16[16,32,256]{2,1,0:T(8,128)(2,1)S(1)}, bf16[16,32,256]{2,1,0:T(8,128)(2,1)S(1)}, u32[]{:S(2)}, u32[]{:S(2)}) collective-permute-start(bf16[16,32,256]{2,1,0:T(8,128)(2,1)S(1)} %all_to_all.32.own0), channel_id=1, source_target_pairs={{0,128},{8,136},{16,144},{24,152},{32,160},{40,168},{48,176},{56,1... | collective-permute-start | bytes 786440 | tf_op jit(solution)/shard_map/ppermute | solution.py:38
  143.5 9.2 %copy-start.1 = (bf16[256,2048]{1,0:T(8,128)(2,1)S(1)}, bf16[256,2048]{1,0:T(8,128)(2,1)}, u32[]{:S(2)}) copy-start(bf16[256,2048]{1,0:T(8,128)(2,1)} %coeffs_ref.2) | copy-start | bytes 3145732
  144.2 10.8 %all-to-all-start.5 = ((bf16[8,32,512]{2,1,0:T(8,128)(2,1)}), bf16[8,32,512]{2,1,0:T(8,128)(2,1)S(1)}, u32[]{:S(2)}, u32[]{:S(2)}) async-start(bf16[8,32,512]{2,1,0:T(8,128)(2,1)} %get-tuple-element.67), calls=%async_computation.5 | async-start | bytes 524288 | tf_op jit(solution)/shard_map/all_to_all | solution.py:28

commit v14 on v13

--- a/solution.py
+++ b/solution.py
@@ -12,6 +12,7 @@
 f32 = jnp.float32
 
 XS, ZS, CORES, COLS = 4, 8, 2, 8
+x_steps = (0, 1, 3, 2)
 
 
 def row_index(x, z, core):
@@ -19,7 +20,7 @@
 
 
 z_groups = [[row_index(x, z, k) for z in range(ZS)] for x in range(XS) for k in range(CORES)]
-z_order = [4, 5, 6, 7, 0, 1, 2, 3]
+z_order = [7, 6, 5, 4, 3, 2, 1, 0]
 col_order = [4, 5, 6, 7, 3, 2, 1, 0]
 plane_groups = [[row_index(x, z, k) for z in z_order for k in range(CORES)] for x in range(XS)]
 
@@ -167,18 +168,16 @@
     core = place_ref[1]
     per = ZS * XS // COLS
     steps = lax.rem(place_ref[0] + XS - k * per // ZS, XS)
+    where = sum(jnp.where(steps == step, i, 0) for i, step in enumerate(x_steps))
     parts = []
     for z in range(k * per % ZS, k * per % ZS + per):
-        own, away = own_ref[steps, z], away_ref[steps, z]
+        own, away = own_ref[where, z], away_ref[where, z]
         parts += [jnp.where(core == 0, own, away), jnp.where(core == 0, away, own)]
     return jnp.concatenate(parts, axis=0)
 
 
-def square_kernel(
-    scale, place_ref, across_ref, block_ref, own_ref, away_ref,
-    base_ref, sent_ref, step_ref, rows_ref, diag_ref, turned_ref,
-):
-    mine, low, col = place_ref[2], place_ref[3], place_ref[4]
+def rows_kernel(scale, place_ref, across_ref, rows_ref, diag_ref, turned_ref):
+    mine, low = place_ref[2], place_ref[3]
     rows, width = rows_ref.shape[1:]
     terms = across_ref[:, :, -128:].astype(f32)
     per = width // 128
@@ -200,6 +199,14 @@
         cos_part = cells[:, :width] * (diag_ref[0, k : k + 1, :] - down[0])
         sin_part = cells[:, width : 2 * width] * (diag_ref[1, k : k + 1, :] - down[1])
         rows_ref[k] = (cos_part + sin_part) * scale
+
+
+def square_kernel(
+    scale, place_ref, rows_ref, diag_ref, turned_ref, block_ref, own_ref, away_ref,
+    base_ref, sent_ref, step_ref,
+):
+    col = place_ref[4]
+    rows, width = rows_ref.shape[1:]
     across_diag = [diag_ref[p, pl.ds(col, 1), :] for p in range(2)]
     square = jnp.zeros((rows, width), f32)
     base = block_ref[...]
@@ -243,12 +250,15 @@
 def pieces_of(place_ref, refs):
     width = refs[0].shape[-1]
     per = COLS // XS
-    count = refs[0].shape[0] // per
-    for steps, ref in enumerate(refs):
+    for steps, ref in zip(x_steps, refs):
         source = lax.rem(place_ref[0] + XS - steps, XS)
         for part in range(per):
-            first = z_order.index(part * ZS // per) * CORES
-            yield source * per + part, ref[first : first + count].reshape(-1, width)
+            places = [
+                z_order.index(z) * CORES
+                for z in range(part * ZS // per, (part + 1) * ZS // per)
+            ]
+            cells = [ref[first : first + CORES].reshape(-1, width) for first in places]
+            yield source * per + part, jnp.concatenate(cells, axis=0)
 
 
 def orbitals_kernel(
@@ -379,11 +389,24 @@
 
     panel = swap(z_sent, "rows", z_groups)
     packed, panel = lax.optimization_barrier((packed, panel))
-    panels = [panel] + [along_x(panel, steps) for steps in (1, 2, 3)]
+    panels = [panel] + [along_x(panel, steps) for steps in x_steps[1:]]
     across = swap(packed, "cols")
     stacked, across = lax.optimization_barrier((jnp.stack(panels), across))
     away = other_core(stacked)
     block = (row_count, col_count)
+    gen_rows, diag_all, turned_diag = call(
+        functools.partial(rows_kernel, scale_factor),
+        [
+            ((COLS,) + block, f32),
+            ((2, COLS, col_count), f32),
+            ((2, col_count, COLS), f32),
+        ],
+        [smem, vmem],
+        [],
+        place,
+        across,
+        flops=2**33,
+    )
     base, square, step = call(
         functools.partial(square_kernel, scale_factor),
         [
@@ -391,14 +414,12 @@
             ((COLS, row_count, both), bf16),
             ((ZS * CORES,) + block, bf16),
         ],
-        [smem] + [vmem] * 4,
-        [
-            pltpu.VMEM((COLS,) + block, f32),
-            pltpu.VMEM((2, COLS, col_count), f32),
-            pltpu.VMEM((2, col_count, COLS), f32),
-        ],
-        place,
-        across,
+        [smem] + [vmem] * 6,
+        [],
+        place,
+        gen_rows,
+        diag_all,
+        turned_diag,
         z_block,
         stacked,
         away,
@@ -406,7 +427,7 @@
 
     step = swap(step, "rows", plane_groups)
     square, step = lax.optimization_barrier((square, step))
-    steps_x = [step] + [along_x(step, steps) for steps in (1, 2, 3)]
+    steps_x = [step] + [along_x(step, steps) for steps in x_steps[1:]]
     square = swap(square, "cols")
     half_block, half_sent = call(
         half_kernel,

time: 159 us -> 158 us (level)
  starting transfers between devices: 70 us -> 72.6 us
  blocking collectives: 42.4 us -> 40.8 us
    ppermute x9, waiting for transfers between devices: 19.3 us -> 14.9 us  [along_x(): lax.ppermute(cells, 'rows', [(i, (i + steps * line) % count) for i in ran...]
    all_to_all x3, waiting for transfers between devices: 3.83 us -> 8.01 us  [swap(): lax.all_to_all(cells, axis, 0, 0, tiled=True, axis_index_groups=groups)]
    pallas_call x8 -> x9, Pallas kernels: 10.8 us -> 11.4 us  [call(): pl.pallas_call(kernel, out_shape=[jax.ShapeDtypeStruct(*shape) for shape...]
  transfers between devices with their start and end apart: 17 -> 17, of which waited for: 9 -> 8; matrix products, arithmetic and copies ran while one was open for 0% -> 0% of each run, Pallas kernels for 3% -> 3%
where the time goes in v14:
time: 158 us; the launch traced here: 157 us
  starting transfers between devices  72.6 us (46%)
  blocking collectives  40.8 us (26%)
  waiting for transfers between devices  25.9 us (16%)
  Pallas kernels  11.4 us (7%)
  local copies, waits for them, and re-layouts  3.76 us (2%)
  other arithmetic  1.68 us (1%)
    all_to_all x3, blocking collectives, swap(): lax.all_to_all(cells, axis, 0, 0, tiled=True, axis_index_groups=groups)  40.8 us
    ppermute x9, starting transfers between devices, along_x(): lax.ppermute(cells, 'rows', [(i, (i + steps * line) % count) for i in ran...  26.2 us
    all_to_all x3, starting transfers between devices, swap(): lax.all_to_all(cells, axis, 0, 0, tiled=True, axis_index_groups=groups)  20.4 us
    ppermute x3, starting transfers between devices, other_core(): return lax.ppermute(cells, 'rows', [(i, i ^ 1) for i in range(count)])  15.3 us
    ppermute x9, waiting for transfers between devices, along_x(): lax.ppermute(cells, 'rows', [(i, (i + steps * line) % count) for i in ran...  14.9 us
    pallas_call x9, Pallas kernels, call(): pl.pallas_call(kernel, out_shape=[jax.ShapeDtypeStruct(*shape) for shape...  11.4 us
    all_to_all x3, waiting for transfers between devices, swap(): lax.all_to_all(cells, axis, 0, 0, tiled=True, axis_index_groups=groups)  8.01 us
    ppermute x1, starting transfers between devices, on_device(): from_up = lax.ppermute(own_cols[rows_dev - width:], 'rows', up)  5.39 us
  transfers between devices with their start and end apart: 17, of which 8 were waited for; matrix products, arithmetic and copies ran while one was open for 0% of the time, Pallas kernels for 3%

profile of v14, /device:TPU:1, one launch (start us, length us, event | category | flops | bytes accessed | tf_op | source)
XLA Modules:
  0.0 157.1 jit_solution(80302140544091517)
XLA Ops:
  2.4 5.4 %collective-permute-start.1 = (bf16[256,256]{1,0:T(8,128)(2,1)S(1)}, bf16[256,256]{1,0:T(8,128)(2,1)S(1)}, u32[]{:S(2)}, u32[]{:S(2)}) collective-permute-start(bf16[256,256]{1,0:T(8,128)(2,1)S(1)} %dynamic-slice_select_fusion.cols_ref), channel_id=1, source_target_pairs={{0,8},{8,16},{16,24},{24,32},{32,40},{40,48},{48,56},{56,64},{64,7... | collective-permute-start | bytes 393224 | tf_op jit(solution)/shard_map/ppermute | solution.py:319
  7.8 5.3 %collective-permute-start = (bf16[256,256]{1,0:T(8,128)(2,1)S(1)}, bf16[256,256]{1,0:T(8,128)(2,1)S(1)}, u32[]{:S(2)}, u32[]{:S(2)}) collective-permute-start(bf16[256,256]{1,0:T(8,128)(2,1)S(1)} %dynamic-slice_select_fusion.cols_ref), channel_id=1, source_target_pairs={{8,0},{16,8},{24,16},{32,24},{40,32},{48,40},{56,48},{64,56},{72,6... | collective-permute-start | bytes 393224 | tf_op jit(solution)/shard_map/ppermute | solution.py:320
  17.3 7.2 %collective-permute-start.2 = (bf16[1024,256]{1,0:T(8,128)(2,1)S(1)}, bf16[1024,256]{1,0:T(8,128)(2,1)S(1)}, u32[]{:S(2)}, u32[]{:S(2)}) collective-permute-start(bf16[1024,256]{1,0:T(8,128)(2,1)S(1)} %get-tuple-element.45), channel_id=1, source_target_pairs={{0,8},{8,0},{16,24},{24,16},{32,40},{40,32},{48,56},{56,48},{64,72... | collective-permute-start | bytes 1572872 | tf_op jit(solution)/shard_map/ppermute | solution.py:34
  29.7 2.4 %collective-permute-start.4 = (bf16[272,512]{1,0:T(8,128)(2,1)S(1)}, bf16[272,512]{1,0:T(8,128)(2,1)S(1)}, u32[]{:S(2)}, u32[]{:S(2)}) collective-permute-start(bf16[272,512]{1,0:T(8,128)(2,1)S(1)} %get-tuple-element.53), channel_id=1, source_target_pairs={{0,256},{8,264},{16,272},{24,280},{32,288},{40,296},{48,304},{56,3... | collective-permute-start | bytes 835592 | tf_op jit(solution)/shard_map/ppermute | solution.py:39
  32.2 2.5 %collective-permute-start.5 = (bf16[272,512]{1,0:T(8,128)(2,1)S(1)}, bf16[272,512]{1,0:T(8,128)(2,1)S(1)}, u32[]{:S(2)}, u32[]{:S(2)}) collective-permute-start(bf16[272,512]{1,0:T(8,128)(2,1)S(1)} %get-tuple-element.54), channel_id=1, source_target_pairs={{0,128},{8,136},{16,144},{24,152},{32,160},{40,168},{48,176},{56,1... | collective-permute-start | bytes 835592 | tf_op jit(solution)/shard_map/ppermute | solution.py:39
  34.7 4.0 %collective-permute-start.6 = (bf16[272,512]{1,0:T(8,128)(2,1)S(1)}, bf16[272,512]{1,0:T(8,128)(2,1)S(1)}, u32[]{:S(2)}, u32[]{:S(2)}) collective-permute-start(bf16[272,512]{1,0:T(8,128)(2,1)S(1)} %get-tuple-element.55), channel_id=1, source_target_pairs={{0,384},{8,392},{16,400},{24,408},{32,416},{40,424},{48,432},{56,4... | collective-permute-start | bytes 835592 | tf_op jit(solution)/shard_map/ppermute | solution.py:39
  38.7 2.6 %collective-permute-done.4 = bf16[272,512]{1,0:T(8,128)(2,1)S(1)} collective-permute-done((bf16[272,512]{1,0:T(8,128)(2,1)S(1)}, bf16[272,512]{1,0:T(8,128)(2,1)S(1)}, u32[]{:S(2)}, u32[]{:S(2)}) %collective-permute-start.4) | collective-permute-done | bytes 278560 | tf_op jit(solution)/shard_map/ppermute | solution.py:39
  41.4 6.3 %collective-permute-done.5 = bf16[272,512]{1,0:T(8,128)(2,1)S(1)} collective-permute-done((bf16[272,512]{1,0:T(8,128)(2,1)S(1)}, bf16[272,512]{1,0:T(8,128)(2,1)S(1)}, u32[]{:S(2)}, u32[]{:S(2)}) %collective-permute-start.5) | collective-permute-done | bytes 278560 | tf_op jit(solution)/shard_map/ppermute | solution.py:39
  48.2 15.5 %all_to_all.30.got_ref = bf16[8,32,640]{2,1,0:T(8,128)(2,1)S(1)} all-to-all(bf16[8,32,640]{2,1,0:T(8,128)(2,1)S(1)} %pad_maximum_fusion.1), channel_id=1, replica_groups={{0,16,32,48,64,80,96,112},{8,24,40,56,72,88,104,120},{128,144,160,176,1..., dimensions={0} | all-to-all | bytes 655360 | tf_op jit(solution)/shard_map/all_to_all | solution.py:29
  64.5 12.6 %all_to_all.31 = bf16[8,32,512]{2,1,0:T(8,128)(2,1)S(1)} all-to-all(bf16[8,32,512]{2,1,0:T(8,128)(2,1)S(1)} %get-tuple-element.58), channel_id=1, replica_groups={{0,16,32,48,64,80,96,112},{8,24,40,56,72,88,104,120},{128,144,160,176,1..., dimensions={0} | all-to-all | bytes 524288 | tf_op jit(solution)/shard_map/all_to_all | solution.py:29
  77.1 6.8 %all-to-all-start.2 = ((bf16[8,32,896]{2,1,0:T(8,128)(2,1)}), bf16[8,32,896]{2,1,0:T(8,128)(2,1)S(1)}, u32[]{:S(2)}, u32[]{:S(2)}) async-start(bf16[8,32,896]{2,1,0:T(8,128)(2,1)} %get-tuple-element.60), calls=%async_computation.2 | async-start | bytes 917504 | tf_op jit(solution)/shard_map/all_to_all | solution.py:29
  83.9 3.5 %collective-permute-start.9 = (bf16[8,32,512]{2,1,0:T(8,128)(2,1)S(1)}, bf16[8,32,512]{2,1,0:T(8,128)(2,1)S(1)}, u32[]{:S(2)}, u32[]{:S(2)}) collective-permute-start(bf16[8,32,512]{2,1,0:T(8,128)(2,1)S(1)} %all_to_all.31), channel_id=1, source_target_pairs={{0,256},{8,264},{16,272},{24,280},{32,288},{40,296},{48,304},{56,3... | collective-permute-start | bytes 786440 | tf_op jit(solution)/shard_map/ppermute | solution.py:39
  89.4 3.4 %collective-permute-start.7 = (bf16[8,32,512]{2,1,0:T(8,128)(2,1)S(1)}, bf16[8,32,512]{2,1,0:T(8,128)(2,1)S(1)}, u32[]{:S(2)}, u32[]{:S(2)}) collective-permute-start(bf16[8,32,512]{2,1,0:T(8,128)(2,1)S(1)} %all_to_all.31), channel_id=1, source_target_pairs={{0,128},{8,136},{16,144},{24,152},{32,160},{40,168},{48,176},{56,1... | collective-permute-start | bytes 786440 | tf_op jit(solution)/shard_map/ppermute | solution.py:39
  92.8 4.9 %collective-permute-done.8 = bf16[8,32,512]{2,1,0:T(8,128)(2,1)S(1)} collective-permute-done((bf16[8,32,512]{2,1,0:T(8,128)(2,1)S(1)}, bf16[8,32,512]{2,1,0:T(8,128)(2,1)S(1)}, u32[]{:S(2)}, u32[]{:S(2)}) %collective-permute-start.8) | collective-permute-done | bytes 262176 | tf_op jit(solution)/shard_map/ppermute | solution.py:39
  98.9 6.1 %collective-permute-start.10 = (bf16[4,8,32,512]{3,2,1,0:T(8,128)(2,1)S(1)}, bf16[4,8,32,512]{3,2,1,0:T(8,128)(2,1)S(1)}, u32[]{:S(2)}, u32[]{:S(2)}) collective-permute-start(bf16[4,8,32,512]{3,2,1,0:T(8,128)(2,1)S(1)} %pad_maximum_fusion.own_ref), channel_id=1, source_target_pairs={{0,8},{8,0},{16,24},{24,16},{32,40},{40,32},{48,56},{56,48},{64,72... | collective-permute-start | bytes 3145736 | tf_op jit(solution)/shard_map/ppermute | solution.py:34
  107.3 2.9 %shard_map.89 = (f32[32,512]{1,0:T(8,128)S(1)}, bf16[8,32,512]{2,1,0:T(8,128)(2,1)}, bf16[16,32,256]{2,1,0:T(8,128)(2,1)S(1)}) custom-call(s32[5]{0:T(128)S(1)} %stack.44.place_ref, f32[8,32,256]{2,1,0:T(8,128)S(1)} %get-tuple-element.62.rows_ref, f32[2,8,256]{2,1,0:T(8,128)S(1)} %get-tuple-element.63.diag_ref, ...), custom_call_target="tpu_custom_call" | custom-call | bytes 1048576 | tf_op jit(solution)/shard_map/pallas_call | solution.py:51
  110.2 12.8 %all_to_all.32.own0 = bf16[16,32,256]{2,1,0:T(8,128)(2,1)S(1)} all-to-all(bf16[16,32,256]{2,1,0:T(8,128)(2,1)S(1)} %get-tuple-element.68), channel_id=1, replica_groups={{112,120,96,104,80,88,64,72,48,56,32,40,16,24,0,8},{240,248,224,232,208..., dimensions={0} | all-to-all | bytes 524288 | tf_op jit(solution)/shard_map/all_to_all | solution.py:29
  123.0 6.9 %all-to-all-start.4 = ((bf16[8,32,512]{2,1,0:T(8,128)(2,1)}), bf16[8,32,512]{2,1,0:T(8,128)(2,1)S(1)}, u32[]{:S(2)}, u32[]{:S(2)}) async-start(bf16[8,32,512]{2,1,0:T(8,128)(2,1)} %get-tuple-element.71), calls=%async_computation.4 | async-start | bytes 524288 | tf_op jit(solution)/shard_map/all_to_all | solution.py:29
  129.9 3.2 %collective-permute-start.13 = (bf16[16,32,256]{2,1,0:T(8,128)(2,1)S(1)}, bf16[16,32,256]{2,1,0:T(8,128)(2,1)S(1)}, u32[]{:S(2)}, u32[]{:S(2)}) collective-permute-start(bf16[16,32,256]{2,1,0:T(8,128)(2,1)S(1)} %all_to_all.32.own0), channel_id=1, source_target_pairs={{0,256},{8,264},{16,272},{24,280},{32,288},{40,296},{48,304},{56,3... | collective-permute-start | bytes 786440 | tf_op jit(solution)/shard_map/ppermute | solution.py:39
  133.1 3.0 %collective-permute-start.12 = (bf16[16,32,256]{2,1,0:T(8,128)(2,1)S(1)}, bf16[16,32,256]{2,1,0:T(8,128)(2,1)S(1)}, u32[]{:S(2)}, u32[]{:S(2)}) collective-permute-start(bf16[16,32,256]{2,1,0:T(8,128)(2,1)S(1)} %all_to_all.32.own0), channel_id=1, source_target_pairs={{0,384},{8,392},{16,400},{24,408},{32,416},{40,424},{48,432},{56,4... | collective-permute-start | bytes 786440 | tf_op jit(solution)/shard_map/ppermute | solution.py:39
  136.2 2.2 %collective-permute-start.11 = (bf16[16,32,256]{2,1,0:T(8,128)(2,1)S(1)}, bf16[16,32,256]{2,1,0:T(8,128)(2,1)S(1)}, u32[]{:S(2)}, u32[]{:S(2)}) collective-permute-start(bf16[16,32,256]{2,1,0:T(8,128)(2,1)S(1)} %all_to_all.32.own0), channel_id=1, source_target_pairs={{0,128},{8,136},{16,144},{24,152},{32,160},{40,168},{48,176},{56,1... | collective-permute-start | bytes 786440 | tf_op jit(solution)/shard_map/ppermute | solution.py:39
  138.4 3.9 %all-to-all-done.4.got_ref = bf16[8,32,512]{2,1,0:T(8,128)(2,1)S(1)} async-done(((bf16[8,32,512]{2,1,0:T(8,128)(2,1)}), bf16[8,32,512]{2,1,0:T(8,128)(2,1)S(1)}, u32[]{:S(2)}, u32[]{:S(2)}) %all-to-all-start.4) | async-done | bytes 262176 | tf_op jit(solution)/shard_map/all_to_all | solution.py:29
  143.0 6.6 %all-to-all-start.5 = ((bf16[8,32,512]{2,1,0:T(8,128)(2,1)}), bf16[8,32,512]{2,1,0:T(8,128)(2,1)S(1)}, u32[]{:S(2)}, u32[]{:S(2)}) async-start(bf16[8,32,512]{2,1,0:T(8,128)(2,1)} %get-tuple-element.73), calls=%async_computation.5 | async-start | bytes 524288 | tf_op jit(solution)/shard_map/all_to_all | solution.py:29
  151.5 4.1 %all-to-all-done.5.half_ref = bf16[8,32,512]{2,1,0:T(8,128)(2,1)S(1)} async-done(((bf16[8,32,512]{2,1,0:T(8,128)(2,1)}), bf16[8,32,512]{2,1,0:T(8,128)(2,1)S(1)}, u32[]{:S(2)}, u32[]{:S(2)}) %all-to-all-start.5) | async-done | bytes 262176 | tf_op jit(solution)/shard_map/all_to_all | solution.py:29
  (50 shorter events, 21.8 us)
Async XLA Ops:
  0.6 0.7 copy-start.5
  2.4 14.9 %collective-permute-start.1 = (bf16[256,256]{1,0:T(8,128)(2,1)S(1)}, bf16[256,256]{1,0:T(8,128)(2,1)S(1)}, u32[]{:S(2)}, u32[]{:S(2)}) collective-permute-start(bf16[256,256]{1,0:T(8,128)(2,1)S(1)} %dynamic-slice_select_fusion.cols_ref), channel_id=1, source_target_pairs={{0,8},{8,16},{16,24},{24,32},{32,40},{40,48},{48,56},{56,64},{64,7... | collective-permute-start | bytes 393224 | tf_op jit(solution)/shard_map/ppermute | solution.py:319
  7.8 9.6 %collective-permute-start = (bf16[256,256]{1,0:T(8,128)(2,1)S(1)}, bf16[256,256]{1,0:T(8,128)(2,1)S(1)}, u32[]{:S(2)}, u32[]{:S(2)}) collective-permute-start(bf16[256,256]{1,0:T(8,128)(2,1)S(1)} %dynamic-slice_select_fusion.cols_ref), channel_id=1, source_target_pairs={{8,0},{16,8},{24,16},{32,24},{40,32},{48,40},{56,48},{64,56},{72,6... | collective-permute-start | bytes 393224 | tf_op jit(solution)/shard_map/ppermute | solution.py:320
  13.3 0.7 copy-start.4
  13.9 1.2 copy-start
  15.2 1.1 copy-start.2
  17.3 11.1 %collective-permute-start.2 = (bf16[1024,256]{1,0:T(8,128)(2,1)S(1)}, bf16[1024,256]{1,0:T(8,128)(2,1)S(1)}, u32[]{:S(2)}, u32[]{:S(2)}) collective-permute-start(bf16[1024,256]{1,0:T(8,128)(2,1)S(1)} %get-tuple-element.45), channel_id=1, source_target_pairs={{0,8},{8,0},{16,24},{24,16},{32,40},{40,32},{48,56},{56,48},{64,72... | collective-permute-start | bytes 1572872 | tf_op jit(solution)/shard_map/ppermute | solution.py:34
  25.0 3.4 %collective-permute-start.3 = (bf16[256,512]{1,0:T(8,128)(2,1)S(1)}, bf16[256,512]{1,0:T(8,128)(2,1)S(1)}, u32[]{:S(2)}, u32[]{:S(2)}) collective-permute-start(bf16[256,512]{1,0:T(8,128)(2,1)S(1)} %get-tuple-element.50.applied_ref), channel_id=1, source_target_pairs={{0,8},{8,0},{16,24},{24,16},{32,40},{40,32},{48,56},{56,48},{64,72... | collective-permute-start | bytes 786440 | tf_op jit(solution)/shard_map/ppermute | solution.py:34
  29.7 11.6 %collective-permute-start.4 = (bf16[272,512]{1,0:T(8,128)(2,1)S(1)}, bf16[272,512]{1,0:T(8,128)(2,1)S(1)}, u32[]{:S(2)}, u32[]{:S(2)}) collective-permute-start(bf16[272,512]{1,0:T(8,128)(2,1)S(1)} %get-tuple-element.53), channel_id=1, source_target_pairs={{0,256},{8,264},{16,272},{24,280},{32,288},{40,296},{48,304},{56,3... | collective-permute-start | bytes 835592 | tf_op jit(solution)/shard_map/ppermute | solution.py:39
  32.2 15.5 %collective-permute-start.5 = (bf16[272,512]{1,0:T(8,128)(2,1)S(1)}, bf16[272,512]{1,0:T(8,128)(2,1)S(1)}, u32[]{:S(2)}, u32[]{:S(2)}) collective-permute-start(bf16[272,512]{1,0:T(8,128)(2,1)S(1)} %get-tuple-element.54), channel_id=1, source_target_pairs={{0,128},{8,136},{16,144},{24,152},{32,160},{40,168},{48,176},{56,1... | collective-permute-start | bytes 835592 | tf_op jit(solution)/shard_map/ppermute | solution.py:39
  34.7 13.1 %collective-permute-start.6 = (bf16[272,512]{1,0:T(8,128)(2,1)S(1)}, bf16[272,512]{1,0:T(8,128)(2,1)S(1)}, u32[]{:S(2)}, u32[]{:S(2)}) collective-permute-start(bf16[272,512]{1,0:T(8,128)(2,1)S(1)} %get-tuple-element.55), channel_id=1, source_target_pairs={{0,384},{8,392},{16,400},{24,408},{32,416},{40,424},{48,432},{56,4... | collective-permute-start | bytes 835592 | tf_op jit(solution)/shard_map/ppermute | solution.py:39
  48.2 15.5 %copy-start.3 = (f32[32,256]{1,0:T(8,128)S(1)}, f32[32,256]{1,0:T(8,128)}, u32[]{:S(2)}) copy-start(f32[32,256]{1,0:T(8,128)} %rotation_ref.3) | copy-start | bytes 98308
  77.1 21.8 %all-to-all-start.2 = ((bf16[8,32,896]{2,1,0:T(8,128)(2,1)}), bf16[8,32,896]{2,1,0:T(8,128)(2,1)S(1)}, u32[]{:S(2)}, u32[]{:S(2)}) async-start(bf16[8,32,896]{2,1,0:T(8,128)(2,1)} %get-tuple-element.60), calls=%async_computation.2 | async-start | bytes 917504 | tf_op jit(solution)/shard_map/all_to_all | solution.py:29
  83.9 8.8 %collective-permute-start.9 = (bf16[8,32,512]{2,1,0:T(8,128)(2,1)S(1)}, bf16[8,32,512]{2,1,0:T(8,128)(2,1)S(1)}, u32[]{:S(2)}, u32[]{:S(2)}) collective-permute-start(bf16[8,32,512]{2,1,0:T(8,128)(2,1)S(1)} %all_to_all.31), channel_id=1, source_target_pairs={{0,256},{8,264},{16,272},{24,280},{32,288},{40,296},{48,304},{56,3... | collective-permute-start | bytes 786440 | tf_op jit(solution)/shard_map/ppermute | solution.py:39
  87.5 10.2 %collective-permute-start.8 = (bf16[8,32,512]{2,1,0:T(8,128)(2,1)S(1)}, bf16[8,32,512]{2,1,0:T(8,128)(2,1)S(1)}, u32[]{:S(2)}, u32[]{:S(2)}) collective-permute-start(bf16[8,32,512]{2,1,0:T(8,128)(2,1)S(1)} %all_to_all.31), channel_id=1, source_target_pairs={{0,384},{8,392},{16,400},{24,408},{32,416},{40,424},{48,432},{56,4... | collective-permute-start | bytes 786440 | tf_op jit(solution)/shard_map/ppermute | solution.py:39
  89.4 9.3 %collective-permute-start.7 = (bf16[8,32,512]{2,1,0:T(8,128)(2,1)S(1)}, bf16[8,32,512]{2,1,0:T(8,128)(2,1)S(1)}, u32[]{:S(2)}, u32[]{:S(2)}) collective-permute-start(bf16[8,32,512]{2,1,0:T(8,128)(2,1)S(1)} %all_to_all.31), channel_id=1, source_target_pairs={{0,128},{8,136},{16,144},{24,152},{32,160},{40,168},{48,176},{56,1... | collective-permute-start | bytes 786440 | tf_op jit(solution)/shard_map/ppermute | solution.py:39
  98.9 8.4 %collective-permute-start.10 = (bf16[4,8,32,512]{3,2,1,0:T(8,128)(2,1)S(1)}, bf16[4,8,32,512]{3,2,1,0:T(8,128)(2,1)S(1)}, u32[]{:S(2)}, u32[]{:S(2)}) collective-permute-start(bf16[4,8,32,512]{3,2,1,0:T(8,128)(2,1)S(1)} %pad_maximum_fusion.own_ref), channel_id=1, source_target_pairs={{0,8},{8,0},{16,24},{24,16},{32,40},{40,32},{48,56},{56,48},{64,72... | collective-permute-start | bytes 3145736 | tf_op jit(solution)/shard_map/ppermute | solution.py:34
  123.0 19.3 %all-to-all-start.4 = ((bf16[8,32,512]{2,1,0:T(8,128)(2,1)}), bf16[8,32,512]{2,1,0:T(8,128)(2,1)S(1)}, u32[]{:S(2)}, u32[]{:S(2)}) async-start(bf16[8,32,512]{2,1,0:T(8,128)(2,1)} %get-tuple-element.71), calls=%async_computation.4 | async-start | bytes 524288 | tf_op jit(solution)/shard_map/all_to_all | solution.py:29
  129.9 19.8 %collective-permute-start.13 = (bf16[16,32,256]{2,1,0:T(8,128)(2,1)S(1)}, bf16[16,32,256]{2,1,0:T(8,128)(2,1)S(1)}, u32[]{:S(2)}, u32[]{:S(2)}) collective-permute-start(bf16[16,32,256]{2,1,0:T(8,128)(2,1)S(1)} %all_to_all.32.own0), channel_id=1, source_target_pairs={{0,256},{8,264},{16,272},{24,280},{32,288},{40,296},{48,304},{56,3... | collective-permute-start | bytes 786440 | tf_op jit(solution)/shard_map/ppermute | solution.py:39
  133.1 16.6 %collective-permute-start.12 = (bf16[16,32,256]{2,1,0:T(8,128)(2,1)S(1)}, bf16[16,32,256]{2,1,0:T(8,128)(2,1)S(1)}, u32[]{:S(2)}, u32[]{:S(2)}) collective-permute-start(bf16[16,32,256]{2,1,0:T(8,128)(2,1)S(1)} %all_to_all.32.own0), channel_id=1, source_target_pairs={{0,384},{8,392},{16,400},{24,408},{32,416},{40,424},{48,432},{56,4... | collective-permute-start | bytes 786440 | tf_op jit(solution)/shard_map/ppermute | solution.py:39
  136.2 13.5 %collective-permute-start.11 = (bf16[16,32,256]{2,1,0:T(8,128)(2,1)S(1)}, bf16[16,32,256]{2,1,0:T(8,128)(2,1)S(1)}, u32[]{:S(2)}, u32[]{:S(2)}) collective-permute-start(bf16[16,32,256]{2,1,0:T(8,128)(2,1)S(1)} %all_to_all.32.own0), channel_id=1, source_target_pairs={{0,128},{8,136},{16,144},{24,152},{32,160},{40,168},{48,176},{56,1... | collective-permute-start | bytes 786440 | tf_op jit(solution)/shard_map/ppermute | solution.py:39
  142.3 7.4 %copy-start.1 = (bf16[256,2048]{1,0:T(8,128)(2,1)S(1)}, bf16[256,2048]{1,0:T(8,128)(2,1)}, u32[]{:S(2)}) copy-start(bf16[256,2048]{1,0:T(8,128)(2,1)} %coeffs_ref.2) | copy-start | bytes 3145732
  143.0 12.6 %all-to-all-start.5 = ((bf16[8,32,512]{2,1,0:T(8,128)(2,1)}), bf16[8,32,512]{2,1,0:T(8,128)(2,1)S(1)}, u32[]{:S(2)}, u32[]{:S(2)}) async-start(bf16[8,32,512]{2,1,0:T(8,128)(2,1)} %get-tuple-element.73), calls=%async_computation.5 | async-start | bytes 524288 | tf_op jit(solution)/shard_map/all_to_all | solution.py:29

commit v15 on v14

--- a/solution.py
+++ b/solution.py
@@ -114,8 +114,15 @@
         diag_ref[:, p * width : (p + 1) * width] = sums
 
 
+def own_kernel(place_ref, own_ref, applied_ref, part_ref):
+    rows = part_ref.shape[1]
+    for steps in range(XS):
+        start = pl.multiple_of(lax.rem(place_ref[0] + steps, XS) * rows, rows)
+        part_ref[steps] = small_product(own_ref[pl.ds(start, rows), :], applied_ref[...])
+
+
 def product_kernel(
-    place_ref, own_ref, far_ref, applied_ref, far_applied_ref, up_ref, down_ref, own_diag_ref,
+    place_ref, part_ref, far_ref, far_applied_ref, up_ref, down_ref, own_diag_ref,
     one_ref, three_ref, two_ref, none_ref, diag_ref,
 ):
     x, core = place_ref[0], place_ref[1]
@@ -139,8 +146,8 @@
     tail = jnp.concatenate([high, diag - high, fill], axis=0).astype(bf16)
     for steps, out_ref in ((2, two_ref), (1, one_ref), (3, three_ref), (0, none_ref)):
         start = pl.multiple_of(lax.rem(x + steps, XS) * rows, rows)
-        total = small_product(own_ref[pl.ds(start, rows), :], applied_ref[...])
-        total = total + small_product(far_ref[pl.ds(start, rows), :], far_applied_ref[...])
+        total = small_product(far_ref[pl.ds(start, rows), :], far_applied_ref[...])
+        total = part_ref[steps] + total
         out_ref[:rows, :] = total.astype(out_ref.dtype)
         if steps:
             out_ref[rows:, :] = tail
@@ -183,7 +190,7 @@
     per = width // 128
     for p in range(2):
         parts = [terms[:, p * per + h] + terms[:, 2 * per + p * per + h] for h in range(per)]
-        diag_ref[p] = jnp.concatenate(parts, axis=1)
+        diag_ref[p] = jnp.concatenate(parts, axis=1) * scale
         turned_ref[p] = diag_ref[p].T
     lane = lax.broadcasted_iota(jnp.int32, (rows, COLS), 1)
     down = [
@@ -198,11 +205,11 @@
         cells = across_ref[k].astype(f32)
         cos_part = cells[:, :width] * (diag_ref[0, k : k + 1, :] - down[0])
         sin_part = cells[:, width : 2 * width] * (diag_ref[1, k : k + 1, :] - down[1])
-        rows_ref[k] = (cos_part + sin_part) * scale
+        rows_ref[k] = cos_part + sin_part
 
 
 def square_kernel(
-    scale, place_ref, rows_ref, diag_ref, turned_ref, block_ref, own_ref, away_ref,
+    place_ref, rows_ref, diag_ref, turned_ref, block_ref, own_ref, away_ref,
     base_ref, sent_ref, step_ref,
 ):
     col = place_ref[4]
@@ -217,7 +224,7 @@
         cells = panel.astype(f32)
         cos_part = cells[:, :width] * (across_diag[0] - turned_ref[0, :, k : k + 1])
         sin_part = cells[:, width:] * (across_diag[1] - turned_ref[1, :, k : k + 1])
-        cells = ((cos_part + sin_part) * scale).astype(bf16)
+        cells = (cos_part + sin_part).astype(bf16)
         square = square + small_product(near, cells)
     base_ref[...] = base
     step = (rows_ref[col] + 0.5 * square).astype(bf16)
@@ -349,16 +356,25 @@
     far_applied = other_core(applied)
 
     plane = ZS * row_count
+    (part,) = call(
+        own_kernel,
+        [((XS, plane, both), f32)],
+        [smem] + [vmem] * 2,
+        [],
+        place,
+        own_turned,
+        applied,
+        flops=2**32,
+    )
     sent = ((plane + 16, both), bf16)
     one, three, two, chip, diag = call(
         product_kernel,
         [sent, sent, sent, ((plane, both), f32), ((1, both), f32)],
-        [smem] + [vmem] * 7,
-        [],
-        place,
-        own_turned,
+        [smem] + [vmem] * 6,
+        [],
+        place,
+        part,
         far_turned,
-        applied,
         far_applied,
         from_up,
         from_down,
@@ -408,7 +424,7 @@
         flops=2**33,
     )
     base, square, step = call(
-        functools.partial(square_kernel, scale_factor),
+        square_kernel,
         [
             ((row_count, both), f32),
             ((COLS, row_count, both), bf16),

time: 158 us -> 158 us (level)
    pallas_call x9 -> x10, Pallas kernels: 11.4 us -> 12.1 us  [call(): pl.pallas_call(kernel, out_shape=[jax.ShapeDtypeStruct(*shape) for shape...]
  transfers between devices with their start and end apart: 17 -> 17, of which waited for: 8 -> 8; matrix products, arithmetic and copies ran while one was open for 0% -> 0% of each run, Pallas kernels for 3% -> 4%
where the time goes in v15:
time: 158 us; the launch traced here: 157 us
  starting transfers between devices  72.6 us (46%)
  blocking collectives  40.8 us (26%)
  waiting for transfers between devices  24.9 us (16%)
  Pallas kernels  12.1 us (8%)
  local copies, waits for them, and re-layouts  3.12 us (2%)
  other arithmetic  2.34 us (1%)
    all_to_all x3, blocking collectives, swap(): lax.all_to_all(cells, axis, 0, 0, tiled=True, axis_index_groups=groups)  40.8 us
    ppermute x9, starting transfers between devices, along_x(): lax.ppermute(cells, 'rows', [(i, (i + steps * line) % count) for i in ran...  26.2 us
    all_to_all x3, starting transfers between devices, swap(): lax.all_to_all(cells, axis, 0, 0, tiled=True, axis_index_groups=groups)  20.4 us
    ppermute x3, starting transfers between devices, other_core(): return lax.ppermute(cells, 'rows', [(i, i ^ 1) for i in range(count)])  15.3 us
    ppermute x9, waiting for transfers between devices, along_x(): lax.ppermute(cells, 'rows', [(i, (i + steps * line) % count) for i in ran...  14.9 us
    pallas_call x10, Pallas kernels, call(): pl.pallas_call(kernel, out_shape=[jax.ShapeDtypeStruct(*shape) for shape...  12.1 us
    all_to_all x3, waiting for transfers between devices, swap(): lax.all_to_all(cells, axis, 0, 0, tiled=True, axis_index_groups=groups)  8 us
    ppermute x1, starting transfers between devices, on_device(): from_up = lax.ppermute(own_cols[rows_dev - width:], 'rows', up)  5.39 us
  transfers between devices with their start and end apart: 17, of which 8 were waited for; matrix products, arithmetic and copies ran while one was open for 0% of the time, Pallas kernels for 4%

profile of v15, /device:TPU:1, one launch (start us, length us, event | category | flops | bytes accessed | tf_op | source)
XLA Modules:
  0.0 156.8 jit_solution(9902692585346531093)
XLA Ops:
  2.4 5.4 %collective-permute-start.1 = (bf16[256,256]{1,0:T(8,128)(2,1)S(1)}, bf16[256,256]{1,0:T(8,128)(2,1)S(1)}, u32[]{:S(2)}, u32[]{:S(2)}) collective-permute-start(bf16[256,256]{1,0:T(8,128)(2,1)S(1)} %dynamic-slice_select_fusion.cols_ref), channel_id=1, source_target_pairs={{0,8},{8,16},{16,24},{24,32},{32,40},{40,48},{48,56},{56,64},{64,7... | collective-permute-start | bytes 393224 | tf_op jit(solution)/shard_map/ppermute | solution.py:326
  7.8 5.3 %collective-permute-start = (bf16[256,256]{1,0:T(8,128)(2,1)S(1)}, bf16[256,256]{1,0:T(8,128)(2,1)S(1)}, u32[]{:S(2)}, u32[]{:S(2)}) collective-permute-start(bf16[256,256]{1,0:T(8,128)(2,1)S(1)} %dynamic-slice_select_fusion.cols_ref), channel_id=1, source_target_pairs={{8,0},{16,8},{24,16},{32,24},{40,32},{48,40},{56,48},{64,56},{72,6... | collective-permute-start | bytes 393224 | tf_op jit(solution)/shard_map/ppermute | solution.py:327
  17.3 7.2 %collective-permute-start.2 = (bf16[1024,256]{1,0:T(8,128)(2,1)S(1)}, bf16[1024,256]{1,0:T(8,128)(2,1)S(1)}, u32[]{:S(2)}, u32[]{:S(2)}) collective-permute-start(bf16[1024,256]{1,0:T(8,128)(2,1)S(1)} %get-tuple-element.50), channel_id=1, source_target_pairs={{0,8},{8,0},{16,24},{24,16},{32,40},{40,32},{48,56},{56,48},{64,72... | collective-permute-start | bytes 1572872 | tf_op jit(solution)/shard_map/ppermute | solution.py:34
  29.5 2.4 %collective-permute-start.4 = (bf16[272,512]{1,0:T(8,128)(2,1)S(1)}, bf16[272,512]{1,0:T(8,128)(2,1)S(1)}, u32[]{:S(2)}, u32[]{:S(2)}) collective-permute-start(bf16[272,512]{1,0:T(8,128)(2,1)S(1)} %get-tuple-element.53), channel_id=1, source_target_pairs={{0,256},{8,264},{16,272},{24,280},{32,288},{40,296},{48,304},{56,3... | collective-permute-start | bytes 835592 | tf_op jit(solution)/shard_map/ppermute | solution.py:39
  31.9 2.5 %collective-permute-start.5 = (bf16[272,512]{1,0:T(8,128)(2,1)S(1)}, bf16[272,512]{1,0:T(8,128)(2,1)S(1)}, u32[]{:S(2)}, u32[]{:S(2)}) collective-permute-start(bf16[272,512]{1,0:T(8,128)(2,1)S(1)} %get-tuple-element.54), channel_id=1, source_target_pairs={{0,128},{8,136},{16,144},{24,152},{32,160},{40,168},{48,176},{56,1... | collective-permute-start | bytes 835592 | tf_op jit(solution)/shard_map/ppermute | solution.py:39
  34.5 4.0 %collective-permute-start.6 = (bf16[272,512]{1,0:T(8,128)(2,1)S(1)}, bf16[272,512]{1,0:T(8,128)(2,1)S(1)}, u32[]{:S(2)}, u32[]{:S(2)}) collective-permute-start(bf16[272,512]{1,0:T(8,128)(2,1)S(1)} %get-tuple-element.55), channel_id=1, source_target_pairs={{0,384},{8,392},{16,400},{24,408},{32,416},{40,424},{48,432},{56,4... | collective-permute-start | bytes 835592 | tf_op jit(solution)/shard_map/ppermute | solution.py:39
  38.4 2.6 %collective-permute-done.4 = bf16[272,512]{1,0:T(8,128)(2,1)S(1)} collective-permute-done((bf16[272,512]{1,0:T(8,128)(2,1)S(1)}, bf16[272,512]{1,0:T(8,128)(2,1)S(1)}, u32[]{:S(2)}, u32[]{:S(2)}) %collective-permute-start.4) | collective-permute-done | bytes 278560 | tf_op jit(solution)/shard_map/ppermute | solution.py:39
  41.1 6.3 %collective-permute-done.5 = bf16[272,512]{1,0:T(8,128)(2,1)S(1)} collective-permute-done((bf16[272,512]{1,0:T(8,128)(2,1)S(1)}, bf16[272,512]{1,0:T(8,128)(2,1)S(1)}, u32[]{:S(2)}, u32[]{:S(2)}) %collective-permute-start.5) | collective-permute-done | bytes 278560 | tf_op jit(solution)/shard_map/ppermute | solution.py:39
  48.0 15.5 %all_to_all.30.got_ref = bf16[8,32,640]{2,1,0:T(8,128)(2,1)S(1)} all-to-all(bf16[8,32,640]{2,1,0:T(8,128)(2,1)S(1)} %pad_maximum_fusion.1), channel_id=1, replica_groups={{0,16,32,48,64,80,96,112},{8,24,40,56,72,88,104,120},{128,144,160,176,1..., dimensions={0} | all-to-all | bytes 655360 | tf_op jit(solution)/shard_map/all_to_all | solution.py:29
  64.3 12.6 %all_to_all.31 = bf16[8,32,512]{2,1,0:T(8,128)(2,1)S(1)} all-to-all(bf16[8,32,512]{2,1,0:T(8,128)(2,1)S(1)} %get-tuple-element.58), channel_id=1, replica_groups={{0,16,32,48,64,80,96,112},{8,24,40,56,72,88,104,120},{128,144,160,176,1..., dimensions={0} | all-to-all | bytes 524288 | tf_op jit(solution)/shard_map/all_to_all | solution.py:29
  76.9 6.8 %all-to-all-start.2 = ((bf16[8,32,896]{2,1,0:T(8,128)(2,1)}), bf16[8,32,896]{2,1,0:T(8,128)(2,1)S(1)}, u32[]{:S(2)}, u32[]{:S(2)}) async-start(bf16[8,32,896]{2,1,0:T(8,128)(2,1)} %get-tuple-element.60), calls=%async_computation.2 | async-start | bytes 917504 | tf_op jit(solution)/shard_map/all_to_all | solution.py:29
  83.7 3.5 %collective-permute-start.9 = (bf16[8,32,512]{2,1,0:T(8,128)(2,1)S(1)}, bf16[8,32,512]{2,1,0:T(8,128)(2,1)S(1)}, u32[]{:S(2)}, u32[]{:S(2)}) collective-permute-start(bf16[8,32,512]{2,1,0:T(8,128)(2,1)S(1)} %all_to_all.31), channel_id=1, source_target_pairs={{0,256},{8,264},{16,272},{24,280},{32,288},{40,296},{48,304},{56,3... | collective-permute-start | bytes 786440 | tf_op jit(solution)/shard_map/ppermute | solution.py:39
  89.2 3.4 %collective-permute-start.7 = (bf16[8,32,512]{2,1,0:T(8,128)(2,1)S(1)}, bf16[8,32,512]{2,1,0:T(8,128)(2,1)S(1)}, u32[]{:S(2)}, u32[]{:S(2)}) collective-permute-start(bf16[8,32,512]{2,1,0:T(8,128)(2,1)S(1)} %all_to_all.31), channel_id=1, source_target_pairs={{0,128},{8,136},{16,144},{24,152},{32,160},{40,168},{48,176},{56,1... | collective-permute-start | bytes 786440 | tf_op jit(solution)/shard_map/ppermute | solution.py:39
  92.6 4.9 %collective-permute-done.8 = bf16[8,32,512]{2,1,0:T(8,128)(2,1)S(1)} collective-permute-done((bf16[8,32,512]{2,1,0:T(8,128)(2,1)S(1)}, bf16[8,32,512]{2,1,0:T(8,128)(2,1)S(1)}, u32[]{:S(2)}, u32[]{:S(2)}) %collective-permute-start.8) | collective-permute-done | bytes 262176 | tf_op jit(solution)/shard_map/ppermute | solution.py:39
  98.6 6.1 %collective-permute-start.10 = (bf16[4,8,32,512]{3,2,1,0:T(8,128)(2,1)S(1)}, bf16[4,8,32,512]{3,2,1,0:T(8,128)(2,1)S(1)}, u32[]{:S(2)}, u32[]{:S(2)}) collective-permute-start(bf16[4,8,32,512]{3,2,1,0:T(8,128)(2,1)S(1)} %pad_maximum_fusion.own_ref), channel_id=1, source_target_pairs={{0,8},{8,0},{16,24},{24,16},{32,40},{40,32},{48,56},{56,48},{64,72... | collective-permute-start | bytes 3145736 | tf_op jit(solution)/shard_map/ppermute | solution.py:34
  107.1 2.9 %shard_map.90 = (f32[32,512]{1,0:T(8,128)S(1)}, bf16[8,32,512]{2,1,0:T(8,128)(2,1)}, bf16[16,32,256]{2,1,0:T(8,128)(2,1)S(1)}) custom-call(s32[5]{0:T(128)S(1)} %stack.44.place_ref, f32[8,32,256]{2,1,0:T(8,128)S(1)} %get-tuple-element.62.rows_ref, f32[2,8,256]{2,1,0:T(8,128)S(1)} %get-tuple-element.63.diag_ref, ...), custom_call_target="tpu_custom_call" | custom-call | bytes 1048576 | tf_op jit(solution)/shard_map/pallas_call | solution.py:51
  109.9 12.8 %all_to_all.32.own0 = bf16[16,32,256]{2,1,0:T(8,128)(2,1)S(1)} all-to-all(bf16[16,32,256]{2,1,0:T(8,128)(2,1)S(1)} %get-tuple-element.68), channel_id=1, replica_groups={{112,120,96,104,80,88,64,72,48,56,32,40,16,24,0,8},{240,248,224,232,208..., dimensions={0} | all-to-all | bytes 524288 | tf_op jit(solution)/shard_map/all_to_all | solution.py:29
  122.7 6.9 %all-to-all-start.4 = ((bf16[8,32,512]{2,1,0:T(8,128)(2,1)}), bf16[8,32,512]{2,1,0:T(8,128)(2,1)S(1)}, u32[]{:S(2)}, u32[]{:S(2)}) async-start(bf16[8,32,512]{2,1,0:T(8,128)(2,1)} %get-tuple-element.71), calls=%async_computation.4 | async-start | bytes 524288 | tf_op jit(solution)/shard_map/all_to_all | solution.py:29
  129.6 3.2 %collective-permute-start.13 = (bf16[16,32,256]{2,1,0:T(8,128)(2,1)S(1)}, bf16[16,32,256]{2,1,0:T(8,128)(2,1)S(1)}, u32[]{:S(2)}, u32[]{:S(2)}) collective-permute-start(bf16[16,32,256]{2,1,0:T(8,128)(2,1)S(1)} %all_to_all.32.own0), channel_id=1, source_target_pairs={{0,256},{8,264},{16,272},{24,280},{32,288},{40,296},{48,304},{56,3... | collective-permute-start | bytes 786440 | tf_op jit(solution)/shard_map/ppermute | solution.py:39
  132.8 3.0 %collective-permute-start.12 = (bf16[16,32,256]{2,1,0:T(8,128)(2,1)S(1)}, bf16[16,32,256]{2,1,0:T(8,128)(2,1)S(1)}, u32[]{:S(2)}, u32[]{:S(2)}) collective-permute-start(bf16[16,32,256]{2,1,0:T(8,128)(2,1)S(1)} %all_to_all.32.own0), channel_id=1, source_target_pairs={{0,384},{8,392},{16,400},{24,408},{32,416},{40,424},{48,432},{56,4... | collective-permute-start | bytes 786440 | tf_op jit(solution)/shard_map/ppermute | solution.py:39
  135.9 2.2 %collective-permute-start.11 = (bf16[16,32,256]{2,1,0:T(8,128)(2,1)S(1)}, bf16[16,32,256]{2,1,0:T(8,128)(2,1)S(1)}, u32[]{:S(2)}, u32[]{:S(2)}) collective-permute-start(bf16[16,32,256]{2,1,0:T(8,128)(2,1)S(1)} %all_to_all.32.own0), channel_id=1, source_target_pairs={{0,128},{8,136},{16,144},{24,152},{32,160},{40,168},{48,176},{56,1... | collective-permute-start | bytes 786440 | tf_op jit(solution)/shard_map/ppermute | solution.py:39
  138.1 3.9 %all-to-all-done.4.got_ref = bf16[8,32,512]{2,1,0:T(8,128)(2,1)S(1)} async-done(((bf16[8,32,512]{2,1,0:T(8,128)(2,1)}), bf16[8,32,512]{2,1,0:T(8,128)(2,1)S(1)}, u32[]{:S(2)}, u32[]{:S(2)}) %all-to-all-start.4) | async-done | bytes 262176 | tf_op jit(solution)/shard_map/all_to_all | solution.py:29
  142.7 6.6 %all-to-all-start.5 = ((bf16[8,32,512]{2,1,0:T(8,128)(2,1)}), bf16[8,32,512]{2,1,0:T(8,128)(2,1)S(1)}, u32[]{:S(2)}, u32[]{:S(2)}) async-start(bf16[8,32,512]{2,1,0:T(8,128)(2,1)} %get-tuple-element.73), calls=%async_computation.5 | async-start | bytes 524288 | tf_op jit(solution)/shard_map/all_to_all | solution.py:29
  151.2 4.1 %all-to-all-done.5.half_ref = bf16[8,32,512]{2,1,0:T(8,128)(2,1)S(1)} async-done(((bf16[8,32,512]{2,1,0:T(8,128)(2,1)}), bf16[8,32,512]{2,1,0:T(8,128)(2,1)S(1)}, u32[]{:S(2)}, u32[]{:S(2)}) %all-to-all-start.5) | async-done | bytes 262176 | tf_op jit(solution)/shard_map/all_to_all | solution.py:29
  (51 shorter events, 21.6 us)
Async XLA Ops:
  2.4 14.9 %collective-permute-start.1 = (bf16[256,256]{1,0:T(8,128)(2,1)S(1)}, bf16[256,256]{1,0:T(8,128)(2,1)S(1)}, u32[]{:S(2)}, u32[]{:S(2)}) collective-permute-start(bf16[256,256]{1,0:T(8,128)(2,1)S(1)} %dynamic-slice_select_fusion.cols_ref), channel_id=1, source_target_pairs={{0,8},{8,16},{16,24},{24,32},{32,40},{40,48},{48,56},{56,64},{64,7... | collective-permute-start | bytes 393224 | tf_op jit(solution)/shard_map/ppermute | solution.py:326
  7.8 9.6 %collective-permute-start = (bf16[256,256]{1,0:T(8,128)(2,1)S(1)}, bf16[256,256]{1,0:T(8,128)(2,1)S(1)}, u32[]{:S(2)}, u32[]{:S(2)}) collective-permute-start(bf16[256,256]{1,0:T(8,128)(2,1)S(1)} %dynamic-slice_select_fusion.cols_ref), channel_id=1, source_target_pairs={{8,0},{16,8},{24,16},{32,24},{40,32},{48,40},{56,48},{64,56},{72,6... | collective-permute-start | bytes 393224 | tf_op jit(solution)/shard_map/ppermute | solution.py:327
  13.3 1.2 copy-start
  14.5 1.1 copy-start.2
  15.6 0.7 copy-start.4
  17.3 11.1 %collective-permute-start.2 = (bf16[1024,256]{1,0:T(8,128)(2,1)S(1)}, bf16[1024,256]{1,0:T(8,128)(2,1)S(1)}, u32[]{:S(2)}, u32[]{:S(2)}) collective-permute-start(bf16[1024,256]{1,0:T(8,128)(2,1)S(1)} %get-tuple-element.50), channel_id=1, source_target_pairs={{0,8},{8,0},{16,24},{24,16},{32,40},{40,32},{48,56},{56,48},{64,72... | collective-permute-start | bytes 1572872 | tf_op jit(solution)/shard_map/ppermute | solution.py:34
  25.0 3.4 %collective-permute-start.3 = (bf16[256,512]{1,0:T(8,128)(2,1)S(1)}, bf16[256,512]{1,0:T(8,128)(2,1)S(1)}, u32[]{:S(2)}, u32[]{:S(2)}) collective-permute-start(bf16[256,512]{1,0:T(8,128)(2,1)S(1)} %get-tuple-element.49.applied_ref), channel_id=1, source_target_pairs={{0,8},{8,0},{16,24},{24,16},{32,40},{40,32},{48,56},{56,48},{64,72... | collective-permute-start | bytes 786440 | tf_op jit(solution)/shard_map/ppermute | solution.py:34
  29.5 11.6 %collective-permute-start.4 = (bf16[272,512]{1,0:T(8,128)(2,1)S(1)}, bf16[272,512]{1,0:T(8,128)(2,1)S(1)}, u32[]{:S(2)}, u32[]{:S(2)}) collective-permute-start(bf16[272,512]{1,0:T(8,128)(2,1)S(1)} %get-tuple-element.53), channel_id=1, source_target_pairs={{0,256},{8,264},{16,272},{24,280},{32,288},{40,296},{48,304},{56,3... | collective-permute-start | bytes 835592 | tf_op jit(solution)/shard_map/ppermute | solution.py:39
  31.9 15.5 %collective-permute-start.5 = (bf16[272,512]{1,0:T(8,128)(2,1)S(1)}, bf16[272,512]{1,0:T(8,128)(2,1)S(1)}, u32[]{:S(2)}, u32[]{:S(2)}) collective-permute-start(bf16[272,512]{1,0:T(8,128)(2,1)S(1)} %get-tuple-element.54), channel_id=1, source_target_pairs={{0,128},{8,136},{16,144},{24,152},{32,160},{40,168},{48,176},{56,1... | collective-permute-start | bytes 835592 | tf_op jit(solution)/shard_map/ppermute | solution.py:39
  34.5 13.1 %collective-permute-start.6 = (bf16[272,512]{1,0:T(8,128)(2,1)S(1)}, bf16[272,512]{1,0:T(8,128)(2,1)S(1)}, u32[]{:S(2)}, u32[]{:S(2)}) collective-permute-start(bf16[272,512]{1,0:T(8,128)(2,1)S(1)} %get-tuple-element.55), channel_id=1, source_target_pairs={{0,384},{8,392},{16,400},{24,408},{32,416},{40,424},{48,432},{56,4... | collective-permute-start | bytes 835592 | tf_op jit(solution)/shard_map/ppermute | solution.py:39
  47.6 15.9 %copy-start.3 = (f32[32,256]{1,0:T(8,128)S(1)}, f32[32,256]{1,0:T(8,128)}, u32[]{:S(2)}) copy-start(f32[32,256]{1,0:T(8,128)} %rotation_ref.3) | copy-start | bytes 98308
  76.9 21.8 %all-to-all-start.2 = ((bf16[8,32,896]{2,1,0:T(8,128)(2,1)}), bf16[8,32,896]{2,1,0:T(8,128)(2,1)S(1)}, u32[]{:S(2)}, u32[]{:S(2)}) async-start(bf16[8,32,896]{2,1,0:T(8,128)(2,1)} %get-tuple-element.60), calls=%async_computation.2 | async-start | bytes 917504 | tf_op jit(solution)/shard_map/all_to_all | solution.py:29
  83.7 8.8 %collective-permute-start.9 = (bf16[8,32,512]{2,1,0:T(8,128)(2,1)S(1)}, bf16[8,32,512]{2,1,0:T(8,128)(2,1)S(1)}, u32[]{:S(2)}, u32[]{:S(2)}) collective-permute-start(bf16[8,32,512]{2,1,0:T(8,128)(2,1)S(1)} %all_to_all.31), channel_id=1, source_target_pairs={{0,256},{8,264},{16,272},{24,280},{32,288},{40,296},{48,304},{56,3... | collective-permute-start | bytes 786440 | tf_op jit(solution)/shard_map/ppermute | solution.py:39
  87.2 10.2 %collective-permute-start.8 = (bf16[8,32,512]{2,1,0:T(8,128)(2,1)S(1)}, bf16[8,32,512]{2,1,0:T(8,128)(2,1)S(1)}, u32[]{:S(2)}, u32[]{:S(2)}) collective-permute-start(bf16[8,32,512]{2,1,0:T(8,128)(2,1)S(1)} %all_to_all.31), channel_id=1, source_target_pairs={{0,384},{8,392},{16,400},{24,408},{32,416},{40,424},{48,432},{56,4... | collective-permute-start | bytes 786440 | tf_op jit(solution)/shard_map/ppermute | solution.py:39
  89.2 9.3 %collective-permute-start.7 = (bf16[8,32,512]{2,1,0:T(8,128)(2,1)S(1)}, bf16[8,32,512]{2,1,0:T(8,128)(2,1)S(1)}, u32[]{:S(2)}, u32[]{:S(2)}) collective-permute-start(bf16[8,32,512]{2,1,0:T(8,128)(2,1)S(1)} %all_to_all.31), channel_id=1, source_target_pairs={{0,128},{8,136},{16,144},{24,152},{32,160},{40,168},{48,176},{56,1... | collective-permute-start | bytes 786440 | tf_op jit(solution)/shard_map/ppermute | solution.py:39
  98.6 8.4 %collective-permute-start.10 = (bf16[4,8,32,512]{3,2,1,0:T(8,128)(2,1)S(1)}, bf16[4,8,32,512]{3,2,1,0:T(8,128)(2,1)S(1)}, u32[]{:S(2)}, u32[]{:S(2)}) collective-permute-start(bf16[4,8,32,512]{3,2,1,0:T(8,128)(2,1)S(1)} %pad_maximum_fusion.own_ref), channel_id=1, source_target_pairs={{0,8},{8,0},{16,24},{24,16},{32,40},{40,32},{48,56},{56,48},{64,72... | collective-permute-start | bytes 3145736 | tf_op jit(solution)/shard_map/ppermute | solution.py:34
  122.7 19.3 %all-to-all-start.4 = ((bf16[8,32,512]{2,1,0:T(8,128)(2,1)}), bf16[8,32,512]{2,1,0:T(8,128)(2,1)S(1)}, u32[]{:S(2)}, u32[]{:S(2)}) async-start(bf16[8,32,512]{2,1,0:T(8,128)(2,1)} %get-tuple-element.71), calls=%async_computation.4 | async-start | bytes 524288 | tf_op jit(solution)/shard_map/all_to_all | solution.py:29
  129.6 19.8 %collective-permute-start.13 = (bf16[16,32,256]{2,1,0:T(8,128)(2,1)S(1)}, bf16[16,32,256]{2,1,0:T(8,128)(2,1)S(1)}, u32[]{:S(2)}, u32[]{:S(2)}) collective-permute-start(bf16[16,32,256]{2,1,0:T(8,128)(2,1)S(1)} %all_to_all.32.own0), channel_id=1, source_target_pairs={{0,256},{8,264},{16,272},{24,280},{32,288},{40,296},{48,304},{56,3... | collective-permute-start | bytes 786440 | tf_op jit(solution)/shard_map/ppermute | solution.py:39
  132.8 16.6 %collective-permute-start.12 = (bf16[16,32,256]{2,1,0:T(8,128)(2,1)S(1)}, bf16[16,32,256]{2,1,0:T(8,128)(2,1)S(1)}, u32[]{:S(2)}, u32[]{:S(2)}) collective-permute-start(bf16[16,32,256]{2,1,0:T(8,128)(2,1)S(1)} %all_to_all.32.own0), channel_id=1, source_target_pairs={{0,384},{8,392},{16,400},{24,408},{32,416},{40,424},{48,432},{56,4... | collective-permute-start | bytes 786440 | tf_op jit(solution)/shard_map/ppermute | solution.py:39
  135.9 13.5 %collective-permute-start.11 = (bf16[16,32,256]{2,1,0:T(8,128)(2,1)S(1)}, bf16[16,32,256]{2,1,0:T(8,128)(2,1)S(1)}, u32[]{:S(2)}, u32[]{:S(2)}) collective-permute-start(bf16[16,32,256]{2,1,0:T(8,128)(2,1)S(1)} %all_to_all.32.own0), channel_id=1, source_target_pairs={{0,128},{8,136},{16,144},{24,152},{32,160},{40,168},{48,176},{56,1... | collective-permute-start | bytes 786440 | tf_op jit(solution)/shard_map/ppermute | solution.py:39
  142.0 7.4 %copy-start.1 = (bf16[256,2048]{1,0:T(8,128)(2,1)S(1)}, bf16[256,2048]{1,0:T(8,128)(2,1)}, u32[]{:S(2)}) copy-start(bf16[256,2048]{1,0:T(8,128)(2,1)} %coeffs_ref.2) | copy-start | bytes 3145732
  142.0 7.4 %copy-start.5 = (s32[2]{0:T(128)S(1)}, s32[2]{0:T(128)}, u32[]{:S(2)}) copy-start(s32[2]{0:T(128)} %size_ref.1) | copy-start | bytes 28
  142.7 12.6 %all-to-all-start.5 = ((bf16[8,32,512]{2,1,0:T(8,128)(2,1)}), bf16[8,32,512]{2,1,0:T(8,128)(2,1)S(1)}, u32[]{:S(2)}, u32[]{:S(2)}) async-start(bf16[8,32,512]{2,1,0:T(8,128)(2,1)} %get-tuple-element.73), calls=%async_computation.5 | async-start | bytes 524288 | tf_op jit(solution)/shard_map/all_to_all | solution.py:29
